TPU v7x, 32 devices: a whole 2x2x4 slice. The times are simulated.
32 devices in a mesh: dp: 8 (over z, x), seq: 4 (over y, core).
Axes of the slice: x: 2, y: 2, z: 4, core: 2. Of those that a mesh axis runs over, the one named last changes fastest.
Arguments:
- grad_out: bfloat16 [8, 1024, 4096], P('dp', 'seq'), may hold values from -6 to 6
- queries: bfloat16 [8, 1024, 4096], P('dp', 'seq'), may hold values from -45 to 45
- keys: bfloat16 [8, 1024, 1024], P('dp', 'seq'), may hold values from -4 to 4
- values: bfloat16 [8, 1024, 1024], P('dp', 'seq'), may hold values from -6 to 6
- out_weight: bfloat16 [4096, 4096], P('seq'), may hold values from -0.09375 to 0.09375
- doc_starts: int32 [8, 8], P('dp'), may hold values from 0 to 1020, as said below
Outputs:
- grad_queries: bfloat16 [8, 1024, 4096], P('dp', 'seq')
- grad_keys: bfloat16 [8, 1024, 1024], P('dp', 'seq')
- grad_values: bfloat16 [8, 1024, 1024], P('dp', 'seq')
- grad_weight: float32 [4096, 4096], P('seq', 'dp')
Inputs may be any that keep to these rules, and one draw needn't show every extreme that they name: `doc_starts`: each row strictly increases, holds multiples of 4, begins with 0 and ends with 1020.
All inputs are finite; a program needn't handle non-finite values.
Results may differ from a plain program's by a relative error of at most 0.015.
Values may be sent and summed in bfloat16 or wider, within the bound.
No kernel may reach another device: no remote copies, remote signals or barrier semaphores. Data moves between devices by JAX's collectives and lax.ppermute only.
A program may use at most 128 MiB of HBM per device.

v0:
```python
import functools
import math

import jax
import jax.numpy as jnp
from jax import lax
from jax.experimental import pallas as pl
from jax.experimental.pallas import tpu as pltpu
from jax.sharding import PartitionSpec as P

HEADS = 32
KV_HEADS = 8
HEAD_DIM = 128
GROUP = HEADS // KV_HEADS
MASKED = -1e30
NT = (((1,), (1,)), ((), ()))
NN = (((1,), (0,)), ((), ()))


def mm(a, b, dims=NN):
    return lax.dot_general(a, b, dims, preferred_element_type=jnp.float32)


def params(mib):
    return pltpu.CompilerParams(vmem_limit_bytes=mib * 2**20)


def cost(flops, nbytes):
    return pl.CostEstimate(flops=int(flops) // 1000, bytes_accessed=int(nbytes) // 1000, transcendentals=0)


ANY = pl.BlockSpec(memory_space=pl.ANY)


def shape(dims, dtype=jnp.bfloat16):
    return jax.ShapeDtypeStruct(dims, dtype)


def gate(arrays, *tokens):
    return list(lax.optimization_barrier((*arrays, *tokens)))[: len(arrays)]


def pack_kernel(parts, info_ref, *refs):
    q_refs, k_refs, v_refs, out_refs = (refs[i * parts : (i + 1) * parts] for i in range(4))
    wide = GROUP * HEAD_DIM
    for d in range(parts):
        out_refs[d][:, :wide] = q_refs[d][...]
        out_refs[d][:, wide : wide + HEAD_DIM] = k_refs[d][...]
        out_refs[d][:, wide + HEAD_DIM :] = v_refs[d][...]


def pack(info, queries, keys, values, parts, groups, gp):
    rows = queries.shape[0]
    wide = GROUP * HEAD_DIM
    step = min(128, rows)

    def pick(d):
        return lambda i, info: (i, (info[0] ^ d) * groups + gp)

    return pl.pallas_call(
        functools.partial(pack_kernel, parts),
        grid_spec=pltpu.PrefetchScalarGridSpec(
            num_scalar_prefetch=1,
            grid=(rows // step,),
            in_specs=[pl.BlockSpec((step, wide), pick(d)) for d in range(parts)]
            + [pl.BlockSpec((step, HEAD_DIM), pick(d)) for d in range(parts)] * 2,
            out_specs=[
                pl.BlockSpec((step, wide + 2 * HEAD_DIM), lambda i, info: (i, 0))
                for d in range(parts)
            ],
        ),
        out_shape=[shape((rows, wide + 2 * HEAD_DIM)) for d in range(parts)],
        compiler_params=params(56),
        cost_estimate=cost(0, 4 * parts * rows * (wide + 2 * HEAD_DIM)),
        name="pack",
    )(info, *[queries] * parts, *[keys] * parts, *[values] * parts)


def column(share, c, chunks, width):
    return slice((share * chunks + c) * width, (share * chunks + c + 1) * width)


def pack_chunks_kernel(orders, shares, width, g_ref, *out_refs):
    for c, order in enumerate(orders):
        for place in range(shares):
            share = unplace(place, order)
            out_refs[c][:, place * width : (place + 1) * width] = g_ref[
                :, column(share, c, len(orders), width)
            ]


def pack_chunks(cotangent, orders, shares, width):
    rows, model = cotangent.shape
    step = min(64, rows)
    return pl.pallas_call(
        functools.partial(pack_chunks_kernel, orders, shares, width),
        grid=(rows // step,),
        in_specs=[pl.BlockSpec((step, model), lambda i: (i, 0))],
        out_specs=[pl.BlockSpec((step, shares * width), lambda i: (i, 0))] * len(orders),
        out_shape=[shape((rows, shares * width)) for order in orders],
        compiler_params=params(56),
        cost_estimate=cost(0, 4 * rows * model),
        name="pack_chunks",
    )(cotangent)


def unpack_kernel(parts, groups, info_ref, *refs):
    count = parts * groups
    q_ref, k_ref, v_ref = refs[count:]
    wide = GROUP * HEAD_DIM
    for gp in range(groups):
        for d in range(parts):
            piece = refs[gp * parts + d]
            place = (info_ref[0] ^ d) * groups + gp
            q_ref[:, pl.ds(pl.multiple_of(place * wide, wide), wide)] = piece[:, :wide]
            narrow = pl.ds(pl.multiple_of(place * HEAD_DIM, HEAD_DIM), HEAD_DIM)
            k_ref[:, narrow] = piece[:, wide : wide + HEAD_DIM]
            v_ref[:, narrow] = piece[:, wide + HEAD_DIM :]


def unpack(info, pieces, parts, groups):
    rows, cols = pieces[0].shape
    wide = GROUP * HEAD_DIM
    step = min(64, rows)
    total = parts * groups
    widths = (total * wide, total * HEAD_DIM, total * HEAD_DIM)
    return pl.pallas_call(
        functools.partial(unpack_kernel, parts, groups),
        grid_spec=pltpu.PrefetchScalarGridSpec(
            num_scalar_prefetch=1,
            grid=(rows // step,),
            in_specs=[pl.BlockSpec((step, cols), lambda i, info: (i, 0))] * total,
            out_specs=[pl.BlockSpec((step, w), lambda i, info: (i, 0)) for w in widths],
        ),
        out_shape=[shape((rows, w)) for w in widths],
        compiler_params=params(16),
        cost_estimate=cost(0, 4 * total * rows * cols),
        name="unpack",
    )(info, *pieces)


def pair_index(qb, kb):
    return qb * (qb + 1) // 2 + kb


def prepare(parts, block, docs, info_ref, bias_ref, open_ref):
    down = lax.broadcasted_iota(jnp.int32, (block, block), 0)
    across = lax.broadcasted_iota(jnp.int32, (1, block), 1)
    for qb in range(parts):
        lanes = qb * block + across
        opening = jnp.zeros((1, block), jnp.int32)
        first = jnp.int32(0)
        for n in range(docs):
            start = info_ref[2 + n]
            opening = jnp.where(start <= lanes, jnp.maximum(opening, start), opening)
            first = jnp.where(start <= qb * block, jnp.maximum(first, start), first)
        open_ref[qb] = first // block
        for kb in range(qb + 1):
            seen = down >= opening - kb * block
            if kb == qb:
                seen = seen & (down <= across)
            bias_ref[pair_index(qb, kb)] = jnp.where(seen, 0.0, MASKED).astype(jnp.float32)


def flip(x):
    return jnp.transpose(x.astype(jnp.float32))


def head_cols(h):
    return slice(h * HEAD_DIM, (h + 1) * HEAD_DIM)


def forward_kernel(parts, block, docs, info_ref, *refs):
    pieces = refs[:parts]
    out_ref, lse_ref = refs[parts : parts + 2]
    bias_ref, open_ref, q_s, k_s, vt_s, top_s, sum_s, acc_s = refs[parts + 2 :]
    me = info_ref[0]
    wide = GROUP * HEAD_DIM
    factor = math.log2(math.e) / math.sqrt(HEAD_DIM)
    prepare(parts, block, docs, info_ref, bias_ref, open_ref)
    for d in range(parts):
        q_s[me ^ d] = pieces[d][:, :wide]
        k_s[me ^ d] = pieces[d][:, wide : wide + HEAD_DIM]
        vt_s[me ^ d] = flip(pieces[d][:, wide + HEAD_DIM :]).astype(jnp.bfloat16)

    def rows_of(qb, carry):
        top_s[...] = jnp.full_like(top_s, 2.0 * MASKED)
        sum_s[...] = jnp.zeros_like(sum_s)
        acc_s[...] = jnp.zeros_like(acc_s)

        def pair(back, carry):
            kb = qb - back
            bias = bias_ref.at[pair_index(qb, kb)]
            for h in range(GROUP):
                raw = mm(k_s[kb], q_s[qb, :, head_cols(h)], NT) * factor + bias[...]
                old = top_s[h]
                top = jnp.maximum(old, jnp.max(raw, axis=0, keepdims=True))
                shrink = jnp.exp2(old - top)
                raised = jnp.exp2(raw - top)
                top_s[h] = top
                sum_s[h] = sum_s[h] * shrink + jnp.sum(raised, axis=0, keepdims=True)
                acc_s[h] = acc_s[h] * shrink + mm(vt_s[kb], raised.astype(jnp.bfloat16))
            return carry

        lax.fori_loop(0, qb - open_ref[qb] + 1, pair, 0)
        for h in range(GROUP):
            out_ref[me ^ qb, head_cols(h)] = (acc_s[h] / sum_s[h]).astype(jnp.bfloat16)
            lse_ref[h, me ^ qb] = jnp.broadcast_to(top_s[h] + jnp.log2(sum_s[h]), (8, block))
        return carry

    lax.fori_loop(0, parts, rows_of, 0)


def whole_block(dims):
    return pl.BlockSpec(dims, lambda i, info: (0,) * len(dims))


def attention(info, pieces, token, parts, docs):
    block, cols = pieces[0].shape
    pairs = parts * (parts + 1) // 2
    wide = GROUP * HEAD_DIM
    vm = pltpu.VMEM
    return pl.pallas_call(
        functools.partial(forward_kernel, parts, block, docs),
        grid_spec=pltpu.PrefetchScalarGridSpec(
            num_scalar_prefetch=1,
            grid=(1,),
            in_specs=[whole_block((block, cols))] * parts,
            out_specs=[
                whole_block((parts, wide, block)),
                whole_block((GROUP, parts, 8, block)),
            ],
            scratch_shapes=[
                vm((pairs, block, block), jnp.float32),
                pltpu.SMEM((parts,), jnp.int32),
                vm((parts, block, wide), jnp.bfloat16),
                vm((parts, block, HEAD_DIM), jnp.bfloat16),
                vm((parts, HEAD_DIM, block), jnp.bfloat16),
                vm((GROUP, 1, block), jnp.float32),
                vm((GROUP, 1, block), jnp.float32),
                vm((GROUP, HEAD_DIM, block), jnp.float32),
            ],
        ),
        out_shape=[
            shape((parts, wide, block)),
            shape((GROUP, parts, 8, block), jnp.float32),
        ],
        compiler_params=params(16),
        cost_estimate=cost(8e9, 4 * parts * block * cols),
        name="attention",
    )(gate([info], token)[0], *pieces)


def backward_kernel(parts, block, docs, info_ref, *refs):
    pieces = refs[:parts]
    grad_ref, out_ref, lse_ref = refs[parts : parts + 3]
    res_ref = refs[parts + 3]
    bias_ref, open_ref, q_s, k_s, kt_s, v_s, dk_s, dv_s, dq_s, delta_s = refs[parts + 4 :]
    me = info_ref[0]
    wide = GROUP * HEAD_DIM
    scale = 1.0 / math.sqrt(HEAD_DIM)
    factor = math.log2(math.e) * scale
    prepare(parts, block, docs, info_ref, bias_ref, open_ref)
    for d in range(parts):
        q_s[me ^ d] = pieces[d][:, :wide]
        k_s[me ^ d] = pieces[d][:, wide : wide + HEAD_DIM]
        kt_s[me ^ d] = flip(pieces[d][:, wide : wide + HEAD_DIM]).astype(jnp.bfloat16)
        v_s[me ^ d] = pieces[d][:, wide + HEAD_DIM :]
    dk_s[...] = jnp.zeros_like(dk_s)
    dv_s[...] = jnp.zeros_like(dv_s)

    def rows_of(qb, carry):
        spot = me ^ qb
        dq_s[...] = jnp.zeros_like(dq_s)
        for h in range(GROUP):
            product = flip(grad_ref[spot, :, head_cols(h)]) * out_ref[spot, head_cols(h)].astype(
                jnp.float32
            )
            delta_s[h] = jnp.sum(product, axis=0, keepdims=True)

        def pair(back, carry):
            kb = qb - back
            bias = bias_ref.at[pair_index(qb, kb)]
            key, value = k_s[kb], v_s[kb]
            dk = dk_s[kb]
            dv = dv_s[kb]
            for h in range(GROUP):
                query, grad = q_s[qb, :, head_cols(h)], grad_ref[spot, :, head_cols(h)]
                raw = mm(key, query, NT) * factor + bias[...]
                probs = jnp.exp2(raw - lse_ref[h, spot, :1])
                dv += mm(probs.astype(jnp.bfloat16), grad)
                slope = (probs * (mm(value, grad, NT) - delta_s[h])).astype(jnp.bfloat16)
                dk += mm(slope, query)
                dq_s[h] += mm(kt_s[kb], slope)
            dk_s[kb] = dk
            dv_s[kb] = dv
            return carry

        lax.fori_loop(0, qb - open_ref[qb] + 1, pair, 0)
        for h in range(GROUP):
            res_ref[spot, :, head_cols(h)] = (jnp.transpose(dq_s[h]) * scale).astype(jnp.bfloat16)
        return carry

    lax.fori_loop(0, parts, rows_of, 0)
    for kb in range(parts):
        res_ref[me ^ kb, :, wide : wide + HEAD_DIM] = (dk_s[kb] * scale).astype(jnp.bfloat16)
        res_ref[me ^ kb, :, wide + HEAD_DIM :] = dv_s[kb].astype(jnp.bfloat16)


def attention_back(info, pieces, grads, out, lse, token, parts, docs, gp):
    block, cols = pieces[0].shape
    pairs = parts * (parts + 1) // 2
    wide = GROUP * HEAD_DIM
    vm = pltpu.VMEM
    return pl.pallas_call(
        functools.partial(backward_kernel, parts, block, docs),
        grid_spec=pltpu.PrefetchScalarGridSpec(
            num_scalar_prefetch=1,
            grid=(1,),
            in_specs=[whole_block((block, cols))] * parts
            + [
                pl.BlockSpec((parts, block, wide), lambda i, info: (0, 0, gp)),
                whole_block((parts, wide, block)),
                whole_block((GROUP, parts, 8, block)),
            ],
            out_specs=whole_block((parts, block, cols)),
            scratch_shapes=[
                vm((pairs, block, block), jnp.float32),
                pltpu.SMEM((parts,), jnp.int32),
                vm((parts, block, wide), jnp.bfloat16),
                vm((parts, block, HEAD_DIM), jnp.bfloat16),
                vm((parts, HEAD_DIM, block), jnp.bfloat16),
                vm((parts, block, HEAD_DIM), jnp.bfloat16),
                vm((parts, block, HEAD_DIM), jnp.float32),
                vm((parts, block, HEAD_DIM), jnp.float32),
                vm((GROUP, HEAD_DIM, block), jnp.float32),
                vm((GROUP, 1, block), jnp.float32),
            ],
        ),
        out_shape=shape((parts, block, cols)),
        compiler_params=params(20),
        cost_estimate=cost(14e9, 8 * parts * block * cols),
        name="attention_back",
    )(gate([info], token)[0], *pieces, grads, out, lse)


def place_of(share, order):
    out = 0 * share
    for k, bit in enumerate(order):
        out = out + ((share >> bit) & 1) * (1 << k)
    return out


def unplace(place, order):
    out = 0 * place
    for k, bit in enumerate(order):
        out = out + ((place >> k) & 1) * (1 << bit)
    return out


def reverse_bits(x, bits):
    out = 0 * x
    for b in range(bits):
        out = out + ((x >> b) & 1) * (1 << (bits - 1 - b))
    return out


def weight_kernel(parts, groups, width, order, info_ref, *refs):
    outs, lows, highs = refs[:groups], refs[groups : groups + 2], refs[groups + 2 : groups + 4]
    chunk = refs[groups + 4 : groups + 2 + parts]
    keep_ref, send_ref = refs[groups + 2 + parts :]
    odd = ((info_ref[1] >> order[0]) & 1) == 1
    rows = GROUP * HEAD_DIM
    grads = [jnp.concatenate([lows[d][...], highs[d][...]], axis=1) for d in range(2)]
    for gp in range(groups):
        total = mm(outs[gp][0], grads[0]) + mm(outs[gp][1], grads[1])
        for d in range(2, parts):
            total += mm(outs[gp][d], chunk[d - 2][...])
        low, high = total[:, :width], total[:, width:]
        spot = slice(gp * rows, (gp + 1) * rows)
        keep_ref[0, spot] = jnp.where(odd, high, low)
        send_ref[0, spot] = jnp.where(odd, low, high).astype(jnp.bfloat16)


def weight_terms(info, outs, near, chunk, token, shares, c, chunks, width, order):
    groups, parts = len(outs), 2 + len(chunk)
    _, rows, block = outs[0].shape
    half = shares // 2
    bits = half.bit_length() - 1
    spot = pl.BlockSpec((1, groups * rows, width), lambda t, info: (reverse_bits(t, bits), 0, 0))

    def mate(t, info):
        return t ^ (place_of(info[1], order) >> 1)

    def original(side):
        return pl.BlockSpec(
            (block, width),
            lambda t, info: (0, unplace(2 * mate(t, info) + side, order) * chunks + c),
        )

    return pl.pallas_call(
        functools.partial(weight_kernel, parts, groups, width, order),
        grid_spec=pltpu.PrefetchScalarGridSpec(
            num_scalar_prefetch=1,
            grid=(half,),
            in_specs=[pl.BlockSpec((parts, rows, block), lambda t, info: (0, 0, 0))] * groups
            + [original(0)] * 2
            + [original(1)] * 2
            + [pl.BlockSpec((block, 2 * width), lambda t, info: (0, mate(t, info)))] * len(chunk),
            out_specs=[spot, spot],
        ),
        out_shape=[
            shape((half, groups * rows, width), jnp.float32),
            shape((half, groups * rows, width)),
        ],
        compiler_params=params(16),
        cost_estimate=cost(
            2 * groups * rows * block * parts * shares * width, 8 * groups * rows * shares * width
        ),
        name="weight_terms",
    )(gate([info], token)[0], *outs, *near, *near, *chunk)


def merge_kernel(keep_low, keep_high, got_low, got_high, keep_ref, send_ref):
    keep_ref[...] = keep_low[...] + got_low[...].astype(jnp.float32)
    send_ref[...] = (keep_high[...] + got_high[...].astype(jnp.float32)).astype(jnp.bfloat16)


def merge(keep, got, token):
    count, rows, width = keep.shape
    half = count // 2
    keep = gate([keep], token)[0]
    low = pl.BlockSpec((1, rows, width), lambda t: (t, 0, 0))
    high = pl.BlockSpec((1, rows, width), lambda t: (t + half, 0, 0))
    return pl.pallas_call(
        merge_kernel,
        grid=(half,),
        in_specs=[low, high, low, high],
        out_specs=[low, low],
        out_shape=[
            shape((half, rows, width), jnp.float32),
            shape((half, rows, width)),
        ],
        compiler_params=params(12),
        cost_estimate=cost(0, 8 * count * rows * width),
        name="merge",
    )(keep, keep, got, got)


def finish_kernel(scale, keep_ref, got_ref, *refs):
    refs[-1][...] = (keep_ref[0] + got_ref[0].astype(jnp.float32)) * scale


def finish(keep, got, so_far, token, c, chunks, scale):
    _, rows, width = keep.shape
    more = [] if so_far is None else [so_far]
    step = rows // 2
    spec = pl.BlockSpec((1, step, width), lambda i: (0, i, 0))
    return pl.pallas_call(
        functools.partial(finish_kernel, scale),
        grid=(rows // step,),
        in_specs=[spec, spec] + [ANY] * len(more),
        out_specs=pl.BlockSpec((step, width), lambda i: (i, c)),
        out_shape=shape((rows, width * chunks), jnp.float32),
        input_output_aliases={2: 0} if more else {},
        compiler_params=params(8),
        cost_estimate=cost(0, 10 * rows * width),
        name="finish",
    )(gate([keep], token)[0], got, *more)


def project_kernel(parts, shares, width, chunks, orders, picked, first, last, *refs):
    w_ref, near = refs[0], refs[1:3]
    far = refs[3 : 3 + len(picked) * (parts - 2)]
    acc_ref, out_ref = refs[-2] if not first else None, refs[-1]
    columns = [(c, unplace(p, orders[c])) for c in picked for p in range(shares)]
    weights = jnp.concatenate([w_ref[:, column(j, c, chunks, width)] for c, j in columns], axis=1)
    for d in range(parts):
        if d < 2:
            rows = jnp.concatenate([near[d][:, column(j, c, chunks, width)] for c, j in columns], axis=1)
        else:
            mine = [far[i * (parts - 2) + d - 2][...] for i in range(len(picked))]
            rows = mine[0] if len(mine) == 1 else jnp.concatenate(mine, axis=1)
        total = mm(rows, weights, NT)
        if not first:
            total += acc_ref[d]
        out_ref[d] = total.astype(out_ref.dtype)


def project(out_weight, near, far, acc, token, orders, picked, shares, width, last):
    feats, model = out_weight.shape
    rows = near[0].shape[0]
    parts = 2 + len(far[0])
    step = min(256, feats)
    flat = [x for group in far for x in group]
    first = acc is None
    block = pl.BlockSpec((parts, rows, step), lambda i: (0, 0, i))
    return pl.pallas_call(
        functools.partial(
            project_kernel, parts, shares, width, len(orders), orders, picked, first, last
        ),
        grid=(feats // step,),
        in_specs=[pl.BlockSpec((step, model), lambda i: (i, 0))]
        + [pl.BlockSpec((rows, model), lambda i: (0, 0))] * 2
        + [pl.BlockSpec((rows, shares * width), lambda i: (0, 0))] * len(flat)
        + ([] if first else [block]),
        out_specs=block,
        out_shape=shape((parts, rows, feats), jnp.bfloat16 if last else jnp.float32),
        compiler_params=params(24),
        cost_estimate=cost(
            2 * feats * rows * parts * shares * width * len(picked), 4 * feats * rows * parts
        ),
        name="project",
    )(gate([out_weight], token)[0], *near, *flat, *([] if first else [acc]))


def body(grad_out, queries, keys, values, out_weight, doc_starts):
    parts, shares = lax.axis_size("seq"), lax.axis_size("dp")
    groups = KV_HEADS // parts
    docs = doc_starts.shape[-1]
    cotangent = grad_out[0]
    rows, model = cotangent.shape
    chunks = max(1, min(4, model // shares // 128))
    width = model // shares // chunks
    bits = tuple(range(shares.bit_length() - 1))
    turned = bits[1:] + bits[:1]
    orders = [turned if c == 1 else bits for c in range(chunks)]
    scale = 1.0 / math.sqrt(rows * parts * shares)
    info = jnp.concatenate(
        [
            jnp.stack([lax.axis_index("seq"), lax.axis_index("dp")]).astype(jnp.int32),
            doc_starts[0],
        ]
    )

    def over_seq(x, d):
        return lax.ppermute(x, "seq", [(i, i ^ d) for i in range(parts)])

    def over_dp(x, d):
        return lax.ppermute(x, "dp", [(i, i ^ d) for i in range(shares)])

    near = [cotangent, over_seq(cotangent, 1)]
    packed = [pack(info, queries[0], keys[0], values[0], parts, groups, gp) for gp in range(groups)]
    sends = pack_chunks(cotangent, orders, shares, width)

    pieces, fwd = [], []
    token = near[1]
    for gp in range(groups):
        sent = packed[gp]
        if gp:
            sent = [sent[0]] + gate(sent[1:], *pieces[-1][1:])
        pieces.append([sent[0]] + [over_seq(sent[d], d) for d in range(1, parts)])
    far_half = {}

    def send_chunk(c, *tokens):
        mine = gate([sends[c]], *tokens)[0]
        far_half[c] = [over_seq(mine, d) for d in range(2, parts, 2)]

    def chunk_pieces(c):
        out = []
        for x in far_half[c]:
            out += [x, over_seq(x, 1)]
        return out

    for gp in range(groups):
        fwd.append(attention(info, pieces[gp], token, parts, docs))
        token = fwd[-1][0]
        if gp == 0:
            send_chunk(0, token)
    outs = [pair[0] for pair in fwd]

    state = {}
    result = None

    def run_merge(c):
        nonlocal token, result
        keep, send, hop = state[c]
        got = over_dp(send, 1 << orders[c][hop])
        if hop == len(bits) - 1:
            result = finish(keep, got, result, token, c, chunks, scale)
            token = result
            state[c] = (None, None, None)
        else:
            keep, send = merge(keep, got, token)
            state[c] = (keep, send, hop + 1)
            token = send

    fars = {}
    back, results = {}, {}
    acc = None

    def weigh(c):
        nonlocal token
        fars[c] = chunk_pieces(c)
        keep, send = weight_terms(
            info, outs, near, fars[c], token, shares, c, chunks, width, orders[c]
        )
        state[c] = (keep, send, 0)
        token = send

    def project_step(picked, last):
        nonlocal token, acc
        acc = project(
            out_weight, near, [fars[c] for c in picked], acc, token, orders, picked, shares, width, last
        )
        token = acc

    def send_back(gp):
        nonlocal token
        res = attention_back(info, pieces[gp], acc, outs[gp], fwd[gp][1], token, parts, docs, gp)
        token = results[gp] = res
        back[gp] = [res[0], None] + [over_seq(res[d], d) for d in range(2, parts)]

    for c in range(1, chunks):
        if c == 1:
            send_chunk(1, *pieces[-1][1:])
        else:
            send_chunk(c, *far_half[c - 2])
    last = chunks - 1
    done = set()

    def step_merge(c):
        if c in state and c not in done:
            run_merge(c)
            if state[c][2] is None:
                done.add(c)

    weigh(0)
    if chunks > 1:
        weigh(1)
    step_merge(0)
    if chunks > 2:
        weigh(2)
    if last:
        project_step(list(range(last)), False)
    step_merge(1)
    if chunks > 3:
        weigh(3)
    project_step([last], True)
    step_merge(0)
    send_back(0)
    step_merge(2)
    step_merge(0)
    step_merge(1)
    for gp in range(1, groups):
        send_back(gp)
    step_merge(2)
    if groups > 1:
        token = gate([token], *back[0][2:])[0]
    step_merge(3)
    step_merge(1)
    step_merge(2)
    for gp in range(groups):
        mine = gate([results[gp][1]], *back[0][2:])[0]
        back[gp][1] = over_seq(mine, 1)
    step_merge(3)
    if groups > 1:
        token = gate([token], *back[groups - 1][2:])[0]
    for _ in bits:
        for c in range(chunks):
            step_merge(c)
    back = [x for gp in range(groups) for x in back[gp]]
    grad_q, grad_k, grad_v = unpack(info, back, parts, groups)
    return (grad_q[None], grad_k[None], grad_v[None], result)


def solution(mesh):
    return jax.shard_map(
        body,
        mesh=mesh,
        in_specs=(
            P("dp", "seq", None),
            P("dp", "seq", None),
            P("dp", "seq", None),
            P("dp", "seq", None),
            P("seq", None),
            P("dp", None),
        ),
        out_specs=(
            P("dp", "seq", None),
            P("dp", "seq", None),
            P("dp", "seq", None),
            P("seq", "dp"),
        ),
        check_vma=False,
    )
```

profile of v0, /device:TPU:0, one launch (start us, length us, event | category | flops | bytes accessed | tf_op | source)
XLA Modules:
  0.0 250.6 jit_solution(14542608922615305139)
XLA Ops:
  2.4 3.2 %pack.2 = (bf16[256,768]{1,0:T(8,128)(2,1)}, bf16[256,768]{1,0:T(8,128)(2,1)}, bf16[256,768]{1,0:T(8,128)(2,1)}, bf16[256,768]{1,0:T(8,128)(2,1)}) custom-call(s32[10]{0:T(128)} %pad_add_fusion.info_ref, bf16[256,4096]{1,0:T(8,128)(2,1)} %bitcast.40, bf16[256,4096]{1,0:T(8,128)(2,1)} %bitcast.41, bf16[256,4096]{1,0:T(8,128)(2,1)} %bitcast.42, ...), custom_call_target="tpu_custom_call" | custom-call | bytes 3145 | tf_op jit(solution)/shard_map/pack/pallas_call | solution.py:60
  5.8 3.0 %collective-permute-start.2 = (bf16[256,768]{1,0:T(8,128)(2,1)}, bf16[256,768]{1,0:T(8,128)(2,1)S(1)}, u32[]{:S(2)}, u32[]{:S(2)}) collective-permute-start(bf16[256,768]{1,0:T(8,128)(2,1)} %get-tuple-element.79), channel_id=1, source_target_pairs={{0,2},{1,3},{2,0},{3,1},{4,6},{5,7},{6,4},{7,5},{8,10},{9,11},{10,... | collective-permute-start | bytes 1179656 | tf_op jit(solution)/shard_map/ppermute | solution.py:537
  8.8 3.9 %pack_chunks.1 = (bf16[256,1024]{1,0:T(8,128)(2,1)}, bf16[256,1024]{1,0:T(8,128)(2,1)}, bf16[256,1024]{1,0:T(8,128)(2,1)}, bf16[256,1024]{1,0:T(8,128)(2,1)}) custom-call(bf16[256,4096]{1,0:T(8,128)(2,1)} %bitcast.27), custom_call_target="tpu_custom_call" | custom-call | bytes 4194 | tf_op jit(solution)/shard_map/pack_chunks/pallas_call | solution.py:95
  12.6 6.2 %collective-permute-done.2.refs_2_ = bf16[256,768]{1,0:T(8,128)(2,1)S(1)} collective-permute-done((bf16[256,768]{1,0:T(8,128)(2,1)}, bf16[256,768]{1,0:T(8,128)(2,1)S(1)}, u32[]{:S(2)}, u32[]{:S(2)}) %collective-permute-start.2) | collective-permute-done | bytes 393248 | tf_op jit(solution)/shard_map/ppermute | solution.py:537
  18.9 7.3 %collective-permute-done.3.refs_3_ = bf16[256,768]{1,0:T(8,128)(2,1)S(1)} collective-permute-done((bf16[256,768]{1,0:T(8,128)(2,1)}, bf16[256,768]{1,0:T(8,128)(2,1)S(1)}, u32[]{:S(2)}, u32[]{:S(2)}) %collective-permute-start.3) | collective-permute-done | bytes 393248 | tf_op jit(solution)/shard_map/ppermute | solution.py:537
  26.2 10.3 %attention.2 = (bf16[4,512,256]{2,1,0:T(8,128)(2,1)S(1)}, f32[4,4,8,256]{3,2,1,0:T(8,128)S(1)}) custom-call(s32[10]{0:T(128)S(1)} %copy-done.6, bf16[256,768]{1,0:T(8,128)(2,1)S(1)} %copy-done.3, bf16[256,768]{1,0:T(8,128)(2,1)S(1)} %collective-permute-done.1.refs_1_, bf16[256,768]{1,0:T(8,128)(2,1)S(1)} %collective-permute-done.2.refs_2_, ...), custom_call_target="tpu_custom_call" | custom-call | flops 8000000 | bytes 3145 | tf_op jit(solution)/shard_map/attention/pallas_call | solution.py:223
  38.1 3.4 %pack.3 = (bf16[256,768]{1,0:T(8,128)(2,1)}, bf16[256,768]{1,0:T(8,128)(2,1)}, bf16[256,768]{1,0:T(8,128)(2,1)}, bf16[256,768]{1,0:T(8,128)(2,1)}) custom-call(s32[10]{0:T(128)} %pad_add_fusion.info_ref, bf16[256,4096]{1,0:T(8,128)(2,1)} %bitcast.44, bf16[256,4096]{1,0:T(8,128)(2,1)} %bitcast.45, bf16[256,4096]{1,0:T(8,128)(2,1)} %bitcast.46, ...), custom_call_target="tpu_custom_call" | custom-call | bytes 3145 | tf_op jit(solution)/shard_map/pack/pallas_call | solution.py:60
  43.4 16.6 %collective-permute-done.5.refs_2_ = bf16[256,768]{1,0:T(8,128)(2,1)S(1)} collective-permute-done((bf16[256,768]{1,0:T(8,128)(2,1)}, bf16[256,768]{1,0:T(8,128)(2,1)S(1)}, u32[]{:S(2)}, u32[]{:S(2)}) %collective-permute-start.5) | collective-permute-done | bytes 393248 | tf_op jit(solution)/shard_map/ppermute | solution.py:537
  60.0 7.3 %collective-permute-done.6.refs_3_ = bf16[256,768]{1,0:T(8,128)(2,1)S(1)} collective-permute-done((bf16[256,768]{1,0:T(8,128)(2,1)}, bf16[256,768]{1,0:T(8,128)(2,1)S(1)}, u32[]{:S(2)}, u32[]{:S(2)}) %collective-permute-start.6) | collective-permute-done | bytes 393248 | tf_op jit(solution)/shard_map/ppermute | solution.py:537
  67.3 2.0 collective-permute-start.9
  69.4 12.2 %collective-permute-done.9.refs_6_.refs_5_ = bf16[256,1024]{1,0:T(8,128)(2,1)S(1)} collective-permute-done((bf16[256,1024]{1,0:T(8,128)(2,1)S(1)}, bf16[256,1024]{1,0:T(8,128)(2,1)S(1)}, u32[]{:S(2)}, u32[]{:S(2)}) %collective-permute-start.9) | collective-permute-done | bytes 524320 | tf_op jit(solution)/shard_map/ppermute | solution.py:537
  82.6 10.3 %attention.3 = (bf16[4,512,256]{2,1,0:T(8,128)(2,1)S(1)}, f32[4,4,8,256]{3,2,1,0:T(8,128)S(1)}) custom-call(s32[10]{0:T(128)S(1)} %copy-done.7, bf16[256,768]{1,0:T(8,128)(2,1)S(1)} %copy-done.1, bf16[256,768]{1,0:T(8,128)(2,1)S(1)} %collective-permute-done.4.refs_1_, bf16[256,768]{1,0:T(8,128)(2,1)S(1)} %collective-permute-done.5.refs_2_, ...), custom_call_target="tpu_custom_call" | custom-call | flops 8000000 | bytes 3145 | tf_op jit(solution)/shard_map/attention/pallas_call | solution.py:223
  92.9 4.3 %weight_terms.4 = (f32[4,1024,128]{2,1,0:T(8,128)S(1)}, bf16[4,1024,128]{2,1,0:T(8,128)(2,1)S(1)}) custom-call(s32[10]{0:T(128)S(1)} %copy-done.7, bf16[4,512,256]{2,1,0:T(8,128)(2,1)S(1)} %get-tuple-element.81.refs_0_.refs_5_, bf16[4,512,256]{2,1,0:T(8,128)(2,1)S(1)} %get-tuple-element.90.refs_1_.refs_5_, bf16[256,4096]{1,0:T(8,128)(2,1)S(1)} %bitcast.28, ...), custom_call_target="tpu_custom_call" | custom-call | flops 2147483 | bytes 8388 | tf_op jit(solution)/shard_map/weight_terms/pallas_call | solution.py:401
  97.3 4.3 %collective-permute-start.11 = (bf16[4,1024,128]{2,1,0:T(8,128)(2,1)S(1)}, bf16[4,1024,128]{2,1,0:T(8,128)(2,1)S(1)}, u32[]{:S(2)}, u32[]{:S(2)}) collective-permute-start(bf16[4,1024,128]{2,1,0:T(8,128)(2,1)S(1)} %get-tuple-element.95), channel_id=1, source_target_pairs={{0,4},{4,0},{8,12},{12,8},{16,20},{20,16},{24,28},{28,24},{1,5},{5... | collective-permute-start | bytes 3145736 | tf_op jit(solution)/shard_map/ppermute | solution.py:540
  103.1 4.3 %weight_terms.5 = (f32[4,1024,128]{2,1,0:T(8,128)S(1)}, bf16[4,1024,128]{2,1,0:T(8,128)(2,1)S(1)}) custom-call(s32[10]{0:T(128)S(1)} %copy-done.7, bf16[4,512,256]{2,1,0:T(8,128)(2,1)S(1)} %get-tuple-element.81.refs_0_.refs_5_, bf16[4,512,256]{2,1,0:T(8,128)(2,1)S(1)} %get-tuple-element.90.refs_1_.refs_5_, bf16[256,4096]{1,0:T(8,128)(2,1)S(1)} %bitcast.30, ...), custom_call_target="tpu_custom_call" | custom-call | flops 2147483 | bytes 8388 | tf_op jit(solution)/shard_map/weight_terms/pallas_call | solution.py:401
  109.6 6.7 %collective-permute-done.12.refs_6_.refs_7_ = bf16[256,1024]{1,0:T(8,128)(2,1)S(1)} collective-permute-done((bf16[256,1024]{1,0:T(8,128)(2,1)S(1)}, bf16[256,1024]{1,0:T(8,128)(2,1)S(1)}, u32[]{:S(2)}, u32[]{:S(2)}) %collective-permute-start.12) | collective-permute-done | bytes 524320 | tf_op jit(solution)/shard_map/ppermute | solution.py:537
  116.3 10.5 %collective-permute-done.15.refs_6_.refs_3_ = bf16[256,1024]{1,0:T(8,128)(2,1)S(1)} collective-permute-done((bf16[256,1024]{1,0:T(8,128)(2,1)S(1)}, bf16[256,1024]{1,0:T(8,128)(2,1)S(1)}, u32[]{:S(2)}, u32[]{:S(2)}) %collective-permute-start.15) | collective-permute-done | bytes 524320 | tf_op jit(solution)/shard_map/ppermute | solution.py:537
  127.1 4.3 %weight_terms.6 = (f32[4,1024,128]{2,1,0:T(8,128)S(1)}, bf16[4,1024,128]{2,1,0:T(8,128)(2,1)S(1)}) custom-call(s32[10]{0:T(128)S(1)} %copy-done.7, bf16[4,512,256]{2,1,0:T(8,128)(2,1)S(1)} %get-tuple-element.81.refs_0_.refs_5_, bf16[4,512,256]{2,1,0:T(8,128)(2,1)S(1)} %get-tuple-element.90.refs_1_.refs_5_, bf16[256,4096]{1,0:T(8,128)(2,1)S(1)} %bitcast.32, ...), custom_call_target="tpu_custom_call" | custom-call | flops 2147483 | bytes 8388 | tf_op jit(solution)/shard_map/weight_terms/pallas_call | solution.py:401
  131.9 7.9 %project.2.refs_5_ = f32[4,256,1024]{2,1,0:T(8,128)S(1)} custom-call(bf16[1024,4096]{1,0:T(8,128)(2,1)S(1)} %bitcast.39, bf16[256,4096]{1,0:T(8,128)(2,1)S(1)} %bitcast.34, bf16[256,4096]{1,0:T(8,128)(2,1)S(1)} %collective-permute-done.refs_3_.refs_5_.refs_2_, bf16[256,1024]{1,0:T(8,128)(2,1)S(1)} %collective-permute-done.7.refs_6_.refs_3_, ...), custom_call_target="tpu_custom_call" | custom-call | flops 6442450 | bytes 4194 | tf_op jit(solution)/shard_map/project/pallas_call | solution.py:498
  140.0 4.3 %weight_terms.7 = (f32[4,1024,128]{2,1,0:T(8,128)S(1)}, bf16[4,1024,128]{2,1,0:T(8,128)(2,1)S(1)}) custom-call(s32[10]{0:T(128)S(1)} %copy-done.7, bf16[4,512,256]{2,1,0:T(8,128)(2,1)S(1)} %get-tuple-element.81.refs_0_.refs_5_, bf16[4,512,256]{2,1,0:T(8,128)(2,1)S(1)} %get-tuple-element.90.refs_1_.refs_5_, bf16[256,4096]{1,0:T(8,128)(2,1)S(1)} %bitcast.35, ...), custom_call_target="tpu_custom_call" | custom-call | flops 2147483 | bytes 8388 | tf_op jit(solution)/shard_map/weight_terms/pallas_call | solution.py:401
  148.6 3.6 %project.3.refs_4_ = bf16[4,256,1024]{2,1,0:T(8,128)(2,1)S(1)} custom-call(bf16[1024,4096]{1,0:T(8,128)(2,1)S(1)} %bitcast.39, bf16[256,4096]{1,0:T(8,128)(2,1)S(1)} %bitcast.37, bf16[256,4096]{1,0:T(8,128)(2,1)S(1)} %collective-permute-done.refs_3_.refs_5_.refs_2_, bf16[256,1024]{1,0:T(8,128)(2,1)S(1)} %collective-permute-done.15.refs_6_.refs_3_, ...), custom_call_target="tpu_custom_call" | custom-call | flops 2147483 | bytes 4194 | tf_op jit(solution)/shard_map/project/pallas_call | solution.py:498
  152.3 18.6 %collective-permute-done.17.got_low.got_high = bf16[2,1024,128]{2,1,0:T(8,128)(2,1)S(1)} collective-permute-done((bf16[2,1024,128]{2,1,0:T(8,128)(2,1)S(1)}, bf16[2,1024,128]{2,1,0:T(8,128)(2,1)S(1)}, u32[]{:S(2)}, u32[]{:S(2)}) %collective-permute-start.17) | collective-permute-done | bytes 524320 | tf_op jit(solution)/shard_map/ppermute | solution.py:540
  171.0 12.6 %attention_back.2 = bf16[4,256,768]{2,1,0:T(8,128)(2,1)S(1)} custom-call(s32[10]{0:T(128)S(1)} %copy-done.7, bf16[256,768]{1,0:T(8,128)(2,1)S(1)} %copy-done.3, bf16[256,768]{1,0:T(8,128)(2,1)S(1)} %collective-permute-done.1.refs_1_, bf16[256,768]{1,0:T(8,128)(2,1)S(1)} %collective-permute-done.2.refs_2_, bf16[256,768]{1,0:T(8,128)(2,1)S(1)} %copy-done.5, ...), custom_call_target="tpu_custom_call" | custom-call | flops 14000000 | bytes 6291 | tf_op jit(solution)/shard_map/attention_back/pallas_call | solution.py:315
  187.6 7.8 %collective-permute-done.19.refs_3_ = bf16[256,768]{1,0:T(8,128)(2,1)S(1)} collective-permute-done((bf16[256,768]{1,0:T(8,128)(2,1)S(1)}, bf16[256,768]{1,0:T(8,128)(2,1)S(1)}, u32[]{:S(2)}, u32[]{:S(2)}) %collective-permute-start.19) | collective-permute-done | bytes 393248 | tf_op jit(solution)/shard_map/ppermute | solution.py:537
  195.4 2.0 collective-permute-start.31
  197.4 6.5 %collective-permute-done.18.refs_2_ = bf16[256,768]{1,0:T(8,128)(2,1)S(1)} collective-permute-done((bf16[256,768]{1,0:T(8,128)(2,1)S(1)}, bf16[256,768]{1,0:T(8,128)(2,1)S(1)}, u32[]{:S(2)}, u32[]{:S(2)}) %collective-permute-start.18) | collective-permute-done | bytes 393248 | tf_op jit(solution)/shard_map/ppermute | solution.py:537
  204.9 1.8 collective-permute-start.29
  206.7 12.4 %attention_back.3 = bf16[4,256,768]{2,1,0:T(8,128)(2,1)S(1)} custom-call(s32[10]{0:T(128)S(1)} %copy-done.7, bf16[256,768]{1,0:T(8,128)(2,1)S(1)} %copy-done.2, bf16[256,768]{1,0:T(8,128)(2,1)S(1)} %collective-permute-done.4.refs_1_, bf16[256,768]{1,0:T(8,128)(2,1)S(1)} %collective-permute-done.5.refs_2_, ...), custom_call_target="tpu_custom_call" | custom-call | flops 14000000 | bytes 6291 | tf_op jit(solution)/shard_map/attention_back/pallas_call | solution.py:315
  221.3 12.9 %collective-permute-done.30.got_ref = bf16[1,1024,128]{2,1,0:T(8,128)(2,1)S(1)} collective-permute-done((bf16[1,1024,128]{2,1,0:T(8,128)(2,1)S(1)}, bf16[1,1024,128]{2,1,0:T(8,128)(2,1)S(1)}, u32[]{:S(2)}, u32[]{:S(2)}) %collective-permute-start.30) | collective-permute-done | bytes 262176 | tf_op jit(solution)/shard_map/ppermute | solution.py:540
  236.0 3.3 %collective-permute-done.25.refs_6_ = bf16[256,768]{1,0:T(8,128)(2,1)S(1)} collective-permute-done((bf16[256,768]{1,0:T(8,128)(2,1)S(1)}, bf16[256,768]{1,0:T(8,128)(2,1)S(1)}, u32[]{:S(2)}, u32[]{:S(2)}) %collective-permute-start.25) | collective-permute-done | bytes 393248 | tf_op jit(solution)/shard_map/ppermute | solution.py:537
  239.3 2.8 %unpack.1 = (bf16[256,4096]{1,0:T(8,128)(2,1)}, bf16[256,1024]{1,0:T(8,128)(2,1)}, bf16[256,1024]{1,0:T(8,128)(2,1)}) custom-call(s32[10]{0:T(128)S(1)} %copy-done.7, bf16[256,768]{1,0:T(8,128)(2,1)S(1)} %get-tuple-element.155.refs_0_, bf16[256,768]{1,0:T(8,128)(2,1)S(1)} %collective-permute-done.20.refs_1_, ...), custom_call_target="tpu_custom_call" | custom-call | bytes 6291 | tf_op jit(solution)/shard_map/unpack/pallas_call | solution.py:127
  242.1 7.7 %collective-permute-done.32.got_ref = bf16[1,1024,128]{2,1,0:T(8,128)(2,1)S(1)} collective-permute-done((bf16[1,1024,128]{2,1,0:T(8,128)(2,1)S(1)}, bf16[1,1024,128]{2,1,0:T(8,128)(2,1)S(1)}, u32[]{:S(2)}, u32[]{:S(2)}) %collective-permute-start.32) | collective-permute-done | bytes 262176 | tf_op jit(solution)/shard_map/ppermute | solution.py:540
  (90 shorter events, 25.2 us)
Async XLA Ops:
  0.6 12.0 %collective-permute-start = (bf16[256,4096]{1,0:T(8,128)(2,1)}, bf16[256,4096]{1,0:T(8,128)(2,1)S(1)}, u32[]{:S(2)}, u32[]{:S(2)}) collective-permute-start(bf16[256,4096]{1,0:T(8,128)(2,1)} %bitcast.26), channel_id=1, source_target_pairs={{0,1},{1,0},{2,3},{3,2},{4,5},{5,4},{6,7},{7,6},{8,9},{9,8},{10,11... | collective-permute-start | bytes 6291464 | tf_op jit(solution)/shard_map/ppermute | solution.py:537
  5.7 7.0 %collective-permute-start.1 = (bf16[256,768]{1,0:T(8,128)(2,1)}, bf16[256,768]{1,0:T(8,128)(2,1)S(1)}, u32[]{:S(2)}, u32[]{:S(2)}) collective-permute-start(bf16[256,768]{1,0:T(8,128)(2,1)} %get-tuple-element.78), channel_id=1, source_target_pairs={{0,1},{1,0},{2,3},{3,2},{4,5},{5,4},{6,7},{7,6},{8,9},{9,8},{10,11... | collective-permute-start | bytes 1179656 | tf_op jit(solution)/shard_map/ppermute | solution.py:537
  5.8 13.1 %collective-permute-start.2 = (bf16[256,768]{1,0:T(8,128)(2,1)}, bf16[256,768]{1,0:T(8,128)(2,1)S(1)}, u32[]{:S(2)}, u32[]{:S(2)}) collective-permute-start(bf16[256,768]{1,0:T(8,128)(2,1)} %get-tuple-element.79), channel_id=1, source_target_pairs={{0,2},{1,3},{2,0},{3,1},{4,6},{5,7},{6,4},{7,5},{8,10},{9,11},{10,... | collective-permute-start | bytes 1179656 | tf_op jit(solution)/shard_map/ppermute | solution.py:537
  8.8 17.4 %collective-permute-start.3 = (bf16[256,768]{1,0:T(8,128)(2,1)}, bf16[256,768]{1,0:T(8,128)(2,1)S(1)}, u32[]{:S(2)}, u32[]{:S(2)}) collective-permute-start(bf16[256,768]{1,0:T(8,128)(2,1)} %get-tuple-element.80), channel_id=1, source_target_pairs={{0,3},{1,2},{2,1},{3,0},{4,7},{5,6},{6,5},{7,4},{8,11},{9,10},{10,... | collective-permute-start | bytes 1179656 | tf_op jit(solution)/shard_map/ppermute | solution.py:537
  36.6 32.8 %collective-permute-start.7 = (bf16[256,1024]{1,0:T(8,128)(2,1)}, bf16[256,1024]{1,0:T(8,128)(2,1)S(1)}, u32[]{:S(2)}, u32[]{:S(2)}) collective-permute-start(bf16[256,1024]{1,0:T(8,128)(2,1)} %get-tuple-element.93), channel_id=1, source_target_pairs={{0,2},{1,3},{2,0},{3,1},{4,6},{5,7},{6,4},{7,5},{8,10},{9,11},{10,... | collective-permute-start | bytes 1572872 | tf_op jit(solution)/shard_map/ppermute | solution.py:537
  41.9 18.1 %collective-permute-start.5 = (bf16[256,768]{1,0:T(8,128)(2,1)}, bf16[256,768]{1,0:T(8,128)(2,1)S(1)}, u32[]{:S(2)}, u32[]{:S(2)}) collective-permute-start(bf16[256,768]{1,0:T(8,128)(2,1)} %get-tuple-element.88), channel_id=1, source_target_pairs={{0,2},{1,3},{2,0},{3,1},{4,6},{5,7},{6,4},{7,5},{8,10},{9,11},{10,... | collective-permute-start | bytes 1179656 | tf_op jit(solution)/shard_map/ppermute | solution.py:537
  42.2 25.1 %collective-permute-start.6 = (bf16[256,768]{1,0:T(8,128)(2,1)}, bf16[256,768]{1,0:T(8,128)(2,1)S(1)}, u32[]{:S(2)}, u32[]{:S(2)}) collective-permute-start(bf16[256,768]{1,0:T(8,128)(2,1)} %get-tuple-element.89), channel_id=1, source_target_pairs={{0,3},{1,2},{2,1},{3,0},{4,7},{5,6},{6,5},{7,4},{8,11},{9,10},{10,... | collective-permute-start | bytes 1179656 | tf_op jit(solution)/shard_map/ppermute | solution.py:537
  67.3 14.2 %collective-permute-start.9 = (bf16[256,1024]{1,0:T(8,128)(2,1)S(1)}, bf16[256,1024]{1,0:T(8,128)(2,1)S(1)}, u32[]{:S(2)}, u32[]{:S(2)}) collective-permute-start(bf16[256,1024]{1,0:T(8,128)(2,1)S(1)} %copy-done.10), channel_id=1, source_target_pairs={{0,2},{1,3},{2,0},{3,1},{4,6},{5,7},{6,4},{7,5},{8,10},{9,11},{10,... | collective-permute-start | bytes 1572872 | tf_op jit(solution)/shard_map/ppermute | solution.py:537
  69.4 23.6 %collective-permute-start.8 = (bf16[256,1024]{1,0:T(8,128)(2,1)S(1)}, bf16[256,1024]{1,0:T(8,128)(2,1)S(1)}, u32[]{:S(2)}, u32[]{:S(2)}) collective-permute-start(bf16[256,1024]{1,0:T(8,128)(2,1)S(1)} %collective-permute-done.7.refs_6_.refs_3_), channel_id=1, source_target_pairs={{0,1},{1,0},{2,3},{3,2},{4,5},{5,4},{6,7},{7,6},{8,9},{9,8},{10,11... | collective-permute-start | bytes 1572872 | tf_op jit(solution)/shard_map/ppermute | solution.py:537
  81.6 21.5 %collective-permute-start.10 = (bf16[256,1024]{1,0:T(8,128)(2,1)S(1)}, bf16[256,1024]{1,0:T(8,128)(2,1)S(1)}, u32[]{:S(2)}, u32[]{:S(2)}) collective-permute-start(bf16[256,1024]{1,0:T(8,128)(2,1)S(1)} %collective-permute-done.9.refs_6_.refs_5_), channel_id=1, source_target_pairs={{0,1},{1,0},{2,3},{3,2},{4,5},{5,4},{6,7},{7,6},{8,9},{9,8},{10,11... | collective-permute-start | bytes 1572872 | tf_op jit(solution)/shard_map/ppermute | solution.py:537
  97.3 29.6 %collective-permute-start.11 = (bf16[4,1024,128]{2,1,0:T(8,128)(2,1)S(1)}, bf16[4,1024,128]{2,1,0:T(8,128)(2,1)S(1)}, u32[]{:S(2)}, u32[]{:S(2)}) collective-permute-start(bf16[4,1024,128]{2,1,0:T(8,128)(2,1)S(1)} %get-tuple-element.95), channel_id=1, source_target_pairs={{0,4},{4,0},{8,12},{12,8},{16,20},{20,16},{24,28},{28,24},{1,5},{5... | collective-permute-start | bytes 3145736 | tf_op jit(solution)/shard_map/ppermute | solution.py:540
  101.6 14.8 %collective-permute-start.12 = (bf16[256,1024]{1,0:T(8,128)(2,1)S(1)}, bf16[256,1024]{1,0:T(8,128)(2,1)S(1)}, u32[]{:S(2)}, u32[]{:S(2)}) collective-permute-start(bf16[256,1024]{1,0:T(8,128)(2,1)S(1)} %copy-done.9), channel_id=1, source_target_pairs={{0,2},{1,3},{2,0},{3,1},{4,6},{5,7},{6,4},{7,5},{8,10},{9,11},{10,... | collective-permute-start | bytes 1572872 | tf_op jit(solution)/shard_map/ppermute | solution.py:537
  107.4 32.3 %collective-permute-start.14 = (bf16[4,1024,128]{2,1,0:T(8,128)(2,1)S(1)}, bf16[4,1024,128]{2,1,0:T(8,128)(2,1)S(1)}, u32[]{:S(2)}, u32[]{:S(2)}) collective-permute-start(bf16[4,1024,128]{2,1,0:T(8,128)(2,1)S(1)} %get-tuple-element.99), channel_id=1, source_target_pairs={{0,8},{4,12},{8,0},{12,4},{16,24},{20,28},{24,16},{28,20},{1,9},{5... | collective-permute-start | bytes 3145736 | tf_op jit(solution)/shard_map/ppermute | solution.py:540
  109.1 17.8 %collective-permute-start.15 = (bf16[256,1024]{1,0:T(8,128)(2,1)S(1)}, bf16[256,1024]{1,0:T(8,128)(2,1)S(1)}, u32[]{:S(2)}, u32[]{:S(2)}) collective-permute-start(bf16[256,1024]{1,0:T(8,128)(2,1)S(1)} %copy-done.8), channel_id=1, source_target_pairs={{0,2},{1,3},{2,0},{3,1},{4,6},{5,7},{6,4},{7,5},{8,10},{9,11},{10,... | collective-permute-start | bytes 1572872 | tf_op jit(solution)/shard_map/ppermute | solution.py:537
  116.3 10.8 %collective-permute-start.13 = (bf16[256,1024]{1,0:T(8,128)(2,1)S(1)}, bf16[256,1024]{1,0:T(8,128)(2,1)S(1)}, u32[]{:S(2)}, u32[]{:S(2)}) collective-permute-start(bf16[256,1024]{1,0:T(8,128)(2,1)S(1)} %collective-permute-done.12.refs_6_.refs_7_), channel_id=1, source_target_pairs={{0,1},{1,0},{2,3},{3,2},{4,5},{5,4},{6,7},{7,6},{8,9},{9,8},{10,11... | collective-permute-start | bytes 1572872 | tf_op jit(solution)/shard_map/ppermute | solution.py:537
  126.8 13.2 %collective-permute-start.16 = (bf16[256,1024]{1,0:T(8,128)(2,1)S(1)}, bf16[256,1024]{1,0:T(8,128)(2,1)S(1)}, u32[]{:S(2)}, u32[]{:S(2)}) collective-permute-start(bf16[256,1024]{1,0:T(8,128)(2,1)S(1)} %collective-permute-done.15.refs_6_.refs_3_), channel_id=1, source_target_pairs={{0,1},{1,0},{2,3},{3,2},{4,5},{5,4},{6,7},{7,6},{8,9},{9,8},{10,11... | collective-permute-start | bytes 1572872 | tf_op jit(solution)/shard_map/ppermute | solution.py:537
  131.4 52.2 %collective-permute-start.21 = (bf16[4,1024,128]{2,1,0:T(8,128)(2,1)S(1)}, bf16[4,1024,128]{2,1,0:T(8,128)(2,1)S(1)}, u32[]{:S(2)}, u32[]{:S(2)}) collective-permute-start(bf16[4,1024,128]{2,1,0:T(8,128)(2,1)S(1)} %get-tuple-element.107), channel_id=1, source_target_pairs={{0,4},{4,0},{8,12},{12,8},{16,20},{20,16},{24,28},{28,24},{1,5},{5... | collective-permute-start | bytes 3145736 | tf_op jit(solution)/shard_map/ppermute | solution.py:540
  144.3 41.4 %collective-permute-start.27 = (bf16[4,1024,128]{2,1,0:T(8,128)(2,1)S(1)}, bf16[4,1024,128]{2,1,0:T(8,128)(2,1)S(1)}, u32[]{:S(2)}, u32[]{:S(2)}) collective-permute-start(bf16[4,1024,128]{2,1,0:T(8,128)(2,1)S(1)} %get-tuple-element.114), channel_id=1, source_target_pairs={{0,4},{4,0},{8,12},{12,8},{16,20},{20,16},{24,28},{28,24},{1,5},{5... | collective-permute-start | bytes 3145736 | tf_op jit(solution)/shard_map/ppermute | solution.py:540
  146.0 24.9 %collective-permute-start.17 = (bf16[2,1024,128]{2,1,0:T(8,128)(2,1)S(1)}, bf16[2,1024,128]{2,1,0:T(8,128)(2,1)S(1)}, u32[]{:S(2)}, u32[]{:S(2)}) collective-permute-start(bf16[2,1024,128]{2,1,0:T(8,128)(2,1)S(1)} %get-tuple-element.103), channel_id=1, source_target_pairs={{0,8},{4,12},{8,0},{12,4},{16,24},{20,28},{24,16},{28,20},{1,9},{5... | collective-permute-start | bytes 1572872 | tf_op jit(solution)/shard_map/ppermute | solution.py:540
  147.6 57.2 %collective-permute-start.23 = (bf16[2,1024,128]{2,1,0:T(8,128)(2,1)S(1)}, bf16[2,1024,128]{2,1,0:T(8,128)(2,1)S(1)}, u32[]{:S(2)}, u32[]{:S(2)}) collective-permute-start(bf16[2,1024,128]{2,1,0:T(8,128)(2,1)S(1)} %get-tuple-element.110), channel_id=1, source_target_pairs={{0,16},{4,20},{8,24},{12,28},{16,0},{20,4},{24,8},{28,12},{1,17},{... | collective-permute-start | bytes 1572872 | tf_op jit(solution)/shard_map/ppermute | solution.py:540
  183.8 35.3 %collective-permute-start.28 = (bf16[2,1024,128]{2,1,0:T(8,128)(2,1)S(1)}, bf16[2,1024,128]{2,1,0:T(8,128)(2,1)S(1)}, u32[]{:S(2)}, u32[]{:S(2)}) collective-permute-start(bf16[2,1024,128]{2,1,0:T(8,128)(2,1)S(1)} %get-tuple-element.125), channel_id=1, source_target_pairs={{0,8},{4,12},{8,0},{12,4},{16,24},{20,28},{24,16},{28,20},{1,9},{5... | collective-permute-start | bytes 1572872 | tf_op jit(solution)/shard_map/ppermute | solution.py:540
  184.0 11.4 %collective-permute-start.19 = (bf16[256,768]{1,0:T(8,128)(2,1)S(1)}, bf16[256,768]{1,0:T(8,128)(2,1)S(1)}, u32[]{:S(2)}, u32[]{:S(2)}) collective-permute-start(bf16[256,768]{1,0:T(8,128)(2,1)S(1)} %get-tuple-element.152), channel_id=1, source_target_pairs={{0,3},{1,2},{2,1},{3,0},{4,7},{5,6},{6,5},{7,4},{8,11},{9,10},{10,... | collective-permute-start | bytes 1179656 | tf_op jit(solution)/shard_map/ppermute | solution.py:537
  184.3 19.6 %collective-permute-start.18 = (bf16[256,768]{1,0:T(8,128)(2,1)S(1)}, bf16[256,768]{1,0:T(8,128)(2,1)S(1)}, u32[]{:S(2)}, u32[]{:S(2)}) collective-permute-start(bf16[256,768]{1,0:T(8,128)(2,1)S(1)} %get-tuple-element.153), channel_id=1, source_target_pairs={{0,2},{1,3},{2,0},{3,1},{4,6},{5,7},{6,4},{7,5},{8,10},{9,11},{10,... | collective-permute-start | bytes 1179656 | tf_op jit(solution)/shard_map/ppermute | solution.py:537
  185.7 18.2 %collective-permute-start.22 = (bf16[1,1024,128]{2,1,0:T(8,128)(2,1)S(1)}, bf16[1,1024,128]{2,1,0:T(8,128)(2,1)S(1)}, u32[]{:S(2)}, u32[]{:S(2)}) collective-permute-start(bf16[1,1024,128]{2,1,0:T(8,128)(2,1)S(1)} %get-tuple-element.117), channel_id=1, source_target_pairs={{0,16},{4,20},{8,24},{12,28},{16,0},{20,4},{24,8},{28,12},{1,17},{... | collective-permute-start | bytes 786440 | tf_op jit(solution)/shard_map/ppermute | solution.py:540
  195.4 40.4 %collective-permute-start.31 = (bf16[2,1024,128]{2,1,0:T(8,128)(2,1)S(1)}, bf16[2,1024,128]{2,1,0:T(8,128)(2,1)S(1)}, u32[]{:S(2)}, u32[]{:S(2)}) collective-permute-start(bf16[2,1024,128]{2,1,0:T(8,128)(2,1)S(1)} %get-tuple-element.141), channel_id=1, source_target_pairs={{0,8},{4,12},{8,0},{12,4},{16,24},{20,28},{24,16},{28,20},{1,9},{5... | collective-permute-start | bytes 1572872 | tf_op jit(solution)/shard_map/ppermute | solution.py:540
  203.9 32.1 %collective-permute-start.20 = (bf16[256,768]{1,0:T(8,128)(2,1)S(1)}, bf16[256,768]{1,0:T(8,128)(2,1)S(1)}, u32[]{:S(2)}, u32[]{:S(2)}) collective-permute-start(bf16[256,768]{1,0:T(8,128)(2,1)S(1)} %get-tuple-element.120), channel_id=1, source_target_pairs={{0,1},{1,0},{2,3},{3,2},{4,5},{5,4},{6,7},{7,6},{8,9},{9,8},{10,11... | collective-permute-start | bytes 1179656 | tf_op jit(solution)/shard_map/ppermute | solution.py:537
  204.9 14.8 %collective-permute-start.29 = (bf16[1,1024,128]{2,1,0:T(8,128)(2,1)S(1)}, bf16[1,1024,128]{2,1,0:T(8,128)(2,1)S(1)}, u32[]{:S(2)}, u32[]{:S(2)}) collective-permute-start(bf16[1,1024,128]{2,1,0:T(8,128)(2,1)S(1)} %get-tuple-element.128), channel_id=1, source_target_pairs={{0,4},{4,0},{8,12},{12,8},{16,20},{20,16},{24,28},{28,24},{1,5},{5... | collective-permute-start | bytes 786440 | tf_op jit(solution)/shard_map/ppermute | solution.py:540
  219.2 15.0 %collective-permute-start.30 = (bf16[1,1024,128]{2,1,0:T(8,128)(2,1)S(1)}, bf16[1,1024,128]{2,1,0:T(8,128)(2,1)S(1)}, u32[]{:S(2)}, u32[]{:S(2)}) collective-permute-start(bf16[1,1024,128]{2,1,0:T(8,128)(2,1)S(1)} %get-tuple-element.144), channel_id=1, source_target_pairs={{0,16},{4,20},{8,24},{12,28},{16,0},{20,4},{24,8},{28,12},{1,17},{... | collective-permute-start | bytes 786440 | tf_op jit(solution)/shard_map/ppermute | solution.py:540
  219.4 16.6 %collective-permute-start.26 = (bf16[256,768]{1,0:T(8,128)(2,1)S(1)}, bf16[256,768]{1,0:T(8,128)(2,1)S(1)}, u32[]{:S(2)}, u32[]{:S(2)}) collective-permute-start(bf16[256,768]{1,0:T(8,128)(2,1)S(1)} %get-tuple-element.148), channel_id=1, source_target_pairs={{0,3},{1,2},{2,1},{3,0},{4,7},{5,6},{6,5},{7,4},{8,11},{9,10},{10,... | collective-permute-start | bytes 1179656 | tf_op jit(solution)/shard_map/ppermute | solution.py:537
  219.6 19.6 %collective-permute-start.25 = (bf16[256,768]{1,0:T(8,128)(2,1)S(1)}, bf16[256,768]{1,0:T(8,128)(2,1)S(1)}, u32[]{:S(2)}, u32[]{:S(2)}) collective-permute-start(bf16[256,768]{1,0:T(8,128)(2,1)S(1)} %get-tuple-element.149), channel_id=1, source_target_pairs={{0,2},{1,3},{2,0},{3,1},{4,6},{5,7},{6,4},{7,5},{8,10},{9,11},{10,... | collective-permute-start | bytes 1179656 | tf_op jit(solution)/shard_map/ppermute | solution.py:537
  234.2 5.1 %collective-permute-start.24 = (bf16[256,768]{1,0:T(8,128)(2,1)S(1)}, bf16[256,768]{1,0:T(8,128)(2,1)S(1)}, u32[]{:S(2)}, u32[]{:S(2)}) collective-permute-start(bf16[256,768]{1,0:T(8,128)(2,1)S(1)} %get-tuple-element.131), channel_id=1, source_target_pairs={{0,1},{1,0},{2,3},{3,2},{4,5},{5,4},{6,7},{7,6},{8,9},{9,8},{10,11... | collective-permute-start | bytes 1179656 | tf_op jit(solution)/shard_map/ppermute | solution.py:537
  235.9 13.8 %collective-permute-start.32 = (bf16[1,1024,128]{2,1,0:T(8,128)(2,1)S(1)}, bf16[1,1024,128]{2,1,0:T(8,128)(2,1)S(1)}, u32[]{:S(2)}, u32[]{:S(2)}) collective-permute-start(bf16[1,1024,128]{2,1,0:T(8,128)(2,1)S(1)} %get-tuple-element.147), channel_id=1, source_target_pairs={{0,16},{4,20},{8,24},{12,28},{16,0},{20,4},{24,8},{28,12},{1,17},{... | collective-permute-start | bytes 786440 | tf_op jit(solution)/shard_map/ppermute | solution.py:540
  (14 other events, 231.8 us)
where the time goes:
time: 252 us; the launch traced here: 251 us
  waiting for transfers between devices  124 us (49%)
  Pallas kernels  92.2 us (37%)
  starting transfers between devices  31.1 us (12%)
    ppermute x21, waiting for transfers between devices, over_seq(): return lax.ppermute(x, 'seq', [(i, i ^ d) for i in range(parts)])  84.6 us
    ppermute x12, waiting for transfers between devices, over_dp(): return lax.ppermute(x, 'dp', [(i, i ^ d) for i in range(shares)])  39.3 us
    pallas_call x2, Pallas kernels, attention_back(): pl.pallas_call(functools.partial(backward_kernel, parts, block, docs), gr...  25 us
    pallas_call x2, Pallas kernels, attention(): pl.pallas_call(functools.partial(forward_kernel, parts, block, docs), gri...  20.7 us
    pallas_call x4, Pallas kernels, weight_terms(): pl.pallas_call(functools.partial(weight_kernel, parts, groups, width, ord...  17.3 us
    ppermute x12, starting transfers between devices, over_dp(): return lax.ppermute(x, 'dp', [(i, i ^ d) for i in range(shares)])  16.4 us
    ppermute x21, starting transfers between devices, over_seq(): return lax.ppermute(x, 'seq', [(i, i ^ d) for i in range(parts)])  14.7 us
    pallas_call x2, Pallas kernels, project(): pl.pallas_call(functools.partial(project_kernel, parts, shares, width, le...  11.5 us
  transfers between devices with their start and end apart: 33, of which 14 were waited for; matrix products, arithmetic and copies ran while one was open for 1% of the time, Pallas kernels for 32%

commit v1 on v0

v1 whole, which is shorter than its diff:
```python
import functools
import math

import jax
import jax.numpy as jnp
from jax import lax
from jax.experimental import pallas as pl
from jax.experimental.pallas import tpu as pltpu
from jax.sharding import PartitionSpec as P

HEADS = 32
KV_HEADS = 8
HEAD_DIM = 128
GROUP = HEADS // KV_HEADS
MASKED = -1e30
NT = (((1,), (1,)), ((), ()))
NN = (((1,), (0,)), ((), ()))


def mm(a, b, dims=NN):
    return lax.dot_general(a, b, dims, preferred_element_type=jnp.float32)


def params(mib):
    return pltpu.CompilerParams(vmem_limit_bytes=mib * 2**20)


def cost(us):
    return pl.CostEstimate(flops=int(us * 1.15e9), bytes_accessed=1024, transcendentals=0)


ANY = pl.BlockSpec(memory_space=pl.ANY)


def shape(dims, dtype=jnp.bfloat16):
    return jax.ShapeDtypeStruct(dims, dtype)


def gate(arrays, *tokens):
    flat = [x for token in tokens for x in (token if isinstance(token, tuple) else (token,))]
    return list(lax.optimization_barrier((*arrays, *flat)))[: len(arrays)]


def pack_kernel(parts, jobs, *refs):
    sources, outs, sem = refs[:3], refs[4:-1], refs[-1]
    me = lax.axis_index("seq")
    wide = GROUP * HEAD_DIM
    groups = KV_HEADS // parts
    copies = []
    for out, (d, members) in zip(outs, jobs):
        for slot, gp in enumerate(members):
            place = (me ^ d) * groups + gp
            start = slot * (wide + 2 * HEAD_DIM)
            for source, width in zip(sources, (wide, HEAD_DIM, HEAD_DIM)):
                copies.append(
                    pltpu.make_async_copy(
                        source.at[:, pl.ds(pl.multiple_of(place * width, width), width)],
                        out.at[:, pl.ds(start, width)],
                        sem.at[len(copies)],
                    )
                )
                start += width
    for copy in copies:
        copy.start()
    for copy in copies:
        copy.wait()


def pack(queries, keys, values, token, parts, jobs):
    rows = queries.shape[0]
    size = (GROUP + 2) * HEAD_DIM
    count = 3 * sum(len(members) for d, members in jobs)
    return pl.pallas_call(
        functools.partial(pack_kernel, parts, jobs),
        in_specs=[ANY] * 4,
        out_specs=[ANY] * len(jobs),
        out_shape=[shape((rows, size * len(members))) for d, members in jobs],
        scratch_shapes=[pltpu.SemaphoreType.DMA((count,))],
        compiler_params=params(60),
        cost_estimate=cost(2.0),
        name="pack",
    )(queries, keys, values, token)


def column(share, c, chunks, width):
    return slice((share * chunks + c) * width, (share * chunks + c + 1) * width)


def pack_chunks_kernel(chunks, shares, width, g_ref, *out_refs):
    for c in range(chunks):
        for share in range(shares):
            out_refs[c][:, share * width : (share + 1) * width] = g_ref[
                :, column(share, c, chunks, width)
            ]


def pack_chunks(cotangent, chunks, shares, width):
    rows, model = cotangent.shape
    step = min(64, rows)
    return pl.pallas_call(
        functools.partial(pack_chunks_kernel, chunks, shares, width),
        grid=(rows // step,),
        in_specs=[pl.BlockSpec((step, model), lambda i: (i, 0))],
        out_specs=[pl.BlockSpec((step, shares * width), lambda i: (i, 0))] * chunks,
        out_shape=[shape((rows, shares * width)) for c in range(chunks)],
        compiler_params=params(56),
        cost_estimate=cost(3.8),
        name="pack_chunks",
    )(cotangent)


def unpack_kernel(parts, groups, info_ref, *refs):
    count = parts * groups
    q_ref, k_ref, v_ref = refs[count:]
    wide = GROUP * HEAD_DIM
    for gp in range(groups):
        for d in range(parts):
            piece = refs[gp * parts + d]
            place = (info_ref[0] ^ d) * groups + gp
            q_ref[:, pl.ds(pl.multiple_of(place * wide, wide), wide)] = piece[:, :wide]
            narrow = pl.ds(pl.multiple_of(place * HEAD_DIM, HEAD_DIM), HEAD_DIM)
            k_ref[:, narrow] = piece[:, wide : wide + HEAD_DIM]
            v_ref[:, narrow] = piece[:, wide + HEAD_DIM :]


def unpack(info, pieces, parts, groups):
    rows, cols = pieces[0].shape
    wide = GROUP * HEAD_DIM
    step = min(64, rows)
    total = parts * groups
    widths = (total * wide, total * HEAD_DIM, total * HEAD_DIM)
    return pl.pallas_call(
        functools.partial(unpack_kernel, parts, groups),
        grid_spec=pltpu.PrefetchScalarGridSpec(
            num_scalar_prefetch=1,
            grid=(rows // step,),
            in_specs=[pl.BlockSpec((step, cols), lambda i, info: (i, 0))] * total,
            out_specs=[pl.BlockSpec((step, w), lambda i, info: (i, 0)) for w in widths],
        ),
        out_shape=[shape((rows, w)) for w in widths],
        compiler_params=params(16),
        cost_estimate=cost(2.8),
        name="unpack",
    )(info, *pieces)


def pair_index(qb, kb):
    return qb * (qb + 1) // 2 + kb


def prepare(parts, block, docs, info_ref, bias_ref, open_ref):
    down = lax.broadcasted_iota(jnp.int32, (block, block), 0)
    across = lax.broadcasted_iota(jnp.int32, (1, block), 1)
    for qb in range(parts):
        lanes = qb * block + across
        opening = jnp.zeros((1, block), jnp.int32)
        first = jnp.int32(0)
        for n in range(docs):
            start = info_ref[2 + n]
            opening = jnp.where(start <= lanes, jnp.maximum(opening, start), opening)
            first = jnp.where(start <= qb * block, jnp.maximum(first, start), first)
        open_ref[qb] = first // block
        for kb in range(qb + 1):
            seen = down >= opening - kb * block
            if kb == qb:
                seen = seen & (down <= across)
            bias_ref[pair_index(qb, kb)] = jnp.where(seen, 0.0, MASKED).astype(jnp.float32)


def flip(x):
    return jnp.transpose(x.astype(jnp.float32))


def head_cols(h):
    return slice(h * HEAD_DIM, (h + 1) * HEAD_DIM)


def forward_kernel(parts, block, docs, info_ref, *refs):
    pieces = refs[:parts]
    out_ref, lse_ref = refs[parts : parts + 2]
    bias_ref, open_ref, q_s, k_s, vt_s, top_s, sum_s, acc_s = refs[parts + 2 :]
    me = info_ref[0]
    wide = GROUP * HEAD_DIM
    factor = math.log2(math.e) / math.sqrt(HEAD_DIM)
    prepare(parts, block, docs, info_ref, bias_ref, open_ref)
    for d in range(parts):
        q_s[me ^ d] = pieces[d][:, :wide]
        k_s[me ^ d] = pieces[d][:, wide : wide + HEAD_DIM]
        vt_s[me ^ d] = flip(pieces[d][:, wide + HEAD_DIM :]).astype(jnp.bfloat16)

    def rows_of(qb, carry):
        top_s[...] = jnp.full_like(top_s, 2.0 * MASKED)
        sum_s[...] = jnp.zeros_like(sum_s)
        acc_s[...] = jnp.zeros_like(acc_s)

        def pair(back, carry):
            kb = qb - back
            bias = bias_ref.at[pair_index(qb, kb)]
            for h in range(GROUP):
                raw = mm(k_s[kb], q_s[qb, :, head_cols(h)], NT) * factor + bias[...]
                old = top_s[h]
                top = jnp.maximum(old, jnp.max(raw, axis=0, keepdims=True))
                shrink = jnp.exp2(old - top)
                raised = jnp.exp2(raw - top)
                top_s[h] = top
                sum_s[h] = sum_s[h] * shrink + jnp.sum(raised, axis=0, keepdims=True)
                acc_s[h] = acc_s[h] * shrink + mm(vt_s[kb], raised.astype(jnp.bfloat16))
            return carry

        lax.fori_loop(0, qb - open_ref[qb] + 1, pair, 0)
        for h in range(GROUP):
            out_ref[me ^ qb, head_cols(h)] = (acc_s[h] / sum_s[h]).astype(jnp.bfloat16)
            lse_ref[h, me ^ qb] = jnp.broadcast_to(top_s[h] + jnp.log2(sum_s[h]), (8, block))
        return carry

    lax.fori_loop(0, parts, rows_of, 0)


def whole_block(dims):
    return pl.BlockSpec(dims, lambda i, info: (0,) * len(dims))


def piece_block(rows, cols, at):
    return pl.BlockSpec((rows, cols), lambda i, info: (0, at))


def attention(info, pieces, token, parts, docs):
    block, cols = pieces[-1][0].shape
    pairs = parts * (parts + 1) // 2
    wide = GROUP * HEAD_DIM
    vm = pltpu.VMEM
    return pl.pallas_call(
        functools.partial(forward_kernel, parts, block, docs),
        grid_spec=pltpu.PrefetchScalarGridSpec(
            num_scalar_prefetch=1,
            grid=(1,),
            in_specs=[piece_block(block, cols, at) for x, at in pieces],
            out_specs=[
                whole_block((parts, wide, block)),
                whole_block((GROUP, parts, 8, block)),
            ],
            scratch_shapes=[
                vm((pairs, block, block), jnp.float32),
                pltpu.SMEM((parts,), jnp.int32),
                vm((parts, block, wide), jnp.bfloat16),
                vm((parts, block, HEAD_DIM), jnp.bfloat16),
                vm((parts, HEAD_DIM, block), jnp.bfloat16),
                vm((GROUP, 1, block), jnp.float32),
                vm((GROUP, 1, block), jnp.float32),
                vm((GROUP, HEAD_DIM, block), jnp.float32),
            ],
        ),
        out_shape=[
            shape((parts, wide, block)),
            shape((GROUP, parts, 8, block), jnp.float32),
        ],
        compiler_params=params(16),
        cost_estimate=cost(10.0),
        name="attention",
    )(gate([info], token)[0], *[x for x, at in pieces])


def backward_kernel(parts, block, docs, info_ref, *refs):
    pieces = refs[:parts]
    grad_ref, out_ref, lse_ref = refs[parts : parts + 3]
    res_ref = refs[parts + 3]
    bias_ref, open_ref, q_s, k_s, kt_s, v_s, dk_s, dv_s, dq_s, delta_s = refs[parts + 4 :]
    me = info_ref[0]
    wide = GROUP * HEAD_DIM
    scale = 1.0 / math.sqrt(HEAD_DIM)
    factor = math.log2(math.e) * scale
    prepare(parts, block, docs, info_ref, bias_ref, open_ref)
    for d in range(parts):
        q_s[me ^ d] = pieces[d][:, :wide]
        k_s[me ^ d] = pieces[d][:, wide : wide + HEAD_DIM]
        kt_s[me ^ d] = flip(pieces[d][:, wide : wide + HEAD_DIM]).astype(jnp.bfloat16)
        v_s[me ^ d] = pieces[d][:, wide + HEAD_DIM :]
    dk_s[...] = jnp.zeros_like(dk_s)
    dv_s[...] = jnp.zeros_like(dv_s)

    def rows_of(qb, carry):
        spot = me ^ qb
        dq_s[...] = jnp.zeros_like(dq_s)
        for h in range(GROUP):
            product = flip(grad_ref[spot, :, head_cols(h)]) * out_ref[spot, head_cols(h)].astype(
                jnp.float32
            )
            delta_s[h] = jnp.sum(product, axis=0, keepdims=True)

        def pair(back, carry):
            kb = qb - back
            bias = bias_ref.at[pair_index(qb, kb)]
            key, value = k_s[kb], v_s[kb]
            dk = dk_s[kb]
            dv = dv_s[kb]
            for h in range(GROUP):
                query, grad = q_s[qb, :, head_cols(h)], grad_ref[spot, :, head_cols(h)]
                raw = mm(key, query, NT) * factor + bias[...]
                probs = jnp.exp2(raw - lse_ref[h, spot, :1])
                dv += mm(probs.astype(jnp.bfloat16), grad)
                slope = (probs * (mm(value, grad, NT) - delta_s[h])).astype(jnp.bfloat16)
                dk += mm(slope, query)
                dq_s[h] += mm(kt_s[kb], slope)
            dk_s[kb] = dk
            dv_s[kb] = dv
            return carry

        lax.fori_loop(0, qb - open_ref[qb] + 1, pair, 0)
        for h in range(GROUP):
            res_ref[spot, :, head_cols(h)] = (jnp.transpose(dq_s[h]) * scale).astype(jnp.bfloat16)
        return carry

    lax.fori_loop(0, parts, rows_of, 0)
    for kb in range(parts):
        res_ref[me ^ kb, :, wide : wide + HEAD_DIM] = (dk_s[kb] * scale).astype(jnp.bfloat16)
        res_ref[me ^ kb, :, wide + HEAD_DIM :] = dv_s[kb].astype(jnp.bfloat16)


def attention_back(info, pieces, grads, out, lse, token, parts, docs, gp):
    block, cols = pieces[-1][0].shape
    pairs = parts * (parts + 1) // 2
    wide = GROUP * HEAD_DIM
    vm = pltpu.VMEM
    return pl.pallas_call(
        functools.partial(backward_kernel, parts, block, docs),
        grid_spec=pltpu.PrefetchScalarGridSpec(
            num_scalar_prefetch=1,
            grid=(1,),
            in_specs=[piece_block(block, cols, at) for x, at in pieces]
            + [
                pl.BlockSpec((parts, block, wide), lambda i, info: (0, 0, gp)),
                whole_block((parts, wide, block)),
                whole_block((GROUP, parts, 8, block)),
            ],
            out_specs=whole_block((parts, block, cols)),
            scratch_shapes=[
                vm((pairs, block, block), jnp.float32),
                pltpu.SMEM((parts,), jnp.int32),
                vm((parts, block, wide), jnp.bfloat16),
                vm((parts, block, HEAD_DIM), jnp.bfloat16),
                vm((parts, HEAD_DIM, block), jnp.bfloat16),
                vm((parts, block, HEAD_DIM), jnp.bfloat16),
                vm((parts, block, HEAD_DIM), jnp.float32),
                vm((parts, block, HEAD_DIM), jnp.float32),
                vm((GROUP, HEAD_DIM, block), jnp.float32),
                vm((GROUP, 1, block), jnp.float32),
            ],
        ),
        out_shape=shape((parts, block, cols)),
        compiler_params=params(20),
        cost_estimate=cost(3.0),
        name="attention_back",
    )(gate([info], token)[0], *[x for x, at in pieces], grads, out, lse)


def weight_kernel(parts, groups, width, across, info_ref, *refs):
    outs, lows, highs = refs[:groups], refs[groups : groups + 2], refs[groups + 2 : groups + 4]
    chunk = refs[groups + 4 : groups + 2 + parts]
    results = refs[groups + 2 + parts :]
    odd = (info_ref[1] & 1) == 1
    rows = GROUP * HEAD_DIM
    grads = [jnp.concatenate([lows[d][...], highs[d][...]], axis=1) for d in range(2)]
    for gp in range(groups):
        total = mm(outs[gp][0], grads[0]) + mm(outs[gp][1], grads[1])
        for d in range(2, parts):
            total += mm(outs[gp][d], chunk[d - 2][...])
        low, high = total[:, :width], total[:, width:]
        spot = slice(gp * rows, (gp + 1) * rows)
        keep = jnp.where(odd, high, low)
        send = jnp.where(odd, low, high).astype(jnp.bfloat16)
        if across:
            results[0][0, spot] = keep
            results[1][0, spot] = send
        else:
            results[0][0, 0, spot] = keep.astype(jnp.bfloat16)
            results[0][0, 1, spot] = send


def weight_terms(info, outs, near, chunk, token, shares, c, chunks, width, across):
    groups, parts = len(outs), 2 + len(chunk)
    _, rows, block = outs[0].shape
    half = shares // 2
    feats = groups * rows

    def original(side):
        return pl.BlockSpec((block, width), lambda t, info: (0, (2 * t + side) * chunks + c))

    if across:
        out_specs = [pl.BlockSpec((1, feats, width), lambda t, info: (t, 0, 0))] * 2
        out_shape = [shape((half, feats, width), jnp.float32), shape((half, feats, width))]
    else:
        out_specs = [pl.BlockSpec((1, 2, feats, width), lambda t, info: (t, 0, 0, 0))]
        out_shape = [shape((half, 2, feats, width))]
    return pl.pallas_call(
        functools.partial(weight_kernel, parts, groups, width, across),
        grid_spec=pltpu.PrefetchScalarGridSpec(
            num_scalar_prefetch=1,
            grid=(half,),
            in_specs=[pl.BlockSpec((parts, rows, block), lambda t, info: (0, 0, 0))] * groups
            + [original(0)] * 2
            + [original(1)] * 2
            + [pl.BlockSpec((block, 2 * width), lambda t, info: (0, t))] * len(chunk),
            out_specs=out_specs,
        ),
        out_shape=out_shape,
        compiler_params=params(16),
        cost_estimate=cost(1.0),
        name="weight_terms",
    )(gate([info], token)[0], *outs, *near, *near, *chunk)


def merge_kernel(keep_ref, got_ref, sum_ref):
    sum_ref[...] = (keep_ref[...] + got_ref[...].astype(jnp.float32)).astype(jnp.bfloat16)


def merge(keep, got, token):
    count, rows, width = keep.shape
    spec = pl.BlockSpec((1, rows, width), lambda t: (t, 0, 0))
    return pl.pallas_call(
        merge_kernel,
        grid=(count,),
        in_specs=[spec, spec],
        out_specs=spec,
        out_shape=shape((count, rows, width)),
        compiler_params=params(12),
        cost_estimate=cost(0.5),
        name="merge",
    )(gate([keep], token)[0], got)


def finish_kernel(scale, count, *refs):
    total = refs[0][...].astype(jnp.float32)
    for ref in refs[1:count]:
        total += ref[...].astype(jnp.float32)
    refs[-1][...] = total * scale


def finish(terms, so_far, token, c, chunks, scale):
    rows, width = terms[0].shape
    more = [] if so_far is None else [so_far]
    step = rows // 2
    spec = pl.BlockSpec((step, width), lambda i: (i, 0))
    return pl.pallas_call(
        functools.partial(finish_kernel, scale, len(terms)),
        grid=(rows // step,),
        in_specs=[spec] * len(terms) + [ANY] * len(more),
        out_specs=pl.BlockSpec((step, width), lambda i: (i, c)),
        out_shape=shape((rows, width * chunks), jnp.float32),
        input_output_aliases={len(terms): 0} if more else {},
        compiler_params=params(8),
        cost_estimate=cost(0.8),
        name="finish",
    )(*gate(terms, token), *more)


def project_kernel(parts, shares, width, chunks, picked, first, *refs):
    w_ref, near = refs[0], refs[1:3]
    far = refs[3 : 3 + len(picked) * (parts - 2)]
    acc_ref, out_ref = refs[-2] if not first else None, refs[-1]
    columns = [(c, share) for c in picked for share in range(shares)]
    weights = jnp.concatenate([w_ref[:, column(j, c, chunks, width)] for c, j in columns], axis=1)
    for d in range(parts):
        if d < 2:
            rows = jnp.concatenate([near[d][:, column(j, c, chunks, width)] for c, j in columns], axis=1)
        else:
            mine = [far[i * (parts - 2) + d - 2][...] for i in range(len(picked))]
            rows = mine[0] if len(mine) == 1 else jnp.concatenate(mine, axis=1)
        total = mm(rows, weights, NT)
        if not first:
            total += acc_ref[d]
        out_ref[d] = total.astype(out_ref.dtype)


def project(out_weight, near, far, acc, token, chunks, picked, shares, width, last):
    feats, model = out_weight.shape
    rows = near[0].shape[0]
    parts = 2 + len(far[0])
    step = min(256, feats)
    flat = [x for group in far for x in group]
    first = acc is None
    block = pl.BlockSpec((parts, rows, step), lambda i: (0, 0, i))
    return pl.pallas_call(
        functools.partial(
            project_kernel, parts, shares, width, chunks, picked, first
        ),
        grid=(feats // step,),
        in_specs=[pl.BlockSpec((step, model), lambda i: (i, 0))]
        + [pl.BlockSpec((rows, model), lambda i: (0, 0))] * 2
        + [pl.BlockSpec((rows, shares * width), lambda i: (0, 0))] * len(flat)
        + ([] if first else [block]),
        out_specs=block,
        out_shape=shape((parts, rows, feats), jnp.bfloat16 if last else jnp.float32),
        compiler_params=params(24),
        cost_estimate=cost(0.7 * len(picked)),
        name="project",
    )(gate([out_weight], token)[0], *near, *flat, *([] if first else [acc]))


def body(grad_out, queries, keys, values, out_weight, doc_starts):
    parts, shares = lax.axis_size("seq"), lax.axis_size("dp")
    groups = KV_HEADS // parts
    docs = doc_starts.shape[-1]
    cotangent = grad_out[0]
    rows, model = cotangent.shape
    chunks = max(1, min(4, model // shares // 128))
    width = model // shares // chunks
    scale = 1.0 / math.sqrt(rows * parts * shares)
    columns = [list(range(side, shares, 2)) for side in range(2)]
    info = jnp.concatenate(
        [
            jnp.stack([lax.axis_index("seq"), lax.axis_index("dp")]).astype(jnp.int32),
            doc_starts[0],
        ]
    )

    def over_seq(x, d):
        return lax.ppermute(x, "seq", [(i, i ^ d) for i in range(parts)])

    def across(x):
        return lax.ppermute(x, "dp", [(i, i ^ 1) for i in range(shares)])

    def along(x):
        return lax.psum_scatter(
            x, "dp", scatter_dimension=0, axis_index_groups=columns, tiled=True
        )[0]

    far = range(2, parts)
    all_groups = tuple(range(groups))
    sources = (queries[0], keys[0], values[0])
    packed = [pack(*sources, doc_starts, parts, tuple((d, (0,)) for d in far))]
    rest = [(d, (gp,)) for gp in range(1, groups) for d in far]
    rest = pack(*sources, packed[0][0], parts, tuple([(0, all_groups), (1, all_groups)] + rest))
    for gp in range(1, groups):
        packed.append(rest[2 + (gp - 1) * len(far) : 2 + gp * len(far)])
    sent_far = [[over_seq(x, d) for x, d in zip(group, far)] for group in packed]
    core = over_seq(rest[1], 1)
    pieces = [[(rest[0], gp), (core, gp)] + [(x, 0) for x in sent_far[gp]] for gp in range(groups)]
    sends = pack_chunks(gate([cotangent], rest[0])[0], chunks, shares, width)
    near = [cotangent, over_seq(gate([cotangent], *sent_far[0], sends[-1])[0], 1)]

    far_half = {}

    def send_chunk(c, *tokens):
        mine = gate([sends[c]], *tokens)[0]
        far_half[c] = [over_seq(mine, d) for d in range(2, parts, 2)]

    fwd = []
    token = sends[-1]
    for gp in range(groups):
        fwd.append(attention(info, pieces[gp], token, parts, docs))
        token = fwd[-1][0]
        if gp == 0:
            send_chunk(0, *sent_far[0])
            token = (token, near[1])
    for c in range(1, chunks):
        if c < groups:
            send_chunk(c, *sent_far[c])
        else:
            send_chunk(c, *far_half[max(0, c - groups)])
    outs = [pair[0] for pair in fwd]

    fars, waiting, back, results = {}, {}, {}, {}
    acc = weight_grad = None

    def weigh(c):
        nonlocal token
        fars[c] = []
        for x in gate(far_half[c], token):
            fars[c] += [x, over_seq(x, 1)]
        first_across = c != 0
        terms = weight_terms(
            info, outs, near, fars[c], token, shares, c, chunks, width, first_across
        )
        token = terms[-1]
        if first_across:
            waiting[c] = (terms[0], across(terms[1]))
        else:
            waiting[c] = along(terms[0])

    def combine(c):
        nonlocal token
        if c != 0:
            token = merge(*waiting[c], token)
            waiting[c] = (along(token),)
        else:
            keep, send = gate([waiting[c]], token)[0]
            waiting[c] = (keep, across(send))

    def settle(c):
        nonlocal token, weight_grad
        token = weight_grad = finish(waiting[c], weight_grad, token, c, chunks, scale)

    def project_step(picked, last):
        nonlocal token, acc
        token = acc = project(
            out_weight, near, [fars[c] for c in picked], acc, token, chunks, picked, shares, width, last
        )

    def send_back(gp):
        nonlocal token
        res = attention_back(info, pieces[gp], acc, outs[gp], fwd[gp][1], token, parts, docs, gp)
        token = results[gp] = res
        back[gp] = [res[0], None] + [over_seq(res[d], d) for d in far]

    last = chunks - 1
    for c in range(last):
        weigh(c)
    if last:
        project_step(list(range(last)), False)
        combine(0)
    weigh(last)
    project_step([last], True)
    if last > 1:
        combine(1)
    send_back(0)
    for c in range(2, last):
        combine(c)
    if last:
        settle(0)
    for gp in range(1, groups):
        send_back(gp)
    if groups > 1:
        token = (token, *back[0][2:])
    if last:
        combine(last)
    else:
        combine(0)
    token = (token, *back[groups - 1][2:])
    for c in range(1, last):
        settle(c)
    core = over_seq(jnp.concatenate([results[gp][1] for gp in range(groups)], axis=0), 1)
    for gp in range(groups):
        back[gp][1] = core[gp * rows : (gp + 1) * rows]
    back = [x for gp in range(groups) for x in back[gp]]
    grad_q, grad_k, grad_v = unpack(gate([info], token)[0], back, parts, groups)
    token = grad_q
    settle(last)
    return (grad_q[None], grad_k[None], grad_v[None], weight_grad)


def solution(mesh):
    return jax.shard_map(
        body,
        mesh=mesh,
        in_specs=(
            P("dp", "seq", None),
            P("dp", "seq", None),
            P("dp", "seq", None),
            P("dp", "seq", None),
            P("seq", None),
            P("dp", None),
        ),
        out_specs=(
            P("dp", "seq", None),
            P("dp", "seq", None),
            P("dp", "seq", None),
            P("seq", "dp"),
        ),
        check_vma=False,
    )
```

time: 252 us -> 340 us (1.35)
  Pallas kernels: 92.2 us -> 201 us
  waiting for transfers between devices: 124 us -> 70.6 us
  local copies, waits for them, and re-layouts: 1.26 us -> 32.2 us
  between operations: 1 us -> 14.1 us
  starting transfers between devices: 31.1 us -> 19.7 us
    pallas_call x21 -> x16, Pallas kernels: 43.8 us -> 146 us  [the longest x2 97.7 us: pack(): pl.pallas_call(functools.partial(pack_kernel, parts, jobs), in_specs=[ANY...]
    ppermute x21 -> x19, waiting for transfers between devices: 84.6 us -> 42.3 us  [over_seq(): return lax.ppermute(x, 'seq', [(i, i ^ d) for i in range(parts)])]
    unnamed x26 -> x102, local copies, waits for them, and re-layouts: 1.05 us -> 29.2 us
    ppermute x12 -> x4, starting transfers between devices: 16.4 us -> 4.29 us  [across(): return lax.ppermute(x, 'dp', [(i, i ^ 1) for i in range(shares)])]
    ppermute x12 -> x4, waiting for transfers between devices: 39.3 us -> 28.2 us  [across(): return lax.ppermute(x, 'dp', [(i, i ^ 1) for i in range(shares)])]
    pallas_call x2, Pallas kernels: 25 us -> 28.7 us  [attention_back(): pl.pallas_call(functools.partial(backward_kernel, parts, block, docs), gr...]
    pallas_call x2, Pallas kernels: 20.7 us -> 24.3 us  [attention(): pl.pallas_call(functools.partial(forward_kernel, parts, block, docs), gri...]
    ppermute x21 -> x19, starting transfers between devices: 14.7 us -> 15.1 us  [over_seq(): return lax.ppermute(x, 'seq', [(i, i ^ d) for i in range(parts)])]
  transfers between devices with their start and end apart: 33 -> 27, of which waited for: 14 -> 10; matrix products, arithmetic and copies ran while one was open for 1% -> 1% of each run, Pallas kernels for 32% -> 50%
where the time goes in v1:
time: 340 us; the launch traced here: 339 us
  Pallas kernels  201 us (59%)
  waiting for transfers between devices  70.6 us (21%)
  local copies, waits for them, and re-layouts  32.2 us (9%)
  starting transfers between devices  19.7 us (6%)
  between operations  14.1 us (4%)
    pallas_call x2, Pallas kernels, pack(): pl.pallas_call(functools.partial(pack_kernel, parts, jobs), in_specs=[ANY...  97.7 us
    ppermute x19, waiting for transfers between devices, over_seq(): return lax.ppermute(x, 'seq', [(i, i ^ d) for i in range(parts)])  42.3 us
    unnamed x102, local copies, waits for them, and re-layouts  29.2 us
    pallas_call x2, Pallas kernels, attention_back(): pl.pallas_call(functools.partial(backward_kernel, parts, block, docs), gr...  28.7 us
    ppermute x4, waiting for transfers between devices, across(): return lax.ppermute(x, 'dp', [(i, i ^ 1) for i in range(shares)])  28.2 us
    pallas_call x2, Pallas kernels, attention(): pl.pallas_call(functools.partial(forward_kernel, parts, block, docs), gri...  24.3 us
    pallas_call x4, Pallas kernels, weight_terms(): pl.pallas_call(functools.partial(weight_kernel, parts, groups, width, acr...  18.9 us
    ppermute x19, starting transfers between devices, over_seq(): return lax.ppermute(x, 'seq', [(i, i ^ d) for i in range(parts)])  15.1 us
  transfers between devices with their start and end apart: 27, of which 10 were waited for; matrix products, arithmetic and copies ran while one was open for 1% of the time, Pallas kernels for 50%

profile of v1, /device:TPU:0, one launch (start us, length us, event | category | flops | bytes accessed | tf_op | source)
XLA Modules:
  0.0 338.9 jit_solution(4280250813452868278)
XLA Ops:
  7.2 25.0 %pack.2 = (bf16[256,768]{1,0:T(8,128)(2,1)}, bf16[256,768]{1,0:T(8,128)(2,1)}) custom-call(bf16[256,4096]{1,0:T(8,128)(2,1)} %bitcast.53, bf16[256,1024]{1,0:T(8,128)(2,1)} %bitcast.55, bf16[256,1024]{1,0:T(8,128)(2,1)} %bitcast.57, s32[1,8]{1,0:T(1,128)} %refs_3_.1), custom_call_target="tpu_custom_call" | custom-call | flops 2300000000 | bytes 1024 | tf_op jit(solution)/shard_map/pack/pallas_call | solution.py:73
  32.2 2.5 collective-permute-start.2
  35.3 72.7 %pack.3 = (bf16[256,1536]{1,0:T(8,128)(2,1)}, bf16[256,1536]{1,0:T(8,128)(2,1)}, bf16[256,768]{1,0:T(8,128)(2,1)}, bf16[256,768]{1,0:T(8,128)(2,1)}) custom-call(bf16[256,4096]{1,0:T(8,128)(2,1)} %bitcast.54, bf16[256,1024]{1,0:T(8,128)(2,1)} %bitcast.56, bf16[256,1024]{1,0:T(8,128)(2,1)} %bitcast.58, bf16[256,768]{1,0:T(8,128)(2,1)} %get-tuple-element.57.refs_3_), custom_call_target="tpu_custom_call" | custom-call | flops 2300000000 | bytes 1024 | tf_op jit(solution)/shard_map/pack/pallas_call | solution.py:73
  108.1 4.0 %pack_chunks.1 = (bf16[256,1024]{1,0:T(8,128)(2,1)}, bf16[256,1024]{1,0:T(8,128)(2,1)}, bf16[256,1024]{1,0:T(8,128)(2,1)}, bf16[256,1024]{1,0:T(8,128)(2,1)}) custom-call(bf16[256,4096]{1,0:T(8,128)(2,1)} %bitcast.34), custom_call_target="tpu_custom_call" | custom-call | flops 4369999872 | bytes 1024 | tf_op jit(solution)/shard_map/pack_chunks/pallas_call | solution.py:100
  115.6 1.7 collective-permute-start.6
  121.9 11.6 %attention.2 = (bf16[4,512,256]{2,1,0:T(8,128)(2,1)S(1)}, f32[4,4,8,256]{3,2,1,0:T(8,128)S(1)}) custom-call(s32[10]{0:T(128)S(1)} %pad_add_fusion.info_ref, bf16[256,1536]{1,0:T(8,128)(2,1)S(1)} %copy-done.39, bf16[256,1536]{1,0:T(8,128)(2,1)S(1)} %collective-permute-done.refs_1_, bf16[256,768]{1,0:T(8,128)(2,1)S(1)} %copy-done.33, ...), custom_call_target="tpu_custom_call" | custom-call | flops 11500000256 | bytes 1024 | tf_op jit(solution)/shard_map/attention/pallas_call | solution.py:232
  134.2 1.5 copy-done.26
  135.7 12.7 %attention.3 = (bf16[4,512,256]{2,1,0:T(8,128)(2,1)S(1)}, f32[4,4,8,256]{3,2,1,0:T(8,128)S(1)}) custom-call(s32[10]{0:T(128)S(1)} %pad_add_fusion.info_ref, bf16[256,1536]{1,0:T(8,128)(2,1)S(1)} %copy-done.39, bf16[256,1536]{1,0:T(8,128)(2,1)S(1)} %copy-done.26, bf16[256,768]{1,0:T(8,128)(2,1)S(1)} %collective-permute-done.4.refs_2_, ...), custom_call_target="tpu_custom_call" | custom-call | flops 11500000256 | bytes 1024 | tf_op jit(solution)/shard_map/attention/pallas_call | solution.py:232
  149.4 1.5 collective-permute-done.7.refs_7_.refs_4_
  151.0 4.6 %weight_terms.4 = bf16[4,2,1024,128]{3,2,1,0:T(8,128)(2,1)S(1)} custom-call(s32[10]{0:T(128)S(1)} %pad_add_fusion.info_ref, bf16[4,512,256]{2,1,0:T(8,128)(2,1)S(1)} %get-tuple-element.64.refs_0_.refs_5_, bf16[4,512,256]{2,1,0:T(8,128)(2,1)S(1)} %get-tuple-element.69.refs_1_.refs_5_, bf16[256,4096]{1,0:T(8,128)(2,1)S(1)} %bitcast.36, ...), custom_call_target="tpu_custom_call" | custom-call | flops 1150000000 | bytes 1024 | tf_op jit(solution)/shard_map/weight_terms/pallas_call | solution.py:394
  158.6 1.8 collective-permute-start.8
  160.4 12.7 %collective-permute-done.8.refs_6_.refs_5_ = bf16[256,1024]{1,0:T(8,128)(2,1)S(1)} collective-permute-done((bf16[256,1024]{1,0:T(8,128)(2,1)}, bf16[256,1024]{1,0:T(8,128)(2,1)S(1)}, u32[]{:S(2)}, u32[]{:S(2)}) %collective-permute-start.8) | collective-permute-done | bytes 524320 | tf_op jit(solution)/shard_map/ppermute | solution.py:517
  176.3 4.9 %weight_terms.5 = (f32[4,1024,128]{2,1,0:T(8,128)S(1)}, bf16[4,1024,128]{2,1,0:T(8,128)(2,1)S(1)}) custom-call(s32[10]{0:T(128)S(1)} %pad_add_fusion.info_ref, bf16[4,512,256]{2,1,0:T(8,128)(2,1)S(1)} %copy-done.2, bf16[4,512,256]{2,1,0:T(8,128)(2,1)S(1)} %get-tuple-element.69.refs_1_.refs_5_, bf16[256,4096]{1,0:T(8,128)(2,1)S(1)} %bitcast.38, ...), custom_call_target="tpu_custom_call" | custom-call | flops 1150000000 | bytes 1024 | tf_op jit(solution)/shard_map/weight_terms/pallas_call | solution.py:394
  181.2 6.5 %collective-permute-done.10.refs_6_.refs_7_ = bf16[256,1024]{1,0:T(8,128)(2,1)S(1)} collective-permute-done((bf16[256,1024]{1,0:T(8,128)(2,1)}, bf16[256,1024]{1,0:T(8,128)(2,1)S(1)}, u32[]{:S(2)}, u32[]{:S(2)}) %collective-permute-start.10) | collective-permute-done | bytes 524320 | tf_op jit(solution)/shard_map/ppermute | solution.py:517
  187.7 1.6 collective-permute-start.12
  190.7 4.6 %weight_terms.6 = (f32[4,1024,128]{2,1,0:T(8,128)S(1)}, bf16[4,1024,128]{2,1,0:T(8,128)(2,1)S(1)}) custom-call(s32[10]{0:T(128)S(1)} %pad_add_fusion.info_ref, bf16[4,512,256]{2,1,0:T(8,128)(2,1)S(1)} %copy-done.2, bf16[4,512,256]{2,1,0:T(8,128)(2,1)S(1)} %get-tuple-element.69.refs_1_.refs_5_, bf16[256,4096]{1,0:T(8,128)(2,1)S(1)} %bitcast.40, ...), custom_call_target="tpu_custom_call" | custom-call | flops 1150000000 | bytes 1024 | tf_op jit(solution)/shard_map/weight_terms/pallas_call | solution.py:394
  197.7 9.4 %project.2.refs_5_ = f32[4,256,1024]{2,1,0:T(8,128)S(1)} custom-call(bf16[1024,4096]{1,0:T(8,128)(2,1)S(1)} %bitcast.47, bf16[256,4096]{1,0:T(8,128)(2,1)S(1)} %bitcast.42, bf16[256,4096]{1,0:T(8,128)(2,1)} %collective-permute-done.3.refs_3_.refs_5_.refs_2_, bf16[256,1024]{1,0:T(8,128)(2,1)S(1)} %copy-done.14, bf16[256,1024]{1,0:T(8,128)(2,1)S(1)} %copy-done.16, ...), custom_call_target="tpu_custom_call" | custom-call | flops 2415000064 | bytes 1024 | tf_op jit(solution)/shard_map/project/pallas_call | solution.py:482
  207.2 1.9 collective-permute-done.13.refs_7_.refs_4_
  209.1 4.6 %weight_terms.7 = (f32[4,1024,128]{2,1,0:T(8,128)S(1)}, bf16[4,1024,128]{2,1,0:T(8,128)(2,1)S(1)}) custom-call(s32[10]{0:T(128)S(1)} %pad_add_fusion.info_ref, bf16[4,512,256]{2,1,0:T(8,128)(2,1)S(1)} %copy-done.3, bf16[4,512,256]{2,1,0:T(8,128)(2,1)S(1)} %get-tuple-element.69.refs_1_.refs_5_, bf16[256,4096]{1,0:T(8,128)(2,1)S(1)} %bitcast.43, ...), custom_call_target="tpu_custom_call" | custom-call | flops 1150000000 | bytes 1024 | tf_op jit(solution)/shard_map/weight_terms/pallas_call | solution.py:394
  215.1 5.5 %project.3.refs_4_ = bf16[4,256,1024]{2,1,0:T(8,128)(2,1)S(1)} custom-call(bf16[1024,4096]{1,0:T(8,128)(2,1)S(1)} %bitcast.47, bf16[256,4096]{1,0:T(8,128)(2,1)S(1)} %bitcast.45, bf16[256,4096]{1,0:T(8,128)(2,1)} %collective-permute-done.3.refs_3_.refs_5_.refs_2_, bf16[256,1024]{1,0:T(8,128)(2,1)S(1)} %collective-permute-done.12.refs_6_.refs_3_, ...), custom_call_target="tpu_custom_call" | custom-call | flops 805000000 | bytes 1024 | tf_op jit(solution)/shard_map/project/pallas_call | solution.py:482
  221.9 1.7 merge.3
  224.5 1.6 copy-done.7
  231.3 13.8 %attention_back.2 = bf16[4,256,768]{2,1,0:T(8,128)(2,1)S(1)} custom-call(s32[10]{0:T(128)S(1)} %pad_add_fusion.info_ref, bf16[256,1536]{1,0:T(8,128)(2,1)S(1)} %copy-done.40, bf16[256,1536]{1,0:T(8,128)(2,1)S(1)} %copy-done.27, bf16[256,768]{1,0:T(8,128)(2,1)S(1)} %copy-done.34, bf16[256,768]{1,0:T(8,128)(2,1)S(1)} %copy-done.31, ...), custom_call_target="tpu_custom_call" | custom-call | flops 3449999872 | bytes 1024 | tf_op jit(solution)/shard_map/attention_back/pallas_call | solution.py:324
  246.3 2.9 collective-permute-done.15.got_ref
  249.1 1.6 merge.4
  252.5 1.5 collective-permute-start.16
  255.8 25.3 %collective-permute-done.16.refs_1_ = bf16[1024,128]{1,0:T(8,128)(2,1)S(1)} collective-permute-done((bf16[1024,128]{1,0:T(8,128)(2,1)S(1)}, bf16[1024,128]{1,0:T(8,128)(2,1)S(1)}, u32[]{:S(2)}, u32[]{:S(2)}) %collective-permute-start.16) | collective-permute-done | bytes 262176 | tf_op jit(solution)/shard_map/ppermute | solution.py:520
  281.9 14.9 %attention_back.3 = bf16[4,256,768]{2,1,0:T(8,128)(2,1)S(1)} custom-call(s32[10]{0:T(128)S(1)} %pad_add_fusion.info_ref, bf16[256,1536]{1,0:T(8,128)(2,1)S(1)} %copy-done.41, bf16[256,1536]{1,0:T(8,128)(2,1)S(1)} %copy-done.28, bf16[256,768]{1,0:T(8,128)(2,1)S(1)} %collective-permute-done.4.refs_2_, bf16[256,768]{1,0:T(8,128)(2,1)} %collective-permute-done.5.refs_3_, ...), custom_call_target="tpu_custom_call" | custom-call | flops 3449999872 | bytes 1024 | tf_op jit(solution)/shard_map/attention_back/pallas_call | solution.py:324
  298.4 3.5 %merge.5 = bf16[4,1024,128]{2,1,0:T(8,128)(2,1)} custom-call(f32[4,1024,128]{2,1,0:T(8,128)S(1)} %copy-done.10, bf16[4,1024,128]{2,1,0:T(8,128)(2,1)} %collective-permute-done.19.got_ref), custom_call_target="tpu_custom_call" | custom-call | flops 575000000 | bytes 1024 | tf_op jit(solution)/shard_map/merge/pallas_call | solution.py:419
  305.9 8.8 %collective-permute-done.21.refs_7_ = bf16[256,768]{1,0:T(8,128)(2,1)S(1)} collective-permute-done((bf16[256,768]{1,0:T(8,128)(2,1)}, bf16[256,768]{1,0:T(8,128)(2,1)S(1)}, u32[]{:S(2)}, u32[]{:S(2)}) %collective-permute-start.21) | collective-permute-done | bytes 393248 | tf_op jit(solution)/shard_map/ppermute | solution.py:517
  314.8 9.1 %collective-permute-done.20.refs_6_ = bf16[256,768]{1,0:T(8,128)(2,1)S(1)} collective-permute-done((bf16[256,768]{1,0:T(8,128)(2,1)}, bf16[256,768]{1,0:T(8,128)(2,1)S(1)}, u32[]{:S(2)}, u32[]{:S(2)}) %collective-permute-start.20) | collective-permute-done | bytes 393248 | tf_op jit(solution)/shard_map/ppermute | solution.py:517
  327.9 2.8 unpack.1
  (156 shorter events, 45.9 us)
Async XLA Ops:
  7.2 244.3 %reduce-scatter.9.cloned.1.call-start = ((), (), s32[]{:S(2)}) async-start(), calls=%async_computation.6 | async-start | bytes 2621440 | tf_op jit(solution)/shard_map/reduce_scatter | solution.py:523
  32.2 79.9 %collective-permute-start.2 = (bf16[256,768]{1,0:T(8,128)(2,1)}, bf16[256,768]{1,0:T(8,128)(2,1)S(1)}, u32[]{:S(2)}, u32[]{:S(2)}) collective-permute-start(bf16[256,768]{1,0:T(8,128)(2,1)} %get-tuple-element.63), channel_id=1, source_target_pairs={{0,3},{1,2},{2,1},{3,0},{4,7},{5,6},{6,5},{7,4},{8,11},{9,10},{10,... | collective-permute-start | bytes 1179656 | tf_op jit(solution)/shard_map/ppermute | solution.py:517
  34.7 78.2 %collective-permute-start.1 = (bf16[256,768]{1,0:T(8,128)(2,1)}, bf16[256,768]{1,0:T(8,128)(2,1)S(1)}, u32[]{:S(2)}, u32[]{:S(2)}) collective-permute-start(bf16[256,768]{1,0:T(8,128)(2,1)} %get-tuple-element.57.refs_3_), channel_id=1, source_target_pairs={{0,2},{1,3},{2,0},{3,1},{4,6},{5,7},{6,4},{7,5},{8,10},{9,11},{10,... | collective-permute-start | bytes 1179656 | tf_op jit(solution)/shard_map/ppermute | solution.py:517
  113.6 20.6 %collective-permute-start.3 = (bf16[256,4096]{1,0:T(8,128)(2,1)S(1)}, bf16[256,4096]{1,0:T(8,128)(2,1)}, u32[]{:S(2)}, u32[]{:S(2)}) collective-permute-start(bf16[256,4096]{1,0:T(8,128)(2,1)S(1)} %bitcast.35), channel_id=1, source_target_pairs={{0,1},{1,0},{2,3},{3,2},{4,5},{5,4},{6,7},{7,6},{8,9},{9,8},{10,11... | collective-permute-start | bytes 6291464 | tf_op jit(solution)/shard_map/ppermute | solution.py:517
  113.7 5.1 %collective-permute-start = (bf16[256,1536]{1,0:T(8,128)(2,1)}, bf16[256,1536]{1,0:T(8,128)(2,1)S(1)}, u32[]{:S(2)}, u32[]{:S(2)}) collective-permute-start(bf16[256,1536]{1,0:T(8,128)(2,1)} %get-tuple-element.62), channel_id=1, source_target_pairs={{0,1},{1,0},{2,3},{3,2},{4,5},{5,4},{6,7},{7,6},{8,9},{9,8},{10,11... | collective-permute-start | bytes 2359304 | tf_op jit(solution)/shard_map/ppermute | solution.py:517
  114.1 20.1 %collective-permute-start.4 = (bf16[256,768]{1,0:T(8,128)(2,1)}, bf16[256,768]{1,0:T(8,128)(2,1)S(1)}, u32[]{:S(2)}, u32[]{:S(2)}) collective-permute-start(bf16[256,768]{1,0:T(8,128)(2,1)} %get-tuple-element.67), channel_id=1, source_target_pairs={{0,2},{1,3},{2,0},{3,1},{4,6},{5,7},{6,4},{7,5},{8,10},{9,11},{10,... | collective-permute-start | bytes 1179656 | tf_op jit(solution)/shard_map/ppermute | solution.py:517
  115.5 18.7 %collective-permute-start.5 = (bf16[256,768]{1,0:T(8,128)(2,1)}, bf16[256,768]{1,0:T(8,128)(2,1)}, u32[]{:S(2)}, u32[]{:S(2)}) collective-permute-start(bf16[256,768]{1,0:T(8,128)(2,1)} %get-tuple-element.68), channel_id=1, source_target_pairs={{0,3},{1,2},{2,1},{3,0},{4,7},{5,6},{6,5},{7,4},{8,11},{9,10},{10,... | collective-permute-start | bytes 1179656 | tf_op jit(solution)/shard_map/ppermute | solution.py:517
  115.6 33.4 %collective-permute-start.6 = (bf16[256,1024]{1,0:T(8,128)(2,1)}, bf16[256,1024]{1,0:T(8,128)(2,1)S(1)}, u32[]{:S(2)}, u32[]{:S(2)}) collective-permute-start(bf16[256,1024]{1,0:T(8,128)(2,1)} %get-tuple-element.72), channel_id=1, source_target_pairs={{0,2},{1,3},{2,0},{3,1},{4,6},{5,7},{6,4},{7,5},{8,10},{9,11},{10,... | collective-permute-start | bytes 1572872 | tf_op jit(solution)/shard_map/ppermute | solution.py:517
  149.1 1.9 collective-permute-start.7
  158.6 147.3 %reduce-scatter.7.cloned.1.call-start = ((), (), s32[]{:S(2)}) async-start(), calls=%async_computation.5 | async-start | bytes 1310720 | tf_op jit(solution)/shard_map/reduce_scatter | solution.py:523
  158.6 14.5 %collective-permute-start.8 = (bf16[256,1024]{1,0:T(8,128)(2,1)}, bf16[256,1024]{1,0:T(8,128)(2,1)S(1)}, u32[]{:S(2)}, u32[]{:S(2)}) collective-permute-start(bf16[256,1024]{1,0:T(8,128)(2,1)} %get-tuple-element.76), channel_id=1, source_target_pairs={{0,2},{1,3},{2,0},{3,1},{4,6},{5,7},{6,4},{7,5},{8,10},{9,11},{10,... | collective-permute-start | bytes 1572872 | tf_op jit(solution)/shard_map/ppermute | solution.py:517
  173.1 1.9 collective-permute-start.9
  173.1 14.5 %collective-permute-start.10 = (bf16[256,1024]{1,0:T(8,128)(2,1)}, bf16[256,1024]{1,0:T(8,128)(2,1)S(1)}, u32[]{:S(2)}, u32[]{:S(2)}) collective-permute-start(bf16[256,1024]{1,0:T(8,128)(2,1)} %get-tuple-element.81), channel_id=1, source_target_pairs={{0,2},{1,3},{2,0},{3,1},{4,6},{5,7},{6,4},{7,5},{8,10},{9,11},{10,... | collective-permute-start | bytes 1572872 | tf_op jit(solution)/shard_map/ppermute | solution.py:517
  176.3 21.5 %slice-start = ((s8[8388608]{0:T(1024)(128)(4,1)}), s8[4194304]{0:T(1024)(128)(4,1)S(1)}, s32[]{:S(2)}) async-start(s8[8388608]{0:T(1024)(128)(4,1)} %bitcast.46), calls=%async_computation.8 | async-start | bytes 8388608
  187.7 3.1 collective-permute-start.11
  187.7 19.4 %collective-permute-start.12 = (bf16[256,1024]{1,0:T(8,128)(2,1)S(1)}, bf16[256,1024]{1,0:T(8,128)(2,1)S(1)}, u32[]{:S(2)}, u32[]{:S(2)}) collective-permute-start(bf16[256,1024]{1,0:T(8,128)(2,1)S(1)} %copy-done.48), channel_id=1, source_target_pairs={{0,2},{1,3},{2,0},{3,1},{4,6},{5,7},{6,4},{7,5},{8,10},{9,11},{10,... | collective-permute-start | bytes 1572872 | tf_op jit(solution)/shard_map/ppermute | solution.py:517
  189.2 32.7 %collective-permute-start.14 = (bf16[4,1024,128]{2,1,0:T(8,128)(2,1)S(1)}, bf16[4,1024,128]{2,1,0:T(8,128)(2,1)S(1)}, u32[]{:S(2)}, u32[]{:S(2)}) collective-permute-start(bf16[4,1024,128]{2,1,0:T(8,128)(2,1)S(1)} %get-tuple-element.78), channel_id=1, source_target_pairs={{0,4},{4,0},{8,12},{12,8},{16,20},{20,16},{24,28},{28,24},{1,5},{5... | collective-permute-start | bytes 3145736 | tf_op jit(solution)/shard_map/ppermute | solution.py:520
  207.1 2.0 collective-permute-start.13
  223.6 102.0 %reduce-scatter.5.cloned.1.call-start = ((), (), s32[]{:S(2)}) async-start(), calls=%async_computation.4 | async-start | bytes 1310720 | tf_op jit(solution)/shard_map/reduce_scatter | solution.py:523
  223.9 25.3 %collective-permute-start.15 = (bf16[4,1024,128]{2,1,0:T(8,128)(2,1)S(1)}, bf16[4,1024,128]{2,1,0:T(8,128)(2,1)S(1)}, u32[]{:S(2)}, u32[]{:S(2)}) collective-permute-start(bf16[4,1024,128]{2,1,0:T(8,128)(2,1)S(1)} %copy-done.24), channel_id=1, source_target_pairs={{0,4},{4,0},{8,12},{12,8},{16,20},{20,16},{24,28},{28,24},{1,5},{5... | collective-permute-start | bytes 3145736 | tf_op jit(solution)/shard_map/ppermute | solution.py:520
  250.8 79.9 %reduce-scatter.11.cloned.1.call-start = ((), (), s32[]{:S(2)}) async-start(), calls=%async_computation.7 | async-start | bytes 1310720 | tf_op jit(solution)/shard_map/reduce_scatter | solution.py:523
  250.8 47.6 %collective-permute-start.19 = (bf16[4,1024,128]{2,1,0:T(8,128)(2,1)}, bf16[4,1024,128]{2,1,0:T(8,128)(2,1)}, u32[]{:S(2)}, u32[]{:S(2)}) collective-permute-start(bf16[4,1024,128]{2,1,0:T(8,128)(2,1)} %copy-done.22), channel_id=1, source_target_pairs={{0,4},{4,0},{8,12},{12,8},{16,20},{20,16},{24,28},{28,24},{1,5},{5... | collective-permute-start | bytes 3145736 | tf_op jit(solution)/shard_map/ppermute | solution.py:520
  252.5 28.6 %collective-permute-start.16 = (bf16[1024,128]{1,0:T(8,128)(2,1)S(1)}, bf16[1024,128]{1,0:T(8,128)(2,1)S(1)}, u32[]{:S(2)}, u32[]{:S(2)}) collective-permute-start(bf16[1024,128]{1,0:T(8,128)(2,1)S(1)} %get-tuple-element.120), channel_id=1, source_target_pairs={{0,4},{4,0},{8,12},{12,8},{16,20},{20,16},{24,28},{28,24},{1,5},{5... | collective-permute-start | bytes 786440 | tf_op jit(solution)/shard_map/ppermute | solution.py:520
  254.0 27.9 %copy-start.41 = (bf16[256,1536]{1,0:T(8,128)(2,1)S(1)}, bf16[256,1536]{1,0:T(8,128)(2,1)}, u32[]{:S(2)}) copy-start(bf16[256,1536]{1,0:T(8,128)(2,1)} %get-tuple-element.58.refs_0_) | copy-start | bytes 2359300
  254.9 27.0 %copy-start.8 = (bf16[4,256,1024]{2,1,0:T(8,128)(2,1)S(1)}, bf16[4,256,1024]{2,1,0:T(8,128)(2,1)}, u32[]{:S(2)}) copy-start(bf16[4,256,1024]{2,1,0:T(8,128)(2,1)} %copy-done.6) | copy-start | bytes 6291460
  254.9 27.0 %copy-start.28 = (bf16[256,1536]{1,0:T(8,128)(2,1)S(1)}, bf16[256,1536]{1,0:T(8,128)(2,1)}, u32[]{:S(2)}) copy-start(bf16[256,1536]{1,0:T(8,128)(2,1)} %copy-done.25) | copy-start | bytes 2359300
  254.9 27.0 %copy-start.43 = (f32[4,4,8,256]{3,2,1,0:T(8,128)S(1)}, f32[4,4,8,256]{3,2,1,0:T(8,128)}, u32[]{:S(2)}) copy-start(f32[4,4,8,256]{3,2,1,0:T(8,128)} %copy-done.42) | copy-start | bytes 393220
  254.9 42.0 %collective-permute-start.18 = (bf16[256,768]{1,0:T(8,128)(2,1)S(1)}, bf16[256,768]{1,0:T(8,128)(2,1)S(1)}, u32[]{:S(2)}, u32[]{:S(2)}) collective-permute-start(bf16[256,768]{1,0:T(8,128)(2,1)S(1)} %get-tuple-element.116), channel_id=1, source_target_pairs={{0,3},{1,2},{2,1},{3,0},{4,7},{5,6},{6,5},{7,4},{8,11},{9,10},{10,... | collective-permute-start | bytes 1179656 | tf_op jit(solution)/shard_map/ppermute | solution.py:517
  254.9 42.7 %collective-permute-start.17 = (bf16[256,768]{1,0:T(8,128)(2,1)S(1)}, bf16[256,768]{1,0:T(8,128)(2,1)S(1)}, u32[]{:S(2)}, u32[]{:S(2)}) collective-permute-start(bf16[256,768]{1,0:T(8,128)(2,1)S(1)} %get-tuple-element.117), channel_id=1, source_target_pairs={{0,2},{1,3},{2,0},{3,1},{4,6},{5,7},{6,4},{7,5},{8,10},{9,11},{10,... | collective-permute-start | bytes 1179656 | tf_op jit(solution)/shard_map/ppermute | solution.py:517
  303.8 23.6 %collective-permute-start.22 = (bf16[512,768]{1,0:T(8,128)(2,1)}, bf16[512,768]{1,0:T(8,128)(2,1)S(1)}, u32[]{:S(2)}, u32[]{:S(2)}) collective-permute-start(bf16[512,768]{1,0:T(8,128)(2,1)} %pad_maximum_fusion), channel_id=1, source_target_pairs={{0,1},{1,0},{2,3},{3,2},{4,5},{5,4},{6,7},{7,6},{8,9},{9,8},{10,11... | collective-permute-start | bytes 2359304 | tf_op jit(solution)/shard_map/ppermute | solution.py:517
  303.8 11.0 %collective-permute-start.21 = (bf16[256,768]{1,0:T(8,128)(2,1)}, bf16[256,768]{1,0:T(8,128)(2,1)S(1)}, u32[]{:S(2)}, u32[]{:S(2)}) collective-permute-start(bf16[256,768]{1,0:T(8,128)(2,1)} %get-tuple-element.112), channel_id=1, source_target_pairs={{0,3},{1,2},{2,1},{3,0},{4,7},{5,6},{6,5},{7,4},{8,11},{9,10},{10,... | collective-permute-start | bytes 1179656 | tf_op jit(solution)/shard_map/ppermute | solution.py:517
  304.8 19.0 %collective-permute-start.20 = (bf16[256,768]{1,0:T(8,128)(2,1)}, bf16[256,768]{1,0:T(8,128)(2,1)S(1)}, u32[]{:S(2)}, u32[]{:S(2)}) collective-permute-start(bf16[256,768]{1,0:T(8,128)(2,1)} %get-tuple-element.113), channel_id=1, source_target_pairs={{0,2},{1,3},{2,0},{3,1},{4,6},{5,7},{6,4},{7,5},{8,10},{9,11},{10,... | collective-permute-start | bytes 1179656 | tf_op jit(solution)/shard_map/ppermute | solution.py:517
  (46 other events, 174.4 us)
Sparse Core Ops, SparseCore 0:
  158.7 44.3 reduce-scatter.8
  223.7 26.6 reduce-scatter.6
  252.8 25.7 reduce-scatter.4
  302.0 26.2 reduce-scatter.10

commit v2 on v0

--- a/solution.py
+++ b/solution.py
@@ -25,8 +25,8 @@
     return pltpu.CompilerParams(vmem_limit_bytes=mib * 2**20)
 
 
-def cost(flops, nbytes):
-    return pl.CostEstimate(flops=int(flops) // 1000, bytes_accessed=int(nbytes) // 1000, transcendentals=0)
+def cost(us):
+    return pl.CostEstimate(flops=int(us * 0.25 * 1.15e9), bytes_accessed=1024, transcendentals=0)
 
 
 ANY = pl.BlockSpec(memory_space=pl.ANY)
@@ -37,43 +37,54 @@
 
 
 def gate(arrays, *tokens):
-    return list(lax.optimization_barrier((*arrays, *tokens)))[: len(arrays)]
-
-
-def pack_kernel(parts, info_ref, *refs):
-    q_refs, k_refs, v_refs, out_refs = (refs[i * parts : (i + 1) * parts] for i in range(4))
-    wide = GROUP * HEAD_DIM
-    for d in range(parts):
-        out_refs[d][:, :wide] = q_refs[d][...]
-        out_refs[d][:, wide : wide + HEAD_DIM] = k_refs[d][...]
-        out_refs[d][:, wide + HEAD_DIM :] = v_refs[d][...]
-
-
-def pack(info, queries, keys, values, parts, groups, gp):
-    rows = queries.shape[0]
-    wide = GROUP * HEAD_DIM
+    flat = [x for token in tokens for x in (token if isinstance(token, tuple) else (token,))]
+    return list(lax.optimization_barrier((*arrays, *flat)))[: len(arrays)]
+
+
+def pack_kernel(jobs, me_ref, *refs):
+    wide = GROUP * HEAD_DIM
+    size = wide + 2 * HEAD_DIM
+    sources, outs = iter(refs[: len(refs) - len(jobs)]), refs[len(refs) - len(jobs) :]
+    for out, (d, members) in zip(outs, jobs):
+        for slot in range(len(members)):
+            start = slot * size
+            for width in (wide, HEAD_DIM, HEAD_DIM):
+                out[:, start : start + width] = next(sources)[...]
+                start += width
+
+
+def pack(me, sources, parts, jobs):
+    rows = sources[0].shape[0]
+    groups = KV_HEADS // parts
+    wide = GROUP * HEAD_DIM
+    size = wide + 2 * HEAD_DIM
     step = min(128, rows)
 
-    def pick(d):
-        return lambda i, info: (i, (info[0] ^ d) * groups + gp)
-
-    return pl.pallas_call(
-        functools.partial(pack_kernel, parts),
+    def pick(width, d, gp):
+        return pl.BlockSpec((step, width), lambda i, me: (i, (me[0] ^ d) * groups + gp))
+
+    specs = [
+        pick(width, d, gp)
+        for d, members in jobs
+        for gp in members
+        for width in (wide, HEAD_DIM, HEAD_DIM)
+    ]
+    return pl.pallas_call(
+        functools.partial(pack_kernel, jobs),
         grid_spec=pltpu.PrefetchScalarGridSpec(
             num_scalar_prefetch=1,
             grid=(rows // step,),
-            in_specs=[pl.BlockSpec((step, wide), pick(d)) for d in range(parts)]
-            + [pl.BlockSpec((step, HEAD_DIM), pick(d)) for d in range(parts)] * 2,
+            in_specs=specs,
             out_specs=[
-                pl.BlockSpec((step, wide + 2 * HEAD_DIM), lambda i, info: (i, 0))
-                for d in range(parts)
+                pl.BlockSpec((step, size * len(members)), lambda i, me: (i, 0))
+                for d, members in jobs
             ],
         ),
-        out_shape=[shape((rows, wide + 2 * HEAD_DIM)) for d in range(parts)],
-        compiler_params=params(56),
-        cost_estimate=cost(0, 4 * parts * rows * (wide + 2 * HEAD_DIM)),
+        out_shape=[shape((rows, size * len(members))) for d, members in jobs],
+        compiler_params=params(60),
+        cost_estimate=cost(2.0),
         name="pack",
-    )(info, *[queries] * parts, *[keys] * parts, *[values] * parts)
+    )(me, *sources * (len(specs) // 3))
 
 
 def column(share, c, chunks, width):
@@ -98,8 +109,8 @@
         in_specs=[pl.BlockSpec((step, model), lambda i: (i, 0))],
         out_specs=[pl.BlockSpec((step, shares * width), lambda i: (i, 0))] * len(orders),
         out_shape=[shape((rows, shares * width)) for order in orders],
-        compiler_params=params(56),
-        cost_estimate=cost(0, 4 * rows * model),
+        compiler_params=params(40),
+        cost_estimate=cost(3.8),
         name="pack_chunks",
     )(cotangent)
 
@@ -133,8 +144,8 @@
             out_specs=[pl.BlockSpec((step, w), lambda i, info: (i, 0)) for w in widths],
         ),
         out_shape=[shape((rows, w)) for w in widths],
-        compiler_params=params(16),
-        cost_estimate=cost(0, 4 * total * rows * cols),
+        compiler_params=params(40),
+        cost_estimate=cost(2.8),
         name="unpack",
     )(info, *pieces)
 
@@ -215,8 +226,12 @@
     return pl.BlockSpec(dims, lambda i, info: (0,) * len(dims))
 
 
+def piece_block(rows, cols, at):
+    return pl.BlockSpec((rows, cols), lambda i, info: (0, at))
+
+
 def attention(info, pieces, token, parts, docs):
-    block, cols = pieces[0].shape
+    block, cols = pieces[-1][0].shape
     pairs = parts * (parts + 1) // 2
     wide = GROUP * HEAD_DIM
     vm = pltpu.VMEM
@@ -225,7 +240,7 @@
         grid_spec=pltpu.PrefetchScalarGridSpec(
             num_scalar_prefetch=1,
             grid=(1,),
-            in_specs=[whole_block((block, cols))] * parts,
+            in_specs=[piece_block(block, cols, at) for x, at in pieces],
             out_specs=[
                 whole_block((parts, wide, block)),
                 whole_block((GROUP, parts, 8, block)),
@@ -245,10 +260,10 @@
             shape((parts, wide, block)),
             shape((GROUP, parts, 8, block), jnp.float32),
         ],
-        compiler_params=params(16),
-        cost_estimate=cost(8e9, 4 * parts * block * cols),
+        compiler_params=params(40),
+        cost_estimate=cost(10.0),
         name="attention",
-    )(gate([info], token)[0], *pieces)
+    )(gate([info], token)[0], *[x for x, at in pieces])
 
 
 def backward_kernel(parts, block, docs, info_ref, *refs):
@@ -308,7 +323,7 @@
 
 
 def attention_back(info, pieces, grads, out, lse, token, parts, docs, gp):
-    block, cols = pieces[0].shape
+    block, cols = pieces[-1][0].shape
     pairs = parts * (parts + 1) // 2
     wide = GROUP * HEAD_DIM
     vm = pltpu.VMEM
@@ -317,7 +332,7 @@
         grid_spec=pltpu.PrefetchScalarGridSpec(
             num_scalar_prefetch=1,
             grid=(1,),
-            in_specs=[whole_block((block, cols))] * parts
+            in_specs=[piece_block(block, cols, at) for x, at in pieces]
             + [
                 pl.BlockSpec((parts, block, wide), lambda i, info: (0, 0, gp)),
                 whole_block((parts, wide, block)),
@@ -338,10 +353,10 @@
             ],
         ),
         out_shape=shape((parts, block, cols)),
-        compiler_params=params(20),
-        cost_estimate=cost(14e9, 8 * parts * block * cols),
+        compiler_params=params(40),
+        cost_estimate=cost(12.5),
         name="attention_back",
-    )(gate([info], token)[0], *pieces, grads, out, lse)
+    )(gate([info], token)[0], *[x for x, at in pieces], grads, out, lse)
 
 
 def place_of(share, order):
@@ -413,10 +428,8 @@
             shape((half, groups * rows, width), jnp.float32),
             shape((half, groups * rows, width)),
         ],
-        compiler_params=params(16),
-        cost_estimate=cost(
-            2 * groups * rows * block * parts * shares * width, 8 * groups * rows * shares * width
-        ),
+        compiler_params=params(40),
+        cost_estimate=cost(4.3),
         name="weight_terms",
     )(gate([info], token)[0], *outs, *near, *near, *chunk)
 
@@ -441,8 +454,8 @@
             shape((half, rows, width), jnp.float32),
             shape((half, rows, width)),
         ],
-        compiler_params=params(12),
-        cost_estimate=cost(0, 8 * count * rows * width),
+        compiler_params=params(40),
+        cost_estimate=cost(0.5),
         name="merge",
     )(keep, keep, got, got)
 
@@ -463,8 +476,8 @@
         out_specs=pl.BlockSpec((step, width), lambda i: (i, c)),
         out_shape=shape((rows, width * chunks), jnp.float32),
         input_output_aliases={2: 0} if more else {},
-        compiler_params=params(8),
-        cost_estimate=cost(0, 10 * rows * width),
+        compiler_params=params(40),
+        cost_estimate=cost(0.8),
         name="finish",
     )(gate([keep], token)[0], got, *more)
 
@@ -506,10 +519,8 @@
         + ([] if first else [block]),
         out_specs=block,
         out_shape=shape((parts, rows, feats), jnp.bfloat16 if last else jnp.float32),
-        compiler_params=params(24),
-        cost_estimate=cost(
-            2 * feats * rows * parts * shares * width * len(picked), 4 * feats * rows * parts
-        ),
+        compiler_params=params(40),
+        cost_estimate=cost(2.5 * len(picked)),
         name="project",
     )(gate([out_weight], token)[0], *near, *flat, *([] if first else [acc]))
 
@@ -524,7 +535,7 @@
     width = model // shares // chunks
     bits = tuple(range(shares.bit_length() - 1))
     turned = bits[1:] + bits[:1]
-    orders = [turned if c == 1 else bits for c in range(chunks)]
+    orders = [turned if c == 0 else bits for c in range(chunks)]
     scale = 1.0 / math.sqrt(rows * parts * shares)
     info = jnp.concatenate(
         [
@@ -539,129 +550,123 @@
     def over_dp(x, d):
         return lax.ppermute(x, "dp", [(i, i ^ d) for i in range(shares)])
 
-    near = [cotangent, over_seq(cotangent, 1)]
-    packed = [pack(info, queries[0], keys[0], values[0], parts, groups, gp) for gp in range(groups)]
-    sends = pack_chunks(cotangent, orders, shares, width)
-
-    pieces, fwd = [], []
-    token = near[1]
-    for gp in range(groups):
-        sent = packed[gp]
-        if gp:
-            sent = [sent[0]] + gate(sent[1:], *pieces[-1][1:])
-        pieces.append([sent[0]] + [over_seq(sent[d], d) for d in range(1, parts)])
+    far = range(2, parts)
+    all_groups = tuple(range(groups))
+    me = lax.axis_index("seq").astype(jnp.int32).reshape(1)
+    sources = (queries[0], keys[0], values[0])
+    packed = [pack(me, sources, parts, tuple((d, (0,)) for d in far))]
+    rest = [(d, (gp,)) for gp in range(1, groups) for d in far]
+    rest = pack(
+        gate([me], packed[0][0])[0],
+        sources,
+        parts,
+        tuple([(0, all_groups), (1, all_groups)] + rest),
+    )
+    for gp in range(1, groups):
+        packed.append(rest[2 + (gp - 1) * len(far) : 2 + gp * len(far)])
+    sent_far = [[over_seq(x, d) for x, d in zip(group, far)] for group in packed]
+    core = over_seq(rest[1], 1)
+    pieces = [[(rest[0], gp), (core, gp)] + [(x, 0) for x in sent_far[gp]] for gp in range(groups)]
+    sends = pack_chunks(gate([cotangent], rest[0])[0], orders, shares, width)
+    near = [cotangent, over_seq(gate([cotangent], *sent_far[0])[0], 1)]
+
     far_half = {}
 
     def send_chunk(c, *tokens):
         mine = gate([sends[c]], *tokens)[0]
         far_half[c] = [over_seq(mine, d) for d in range(2, parts, 2)]
 
-    def chunk_pieces(c):
-        out = []
-        for x in far_half[c]:
-            out += [x, over_seq(x, 1)]
-        return out
-
+    for c in range(chunks):
+        if c < groups:
+            send_chunk(c, *sent_far[c])
+        else:
+            send_chunk(c, *far_half[max(0, c - groups)])
+
+    fwd = []
+    token = sends[-1]
     for gp in range(groups):
         fwd.append(attention(info, pieces[gp], token, parts, docs))
         token = fwd[-1][0]
         if gp == 0:
-            send_chunk(0, token)
+            token = (token, near[1])
     outs = [pair[0] for pair in fwd]
 
-    state = {}
-    result = None
-
-    def run_merge(c):
-        nonlocal token, result
-        keep, send, hop = state[c]
-        got = over_dp(send, 1 << orders[c][hop])
-        if hop == len(bits) - 1:
-            result = finish(keep, got, result, token, c, chunks, scale)
-            token = result
-            state[c] = (None, None, None)
-        else:
-            keep, send = merge(keep, got, token)
-            state[c] = (keep, send, hop + 1)
-            token = send
-
-    fars = {}
-    back, results = {}, {}
-    acc = None
+    fars, state, back, results = {}, {}, {}, {}
+    acc = weight_grad = None
+
+    def hop(c, send, stage):
+        return over_dp(send, 1 << orders[c][stage])
 
     def weigh(c):
         nonlocal token
-        fars[c] = chunk_pieces(c)
+        fars[c] = []
+        for x in gate(far_half[c], token):
+            fars[c] += [x, over_seq(x, 1)]
         keep, send = weight_terms(
             info, outs, near, fars[c], token, shares, c, chunks, width, orders[c]
         )
-        state[c] = (keep, send, 0)
         token = send
+        state[c] = (keep, hop(c, send, 0), 1)
+
+    def advance(c):
+        nonlocal token, weight_grad
+        if c not in state or state[c] is None:
+            return
+        keep, got, stage = state[c]
+        if stage == len(bits):
+            token = weight_grad = finish(keep, got, weight_grad, token, c, chunks, scale)
+            state[c] = None
+        else:
+            keep, send = merge(keep, got, token)
+            token = send
+            state[c] = (keep, hop(c, send, stage), stage + 1)
 
     def project_step(picked, last):
         nonlocal token, acc
-        acc = project(
+        token = acc = project(
             out_weight, near, [fars[c] for c in picked], acc, token, orders, picked, shares, width, last
         )
-        token = acc
 
     def send_back(gp):
         nonlocal token
         res = attention_back(info, pieces[gp], acc, outs[gp], fwd[gp][1], token, parts, docs, gp)
         token = results[gp] = res
-        back[gp] = [res[0], None] + [over_seq(res[d], d) for d in range(2, parts)]
-
-    for c in range(1, chunks):
-        if c == 1:
-            send_chunk(1, *pieces[-1][1:])
-        else:
-            send_chunk(c, *far_half[c - 2])
+        back[gp] = [res[0], None] + [over_seq(res[d], d) for d in far]
+
     last = chunks - 1
-    done = set()
-
-    def step_merge(c):
-        if c in state and c not in done:
-            run_merge(c)
-            if state[c][2] is None:
-                done.add(c)
-
-    weigh(0)
-    if chunks > 1:
-        weigh(1)
-    step_merge(0)
-    if chunks > 2:
-        weigh(2)
+    for c in range(last):
+        weigh(c)
     if last:
         project_step(list(range(last)), False)
-    step_merge(1)
-    if chunks > 3:
-        weigh(3)
+    advance(0)
+    weigh(last)
     project_step([last], True)
-    step_merge(0)
+    advance(1)
     send_back(0)
-    step_merge(2)
-    step_merge(0)
-    step_merge(1)
+    for c in (0, 1, 2):
+        advance(c)
     for gp in range(1, groups):
         send_back(gp)
-    step_merge(2)
-    if groups > 1:
-        token = gate([token], *back[0][2:])[0]
-    step_merge(3)
-    step_merge(1)
-    step_merge(2)
+    advance(0)
+    token = (token, *back[0][2:])
+    advance(2)
+    both = over_seq(jnp.concatenate([results[gp][1] for gp in range(groups)], axis=0), 1)
+    token = (token, back[groups - 1][-1])
+    advance(3)
+    advance(1)
+    token = (token, *back[groups - 1][2:])
+    advance(3)
     for gp in range(groups):
-        mine = gate([results[gp][1]], *back[0][2:])[0]
-        back[gp][1] = over_seq(mine, 1)
-    step_merge(3)
-    if groups > 1:
-        token = gate([token], *back[groups - 1][2:])[0]
+        back[gp][1] = both[gp * rows : (gp + 1) * rows]
     for _ in bits:
-        for c in range(chunks):
-            step_merge(c)
+        for c in range(last):
+            advance(c)
     back = [x for gp in range(groups) for x in back[gp]]
-    grad_q, grad_k, grad_v = unpack(info, back, parts, groups)
-    return (grad_q[None], grad_k[None], grad_v[None], result)
+    grad_q, grad_k, grad_v = unpack(gate([info], token)[0], back, parts, groups)
+    token = grad_q
+    for _ in bits:
+        advance(last)
+    return (grad_q[None], grad_k[None], grad_v[None], weight_grad)
 
 
 def solution(mesh):

time: 252 us -> 221 us (0.88)
  waiting for transfers between devices: 124 us -> 70.6 us
  Pallas kernels: 92.2 us -> 105 us
  starting transfers between devices: 31.1 us -> 36.6 us
  local copies, waits for them, and re-layouts: 1.26 us -> 6.74 us
    ppermute x21 -> x19, waiting for transfers between devices: 84.6 us -> 37.7 us  [over_seq(): return lax.ppermute(x, 'seq', [(i, i ^ d) for i in range(parts)])]
    ppermute x12, waiting for transfers between devices: 39.3 us -> 32.9 us  [over_dp(): return lax.ppermute(x, 'dp', [(i, i ^ d) for i in range(shares)])]
    pallas_call x2, Pallas kernels: 11.5 us -> 17.3 us  [project(): pl.pallas_call(functools.partial(project_kernel, parts, shares, width, le...]
    unnamed x26 -> x40, local copies, waits for them, and re-layouts: 1.05 us -> 6.48 us
    ppermute x12, starting transfers between devices: 16.4 us -> 20.4 us  [over_dp(): return lax.ppermute(x, 'dp', [(i, i ^ d) for i in range(shares)])]
    pallas_call x4, Pallas kernels: 17.3 us -> 20.7 us  [weight_terms(): pl.pallas_call(functools.partial(weight_kernel, parts, groups, width, ord...]
    ppermute x21 -> x19, starting transfers between devices: 14.7 us -> 16.2 us  [over_seq(): return lax.ppermute(x, 'seq', [(i, i ^ d) for i in range(parts)])]
  transfers between devices with their start and end apart: 33 -> 31, of which waited for: 14 -> 12; matrix products, arithmetic and copies ran while one was open for 1% -> 0% of each run, Pallas kernels for 32% -> 46%
where the time goes in v2:
time: 221 us; the launch traced here: 220 us
  Pallas kernels  105 us (48%)
  waiting for transfers between devices  70.6 us (32%)
  starting transfers between devices  36.6 us (17%)
  local copies, waits for them, and re-layouts  6.74 us (3%)
    ppermute x19, waiting for transfers between devices, over_seq(): return lax.ppermute(x, 'seq', [(i, i ^ d) for i in range(parts)])  37.7 us
    ppermute x12, waiting for transfers between devices, over_dp(): return lax.ppermute(x, 'dp', [(i, i ^ d) for i in range(shares)])  32.9 us
    pallas_call x2, Pallas kernels, attention_back(): pl.pallas_call(functools.partial(backward_kernel, parts, block, docs), gr...  27.4 us
    pallas_call x2, Pallas kernels, attention(): pl.pallas_call(functools.partial(forward_kernel, parts, block, docs), gri...  23 us
    pallas_call x4, Pallas kernels, weight_terms(): pl.pallas_call(functools.partial(weight_kernel, parts, groups, width, ord...  20.7 us
    ppermute x12, starting transfers between devices, over_dp(): return lax.ppermute(x, 'dp', [(i, i ^ d) for i in range(shares)])  20.4 us
    pallas_call x2, Pallas kernels, project(): pl.pallas_call(functools.partial(project_kernel, parts, shares, width, le...  17.3 us
    ppermute x19, starting transfers between devices, over_seq(): return lax.ppermute(x, 'seq', [(i, i ^ d) for i in range(parts)])  16.2 us
  transfers between devices with their start and end apart: 31, of which 12 were waited for; matrix products, arithmetic and copies ran while one was open for 0% of the time, Pallas kernels for 46%

profile of v2, /device:TPU:0, one launch (start us, length us, event | category | flops | bytes accessed | tf_op | source)
XLA Modules:
  0.0 219.8 jit_solution(17382520177246906366)
XLA Ops:
  0.6 2.2 pack.2
  2.8 2.4 %collective-permute-start.2 = (bf16[256,768]{1,0:T(8,128)(2,1)}, bf16[256,768]{1,0:T(8,128)(2,1)S(1)}, u32[]{:S(2)}, u32[]{:S(2)}) collective-permute-start(bf16[256,768]{1,0:T(8,128)(2,1)} %get-tuple-element.86), channel_id=1, source_target_pairs={{0,3},{1,2},{2,1},{3,0},{4,7},{5,6},{6,5},{7,4},{8,11},{9,10},{10,... | collective-permute-start | bytes 1179656 | tf_op jit(solution)/shard_map/ppermute | solution.py:548
  5.8 9.2 %collective-permute-done.2.refs_3_ = bf16[256,768]{1,0:T(8,128)(2,1)S(1)} collective-permute-done((bf16[256,768]{1,0:T(8,128)(2,1)}, bf16[256,768]{1,0:T(8,128)(2,1)S(1)}, u32[]{:S(2)}, u32[]{:S(2)}) %collective-permute-start.2) | collective-permute-done | bytes 393248 | tf_op jit(solution)/shard_map/ppermute | solution.py:548
  15.8 7.7 %collective-permute-done.1.refs_2_ = bf16[256,768]{1,0:T(8,128)(2,1)S(1)} collective-permute-done((bf16[256,768]{1,0:T(8,128)(2,1)}, bf16[256,768]{1,0:T(8,128)(2,1)S(1)}, u32[]{:S(2)}, u32[]{:S(2)}) %collective-permute-start.1) | collective-permute-done | bytes 393248 | tf_op jit(solution)/shard_map/ppermute | solution.py:548
  24.3 3.0 %pack.3 = (bf16[256,1536]{1,0:T(8,128)(2,1)}, bf16[256,1536]{1,0:T(8,128)(2,1)}, bf16[256,768]{1,0:T(8,128)(2,1)}, bf16[256,768]{1,0:T(8,128)(2,1)}) custom-call(s32[1]{0:T(128)} %bitcast.me_ref, bf16[256,4096]{1,0:T(8,128)(2,1)} %bitcast.40, bf16[256,1024]{1,0:T(8,128)(2,1)} %bitcast.48, bf16[256,1024]{1,0:T(8,128)(2,1)} %bitcast.56, ...), custom_call_target="tpu_custom_call" | custom-call | flops 575000000 | bytes 1024 | tf_op jit(solution)/shard_map/pack/pallas_call | solution.py:72
  27.9 2.3 %collective-permute-start.4 = (bf16[256,768]{1,0:T(8,128)(2,1)}, bf16[256,768]{1,0:T(8,128)(2,1)}, u32[]{:S(2)}, u32[]{:S(2)}) collective-permute-start(bf16[256,768]{1,0:T(8,128)(2,1)} %get-tuple-element.90), channel_id=1, source_target_pairs={{0,2},{1,3},{2,0},{3,1},{4,6},{5,7},{6,4},{7,5},{8,10},{9,11},{10,... | collective-permute-start | bytes 1179656 | tf_op jit(solution)/shard_map/ppermute | solution.py:548
  37.0 11.4 %attention.2 = (bf16[4,512,256]{2,1,0:T(8,128)(2,1)S(1)}, f32[4,4,8,256]{3,2,1,0:T(8,128)S(1)}) custom-call(s32[10]{0:T(128)S(1)} %pad_add_fusion.info_ref, bf16[256,1536]{1,0:T(8,128)(2,1)S(1)} %copy-done.5, bf16[256,1536]{1,0:T(8,128)(2,1)} %collective-permute-done.refs_1_, bf16[256,768]{1,0:T(8,128)(2,1)S(1)} %copy-done.15, bf16[256,768]{1,0:T(8,128)(2,1)S(1)} %copy-done.12), custom_call_target="tpu_custom_call" | custom-call | flops 2875000064 | bytes 1024 | tf_op jit(solution)/shard_map/attention/pallas_call | solution.py:238
  48.5 11.6 %attention.3 = (bf16[4,512,256]{2,1,0:T(8,128)(2,1)S(1)}, f32[4,4,8,256]{3,2,1,0:T(8,128)S(1)}) custom-call(s32[10]{0:T(128)S(1)} %pad_add_fusion.info_ref, bf16[256,1536]{1,0:T(8,128)(2,1)S(1)} %copy-done.5, bf16[256,1536]{1,0:T(8,128)(2,1)} %collective-permute-done.refs_1_, bf16[256,768]{1,0:T(8,128)(2,1)} %collective-permute-done.4.refs_2_, ...), custom_call_target="tpu_custom_call" | custom-call | flops 2875000064 | bytes 1024 | tf_op jit(solution)/shard_map/attention/pallas_call | solution.py:238
  60.5 2.0 collective-permute-start.8
  62.5 4.8 %weight_terms.4 = (f32[4,1024,128]{2,1,0:T(8,128)S(1)}, bf16[4,1024,128]{2,1,0:T(8,128)(2,1)S(1)}) custom-call(s32[10]{0:T(128)S(1)} %pad_add_fusion.info_ref, bf16[4,512,256]{2,1,0:T(8,128)(2,1)S(1)} %get-tuple-element.87.refs_0_.refs_5_, bf16[4,512,256]{2,1,0:T(8,128)(2,1)S(1)} %get-tuple-element.92.refs_1_.refs_5_, bf16[256,4096]{1,0:T(8,128)(2,1)S(1)} %bitcast.28, ...), custom_call_target="tpu_custom_call" | custom-call | flops 1236249984 | bytes 1024 | tf_op jit(solution)/shard_map/weight_terms/pallas_call | solution.py:416
  67.3 7.6 %collective-permute-done.8.refs_6_.refs_5_ = bf16[256,1024]{1,0:T(8,128)(2,1)S(1)} collective-permute-done((bf16[256,1024]{1,0:T(8,128)(2,1)}, bf16[256,1024]{1,0:T(8,128)(2,1)S(1)}, u32[]{:S(2)}, u32[]{:S(2)}) %collective-permute-start.8) | collective-permute-done | bytes 524320 | tf_op jit(solution)/shard_map/ppermute | solution.py:548
  74.9 1.8 collective-permute-start.10
  76.7 2.8 %collective-permute-start.12 = (bf16[4,1024,128]{2,1,0:T(8,128)(2,1)S(1)}, bf16[4,1024,128]{2,1,0:T(8,128)(2,1)S(1)}, u32[]{:S(2)}, u32[]{:S(2)}) collective-permute-start(bf16[4,1024,128]{2,1,0:T(8,128)(2,1)S(1)} %get-tuple-element.97), channel_id=1, source_target_pairs={{0,8},{4,12},{8,0},{12,4},{16,24},{20,28},{24,16},{28,20},{1,9},{5... | collective-permute-start | bytes 3145736 | tf_op jit(solution)/shard_map/ppermute | solution.py:551
  79.5 4.8 %weight_terms.5 = (f32[4,1024,128]{2,1,0:T(8,128)S(1)}, bf16[4,1024,128]{2,1,0:T(8,128)(2,1)S(1)}) custom-call(s32[10]{0:T(128)S(1)} %pad_add_fusion.info_ref, bf16[4,512,256]{2,1,0:T(8,128)(2,1)S(1)} %get-tuple-element.87.refs_0_.refs_5_, bf16[4,512,256]{2,1,0:T(8,128)(2,1)S(1)} %get-tuple-element.92.refs_1_.refs_5_, bf16[256,4096]{1,0:T(8,128)(2,1)S(1)} %bitcast.30, ...), custom_call_target="tpu_custom_call" | custom-call | flops 1236249984 | bytes 1024 | tf_op jit(solution)/shard_map/weight_terms/pallas_call | solution.py:416
  85.7 3.5 %collective-permute-done.10.refs_6_.refs_7_ = bf16[256,1024]{1,0:T(8,128)(2,1)S(1)} collective-permute-done((bf16[256,1024]{1,0:T(8,128)(2,1)S(1)}, bf16[256,1024]{1,0:T(8,128)(2,1)S(1)}, u32[]{:S(2)}, u32[]{:S(2)}) %collective-permute-start.10) | collective-permute-done | bytes 524320 | tf_op jit(solution)/shard_map/ppermute | solution.py:548
  89.2 1.7 collective-permute-start.13
  92.4 5.5 %weight_terms.6 = (f32[4,1024,128]{2,1,0:T(8,128)S(1)}, bf16[4,1024,128]{2,1,0:T(8,128)(2,1)}) custom-call(s32[10]{0:T(128)S(1)} %pad_add_fusion.info_ref, bf16[4,512,256]{2,1,0:T(8,128)(2,1)S(1)} %get-tuple-element.87.refs_0_.refs_5_, bf16[4,512,256]{2,1,0:T(8,128)(2,1)S(1)} %get-tuple-element.92.refs_1_.refs_5_, bf16[256,4096]{1,0:T(8,128)(2,1)S(1)} %bitcast.32, ...), custom_call_target="tpu_custom_call" | custom-call | flops 1236249984 | bytes 1024 | tf_op jit(solution)/shard_map/weight_terms/pallas_call | solution.py:416
  98.0 10.8 %project.2.refs_5_ = f32[4,256,1024]{2,1,0:T(8,128)S(1)} custom-call(bf16[1024,4096]{1,0:T(8,128)(2,1)} %refs_0_.1, bf16[256,4096]{1,0:T(8,128)(2,1)S(1)} %bitcast.34, bf16[256,4096]{1,0:T(8,128)(2,1)} %collective-permute-done.3.refs_3_.refs_5_.refs_2_, bf16[256,1024]{1,0:T(8,128)(2,1)S(1)} %collective-permute-done.6.refs_6_.refs_3_, ...), custom_call_target="tpu_custom_call" | custom-call | flops 2156250112 | bytes 1024 | tf_op jit(solution)/shard_map/project/pallas_call | solution.py:511
  109.7 2.6 %collective-permute-start.16 = (bf16[2,1024,128]{2,1,0:T(8,128)(2,1)S(1)}, bf16[2,1024,128]{2,1,0:T(8,128)(2,1)S(1)}, u32[]{:S(2)}, u32[]{:S(2)}) collective-permute-start(bf16[2,1024,128]{2,1,0:T(8,128)(2,1)S(1)} %get-tuple-element.113), channel_id=1, source_target_pairs={{0,16},{4,20},{8,24},{12,28},{16,0},{20,4},{24,8},{28,12},{1,17},{... | collective-permute-start | bytes 1572872 | tf_op jit(solution)/shard_map/ppermute | solution.py:551
  112.3 5.5 %weight_terms.7 = (f32[4,1024,128]{2,1,0:T(8,128)S(1)}, bf16[4,1024,128]{2,1,0:T(8,128)(2,1)}) custom-call(s32[10]{0:T(128)S(1)} %pad_add_fusion.info_ref, bf16[4,512,256]{2,1,0:T(8,128)(2,1)S(1)} %get-tuple-element.87.refs_0_.refs_5_, bf16[4,512,256]{2,1,0:T(8,128)(2,1)S(1)} %get-tuple-element.92.refs_1_.refs_5_, bf16[256,4096]{1,0:T(8,128)(2,1)S(1)} %bitcast.35, ...), custom_call_target="tpu_custom_call" | custom-call | flops 1236249984 | bytes 1024 | tf_op jit(solution)/shard_map/weight_terms/pallas_call | solution.py:416
  119.3 6.5 %project.3.refs_4_ = bf16[4,256,1024]{2,1,0:T(8,128)(2,1)S(1)} custom-call(bf16[1024,4096]{1,0:T(8,128)(2,1)} %refs_0_.1, bf16[256,4096]{1,0:T(8,128)(2,1)S(1)} %bitcast.37, bf16[256,4096]{1,0:T(8,128)(2,1)} %collective-permute-done.3.refs_3_.refs_5_.refs_2_, bf16[256,1024]{1,0:T(8,128)(2,1)S(1)} %collective-permute-done.13.refs_6_.refs_3_, ...), custom_call_target="tpu_custom_call" | custom-call | flops 718750016 | bytes 1024 | tf_op jit(solution)/shard_map/project/pallas_call | solution.py:511
  127.3 2.9 %collective-permute-start.17 = (bf16[2,1024,128]{2,1,0:T(8,128)(2,1)S(1)}, bf16[2,1024,128]{2,1,0:T(8,128)(2,1)S(1)}, u32[]{:S(2)}, u32[]{:S(2)}) collective-permute-start(bf16[2,1024,128]{2,1,0:T(8,128)(2,1)S(1)} %get-tuple-element.122), channel_id=1, source_target_pairs={{0,8},{4,12},{8,0},{12,4},{16,24},{20,28},{24,16},{28,20},{1,9},{5... | collective-permute-start | bytes 1572872 | tf_op jit(solution)/shard_map/ppermute | solution.py:551
  130.2 13.7 %attention_back.2 = bf16[4,256,768]{2,1,0:T(8,128)(2,1)S(1)} custom-call(s32[10]{0:T(128)S(1)} %pad_add_fusion.info_ref, bf16[256,1536]{1,0:T(8,128)(2,1)S(1)} %copy-done.6, bf16[256,1536]{1,0:T(8,128)(2,1)} %collective-permute-done.refs_1_, bf16[256,768]{1,0:T(8,128)(2,1)S(1)} %copy-done.16, bf16[256,768]{1,0:T(8,128)(2,1)S(1)} %copy-done.13, ...), custom_call_target="tpu_custom_call" | custom-call | flops 3593750016 | bytes 1024 | tf_op jit(solution)/shard_map/attention_back/pallas_call | solution.py:330
  150.0 13.7 %attention_back.3 = bf16[4,256,768]{2,1,0:T(8,128)(2,1)S(1)} custom-call(s32[10]{0:T(128)S(1)} %pad_add_fusion.info_ref, bf16[256,1536]{1,0:T(8,128)(2,1)S(1)} %copy-done.6, bf16[256,1536]{1,0:T(8,128)(2,1)} %collective-permute-done.refs_1_, bf16[256,768]{1,0:T(8,128)(2,1)} %collective-permute-done.4.refs_2_, ...), custom_call_target="tpu_custom_call" | custom-call | flops 3593750016 | bytes 1024 | tf_op jit(solution)/shard_map/attention_back/pallas_call | solution.py:330
  163.8 3.0 %collective-permute-done.19.got_ref = bf16[1,1024,128]{2,1,0:T(8,128)(2,1)S(1)} collective-permute-done((bf16[1,1024,128]{2,1,0:T(8,128)(2,1)S(1)}, bf16[1,1024,128]{2,1,0:T(8,128)(2,1)S(1)}, u32[]{:S(2)}, u32[]{:S(2)}) %collective-permute-start.19) | collective-permute-done | bytes 262176 | tf_op jit(solution)/shard_map/ppermute | solution.py:551
  168.3 9.5 %collective-permute-done.23.refs_7_ = bf16[256,768]{1,0:T(8,128)(2,1)S(1)} collective-permute-done((bf16[256,768]{1,0:T(8,128)(2,1)S(1)}, bf16[256,768]{1,0:T(8,128)(2,1)S(1)}, u32[]{:S(2)}, u32[]{:S(2)}) %collective-permute-start.23) | collective-permute-done | bytes 393248 | tf_op jit(solution)/shard_map/ppermute | solution.py:548
  178.0 3.2 %collective-permute-start.27 = (bf16[2,1024,128]{2,1,0:T(8,128)(2,1)S(1)}, bf16[2,1024,128]{2,1,0:T(8,128)(2,1)S(1)}, u32[]{:S(2)}, u32[]{:S(2)}) collective-permute-start(bf16[2,1024,128]{2,1,0:T(8,128)(2,1)S(1)} %get-tuple-element.143), channel_id=1, source_target_pairs={{0,8},{4,12},{8,0},{12,4},{16,24},{20,28},{24,16},{28,20},{1,9},{5... | collective-permute-start | bytes 1572872 | tf_op jit(solution)/shard_map/ppermute | solution.py:551
  182.2 2.7 %collective-permute-start.25 = (bf16[1,1024,128]{2,1,0:T(8,128)(2,1)S(1)}, bf16[1,1024,128]{2,1,0:T(8,128)(2,1)S(1)}, u32[]{:S(2)}, u32[]{:S(2)}) collective-permute-start(bf16[1,1024,128]{2,1,0:T(8,128)(2,1)S(1)} %get-tuple-element.128), channel_id=1, source_target_pairs={{0,16},{4,20},{8,24},{12,28},{16,0},{20,4},{24,8},{28,12},{1,17},{... | collective-permute-start | bytes 786440 | tf_op jit(solution)/shard_map/ppermute | solution.py:551
  185.2 14.0 %collective-permute-done.25.got_ref = bf16[1,1024,128]{2,1,0:T(8,128)(2,1)S(1)} collective-permute-done((bf16[1,1024,128]{2,1,0:T(8,128)(2,1)S(1)}, bf16[1,1024,128]{2,1,0:T(8,128)(2,1)S(1)}, u32[]{:S(2)}, u32[]{:S(2)}) %collective-permute-start.25) | collective-permute-done | bytes 262176 | tf_op jit(solution)/shard_map/ppermute | solution.py:551
  200.0 3.2 %collective-permute-done.27.got_low.got_high = bf16[2,1024,128]{2,1,0:T(8,128)(2,1)S(1)} collective-permute-done((bf16[2,1024,128]{2,1,0:T(8,128)(2,1)S(1)}, bf16[2,1024,128]{2,1,0:T(8,128)(2,1)S(1)}, u32[]{:S(2)}, u32[]{:S(2)}) %collective-permute-start.27) | collective-permute-done | bytes 524320 | tf_op jit(solution)/shard_map/ppermute | solution.py:551
  204.4 10.2 %collective-permute-done.28.got_ref = bf16[1,1024,128]{2,1,0:T(8,128)(2,1)S(1)} collective-permute-done((bf16[1,1024,128]{2,1,0:T(8,128)(2,1)S(1)}, bf16[1,1024,128]{2,1,0:T(8,128)(2,1)S(1)}, u32[]{:S(2)}, u32[]{:S(2)}) %collective-permute-start.28) | collective-permute-done | bytes 262176 | tf_op jit(solution)/shard_map/ppermute | solution.py:551
  215.4 2.8 %unpack.1 = (bf16[256,4096]{1,0:T(8,128)(2,1)}, bf16[256,1024]{1,0:T(8,128)(2,1)}, bf16[256,1024]{1,0:T(8,128)(2,1)}) custom-call(s32[10]{0:T(128)S(1)} %pad_add_fusion.info_ref, bf16[256,768]{1,0:T(8,128)(2,1)S(1)} %get-tuple-element.159.refs_0_, bf16[256,768]{1,0:T(8,128)(2,1)S(1)} %get-tuple-element.163.refs_1_, ...), custom_call_target="tpu_custom_call" | custom-call | flops 805000000 | bytes 1024 | tf_op jit(solution)/shard_map/unpack/pallas_call | solution.py:138
  (101 shorter events, 30.1 us)
Async XLA Ops:
  0.6 23.7 %copy-start = (bf16[1,256,4096]{2,1,0:T(8,128)(2,1)S(1)}, bf16[1,256,4096]{2,1,0:T(8,128)(2,1)}, u32[]{:S(2)}) copy-start(bf16[1,256,4096]{2,1,0:T(8,128)(2,1)} %param.6) | copy-start | bytes 6291460
  2.8 12.2 %collective-permute-start.2 = (bf16[256,768]{1,0:T(8,128)(2,1)}, bf16[256,768]{1,0:T(8,128)(2,1)S(1)}, u32[]{:S(2)}, u32[]{:S(2)}) collective-permute-start(bf16[256,768]{1,0:T(8,128)(2,1)} %get-tuple-element.86), channel_id=1, source_target_pairs={{0,3},{1,2},{2,1},{3,0},{4,7},{5,6},{6,5},{7,4},{8,11},{9,10},{10,... | collective-permute-start | bytes 1179656 | tf_op jit(solution)/shard_map/ppermute | solution.py:548
  5.2 18.3 %collective-permute-start.1 = (bf16[256,768]{1,0:T(8,128)(2,1)}, bf16[256,768]{1,0:T(8,128)(2,1)S(1)}, u32[]{:S(2)}, u32[]{:S(2)}) collective-permute-start(bf16[256,768]{1,0:T(8,128)(2,1)} %get-tuple-element.79), channel_id=1, source_target_pairs={{0,2},{1,3},{2,0},{3,1},{4,6},{5,7},{6,4},{7,5},{8,10},{9,11},{10,... | collective-permute-start | bytes 1179656 | tf_op jit(solution)/shard_map/ppermute | solution.py:548
  24.3 24.0 %collective-permute-start.3 = (bf16[256,4096]{1,0:T(8,128)(2,1)S(1)}, bf16[256,4096]{1,0:T(8,128)(2,1)}, u32[]{:S(2)}, u32[]{:S(2)}) collective-permute-start(bf16[256,4096]{1,0:T(8,128)(2,1)S(1)} %bitcast.26), channel_id=1, source_target_pairs={{0,1},{1,0},{2,3},{3,2},{4,5},{5,4},{6,7},{7,6},{8,9},{9,8},{10,11... | collective-permute-start | bytes 6291464 | tf_op jit(solution)/shard_map/ppermute | solution.py:548
  27.4 7.6 %collective-permute-start = (bf16[256,1536]{1,0:T(8,128)(2,1)}, bf16[256,1536]{1,0:T(8,128)(2,1)}, u32[]{:S(2)}, u32[]{:S(2)}) collective-permute-start(bf16[256,1536]{1,0:T(8,128)(2,1)} %get-tuple-element.85), channel_id=1, source_target_pairs={{0,1},{1,0},{2,3},{3,2},{4,5},{5,4},{6,7},{7,6},{8,9},{9,8},{10,11... | collective-permute-start | bytes 2359304 | tf_op jit(solution)/shard_map/ppermute | solution.py:548
  27.9 20.4 %collective-permute-start.4 = (bf16[256,768]{1,0:T(8,128)(2,1)}, bf16[256,768]{1,0:T(8,128)(2,1)}, u32[]{:S(2)}, u32[]{:S(2)}) collective-permute-start(bf16[256,768]{1,0:T(8,128)(2,1)} %get-tuple-element.90), channel_id=1, source_target_pairs={{0,2},{1,3},{2,0},{3,1},{4,6},{5,7},{6,4},{7,5},{8,10},{9,11},{10,... | collective-permute-start | bytes 1179656 | tf_op jit(solution)/shard_map/ppermute | solution.py:548
  30.2 18.2 %collective-permute-start.5 = (bf16[256,768]{1,0:T(8,128)(2,1)}, bf16[256,768]{1,0:T(8,128)(2,1)}, u32[]{:S(2)}, u32[]{:S(2)}) collective-permute-start(bf16[256,768]{1,0:T(8,128)(2,1)} %get-tuple-element.91), channel_id=1, source_target_pairs={{0,3},{1,2},{2,1},{3,0},{4,7},{5,6},{6,5},{7,4},{8,11},{9,10},{10,... | collective-permute-start | bytes 1179656 | tf_op jit(solution)/shard_map/ppermute | solution.py:548
  33.5 26.6 %collective-permute-start.6 = (bf16[256,1024]{1,0:T(8,128)(2,1)S(1)}, bf16[256,1024]{1,0:T(8,128)(2,1)S(1)}, u32[]{:S(2)}, u32[]{:S(2)}) collective-permute-start(bf16[256,1024]{1,0:T(8,128)(2,1)S(1)} %get-tuple-element.95), channel_id=1, source_target_pairs={{0,2},{1,3},{2,0},{3,1},{4,6},{5,7},{6,4},{7,5},{8,10},{9,11},{10,... | collective-permute-start | bytes 1572872 | tf_op jit(solution)/shard_map/ppermute | solution.py:548
  60.1 2.4 %collective-permute-start.7 = (bf16[256,1024]{1,0:T(8,128)(2,1)S(1)}, bf16[256,1024]{1,0:T(8,128)(2,1)S(1)}, u32[]{:S(2)}, u32[]{:S(2)}) collective-permute-start(bf16[256,1024]{1,0:T(8,128)(2,1)S(1)} %collective-permute-done.6.refs_6_.refs_3_), channel_id=1, source_target_pairs={{0,1},{1,0},{2,3},{3,2},{4,5},{5,4},{6,7},{7,6},{8,9},{9,8},{10,11... | collective-permute-start | bytes 1572872 | tf_op jit(solution)/shard_map/ppermute | solution.py:548
  60.5 14.4 %collective-permute-start.8 = (bf16[256,1024]{1,0:T(8,128)(2,1)}, bf16[256,1024]{1,0:T(8,128)(2,1)S(1)}, u32[]{:S(2)}, u32[]{:S(2)}) collective-permute-start(bf16[256,1024]{1,0:T(8,128)(2,1)} %get-tuple-element.100), channel_id=1, source_target_pairs={{0,2},{1,3},{2,0},{3,1},{4,6},{5,7},{6,4},{7,5},{8,10},{9,11},{10,... | collective-permute-start | bytes 1572872 | tf_op jit(solution)/shard_map/ppermute | solution.py:548
  74.9 4.7 %collective-permute-start.9 = (bf16[256,1024]{1,0:T(8,128)(2,1)S(1)}, bf16[256,1024]{1,0:T(8,128)(2,1)S(1)}, u32[]{:S(2)}, u32[]{:S(2)}) collective-permute-start(bf16[256,1024]{1,0:T(8,128)(2,1)S(1)} %collective-permute-done.8.refs_6_.refs_5_), channel_id=1, source_target_pairs={{0,1},{1,0},{2,3},{3,2},{4,5},{5,4},{6,7},{7,6},{8,9},{9,8},{10,11... | collective-permute-start | bytes 1572872 | tf_op jit(solution)/shard_map/ppermute | solution.py:548
  74.9 14.3 %collective-permute-start.10 = (bf16[256,1024]{1,0:T(8,128)(2,1)S(1)}, bf16[256,1024]{1,0:T(8,128)(2,1)S(1)}, u32[]{:S(2)}, u32[]{:S(2)}) collective-permute-start(bf16[256,1024]{1,0:T(8,128)(2,1)S(1)} %copy-done.10), channel_id=1, source_target_pairs={{0,2},{1,3},{2,0},{3,1},{4,6},{5,7},{6,4},{7,5},{8,10},{9,11},{10,... | collective-permute-start | bytes 1572872 | tf_op jit(solution)/shard_map/ppermute | solution.py:548
  76.7 32.1 %collective-permute-start.12 = (bf16[4,1024,128]{2,1,0:T(8,128)(2,1)S(1)}, bf16[4,1024,128]{2,1,0:T(8,128)(2,1)S(1)}, u32[]{:S(2)}, u32[]{:S(2)}) collective-permute-start(bf16[4,1024,128]{2,1,0:T(8,128)(2,1)S(1)} %get-tuple-element.97), channel_id=1, source_target_pairs={{0,8},{4,12},{8,0},{12,4},{16,24},{20,28},{24,16},{28,20},{1,9},{5... | collective-permute-start | bytes 3145736 | tf_op jit(solution)/shard_map/ppermute | solution.py:551
  89.2 3.2 %collective-permute-start.11 = (bf16[256,1024]{1,0:T(8,128)(2,1)S(1)}, bf16[256,1024]{1,0:T(8,128)(2,1)S(1)}, u32[]{:S(2)}, u32[]{:S(2)}) collective-permute-start(bf16[256,1024]{1,0:T(8,128)(2,1)S(1)} %collective-permute-done.10.refs_6_.refs_7_), channel_id=1, source_target_pairs={{0,1},{1,0},{2,3},{3,2},{4,5},{5,4},{6,7},{7,6},{8,9},{9,8},{10,11... | collective-permute-start | bytes 1572872 | tf_op jit(solution)/shard_map/ppermute | solution.py:548
  89.2 19.8 %collective-permute-start.13 = (bf16[256,1024]{1,0:T(8,128)(2,1)S(1)}, bf16[256,1024]{1,0:T(8,128)(2,1)S(1)}, u32[]{:S(2)}, u32[]{:S(2)}) collective-permute-start(bf16[256,1024]{1,0:T(8,128)(2,1)S(1)} %copy-done.8), channel_id=1, source_target_pairs={{0,2},{1,3},{2,0},{3,1},{4,6},{5,7},{6,4},{7,5},{8,10},{9,11},{10,... | collective-permute-start | bytes 1572872 | tf_op jit(solution)/shard_map/ppermute | solution.py:548
  91.0 34.9 %collective-permute-start.15 = (bf16[4,1024,128]{2,1,0:T(8,128)(2,1)S(1)}, bf16[4,1024,128]{2,1,0:T(8,128)(2,1)}, u32[]{:S(2)}, u32[]{:S(2)}) collective-permute-start(bf16[4,1024,128]{2,1,0:T(8,128)(2,1)S(1)} %get-tuple-element.102), channel_id=1, source_target_pairs={{0,4},{4,0},{8,12},{12,8},{16,20},{20,16},{24,28},{28,24},{1,5},{5... | collective-permute-start | bytes 3145736 | tf_op jit(solution)/shard_map/ppermute | solution.py:551
  109.0 3.3 %collective-permute-start.14 = (bf16[256,1024]{1,0:T(8,128)(2,1)S(1)}, bf16[256,1024]{1,0:T(8,128)(2,1)S(1)}, u32[]{:S(2)}, u32[]{:S(2)}) collective-permute-start(bf16[256,1024]{1,0:T(8,128)(2,1)S(1)} %collective-permute-done.13.refs_6_.refs_3_), channel_id=1, source_target_pairs={{0,1},{1,0},{2,3},{3,2},{4,5},{5,4},{6,7},{7,6},{8,9},{9,8},{10,11... | collective-permute-start | bytes 1572872 | tf_op jit(solution)/shard_map/ppermute | solution.py:548
  109.1 39.4 %collective-permute-start.18 = (bf16[4,1024,128]{2,1,0:T(8,128)(2,1)}, bf16[4,1024,128]{2,1,0:T(8,128)(2,1)}, u32[]{:S(2)}, u32[]{:S(2)}) collective-permute-start(bf16[4,1024,128]{2,1,0:T(8,128)(2,1)} %get-tuple-element.110), channel_id=1, source_target_pairs={{0,4},{4,0},{8,12},{12,8},{16,20},{20,16},{24,28},{28,24},{1,5},{5... | collective-permute-start | bytes 3145736 | tf_op jit(solution)/shard_map/ppermute | solution.py:551
  109.7 34.3 %collective-permute-start.16 = (bf16[2,1024,128]{2,1,0:T(8,128)(2,1)S(1)}, bf16[2,1024,128]{2,1,0:T(8,128)(2,1)S(1)}, u32[]{:S(2)}, u32[]{:S(2)}) collective-permute-start(bf16[2,1024,128]{2,1,0:T(8,128)(2,1)S(1)} %get-tuple-element.113), channel_id=1, source_target_pairs={{0,16},{4,20},{8,24},{12,28},{16,0},{20,4},{24,8},{28,12},{1,17},{... | collective-permute-start | bytes 1572872 | tf_op jit(solution)/shard_map/ppermute | solution.py:551
  117.8 60.0 %collective-permute-start.24 = (bf16[4,1024,128]{2,1,0:T(8,128)(2,1)}, bf16[4,1024,128]{2,1,0:T(8,128)(2,1)S(1)}, u32[]{:S(2)}, u32[]{:S(2)}) collective-permute-start(bf16[4,1024,128]{2,1,0:T(8,128)(2,1)} %get-tuple-element.117), channel_id=1, source_target_pairs={{0,4},{4,0},{8,12},{12,8},{16,20},{20,16},{24,28},{28,24},{1,5},{5... | collective-permute-start | bytes 3145736 | tf_op jit(solution)/shard_map/ppermute | solution.py:551
  127.3 19.7 %collective-permute-start.17 = (bf16[2,1024,128]{2,1,0:T(8,128)(2,1)S(1)}, bf16[2,1024,128]{2,1,0:T(8,128)(2,1)S(1)}, u32[]{:S(2)}, u32[]{:S(2)}) collective-permute-start(bf16[2,1024,128]{2,1,0:T(8,128)(2,1)S(1)} %get-tuple-element.122), channel_id=1, source_target_pairs={{0,8},{4,12},{8,0},{12,4},{16,24},{20,28},{24,16},{28,20},{1,9},{5... | collective-permute-start | bytes 1572872 | tf_op jit(solution)/shard_map/ppermute | solution.py:551
  144.1 22.7 %collective-permute-start.19 = (bf16[1,1024,128]{2,1,0:T(8,128)(2,1)S(1)}, bf16[1,1024,128]{2,1,0:T(8,128)(2,1)S(1)}, u32[]{:S(2)}, u32[]{:S(2)}) collective-permute-start(bf16[1,1024,128]{2,1,0:T(8,128)(2,1)S(1)} %get-tuple-element.126), channel_id=1, source_target_pairs={{0,4},{4,0},{8,12},{12,8},{16,20},{20,16},{24,28},{28,24},{1,5},{5... | collective-permute-start | bytes 786440 | tf_op jit(solution)/shard_map/ppermute | solution.py:551
  145.4 21.4 %collective-permute-start.21 = (bf16[256,768]{1,0:T(8,128)(2,1)S(1)}, bf16[256,768]{1,0:T(8,128)(2,1)S(1)}, u32[]{:S(2)}, u32[]{:S(2)}) collective-permute-start(bf16[256,768]{1,0:T(8,128)(2,1)S(1)} %get-tuple-element.160), channel_id=1, source_target_pairs={{0,3},{1,2},{2,1},{3,0},{4,7},{5,6},{6,5},{7,4},{8,11},{9,10},{10,... | collective-permute-start | bytes 1179656 | tf_op jit(solution)/shard_map/ppermute | solution.py:548
  147.1 21.1 %collective-permute-start.20 = (bf16[256,768]{1,0:T(8,128)(2,1)S(1)}, bf16[256,768]{1,0:T(8,128)(2,1)S(1)}, u32[]{:S(2)}, u32[]{:S(2)}) collective-permute-start(bf16[256,768]{1,0:T(8,128)(2,1)S(1)} %get-tuple-element.161), channel_id=1, source_target_pairs={{0,2},{1,3},{2,0},{3,1},{4,6},{5,7},{6,4},{7,5},{8,10},{9,11},{10,... | collective-permute-start | bytes 1179656 | tf_op jit(solution)/shard_map/ppermute | solution.py:548
  149.9 18.3 %collective-permute-start.22 = (bf16[2,1024,128]{2,1,0:T(8,128)(2,1)S(1)}, bf16[2,1024,128]{2,1,0:T(8,128)(2,1)S(1)}, u32[]{:S(2)}, u32[]{:S(2)}) collective-permute-start(bf16[2,1024,128]{2,1,0:T(8,128)(2,1)S(1)} %get-tuple-element.132), channel_id=1, source_target_pairs={{0,8},{4,12},{8,0},{12,4},{16,24},{20,28},{24,16},{28,20},{1,9},{5... | collective-permute-start | bytes 1572872 | tf_op jit(solution)/shard_map/ppermute | solution.py:551
  166.8 11.0 %collective-permute-start.23 = (bf16[256,768]{1,0:T(8,128)(2,1)S(1)}, bf16[256,768]{1,0:T(8,128)(2,1)S(1)}, u32[]{:S(2)}, u32[]{:S(2)}) collective-permute-start(bf16[256,768]{1,0:T(8,128)(2,1)S(1)} %get-tuple-element.157), channel_id=1, source_target_pairs={{0,3},{1,2},{2,1},{3,0},{4,7},{5,6},{6,5},{7,4},{8,11},{9,10},{10,... | collective-permute-start | bytes 1179656 | tf_op jit(solution)/shard_map/ppermute | solution.py:548
  166.9 37.5 %collective-permute-start.29 = (bf16[512,768]{1,0:T(8,128)(2,1)S(1)}, bf16[512,768]{1,0:T(8,128)(2,1)S(1)}, u32[]{:S(2)}, u32[]{:S(2)}) collective-permute-start(bf16[512,768]{1,0:T(8,128)(2,1)S(1)} %pad_maximum_fusion), channel_id=1, source_target_pairs={{0,1},{1,0},{2,3},{3,2},{4,5},{5,4},{6,7},{7,6},{8,9},{9,8},{10,11... | collective-permute-start | bytes 2359304 | tf_op jit(solution)/shard_map/ppermute | solution.py:548
  178.0 25.2 %collective-permute-start.27 = (bf16[2,1024,128]{2,1,0:T(8,128)(2,1)S(1)}, bf16[2,1024,128]{2,1,0:T(8,128)(2,1)S(1)}, u32[]{:S(2)}, u32[]{:S(2)}) collective-permute-start(bf16[2,1024,128]{2,1,0:T(8,128)(2,1)S(1)} %get-tuple-element.143), channel_id=1, source_target_pairs={{0,8},{4,12},{8,0},{12,4},{16,24},{20,28},{24,16},{28,20},{1,9},{5... | collective-permute-start | bytes 1572872 | tf_op jit(solution)/shard_map/ppermute | solution.py:551
  181.2 18.8 %collective-permute-start.26 = (bf16[256,768]{1,0:T(8,128)(2,1)S(1)}, bf16[256,768]{1,0:T(8,128)(2,1)S(1)}, u32[]{:S(2)}, u32[]{:S(2)}) collective-permute-start(bf16[256,768]{1,0:T(8,128)(2,1)S(1)} %get-tuple-element.156), channel_id=1, source_target_pairs={{0,2},{1,3},{2,0},{3,1},{4,6},{5,7},{6,4},{7,5},{8,10},{9,11},{10,... | collective-permute-start | bytes 1179656 | tf_op jit(solution)/shard_map/ppermute | solution.py:548
  182.2 16.9 %collective-permute-start.25 = (bf16[1,1024,128]{2,1,0:T(8,128)(2,1)S(1)}, bf16[1,1024,128]{2,1,0:T(8,128)(2,1)S(1)}, u32[]{:S(2)}, u32[]{:S(2)}) collective-permute-start(bf16[1,1024,128]{2,1,0:T(8,128)(2,1)S(1)} %get-tuple-element.128), channel_id=1, source_target_pairs={{0,16},{4,20},{8,24},{12,28},{16,0},{20,4},{24,8},{28,12},{1,17},{... | collective-permute-start | bytes 786440 | tf_op jit(solution)/shard_map/ppermute | solution.py:551
  184.9 29.6 %collective-permute-start.28 = (bf16[1,1024,128]{2,1,0:T(8,128)(2,1)S(1)}, bf16[1,1024,128]{2,1,0:T(8,128)(2,1)S(1)}, u32[]{:S(2)}, u32[]{:S(2)}) collective-permute-start(bf16[1,1024,128]{2,1,0:T(8,128)(2,1)S(1)} %get-tuple-element.139), channel_id=1, source_target_pairs={{0,16},{4,20},{8,24},{12,28},{16,0},{20,4},{24,8},{28,12},{1,17},{... | collective-permute-start | bytes 786440 | tf_op jit(solution)/shard_map/ppermute | solution.py:551
  203.3 15.6 %collective-permute-start.30 = (bf16[1,1024,128]{2,1,0:T(8,128)(2,1)S(1)}, bf16[1,1024,128]{2,1,0:T(8,128)(2,1)S(1)}, u32[]{:S(2)}, u32[]{:S(2)}) collective-permute-start(bf16[1,1024,128]{2,1,0:T(8,128)(2,1)S(1)} %get-tuple-element.146), channel_id=1, source_target_pairs={{0,16},{4,20},{8,24},{12,28},{16,0},{20,4},{24,8},{28,12},{1,17},{... | collective-permute-start | bytes 786440 | tf_op jit(solution)/shard_map/ppermute | solution.py:551
  (19 other events, 101.3 us)

commit v3 on v2

--- a/solution.py
+++ b/solution.py
@@ -25,8 +25,8 @@
     return pltpu.CompilerParams(vmem_limit_bytes=mib * 2**20)
 
 
-def cost(us):
-    return pl.CostEstimate(flops=int(us * 0.25 * 1.15e9), bytes_accessed=1024, transcendentals=0)
+def cost(weight):
+    return pl.CostEstimate(flops=int(weight * 1e9), bytes_accessed=1024, transcendentals=0)
 
 
 ANY = pl.BlockSpec(memory_space=pl.ANY)
@@ -41,10 +41,13 @@
     return list(lax.optimization_barrier((*arrays, *flat)))[: len(arrays)]
 
 
-def pack_kernel(jobs, me_ref, *refs):
+def pack_kernel(jobs, joined, me_ref, *refs):
     wide = GROUP * HEAD_DIM
     size = wide + 2 * HEAD_DIM
     sources, outs = iter(refs[: len(refs) - len(jobs)]), refs[len(refs) - len(jobs) :]
+    if joined:
+        outs[1][:, size * len(jobs[1][1]) :] = refs[0][...]
+        next(sources)
     for out, (d, members) in zip(outs, jobs):
         for slot in range(len(members)):
             start = slot * size
@@ -53,7 +56,7 @@
                 start += width
 
 
-def pack(me, sources, parts, jobs):
+def pack(me, sources, parts, jobs, joined=None):
     rows = sources[0].shape[0]
     groups = KV_HEADS // parts
     wide = GROUP * HEAD_DIM
@@ -69,22 +72,23 @@
         for gp in members
         for width in (wide, HEAD_DIM, HEAD_DIM)
     ]
-    return pl.pallas_call(
-        functools.partial(pack_kernel, jobs),
+    more = [] if joined is None else [joined]
+    widths = [size * len(members) for d, members in jobs]
+    if more:
+        widths[1] += joined.shape[1]
+    return pl.pallas_call(
+        functools.partial(pack_kernel, jobs, bool(more)),
         grid_spec=pltpu.PrefetchScalarGridSpec(
             num_scalar_prefetch=1,
             grid=(rows // step,),
-            in_specs=specs,
-            out_specs=[
-                pl.BlockSpec((step, size * len(members)), lambda i, me: (i, 0))
-                for d, members in jobs
-            ],
+            in_specs=[pl.BlockSpec((step, x.shape[1]), lambda i, me: (i, 0)) for x in more] + specs,
+            out_specs=[pl.BlockSpec((step, width), lambda i, me: (i, 0)) for width in widths],
         ),
-        out_shape=[shape((rows, size * len(members))) for d, members in jobs],
+        out_shape=[shape((rows, width)) for width in widths],
         compiler_params=params(60),
-        cost_estimate=cost(2.0),
+        cost_estimate=cost(0.2),
         name="pack",
-    )(me, *sources * (len(specs) // 3))
+    )(me, *more, *sources * (len(specs) // 3))
 
 
 def column(share, c, chunks, width):
@@ -109,8 +113,8 @@
         in_specs=[pl.BlockSpec((step, model), lambda i: (i, 0))],
         out_specs=[pl.BlockSpec((step, shares * width), lambda i: (i, 0))] * len(orders),
         out_shape=[shape((rows, shares * width)) for order in orders],
-        compiler_params=params(40),
-        cost_estimate=cost(3.8),
+        compiler_params=params(60),
+        cost_estimate=cost(0.2),
         name="pack_chunks",
     )(cotangent)
 
@@ -144,8 +148,8 @@
             out_specs=[pl.BlockSpec((step, w), lambda i, info: (i, 0)) for w in widths],
         ),
         out_shape=[shape((rows, w)) for w in widths],
-        compiler_params=params(40),
-        cost_estimate=cost(2.8),
+        compiler_params=params(16),
+        cost_estimate=cost(0.2),
         name="unpack",
     )(info, *pieces)
 
@@ -260,8 +264,8 @@
             shape((parts, wide, block)),
             shape((GROUP, parts, 8, block), jnp.float32),
         ],
-        compiler_params=params(40),
-        cost_estimate=cost(10.0),
+        compiler_params=params(16),
+        cost_estimate=cost(1.0),
         name="attention",
     )(gate([info], token)[0], *[x for x, at in pieces])
 
@@ -353,8 +357,8 @@
             ],
         ),
         out_shape=shape((parts, block, cols)),
-        compiler_params=params(40),
-        cost_estimate=cost(12.5),
+        compiler_params=params(20),
+        cost_estimate=cost(1.5),
         name="attention_back",
     )(gate([info], token)[0], *[x for x, at in pieces], grads, out, lse)
 
@@ -407,10 +411,11 @@
     def mate(t, info):
         return t ^ (place_of(info[1], order) >> 1)
 
-    def original(side):
+    def original(side, x):
+        shift = (x.shape[1] - shares * chunks * width) // width
         return pl.BlockSpec(
             (block, width),
-            lambda t, info: (0, unplace(2 * mate(t, info) + side, order) * chunks + c),
+            lambda t, info: (0, shift + unplace(2 * mate(t, info) + side, order) * chunks + c),
         )
 
     return pl.pallas_call(
@@ -419,8 +424,7 @@
             num_scalar_prefetch=1,
             grid=(half,),
             in_specs=[pl.BlockSpec((parts, rows, block), lambda t, info: (0, 0, 0))] * groups
-            + [original(0)] * 2
-            + [original(1)] * 2
+            + [original(side, x) for side in range(2) for x in near]
             + [pl.BlockSpec((block, 2 * width), lambda t, info: (0, mate(t, info)))] * len(chunk),
             out_specs=[spot, spot],
         ),
@@ -428,8 +432,8 @@
             shape((half, groups * rows, width), jnp.float32),
             shape((half, groups * rows, width)),
         ],
-        compiler_params=params(40),
-        cost_estimate=cost(4.3),
+        compiler_params=params(16),
+        cost_estimate=cost(0.3),
         name="weight_terms",
     )(gate([info], token)[0], *outs, *near, *near, *chunk)
 
@@ -454,8 +458,8 @@
             shape((half, rows, width), jnp.float32),
             shape((half, rows, width)),
         ],
-        compiler_params=params(40),
-        cost_estimate=cost(0.5),
+        compiler_params=params(12),
+        cost_estimate=cost(0.02),
         name="merge",
     )(keep, keep, got, got)
 
@@ -476,10 +480,15 @@
         out_specs=pl.BlockSpec((step, width), lambda i: (i, c)),
         out_shape=shape((rows, width * chunks), jnp.float32),
         input_output_aliases={2: 0} if more else {},
-        compiler_params=params(40),
-        cost_estimate=cost(0.8),
+        compiler_params=params(8),
+        cost_estimate=cost(0.02),
         name="finish",
     )(gate([keep], token)[0], got, *more)
+
+
+def shifted(ref, like, columns):
+    more = ref.shape[1] - like.shape[1]
+    return slice(columns.start + more, columns.stop + more)
 
 
 def project_kernel(parts, shares, width, chunks, orders, picked, first, last, *refs):
@@ -490,7 +499,7 @@
     weights = jnp.concatenate([w_ref[:, column(j, c, chunks, width)] for c, j in columns], axis=1)
     for d in range(parts):
         if d < 2:
-            rows = jnp.concatenate([near[d][:, column(j, c, chunks, width)] for c, j in columns], axis=1)
+            rows = jnp.concatenate([near[d][:, shifted(near[d], w_ref, column(j, c, chunks, width))] for c, j in columns], axis=1)
         else:
             mine = [far[i * (parts - 2) + d - 2][...] for i in range(len(picked))]
             rows = mine[0] if len(mine) == 1 else jnp.concatenate(mine, axis=1)
@@ -514,13 +523,13 @@
         ),
         grid=(feats // step,),
         in_specs=[pl.BlockSpec((step, model), lambda i: (i, 0))]
-        + [pl.BlockSpec((rows, model), lambda i: (0, 0))] * 2
+        + [pl.BlockSpec((rows, x.shape[1]), lambda i: (0, 0)) for x in near]
         + [pl.BlockSpec((rows, shares * width), lambda i: (0, 0))] * len(flat)
         + ([] if first else [block]),
         out_specs=block,
         out_shape=shape((parts, rows, feats), jnp.bfloat16 if last else jnp.float32),
-        compiler_params=params(40),
-        cost_estimate=cost(2.5 * len(picked)),
+        compiler_params=params(24),
+        cost_estimate=cost(0.5),
         name="project",
     )(gate([out_weight], token)[0], *near, *flat, *([] if first else [acc]))
 
@@ -568,7 +577,7 @@
     core = over_seq(rest[1], 1)
     pieces = [[(rest[0], gp), (core, gp)] + [(x, 0) for x in sent_far[gp]] for gp in range(groups)]
     sends = pack_chunks(gate([cotangent], rest[0])[0], orders, shares, width)
-    near = [cotangent, over_seq(gate([cotangent], *sent_far[0])[0], 1)]
+    near = [cotangent, over_seq(gate([cotangent], *sent_far[0], sends[-1])[0], 1)]
 
     far_half = {}
 
@@ -578,7 +587,7 @@
 
     for c in range(chunks):
         if c < groups:
-            send_chunk(c, *sent_far[c])
+            send_chunk(c, *sent_far[c], sends[-1])
         else:
             send_chunk(c, *far_half[max(0, c - groups)])
 
@@ -627,33 +636,33 @@
             out_weight, near, [fars[c] for c in picked], acc, token, orders, picked, shares, width, last
         )
 
-    def send_back(gp):
+    def send_back(gp, *tokens):
         nonlocal token
         res = attention_back(info, pieces[gp], acc, outs[gp], fwd[gp][1], token, parts, docs, gp)
-        token = results[gp] = res
-        back[gp] = [res[0], None] + [over_seq(res[d], d) for d in far]
+        token = res
+        parted = gate([res[d] for d in range(parts)], *tokens)
+        results[gp] = parted
+        back[gp] = [parted[0], None] + [over_seq(parted[d], d) for d in far]
 
     last = chunks - 1
     for c in range(last):
         weigh(c)
+    advance(0)
     if last:
         project_step(list(range(last)), False)
-    advance(0)
     weigh(last)
+    advance(1)
     project_step([last], True)
-    advance(1)
     send_back(0)
-    for c in (0, 1, 2):
+    for c in (0, 1, 2, 0):
         advance(c)
     for gp in range(1, groups):
-        send_back(gp)
-    advance(0)
-    token = (token, *back[0][2:])
+        send_back(gp, *back[gp - 1][2:])
+    advance(1)
     advance(2)
+    token = (token, back[groups - 1][2])
+    advance(3)
     both = over_seq(jnp.concatenate([results[gp][1] for gp in range(groups)], axis=0), 1)
-    token = (token, back[groups - 1][-1])
-    advance(3)
-    advance(1)
     token = (token, *back[groups - 1][2:])
     advance(3)
     for gp in range(groups):

time: 221 us -> 239 us (1.081)
  waiting for transfers between devices: 70.6 us -> 100 us
  Pallas kernels: 105 us -> 93.5 us
    ppermute x12, waiting for transfers between devices: 32.9 us -> 54.6 us  [over_dp(): return lax.ppermute(x, 'dp', [(i, i ^ d) for i in range(shares)])]
    ppermute x19, waiting for transfers between devices: 37.7 us -> 45.7 us  [over_seq(): return lax.ppermute(x, 'seq', [(i, i ^ d) for i in range(parts)])]
    pallas_call x2, Pallas kernels: 27.4 us -> 23.5 us  [attention_back(): pl.pallas_call(functools.partial(backward_kernel, parts, block, docs), gr...]
    pallas_call x2, Pallas kernels: 23 us -> 19.4 us  [attention(): pl.pallas_call(functools.partial(forward_kernel, parts, block, docs), gri...]
    pallas_call x2, Pallas kernels: 17.3 us -> 14.6 us  [project(): pl.pallas_call(functools.partial(project_kernel, parts, shares, width, le...]
    pallas_call x1, Pallas kernels: 1.59 us -> 4.02 us  [pack_chunks(): pl.pallas_call(functools.partial(pack_chunks_kernel, orders, shares, widt...]
    unnamed x40 -> x30, local copies, waits for them, and re-layouts: 6.48 us -> 4.68 us
  transfers between devices with their start and end apart: 31 -> 31, of which waited for: 12 -> 15; matrix products, arithmetic and copies ran while one was open for 0% -> 0% of each run, Pallas kernels for 46% -> 38%
where the time goes in v3:
time: 239 us; the launch traced here: 236 us
  waiting for transfers between devices  100 us (42%)
  Pallas kernels  93.5 us (39%)
  starting transfers between devices  36.6 us (15%)
  local copies, waits for them, and re-layouts  4.94 us (2%)
    ppermute x12, waiting for transfers between devices, over_dp(): return lax.ppermute(x, 'dp', [(i, i ^ d) for i in range(shares)])  54.6 us
    ppermute x19, waiting for transfers between devices, over_seq(): return lax.ppermute(x, 'seq', [(i, i ^ d) for i in range(parts)])  45.7 us
    pallas_call x2, Pallas kernels, attention_back(): pl.pallas_call(functools.partial(backward_kernel, parts, block, docs), gr...  23.5 us
    ppermute x12, starting transfers between devices, over_dp(): return lax.ppermute(x, 'dp', [(i, i ^ d) for i in range(shares)])  22.6 us
    pallas_call x4, Pallas kernels, weight_terms(): pl.pallas_call(functools.partial(weight_kernel, parts, groups, width, ord...  19.6 us
    pallas_call x2, Pallas kernels, attention(): pl.pallas_call(functools.partial(forward_kernel, parts, block, docs), gri...  19.4 us
    pallas_call x2, Pallas kernels, project(): pl.pallas_call(functools.partial(project_kernel, parts, shares, width, le...  14.6 us
    ppermute x19, starting transfers between devices, over_seq(): return lax.ppermute(x, 'seq', [(i, i ^ d) for i in range(parts)])  14 us
  transfers between devices with their start and end apart: 31, of which 15 were waited for; matrix products, arithmetic and copies ran while one was open for 0% of the time, Pallas kernels for 38%

profile of v3, /device:TPU:0, one launch (start us, length us, event | category | flops | bytes accessed | tf_op | source)
XLA Modules:
  0.0 236.5 jit_solution(4492483456600686510)
XLA Ops:
  2.7 2.4 %collective-permute-start.2 = (bf16[256,768]{1,0:T(8,128)(2,1)}, bf16[256,768]{1,0:T(8,128)(2,1)S(1)}, u32[]{:S(2)}, u32[]{:S(2)}) collective-permute-start(bf16[256,768]{1,0:T(8,128)(2,1)} %get-tuple-element.94), channel_id=1, source_target_pairs={{0,3},{1,2},{2,1},{3,0},{4,7},{5,6},{6,5},{7,4},{8,11},{9,10},{10,... | collective-permute-start | bytes 1179656 | tf_op jit(solution)/shard_map/ppermute | solution.py:557
  5.8 3.1 %pack.3 = (bf16[256,1536]{1,0:T(8,128)(2,1)}, bf16[256,1536]{1,0:T(8,128)(2,1)}, bf16[256,768]{1,0:T(8,128)(2,1)}, bf16[256,768]{1,0:T(8,128)(2,1)}) custom-call(s32[1]{0:T(128)} %bitcast.me_ref, bf16[256,4096]{1,0:T(8,128)(2,1)} %bitcast.42, bf16[256,1024]{1,0:T(8,128)(2,1)} %bitcast.50, bf16[256,1024]{1,0:T(8,128)(2,1)} %bitcast.58, ...), custom_call_target="tpu_custom_call" | custom-call | flops 200000000 | bytes 1024 | tf_op jit(solution)/shard_map/pack/pallas_call | solution.py:79
  8.8 4.0 %pack_chunks.1 = (bf16[256,1024]{1,0:T(8,128)(2,1)}, bf16[256,1024]{1,0:T(8,128)(2,1)}, bf16[256,1024]{1,0:T(8,128)(2,1)}, bf16[256,1024]{1,0:T(8,128)(2,1)}) custom-call(bf16[256,4096]{1,0:T(8,128)(2,1)} %bitcast.26), custom_call_target="tpu_custom_call" | custom-call | flops 200000000 | bytes 1024 | tf_op jit(solution)/shard_map/pack_chunks/pallas_call | solution.py:110
  15.7 7.7 %collective-permute-done.1.refs_2_ = bf16[256,768]{1,0:T(8,128)(2,1)S(1)} collective-permute-done((bf16[256,768]{1,0:T(8,128)(2,1)}, bf16[256,768]{1,0:T(8,128)(2,1)S(1)}, u32[]{:S(2)}, u32[]{:S(2)}) %collective-permute-start.1) | collective-permute-done | bytes 393248 | tf_op jit(solution)/shard_map/ppermute | solution.py:557
  32.5 9.1 %attention.2 = (bf16[4,512,256]{2,1,0:T(8,128)(2,1)S(1)}, f32[4,4,8,256]{3,2,1,0:T(8,128)S(1)}) custom-call(s32[10]{0:T(128)S(1)} %pad_add_fusion.info_ref, bf16[256,1536]{1,0:T(8,128)(2,1)S(1)} %copy-done.1, bf16[256,1536]{1,0:T(8,128)(2,1)S(1)} %collective-permute-done.refs_1_, bf16[256,768]{1,0:T(8,128)(2,1)S(1)} %copy-done.7, bf16[256,768]{1,0:T(8,128)(2,1)S(1)} %copy-done.4), custom_call_target="tpu_custom_call" | custom-call | flops 1000000000 | bytes 1024 | tf_op jit(solution)/shard_map/attention/pallas_call | solution.py:242
  41.6 6.9 %collective-permute-done.4.refs_2_ = bf16[256,768]{1,0:T(8,128)(2,1)} collective-permute-done((bf16[256,768]{1,0:T(8,128)(2,1)}, bf16[256,768]{1,0:T(8,128)(2,1)}, u32[]{:S(2)}, u32[]{:S(2)}) %collective-permute-start.4) | collective-permute-done | bytes 393248 | tf_op jit(solution)/shard_map/ppermute | solution.py:557
  48.5 7.4 %collective-permute-done.5.refs_3_ = bf16[256,768]{1,0:T(8,128)(2,1)} collective-permute-done((bf16[256,768]{1,0:T(8,128)(2,1)}, bf16[256,768]{1,0:T(8,128)(2,1)}, u32[]{:S(2)}, u32[]{:S(2)}) %collective-permute-start.5) | collective-permute-done | bytes 393248 | tf_op jit(solution)/shard_map/ppermute | solution.py:557
  55.8 10.3 %attention.3 = (bf16[4,512,256]{2,1,0:T(8,128)(2,1)S(1)}, f32[4,4,8,256]{3,2,1,0:T(8,128)S(1)}) custom-call(s32[10]{0:T(128)S(1)} %pad_add_fusion.info_ref, bf16[256,1536]{1,0:T(8,128)(2,1)S(1)} %copy-done.1, bf16[256,1536]{1,0:T(8,128)(2,1)S(1)} %collective-permute-done.refs_1_, bf16[256,768]{1,0:T(8,128)(2,1)} %collective-permute-done.4.refs_2_, ...), custom_call_target="tpu_custom_call" | custom-call | flops 1000000000 | bytes 1024 | tf_op jit(solution)/shard_map/attention/pallas_call | solution.py:242
  68.3 4.8 %weight_terms.4 = (f32[4,1024,128]{2,1,0:T(8,128)S(1)}, bf16[4,1024,128]{2,1,0:T(8,128)(2,1)S(1)}) custom-call(s32[10]{0:T(128)S(1)} %pad_add_fusion.info_ref, bf16[4,512,256]{2,1,0:T(8,128)(2,1)S(1)} %get-tuple-element.95.refs_0_.refs_5_, bf16[4,512,256]{2,1,0:T(8,128)(2,1)S(1)} %get-tuple-element.100.refs_1_.refs_5_, bf16[256,4096]{1,0:T(8,128)(2,1)S(1)} %bitcast.28, ...), custom_call_target="tpu_custom_call" | custom-call | flops 300000000 | bytes 1024 | tf_op jit(solution)/shard_map/weight_terms/pallas_call | solution.py:421
  73.1 7.4 %collective-permute-done.8.refs_6_.refs_5_ = bf16[256,1024]{1,0:T(8,128)(2,1)S(1)} collective-permute-done((bf16[256,1024]{1,0:T(8,128)(2,1)S(1)}, bf16[256,1024]{1,0:T(8,128)(2,1)S(1)}, u32[]{:S(2)}, u32[]{:S(2)}) %collective-permute-start.8) | collective-permute-done | bytes 524320 | tf_op jit(solution)/shard_map/ppermute | solution.py:557
  82.3 2.8 %collective-permute-start.12 = (bf16[4,1024,128]{2,1,0:T(8,128)(2,1)S(1)}, bf16[4,1024,128]{2,1,0:T(8,128)(2,1)S(1)}, u32[]{:S(2)}, u32[]{:S(2)}) collective-permute-start(bf16[4,1024,128]{2,1,0:T(8,128)(2,1)S(1)} %get-tuple-element.105), channel_id=1, source_target_pairs={{0,8},{4,12},{8,0},{12,4},{16,24},{20,28},{24,16},{28,20},{1,9},{5... | collective-permute-start | bytes 3145736 | tf_op jit(solution)/shard_map/ppermute | solution.py:560
  85.1 5.1 %weight_terms.5 = (f32[4,1024,128]{2,1,0:T(8,128)S(1)}, bf16[4,1024,128]{2,1,0:T(8,128)(2,1)S(1)}) custom-call(s32[10]{0:T(128)S(1)} %pad_add_fusion.info_ref, bf16[4,512,256]{2,1,0:T(8,128)(2,1)S(1)} %get-tuple-element.95.refs_0_.refs_5_, bf16[4,512,256]{2,1,0:T(8,128)(2,1)S(1)} %get-tuple-element.100.refs_1_.refs_5_, bf16[256,4096]{1,0:T(8,128)(2,1)S(1)} %bitcast.30, ...), custom_call_target="tpu_custom_call" | custom-call | flops 300000000 | bytes 1024 | tf_op jit(solution)/shard_map/weight_terms/pallas_call | solution.py:421
  90.3 4.6 %collective-permute-done.10.refs_6_.refs_7_ = bf16[256,1024]{1,0:T(8,128)(2,1)S(1)} collective-permute-done((bf16[256,1024]{1,0:T(8,128)(2,1)S(1)}, bf16[256,1024]{1,0:T(8,128)(2,1)S(1)}, u32[]{:S(2)}, u32[]{:S(2)}) %collective-permute-start.10) | collective-permute-done | bytes 524320 | tf_op jit(solution)/shard_map/ppermute | solution.py:557
  96.6 2.7 %collective-permute-start.15 = (bf16[4,1024,128]{2,1,0:T(8,128)(2,1)S(1)}, bf16[4,1024,128]{2,1,0:T(8,128)(2,1)S(1)}, u32[]{:S(2)}, u32[]{:S(2)}) collective-permute-start(bf16[4,1024,128]{2,1,0:T(8,128)(2,1)S(1)} %get-tuple-element.110), channel_id=1, source_target_pairs={{0,4},{4,0},{8,12},{12,8},{16,20},{20,16},{24,28},{28,24},{1,5},{5... | collective-permute-start | bytes 3145736 | tf_op jit(solution)/shard_map/ppermute | solution.py:560
  99.4 4.8 %weight_terms.6 = (f32[4,1024,128]{2,1,0:T(8,128)S(1)}, bf16[4,1024,128]{2,1,0:T(8,128)(2,1)S(1)}) custom-call(s32[10]{0:T(128)S(1)} %pad_add_fusion.info_ref, bf16[4,512,256]{2,1,0:T(8,128)(2,1)S(1)} %get-tuple-element.95.refs_0_.refs_5_, bf16[4,512,256]{2,1,0:T(8,128)(2,1)S(1)} %get-tuple-element.100.refs_1_.refs_5_, bf16[256,4096]{1,0:T(8,128)(2,1)S(1)} %bitcast.32, ...), custom_call_target="tpu_custom_call" | custom-call | flops 300000000 | bytes 1024 | tf_op jit(solution)/shard_map/weight_terms/pallas_call | solution.py:421
  104.2 4.4 %collective-permute-done.12.got_low.got_high = bf16[4,1024,128]{2,1,0:T(8,128)(2,1)S(1)} collective-permute-done((bf16[4,1024,128]{2,1,0:T(8,128)(2,1)S(1)}, bf16[4,1024,128]{2,1,0:T(8,128)(2,1)S(1)}, u32[]{:S(2)}, u32[]{:S(2)}) %collective-permute-start.12) | collective-permute-done | bytes 1048608 | tf_op jit(solution)/shard_map/ppermute | solution.py:560
  108.9 9.4 %project.2.refs_5_ = f32[4,256,1024]{2,1,0:T(8,128)S(1)} custom-call(bf16[1024,4096]{1,0:T(8,128)(2,1)S(1)} %bitcast.39, bf16[256,4096]{1,0:T(8,128)(2,1)S(1)} %bitcast.34, bf16[256,4096]{1,0:T(8,128)(2,1)} %collective-permute-done.3.refs_3_.refs_5_.refs_2_, bf16[256,1024]{1,0:T(8,128)(2,1)S(1)} %collective-permute-done.6.refs_6_.refs_3_, ...), custom_call_target="tpu_custom_call" | custom-call | flops 500000000 | bytes 1024 | tf_op jit(solution)/shard_map/project/pallas_call | solution.py:520
  118.4 2.8 %collective-permute-start.18 = (bf16[4,1024,128]{2,1,0:T(8,128)(2,1)S(1)}, bf16[4,1024,128]{2,1,0:T(8,128)(2,1)S(1)}, u32[]{:S(2)}, u32[]{:S(2)}) collective-permute-start(bf16[4,1024,128]{2,1,0:T(8,128)(2,1)S(1)} %get-tuple-element.118), channel_id=1, source_target_pairs={{0,4},{4,0},{8,12},{12,8},{16,20},{20,16},{24,28},{28,24},{1,5},{5... | collective-permute-start | bytes 3145736 | tf_op jit(solution)/shard_map/ppermute | solution.py:560
  121.2 2.8 %collective-permute-start.16 = (bf16[2,1024,128]{2,1,0:T(8,128)(2,1)S(1)}, bf16[2,1024,128]{2,1,0:T(8,128)(2,1)S(1)}, u32[]{:S(2)}, u32[]{:S(2)}) collective-permute-start(bf16[2,1024,128]{2,1,0:T(8,128)(2,1)S(1)} %get-tuple-element.120), channel_id=1, source_target_pairs={{0,16},{4,20},{8,24},{12,28},{16,0},{20,4},{24,8},{28,12},{1,17},{... | collective-permute-start | bytes 1572872 | tf_op jit(solution)/shard_map/ppermute | solution.py:560
  123.9 4.8 %weight_terms.7 = (f32[4,1024,128]{2,1,0:T(8,128)S(1)}, bf16[4,1024,128]{2,1,0:T(8,128)(2,1)S(1)}) custom-call(s32[10]{0:T(128)S(1)} %pad_add_fusion.info_ref, bf16[4,512,256]{2,1,0:T(8,128)(2,1)S(1)} %get-tuple-element.95.refs_0_.refs_5_, bf16[4,512,256]{2,1,0:T(8,128)(2,1)S(1)} %get-tuple-element.100.refs_1_.refs_5_, bf16[256,4096]{1,0:T(8,128)(2,1)S(1)} %bitcast.35, ...), custom_call_target="tpu_custom_call" | custom-call | flops 300000000 | bytes 1024 | tf_op jit(solution)/shard_map/weight_terms/pallas_call | solution.py:421
  130.0 5.2 %project.3.refs_4_ = bf16[4,256,1024]{2,1,0:T(8,128)(2,1)S(1)} custom-call(bf16[1024,4096]{1,0:T(8,128)(2,1)S(1)} %bitcast.39, bf16[256,4096]{1,0:T(8,128)(2,1)S(1)} %bitcast.37, bf16[256,4096]{1,0:T(8,128)(2,1)} %collective-permute-done.3.refs_3_.refs_5_.refs_2_, bf16[256,1024]{1,0:T(8,128)(2,1)S(1)} %collective-permute-done.13.refs_6_.refs_3_, ...), custom_call_target="tpu_custom_call" | custom-call | flops 500000000 | bytes 1024 | tf_op jit(solution)/shard_map/project/pallas_call | solution.py:520
  135.2 11.2 %attention_back.2 = bf16[4,256,768]{2,1,0:T(8,128)(2,1)S(1)} custom-call(s32[10]{0:T(128)S(1)} %pad_add_fusion.info_ref, bf16[256,1536]{1,0:T(8,128)(2,1)S(1)} %copy-done.2, bf16[256,1536]{1,0:T(8,128)(2,1)S(1)} %collective-permute-done.refs_1_, bf16[256,768]{1,0:T(8,128)(2,1)S(1)} %copy-done.8, bf16[256,768]{1,0:T(8,128)(2,1)S(1)} %copy-done.5, ...), custom_call_target="tpu_custom_call" | custom-call | flops 1500000000 | bytes 1024 | tf_op jit(solution)/shard_map/attention_back/pallas_call | solution.py:334
  150.1 2.8 %collective-permute-done.17.got_low.got_high = bf16[2,1024,128]{2,1,0:T(8,128)(2,1)S(1)} collective-permute-done((bf16[2,1024,128]{2,1,0:T(8,128)(2,1)S(1)}, bf16[2,1024,128]{2,1,0:T(8,128)(2,1)S(1)}, u32[]{:S(2)}, u32[]{:S(2)}) %collective-permute-start.17) | collective-permute-done | bytes 524320 | tf_op jit(solution)/shard_map/ppermute | solution.py:560
  153.5 19.9 %collective-permute-done.19.got_ref = bf16[1,1024,128]{2,1,0:T(8,128)(2,1)S(1)} collective-permute-done((bf16[1,1024,128]{2,1,0:T(8,128)(2,1)S(1)}, bf16[1,1024,128]{2,1,0:T(8,128)(2,1)S(1)}, u32[]{:S(2)}, u32[]{:S(2)}) %collective-permute-start.19) | collective-permute-done | bytes 262176 | tf_op jit(solution)/shard_map/ppermute | solution.py:560
  174.3 12.3 %attention_back.3 = bf16[4,256,768]{2,1,0:T(8,128)(2,1)S(1)} custom-call(s32[10]{0:T(128)S(1)} %pad_add_fusion.info_ref, bf16[256,1536]{1,0:T(8,128)(2,1)S(1)} %copy-done.2, bf16[256,1536]{1,0:T(8,128)(2,1)S(1)} %collective-permute-done.refs_1_, bf16[256,768]{1,0:T(8,128)(2,1)} %collective-permute-done.4.refs_2_, ...), custom_call_target="tpu_custom_call" | custom-call | flops 1500000000 | bytes 1024 | tf_op jit(solution)/shard_map/attention_back/pallas_call | solution.py:334
  187.2 5.2 %collective-permute-start.20 = (bf16[1,1024,128]{2,1,0:T(8,128)(2,1)S(1)}, bf16[1,1024,128]{2,1,0:T(8,128)(2,1)S(1)}, u32[]{:S(2)}, u32[]{:S(2)}) collective-permute-start(bf16[1,1024,128]{2,1,0:T(8,128)(2,1)S(1)} %get-tuple-element.136), channel_id=1, source_target_pairs={{0,16},{4,20},{8,24},{12,28},{16,0},{20,4},{24,8},{28,12},{1,17},{... | collective-permute-start | bytes 786440 | tf_op jit(solution)/shard_map/ppermute | solution.py:560
  192.5 11.3 %collective-permute-done.20.got_ref = bf16[1,1024,128]{2,1,0:T(8,128)(2,1)S(1)} collective-permute-done((bf16[1,1024,128]{2,1,0:T(8,128)(2,1)S(1)}, bf16[1,1024,128]{2,1,0:T(8,128)(2,1)S(1)}, u32[]{:S(2)}, u32[]{:S(2)}) %collective-permute-start.20) | collective-permute-done | bytes 262176 | tf_op jit(solution)/shard_map/ppermute | solution.py:560
  205.2 2.7 %collective-permute-start.28 = (bf16[1,1024,128]{2,1,0:T(8,128)(2,1)S(1)}, bf16[1,1024,128]{2,1,0:T(8,128)(2,1)S(1)}, u32[]{:S(2)}, u32[]{:S(2)}) collective-permute-start(bf16[1,1024,128]{2,1,0:T(8,128)(2,1)S(1)} %get-tuple-element.149), channel_id=1, source_target_pairs={{0,16},{4,20},{8,24},{12,28},{16,0},{20,4},{24,8},{28,12},{1,17},{... | collective-permute-start | bytes 786440 | tf_op jit(solution)/shard_map/ppermute | solution.py:560
  208.0 8.5 %collective-permute-done.26.refs_7_ = bf16[256,768]{1,0:T(8,128)(2,1)S(1)} collective-permute-done((bf16[256,768]{1,0:T(8,128)(2,1)S(1)}, bf16[256,768]{1,0:T(8,128)(2,1)S(1)}, u32[]{:S(2)}, u32[]{:S(2)}) %collective-permute-start.26) | collective-permute-done | bytes 393248 | tf_op jit(solution)/shard_map/ppermute | solution.py:557
  216.4 7.0 %collective-permute-done.27.got_low.got_high = bf16[2,1024,128]{2,1,0:T(8,128)(2,1)S(1)} collective-permute-done((bf16[2,1024,128]{2,1,0:T(8,128)(2,1)S(1)}, bf16[2,1024,128]{2,1,0:T(8,128)(2,1)S(1)}, u32[]{:S(2)}, u32[]{:S(2)}) %collective-permute-start.27) | collective-permute-done | bytes 524320 | tf_op jit(solution)/shard_map/ppermute | solution.py:560
  224.8 2.8 %unpack.1 = (bf16[256,4096]{1,0:T(8,128)(2,1)}, bf16[256,1024]{1,0:T(8,128)(2,1)}, bf16[256,1024]{1,0:T(8,128)(2,1)}) custom-call(s32[10]{0:T(128)S(1)} %pad_add_fusion.info_ref, bf16[256,768]{1,0:T(8,128)(2,1)S(1)} %get-tuple-element.161.refs_0_, bf16[256,768]{1,0:T(8,128)(2,1)S(1)} %get-tuple-element.179.refs_1_, ...), custom_call_target="tpu_custom_call" | custom-call | flops 200000000 | bytes 1024 | tf_op jit(solution)/shard_map/unpack/pallas_call | solution.py:142
  227.5 8.1 %collective-permute-done.30.got_ref = bf16[1,1024,128]{2,1,0:T(8,128)(2,1)S(1)} collective-permute-done((bf16[1,1024,128]{2,1,0:T(8,128)(2,1)S(1)}, bf16[1,1024,128]{2,1,0:T(8,128)(2,1)S(1)}, u32[]{:S(2)}, u32[]{:S(2)}) %collective-permute-start.30) | collective-permute-done | bytes 262176 | tf_op jit(solution)/shard_map/ppermute | solution.py:560
  (92 shorter events, 31.1 us)
Async XLA Ops:
  2.7 12.2 %collective-permute-start.2 = (bf16[256,768]{1,0:T(8,128)(2,1)}, bf16[256,768]{1,0:T(8,128)(2,1)S(1)}, u32[]{:S(2)}, u32[]{:S(2)}) collective-permute-start(bf16[256,768]{1,0:T(8,128)(2,1)} %get-tuple-element.94), channel_id=1, source_target_pairs={{0,3},{1,2},{2,1},{3,0},{4,7},{5,6},{6,5},{7,4},{8,11},{9,10},{10,... | collective-permute-start | bytes 1179656 | tf_op jit(solution)/shard_map/ppermute | solution.py:557
  5.1 18.3 %collective-permute-start.1 = (bf16[256,768]{1,0:T(8,128)(2,1)}, bf16[256,768]{1,0:T(8,128)(2,1)S(1)}, u32[]{:S(2)}, u32[]{:S(2)}) collective-permute-start(bf16[256,768]{1,0:T(8,128)(2,1)} %get-tuple-element.87), channel_id=1, source_target_pairs={{0,2},{1,3},{2,0},{3,1},{4,6},{5,7},{6,4},{7,5},{8,10},{9,11},{10,... | collective-permute-start | bytes 1179656 | tf_op jit(solution)/shard_map/ppermute | solution.py:557
  24.2 17.4 %collective-permute-start.3 = (bf16[256,4096]{1,0:T(8,128)(2,1)S(1)}, bf16[256,4096]{1,0:T(8,128)(2,1)}, u32[]{:S(2)}, u32[]{:S(2)}) collective-permute-start(bf16[256,4096]{1,0:T(8,128)(2,1)S(1)} %bitcast.27), channel_id=1, source_target_pairs={{0,1},{1,0},{2,3},{3,2},{4,5},{5,4},{6,7},{7,6},{8,9},{9,8},{10,11... | collective-permute-start | bytes 6291464 | tf_op jit(solution)/shard_map/ppermute | solution.py:557
  24.2 5.1 %collective-permute-start = (bf16[256,1536]{1,0:T(8,128)(2,1)}, bf16[256,1536]{1,0:T(8,128)(2,1)S(1)}, u32[]{:S(2)}, u32[]{:S(2)}) collective-permute-start(bf16[256,1536]{1,0:T(8,128)(2,1)} %get-tuple-element.93), channel_id=1, source_target_pairs={{0,1},{1,0},{2,3},{3,2},{4,5},{5,4},{6,7},{7,6},{8,9},{9,8},{10,11... | collective-permute-start | bytes 2359304 | tf_op jit(solution)/shard_map/ppermute | solution.py:557
  24.7 41.4 %collective-permute-start.6 = (bf16[256,1024]{1,0:T(8,128)(2,1)}, bf16[256,1024]{1,0:T(8,128)(2,1)S(1)}, u32[]{:S(2)}, u32[]{:S(2)}) collective-permute-start(bf16[256,1024]{1,0:T(8,128)(2,1)} %get-tuple-element.103), channel_id=1, source_target_pairs={{0,2},{1,3},{2,0},{3,1},{4,6},{5,7},{6,4},{7,5},{8,10},{9,11},{10,... | collective-permute-start | bytes 1572872 | tf_op jit(solution)/shard_map/ppermute | solution.py:557
  27.0 21.5 %collective-permute-start.4 = (bf16[256,768]{1,0:T(8,128)(2,1)}, bf16[256,768]{1,0:T(8,128)(2,1)}, u32[]{:S(2)}, u32[]{:S(2)}) collective-permute-start(bf16[256,768]{1,0:T(8,128)(2,1)} %get-tuple-element.98), channel_id=1, source_target_pairs={{0,2},{1,3},{2,0},{3,1},{4,6},{5,7},{6,4},{7,5},{8,10},{9,11},{10,... | collective-permute-start | bytes 1179656 | tf_op jit(solution)/shard_map/ppermute | solution.py:557
  27.1 28.8 %collective-permute-start.5 = (bf16[256,768]{1,0:T(8,128)(2,1)}, bf16[256,768]{1,0:T(8,128)(2,1)}, u32[]{:S(2)}, u32[]{:S(2)}) collective-permute-start(bf16[256,768]{1,0:T(8,128)(2,1)} %get-tuple-element.99), channel_id=1, source_target_pairs={{0,3},{1,2},{2,1},{3,0},{4,7},{5,6},{6,5},{7,4},{8,11},{9,10},{10,... | collective-permute-start | bytes 1179656 | tf_op jit(solution)/shard_map/ppermute | solution.py:557
  41.6 25.0 %copy-start.12 = (bf16[256,1024]{1,0:T(8,128)(2,1)S(1)}, bf16[256,1024]{1,0:T(8,128)(2,1)}, u32[]{:S(2)}) copy-start(bf16[256,1024]{1,0:T(8,128)(2,1)} %get-tuple-element.108) | copy-start | bytes 1572868
  66.1 2.2 collective-permute-start.7
  66.6 14.0 %collective-permute-start.8 = (bf16[256,1024]{1,0:T(8,128)(2,1)S(1)}, bf16[256,1024]{1,0:T(8,128)(2,1)S(1)}, u32[]{:S(2)}, u32[]{:S(2)}) collective-permute-start(bf16[256,1024]{1,0:T(8,128)(2,1)S(1)} %copy-done.12), channel_id=1, source_target_pairs={{0,2},{1,3},{2,0},{3,1},{4,6},{5,7},{6,4},{7,5},{8,10},{9,11},{10,... | collective-permute-start | bytes 1572872 | tf_op jit(solution)/shard_map/ppermute | solution.py:557
  80.5 4.6 %collective-permute-start.9 = (bf16[256,1024]{1,0:T(8,128)(2,1)S(1)}, bf16[256,1024]{1,0:T(8,128)(2,1)S(1)}, u32[]{:S(2)}, u32[]{:S(2)}) collective-permute-start(bf16[256,1024]{1,0:T(8,128)(2,1)S(1)} %collective-permute-done.8.refs_6_.refs_5_), channel_id=1, source_target_pairs={{0,1},{1,0},{2,3},{3,2},{4,5},{5,4},{6,7},{7,6},{8,9},{9,8},{10,11... | collective-permute-start | bytes 1572872 | tf_op jit(solution)/shard_map/ppermute | solution.py:557
  80.6 14.3 %collective-permute-start.10 = (bf16[256,1024]{1,0:T(8,128)(2,1)S(1)}, bf16[256,1024]{1,0:T(8,128)(2,1)S(1)}, u32[]{:S(2)}, u32[]{:S(2)}) collective-permute-start(bf16[256,1024]{1,0:T(8,128)(2,1)S(1)} %copy-done.11), channel_id=1, source_target_pairs={{0,2},{1,3},{2,0},{3,1},{4,6},{5,7},{6,4},{7,5},{8,10},{9,11},{10,... | collective-permute-start | bytes 1572872 | tf_op jit(solution)/shard_map/ppermute | solution.py:557
  82.3 26.3 %collective-permute-start.12 = (bf16[4,1024,128]{2,1,0:T(8,128)(2,1)S(1)}, bf16[4,1024,128]{2,1,0:T(8,128)(2,1)S(1)}, u32[]{:S(2)}, u32[]{:S(2)}) collective-permute-start(bf16[4,1024,128]{2,1,0:T(8,128)(2,1)S(1)} %get-tuple-element.105), channel_id=1, source_target_pairs={{0,8},{4,12},{8,0},{12,4},{16,24},{20,28},{24,16},{28,20},{1,9},{5... | collective-permute-start | bytes 3145736 | tf_op jit(solution)/shard_map/ppermute | solution.py:560
  94.9 4.5 %collective-permute-start.11 = (bf16[256,1024]{1,0:T(8,128)(2,1)S(1)}, bf16[256,1024]{1,0:T(8,128)(2,1)S(1)}, u32[]{:S(2)}, u32[]{:S(2)}) collective-permute-start(bf16[256,1024]{1,0:T(8,128)(2,1)S(1)} %collective-permute-done.10.refs_6_.refs_7_), channel_id=1, source_target_pairs={{0,1},{1,0},{2,3},{3,2},{4,5},{5,4},{6,7},{7,6},{8,9},{9,8},{10,11... | collective-permute-start | bytes 1572872 | tf_op jit(solution)/shard_map/ppermute | solution.py:557
  94.9 23.4 %collective-permute-start.13 = (bf16[256,1024]{1,0:T(8,128)(2,1)S(1)}, bf16[256,1024]{1,0:T(8,128)(2,1)S(1)}, u32[]{:S(2)}, u32[]{:S(2)}) collective-permute-start(bf16[256,1024]{1,0:T(8,128)(2,1)S(1)} %copy-done.10), channel_id=1, source_target_pairs={{0,2},{1,3},{2,0},{3,1},{4,6},{5,7},{6,4},{7,5},{8,10},{9,11},{10,... | collective-permute-start | bytes 1572872 | tf_op jit(solution)/shard_map/ppermute | solution.py:557
  96.6 32.1 %collective-permute-start.15 = (bf16[4,1024,128]{2,1,0:T(8,128)(2,1)S(1)}, bf16[4,1024,128]{2,1,0:T(8,128)(2,1)S(1)}, u32[]{:S(2)}, u32[]{:S(2)}) collective-permute-start(bf16[4,1024,128]{2,1,0:T(8,128)(2,1)S(1)} %get-tuple-element.110), channel_id=1, source_target_pairs={{0,4},{4,0},{8,12},{12,8},{16,20},{20,16},{24,28},{28,24},{1,5},{5... | collective-permute-start | bytes 3145736 | tf_op jit(solution)/shard_map/ppermute | solution.py:560
  118.3 5.7 %collective-permute-start.14 = (bf16[256,1024]{1,0:T(8,128)(2,1)S(1)}, bf16[256,1024]{1,0:T(8,128)(2,1)S(1)}, u32[]{:S(2)}, u32[]{:S(2)}) collective-permute-start(bf16[256,1024]{1,0:T(8,128)(2,1)S(1)} %collective-permute-done.13.refs_6_.refs_3_), channel_id=1, source_target_pairs={{0,1},{1,0},{2,3},{3,2},{4,5},{5,4},{6,7},{7,6},{8,9},{9,8},{10,11... | collective-permute-start | bytes 1572872 | tf_op jit(solution)/shard_map/ppermute | solution.py:557
  118.4 34.6 %collective-permute-start.18 = (bf16[4,1024,128]{2,1,0:T(8,128)(2,1)S(1)}, bf16[4,1024,128]{2,1,0:T(8,128)(2,1)S(1)}, u32[]{:S(2)}, u32[]{:S(2)}) collective-permute-start(bf16[4,1024,128]{2,1,0:T(8,128)(2,1)S(1)} %get-tuple-element.118), channel_id=1, source_target_pairs={{0,4},{4,0},{8,12},{12,8},{16,20},{20,16},{24,28},{28,24},{1,5},{5... | collective-permute-start | bytes 3145736 | tf_op jit(solution)/shard_map/ppermute | solution.py:560
  121.2 26.4 %collective-permute-start.16 = (bf16[2,1024,128]{2,1,0:T(8,128)(2,1)S(1)}, bf16[2,1024,128]{2,1,0:T(8,128)(2,1)S(1)}, u32[]{:S(2)}, u32[]{:S(2)}) collective-permute-start(bf16[2,1024,128]{2,1,0:T(8,128)(2,1)S(1)} %get-tuple-element.120), channel_id=1, source_target_pairs={{0,16},{4,20},{8,24},{12,28},{16,0},{20,4},{24,8},{28,12},{1,17},{... | collective-permute-start | bytes 1572872 | tf_op jit(solution)/shard_map/ppermute | solution.py:560
  129.0 23.8 %collective-permute-start.17 = (bf16[2,1024,128]{2,1,0:T(8,128)(2,1)S(1)}, bf16[2,1024,128]{2,1,0:T(8,128)(2,1)S(1)}, u32[]{:S(2)}, u32[]{:S(2)}) collective-permute-start(bf16[2,1024,128]{2,1,0:T(8,128)(2,1)S(1)} %get-tuple-element.129), channel_id=1, source_target_pairs={{0,8},{4,12},{8,0},{12,4},{16,24},{20,28},{24,16},{28,20},{1,9},{5... | collective-permute-start | bytes 1572872 | tf_op jit(solution)/shard_map/ppermute | solution.py:560
  129.4 75.3 %collective-permute-start.25 = (bf16[4,1024,128]{2,1,0:T(8,128)(2,1)S(1)}, bf16[4,1024,128]{2,1,0:T(8,128)(2,1)S(1)}, u32[]{:S(2)}, u32[]{:S(2)}) collective-permute-start(bf16[4,1024,128]{2,1,0:T(8,128)(2,1)S(1)} %get-tuple-element.125), channel_id=1, source_target_pairs={{0,4},{4,0},{8,12},{12,8},{16,20},{20,16},{24,28},{28,24},{1,5},{5... | collective-permute-start | bytes 3145736 | tf_op jit(solution)/shard_map/ppermute | solution.py:560
  147.6 25.8 %collective-permute-start.19 = (bf16[1,1024,128]{2,1,0:T(8,128)(2,1)S(1)}, bf16[1,1024,128]{2,1,0:T(8,128)(2,1)S(1)}, u32[]{:S(2)}, u32[]{:S(2)}) collective-permute-start(bf16[1,1024,128]{2,1,0:T(8,128)(2,1)S(1)} %get-tuple-element.134), channel_id=1, source_target_pairs={{0,4},{4,0},{8,12},{12,8},{16,20},{20,16},{24,28},{28,24},{1,5},{5... | collective-permute-start | bytes 786440 | tf_op jit(solution)/shard_map/ppermute | solution.py:560
  149.6 37.1 %collective-permute-start.22 = (bf16[256,768]{1,0:T(8,128)(2,1)S(1)}, bf16[256,768]{1,0:T(8,128)(2,1)S(1)}, u32[]{:S(2)}, u32[]{:S(2)}) collective-permute-start(bf16[256,768]{1,0:T(8,128)(2,1)S(1)} %get-tuple-element.150), channel_id=1, source_target_pairs={{0,2},{1,3},{2,0},{3,1},{4,6},{5,7},{6,4},{7,5},{8,10},{9,11},{10,... | collective-permute-start | bytes 1179656 | tf_op jit(solution)/shard_map/ppermute | solution.py:557
  152.9 33.8 %collective-permute-start.23 = (bf16[256,768]{1,0:T(8,128)(2,1)S(1)}, bf16[256,768]{1,0:T(8,128)(2,1)S(1)}, u32[]{:S(2)}, u32[]{:S(2)}) collective-permute-start(bf16[256,768]{1,0:T(8,128)(2,1)S(1)} %get-tuple-element.151), channel_id=1, source_target_pairs={{0,3},{1,2},{2,1},{3,0},{4,7},{5,6},{6,5},{7,4},{8,11},{9,10},{10,... | collective-permute-start | bytes 1179656 | tf_op jit(solution)/shard_map/ppermute | solution.py:557
  153.2 51.4 %collective-permute-start.21 = (bf16[2,1024,128]{2,1,0:T(8,128)(2,1)S(1)}, bf16[2,1024,128]{2,1,0:T(8,128)(2,1)S(1)}, u32[]{:S(2)}, u32[]{:S(2)}) collective-permute-start(bf16[2,1024,128]{2,1,0:T(8,128)(2,1)S(1)} %get-tuple-element.141), channel_id=1, source_target_pairs={{0,8},{4,12},{8,0},{12,4},{16,24},{20,28},{24,16},{28,20},{1,9},{5... | collective-permute-start | bytes 1572872 | tf_op jit(solution)/shard_map/ppermute | solution.py:560
  186.7 18.1 %collective-permute-start.24 = (bf16[256,768]{1,0:T(8,128)(2,1)S(1)}, bf16[256,768]{1,0:T(8,128)(2,1)S(1)}, u32[]{:S(2)}, u32[]{:S(2)}) collective-permute-start(bf16[256,768]{1,0:T(8,128)(2,1)S(1)} %get-tuple-element.152), channel_id=1, source_target_pairs={{0,2},{1,3},{2,0},{3,1},{4,6},{5,7},{6,4},{7,5},{8,10},{9,11},{10,... | collective-permute-start | bytes 1179656 | tf_op jit(solution)/shard_map/ppermute | solution.py:557
  187.2 16.7 %collective-permute-start.20 = (bf16[1,1024,128]{2,1,0:T(8,128)(2,1)S(1)}, bf16[1,1024,128]{2,1,0:T(8,128)(2,1)S(1)}, u32[]{:S(2)}, u32[]{:S(2)}) collective-permute-start(bf16[1,1024,128]{2,1,0:T(8,128)(2,1)S(1)} %get-tuple-element.136), channel_id=1, source_target_pairs={{0,16},{4,20},{8,24},{12,28},{16,0},{20,4},{24,8},{28,12},{1,17},{... | collective-permute-start | bytes 786440 | tf_op jit(solution)/shard_map/ppermute | solution.py:560
  192.4 31.4 %collective-permute-start.29 = (bf16[512,768]{1,0:T(8,128)(2,1)S(1)}, bf16[512,768]{1,0:T(8,128)(2,1)S(1)}, u32[]{:S(2)}, u32[]{:S(2)}) collective-permute-start(bf16[512,768]{1,0:T(8,128)(2,1)S(1)} %pad_maximum_fusion), channel_id=1, source_target_pairs={{0,1},{1,0},{2,3},{3,2},{4,5},{5,4},{6,7},{7,6},{8,9},{9,8},{10,11... | collective-permute-start | bytes 2359304 | tf_op jit(solution)/shard_map/ppermute | solution.py:557
  205.0 18.4 %collective-permute-start.27 = (bf16[2,1024,128]{2,1,0:T(8,128)(2,1)S(1)}, bf16[2,1024,128]{2,1,0:T(8,128)(2,1)S(1)}, u32[]{:S(2)}, u32[]{:S(2)}) collective-permute-start(bf16[2,1024,128]{2,1,0:T(8,128)(2,1)S(1)} %get-tuple-element.155), channel_id=1, source_target_pairs={{0,8},{4,12},{8,0},{12,4},{16,24},{20,28},{24,16},{28,20},{1,9},{5... | collective-permute-start | bytes 1572872 | tf_op jit(solution)/shard_map/ppermute | solution.py:560
  205.1 11.3 %collective-permute-start.26 = (bf16[256,768]{1,0:T(8,128)(2,1)S(1)}, bf16[256,768]{1,0:T(8,128)(2,1)S(1)}, u32[]{:S(2)}, u32[]{:S(2)}) collective-permute-start(bf16[256,768]{1,0:T(8,128)(2,1)S(1)} %get-tuple-element.156), channel_id=1, source_target_pairs={{0,3},{1,2},{2,1},{3,0},{4,7},{5,6},{6,5},{7,4},{8,11},{9,10},{10,... | collective-permute-start | bytes 1179656 | tf_op jit(solution)/shard_map/ppermute | solution.py:557
  205.2 18.7 %collective-permute-start.28 = (bf16[1,1024,128]{2,1,0:T(8,128)(2,1)S(1)}, bf16[1,1024,128]{2,1,0:T(8,128)(2,1)S(1)}, u32[]{:S(2)}, u32[]{:S(2)}) collective-permute-start(bf16[1,1024,128]{2,1,0:T(8,128)(2,1)S(1)} %get-tuple-element.149), channel_id=1, source_target_pairs={{0,16},{4,20},{8,24},{12,28},{16,0},{20,4},{24,8},{28,12},{1,17},{... | collective-permute-start | bytes 786440 | tf_op jit(solution)/shard_map/ppermute | solution.py:560
  223.5 12.2 %collective-permute-start.30 = (bf16[1,1024,128]{2,1,0:T(8,128)(2,1)S(1)}, bf16[1,1024,128]{2,1,0:T(8,128)(2,1)S(1)}, u32[]{:S(2)}, u32[]{:S(2)}) collective-permute-start(bf16[1,1024,128]{2,1,0:T(8,128)(2,1)S(1)} %get-tuple-element.158), channel_id=1, source_target_pairs={{0,16},{4,20},{8,24},{12,28},{16,0},{20,4},{24,8},{28,12},{1,17},{... | collective-permute-start | bytes 786440 | tf_op jit(solution)/shard_map/ppermute | solution.py:560
  (14 other events, 123.8 us)

commit v4 on v3

--- a/solution.py
+++ b/solution.py
@@ -264,8 +264,8 @@
             shape((parts, wide, block)),
             shape((GROUP, parts, 8, block), jnp.float32),
         ],
-        compiler_params=params(16),
-        cost_estimate=cost(1.0),
+        compiler_params=params(60),
+        cost_estimate=cost(2.5),
         name="attention",
     )(gate([info], token)[0], *[x for x, at in pieces])
 
@@ -357,8 +357,8 @@
             ],
         ),
         out_shape=shape((parts, block, cols)),
-        compiler_params=params(20),
-        cost_estimate=cost(1.5),
+        compiler_params=params(60),
+        cost_estimate=cost(1.0),
         name="attention_back",
     )(gate([info], token)[0], *[x for x, at in pieces], grads, out, lse)
 
@@ -636,13 +636,20 @@
             out_weight, near, [fars[c] for c in picked], acc, token, orders, picked, shares, width, last
         )
 
-    def send_back(gp, *tokens):
+    def send_back(gp):
         nonlocal token
         res = attention_back(info, pieces[gp], acc, outs[gp], fwd[gp][1], token, parts, docs, gp)
-        token = res
-        parted = gate([res[d] for d in range(parts)], *tokens)
-        results[gp] = parted
-        back[gp] = [parted[0], None] + [over_seq(parted[d], d) for d in far]
+        token = results[gp] = res
+        back[gp] = {d: over_seq(res[d : d + 2], d) for d in range(2, parts, 2)}
+
+    def hand_over(gp, *tokens):
+        got = gate([back[gp][d] for d in range(2, parts, 2)], *tokens)
+        mine = [results[gp][1:2]] + [x[1:2] for x in got]
+        crossed = over_seq(jnp.concatenate(mine, axis=0), 1)
+        out = [results[gp][0], crossed[0]]
+        for i, x in enumerate(got):
+            out += [x[0], crossed[1 + i]]
+        return out
 
     last = chunks - 1
     for c in range(last):
@@ -654,23 +661,22 @@
     advance(1)
     project_step([last], True)
     send_back(0)
-    for c in (0, 1, 2, 0):
+    for c in (0, 1, 2):
         advance(c)
     for gp in range(1, groups):
-        send_back(gp, *back[gp - 1][2:])
+        send_back(gp)
     advance(1)
     advance(2)
-    token = (token, back[groups - 1][2])
+    firsts = hand_over(0, token)
+    token = (token, firsts[1])
     advance(3)
-    both = over_seq(jnp.concatenate([results[gp][1] for gp in range(groups)], axis=0), 1)
-    token = (token, *back[groups - 1][2:])
+    advance(0)
+    lasts = [hand_over(gp, token) for gp in range(1, groups)]
     advance(3)
-    for gp in range(groups):
-        back[gp][1] = both[gp * rows : (gp + 1) * rows]
     for _ in bits:
         for c in range(last):
             advance(c)
-    back = [x for gp in range(groups) for x in back[gp]]
+    back = firsts + [x for group in lasts for x in group]
     grad_q, grad_k, grad_v = unpack(gate([info], token)[0], back, parts, groups)
     token = grad_q
     for _ in bits:

time: 239 us -> 235 us (0.983); the launches traced: 236 us -> 238 us
  waiting for transfers between devices: 100 us -> 64.3 us
  Pallas kernels: 93.5 us -> 120 us
  local copies, waits for them, and re-layouts: 4.94 us -> 12.6 us
  starting transfers between devices: 36.6 us -> 39.2 us
    ppermute x12, waiting for transfers between devices: 54.6 us -> 32.2 us  [over_dp(): return lax.ppermute(x, 'dp', [(i, i ^ d) for i in range(shares)])]
    ppermute x19 -> x18, waiting for transfers between devices: 45.7 us -> 32.1 us  [over_seq(): return lax.ppermute(x, 'seq', [(i, i ^ d) for i in range(parts)])]
    pallas_call x2, Pallas kernels: 23.5 us -> 34.5 us  [attention_back(): pl.pallas_call(functools.partial(backward_kernel, parts, block, docs), gr...]
    pallas_call x2, Pallas kernels: 19.4 us -> 28.2 us  [attention(): pl.pallas_call(functools.partial(forward_kernel, parts, block, docs), gri...]
    pallas_call x8, Pallas kernels: 1.23 us -> 6.52 us  [merge(): pl.pallas_call(merge_kernel, grid=(half,), in_specs=[low, high, low, high...]
    unnamed x30 -> x58, local copies, waits for them, and re-layouts: 4.68 us -> 8.11 us
    ppermute x19 -> x18, starting transfers between devices: 14 us -> 15.5 us  [over_seq(): return lax.ppermute(x, 'seq', [(i, i ^ d) for i in range(parts)])]
  transfers between devices with their start and end apart: 31 -> 30, of which waited for: 15 -> 9; matrix products, arithmetic and copies ran while one was open for 0% -> 2% of each run, Pallas kernels for 38% -> 49%
where the time goes in v4:
time: 235 us; the launch traced here: 238 us
  Pallas kernels  120 us (51%)
  waiting for transfers between devices  64.3 us (27%)
  starting transfers between devices  39.2 us (17%)
  local copies, waits for them, and re-layouts  12.6 us (5%)
    pallas_call x2, Pallas kernels, attention_back(): pl.pallas_call(functools.partial(backward_kernel, parts, block, docs), gr...  34.5 us
    ppermute x12, waiting for transfers between devices, over_dp(): return lax.ppermute(x, 'dp', [(i, i ^ d) for i in range(shares)])  32.2 us
    ppermute x18, waiting for transfers between devices, over_seq(): return lax.ppermute(x, 'seq', [(i, i ^ d) for i in range(parts)])  32.1 us
    pallas_call x2, Pallas kernels, attention(): pl.pallas_call(functools.partial(forward_kernel, parts, block, docs), gri...  28.2 us
    ppermute x12, starting transfers between devices, over_dp(): return lax.ppermute(x, 'dp', [(i, i ^ d) for i in range(shares)])  23.8 us
    pallas_call x4, Pallas kernels, weight_terms(): pl.pallas_call(functools.partial(weight_kernel, parts, groups, width, ord...  21.1 us
    ppermute x18, starting transfers between devices, over_seq(): return lax.ppermute(x, 'seq', [(i, i ^ d) for i in range(parts)])  15.5 us
    pallas_call x2, Pallas kernels, project(): pl.pallas_call(functools.partial(project_kernel, parts, shares, width, le...  14.6 us
  transfers between devices with their start and end apart: 30, of which 9 were waited for; matrix products, arithmetic and copies ran while one was open for 2% of the time, Pallas kernels for 49%

profile of v4, /device:TPU:0, one launch (start us, length us, event | category | flops | bytes accessed | tf_op | source)
XLA Modules:
  0.0 238.1 jit_solution(15146348329602532427)
XLA Ops:
  0.6 2.1 pack.2
  2.7 2.4 %collective-permute-start.2 = (bf16[256,768]{1,0:T(8,128)(2,1)}, bf16[256,768]{1,0:T(8,128)(2,1)S(1)}, u32[]{:S(2)}, u32[]{:S(2)}) collective-permute-start(bf16[256,768]{1,0:T(8,128)(2,1)} %get-tuple-element.88), channel_id=1, source_target_pairs={{0,3},{1,2},{2,1},{3,0},{4,7},{5,6},{6,5},{7,4},{8,11},{9,10},{10,... | collective-permute-start | bytes 1179656 | tf_op jit(solution)/shard_map/ppermute | solution.py:557
  5.8 3.0 %pack.3 = (bf16[256,1536]{1,0:T(8,128)(2,1)}, bf16[256,1536]{1,0:T(8,128)(2,1)}, bf16[256,768]{1,0:T(8,128)(2,1)}, bf16[256,768]{1,0:T(8,128)(2,1)}) custom-call(s32[1]{0:T(128)} %bitcast.me_ref, bf16[256,4096]{1,0:T(8,128)(2,1)} %bitcast.42, bf16[256,1024]{1,0:T(8,128)(2,1)} %bitcast.50, bf16[256,1024]{1,0:T(8,128)(2,1)} %bitcast.58, ...), custom_call_target="tpu_custom_call" | custom-call | flops 200000000 | bytes 1024 | tf_op jit(solution)/shard_map/pack/pallas_call | solution.py:79
  8.8 4.0 %pack_chunks.1 = (bf16[256,1024]{1,0:T(8,128)(2,1)}, bf16[256,1024]{1,0:T(8,128)(2,1)}, bf16[256,1024]{1,0:T(8,128)(2,1)}, bf16[256,1024]{1,0:T(8,128)(2,1)}) custom-call(bf16[256,4096]{1,0:T(8,128)(2,1)} %bitcast.26), custom_call_target="tpu_custom_call" | custom-call | flops 200000000 | bytes 1024 | tf_op jit(solution)/shard_map/pack_chunks/pallas_call | solution.py:110
  12.8 2.1 collective-permute-done.2.refs_3_
  14.9 8.5 %collective-permute-done.1.refs_2_ = bf16[256,768]{1,0:T(8,128)(2,1)S(1)} collective-permute-done((bf16[256,768]{1,0:T(8,128)(2,1)}, bf16[256,768]{1,0:T(8,128)(2,1)S(1)}, u32[]{:S(2)}, u32[]{:S(2)}) %collective-permute-start.1) | collective-permute-done | bytes 393248 | tf_op jit(solution)/shard_map/ppermute | solution.py:557
  24.2 2.4 collective-permute-start.4
  30.0 14.1 %attention.2 = (bf16[4,512,256]{2,1,0:T(8,128)(2,1)}, f32[4,4,8,256]{3,2,1,0:T(8,128)}) custom-call(s32[10]{0:T(128)} %pad_add_fusion.info_ref, bf16[256,1536]{1,0:T(8,128)(2,1)} %get-tuple-element.83.refs_0_, bf16[256,1536]{1,0:T(8,128)(2,1)} %copy-done.20, bf16[256,768]{1,0:T(8,128)(2,1)} %copy-done.23, bf16[256,768]{1,0:T(8,128)(2,1)} %copy-done.22), custom_call_target="tpu_custom_call" | custom-call | flops 2500000000 | bytes 1024 | tf_op jit(solution)/shard_map/attention/pallas_call | solution.py:242
  44.8 14.1 %attention.3 = (bf16[4,512,256]{2,1,0:T(8,128)(2,1)}, f32[4,4,8,256]{3,2,1,0:T(8,128)}) custom-call(s32[10]{0:T(128)} %pad_add_fusion.info_ref, bf16[256,1536]{1,0:T(8,128)(2,1)} %get-tuple-element.83.refs_0_, bf16[256,1536]{1,0:T(8,128)(2,1)} %copy-done.20, bf16[256,768]{1,0:T(8,128)(2,1)} %collective-permute-done.4.refs_2_, ...), custom_call_target="tpu_custom_call" | custom-call | flops 2500000000 | bytes 1024 | tf_op jit(solution)/shard_map/attention/pallas_call | solution.py:242
  62.4 4.8 %weight_terms.4 = (f32[4,1024,128]{2,1,0:T(8,128)S(1)}, bf16[4,1024,128]{2,1,0:T(8,128)(2,1)S(1)}) custom-call(s32[10]{0:T(128)S(1)} %copy-done.16, bf16[4,512,256]{2,1,0:T(8,128)(2,1)S(1)} %copy-done.3, bf16[4,512,256]{2,1,0:T(8,128)(2,1)S(1)} %copy-done.1, bf16[256,4096]{1,0:T(8,128)(2,1)S(1)} %bitcast.28, ...), custom_call_target="tpu_custom_call" | custom-call | flops 300000000 | bytes 1024 | tf_op jit(solution)/shard_map/weight_terms/pallas_call | solution.py:421
  67.3 6.3 %collective-permute-done.8.refs_6_.refs_5_ = bf16[256,1024]{1,0:T(8,128)(2,1)S(1)} collective-permute-done((bf16[256,1024]{1,0:T(8,128)(2,1)}, bf16[256,1024]{1,0:T(8,128)(2,1)S(1)}, u32[]{:S(2)}, u32[]{:S(2)}) %collective-permute-start.8) | collective-permute-done | bytes 524320 | tf_op jit(solution)/shard_map/ppermute | solution.py:557
  75.7 5.1 %weight_terms.5 = (f32[4,1024,128]{2,1,0:T(8,128)S(1)}, bf16[4,1024,128]{2,1,0:T(8,128)(2,1)S(1)}) custom-call(s32[10]{0:T(128)S(1)} %copy-done.16, bf16[4,512,256]{2,1,0:T(8,128)(2,1)S(1)} %copy-done.3, bf16[4,512,256]{2,1,0:T(8,128)(2,1)S(1)} %copy-done.1, bf16[256,4096]{1,0:T(8,128)(2,1)S(1)} %bitcast.30, ...), custom_call_target="tpu_custom_call" | custom-call | flops 300000000 | bytes 1024 | tf_op jit(solution)/shard_map/weight_terms/pallas_call | solution.py:421
  80.8 7.1 %collective-permute-done.10.refs_6_.refs_7_ = bf16[256,1024]{1,0:T(8,128)(2,1)S(1)} collective-permute-done((bf16[256,1024]{1,0:T(8,128)(2,1)S(1)}, bf16[256,1024]{1,0:T(8,128)(2,1)S(1)}, u32[]{:S(2)}, u32[]{:S(2)}) %collective-permute-start.10) | collective-permute-done | bytes 524320 | tf_op jit(solution)/shard_map/ppermute | solution.py:557
  89.7 6.3 %collective-permute-start.15 = (bf16[4,1024,128]{2,1,0:T(8,128)(2,1)S(1)}, bf16[4,1024,128]{2,1,0:T(8,128)(2,1)S(1)}, u32[]{:S(2)}, u32[]{:S(2)}) collective-permute-start(bf16[4,1024,128]{2,1,0:T(8,128)(2,1)S(1)} %get-tuple-element.104), channel_id=1, source_target_pairs={{0,4},{4,0},{8,12},{12,8},{16,20},{20,16},{24,28},{28,24},{1,5},{5... | collective-permute-start | bytes 3145736 | tf_op jit(solution)/shard_map/ppermute | solution.py:560
  96.1 5.6 %weight_terms.6 = (f32[4,1024,128]{2,1,0:T(8,128)S(1)}, bf16[4,1024,128]{2,1,0:T(8,128)(2,1)}) custom-call(s32[10]{0:T(128)S(1)} %copy-done.16, bf16[4,512,256]{2,1,0:T(8,128)(2,1)S(1)} %copy-done.3, bf16[4,512,256]{2,1,0:T(8,128)(2,1)S(1)} %copy-done.1, bf16[256,4096]{1,0:T(8,128)(2,1)S(1)} %bitcast.32, ...), custom_call_target="tpu_custom_call" | custom-call | flops 300000000 | bytes 1024 | tf_op jit(solution)/shard_map/weight_terms/pallas_call | solution.py:421
  104.9 9.5 %project.2.refs_5_ = f32[4,256,1024]{2,1,0:T(8,128)S(1)} custom-call(bf16[1024,4096]{1,0:T(8,128)(2,1)S(1)} %bitcast.39, bf16[256,4096]{1,0:T(8,128)(2,1)S(1)} %bitcast.34, bf16[256,4096]{1,0:T(8,128)(2,1)} %collective-permute-done.3.refs_3_.refs_5_.refs_2_, bf16[256,1024]{1,0:T(8,128)(2,1)S(1)} %collective-permute-done.6.refs_6_.refs_3_, ...), custom_call_target="tpu_custom_call" | custom-call | flops 500000000 | bytes 1024 | tf_op jit(solution)/shard_map/project/pallas_call | solution.py:520
  114.5 4.0 %collective-permute-start.18 = (bf16[4,1024,128]{2,1,0:T(8,128)(2,1)}, bf16[4,1024,128]{2,1,0:T(8,128)(2,1)}, u32[]{:S(2)}, u32[]{:S(2)}) collective-permute-start(bf16[4,1024,128]{2,1,0:T(8,128)(2,1)} %get-tuple-element.112), channel_id=1, source_target_pairs={{0,4},{4,0},{8,12},{12,8},{16,20},{20,16},{24,28},{28,24},{1,5},{5... | collective-permute-start | bytes 3145736 | tf_op jit(solution)/shard_map/ppermute | solution.py:560
  118.5 5.5 %weight_terms.7 = (f32[4,1024,128]{2,1,0:T(8,128)S(1)}, bf16[4,1024,128]{2,1,0:T(8,128)(2,1)}) custom-call(s32[10]{0:T(128)S(1)} %copy-done.16, bf16[4,512,256]{2,1,0:T(8,128)(2,1)S(1)} %copy-done.4, bf16[4,512,256]{2,1,0:T(8,128)(2,1)S(1)} %copy-done.2, bf16[256,4096]{1,0:T(8,128)(2,1)S(1)} %bitcast.35, ...), custom_call_target="tpu_custom_call" | custom-call | flops 300000000 | bytes 1024 | tf_op jit(solution)/shard_map/weight_terms/pallas_call | solution.py:421
  126.6 5.1 %project.3.refs_4_ = bf16[4,256,1024]{2,1,0:T(8,128)(2,1)S(1)} custom-call(bf16[1024,4096]{1,0:T(8,128)(2,1)S(1)} %bitcast.39, bf16[256,4096]{1,0:T(8,128)(2,1)S(1)} %bitcast.37, bf16[256,4096]{1,0:T(8,128)(2,1)} %collective-permute-done.3.refs_3_.refs_5_.refs_2_, bf16[256,1024]{1,0:T(8,128)(2,1)S(1)} %collective-permute-done.13.refs_6_.refs_3_, ...), custom_call_target="tpu_custom_call" | custom-call | flops 500000000 | bytes 1024 | tf_op jit(solution)/shard_map/project/pallas_call | solution.py:520
  133.0 17.3 %attention_back.2 = bf16[4,256,768]{2,1,0:T(8,128)(2,1)} custom-call(s32[10]{0:T(128)} %pad_add_fusion.info_ref, bf16[256,1536]{1,0:T(8,128)(2,1)} %get-tuple-element.83.refs_0_, bf16[256,1536]{1,0:T(8,128)(2,1)} %copy-done.20, bf16[256,768]{1,0:T(8,128)(2,1)} %copy-done.23, bf16[256,768]{1,0:T(8,128)(2,1)} %copy-done.22, bf16[4,256,1024]{2,1,0:T(8,128)(2,1)} %copy-done.5, ...), custom_call_target="tpu_custom_call" | custom-call | flops 1000000000 | bytes 1024 | tf_op jit(solution)/shard_map/attention_back/pallas_call | solution.py:334
  150.3 2.1 slice.57
  153.1 2.1 merge.11
  155.2 2.2 merge.12
  157.8 4.2 %collective-permute-start.23 = (bf16[4,1024,128]{2,1,0:T(8,128)(2,1)}, bf16[4,1024,128]{2,1,0:T(8,128)(2,1)S(1)}, u32[]{:S(2)}, u32[]{:S(2)}) collective-permute-start(bf16[4,1024,128]{2,1,0:T(8,128)(2,1)} %get-tuple-element.119), channel_id=1, source_target_pairs={{0,4},{4,0},{8,12},{12,8},{16,20},{20,16},{24,28},{28,24},{1,5},{5... | collective-permute-start | bytes 3145736 | tf_op jit(solution)/shard_map/ppermute | solution.py:560
  162.8 17.2 %attention_back.3 = bf16[4,256,768]{2,1,0:T(8,128)(2,1)} custom-call(s32[10]{0:T(128)} %pad_add_fusion.info_ref, bf16[256,1536]{1,0:T(8,128)(2,1)} %get-tuple-element.83.refs_0_, bf16[256,1536]{1,0:T(8,128)(2,1)} %copy-done.20, bf16[256,768]{1,0:T(8,128)(2,1)} %collective-permute-done.4.refs_2_, bf16[256,768]{1,0:T(8,128)(2,1)} %collective-permute-done.5.refs_3_, ...), custom_call_target="tpu_custom_call" | custom-call | flops 1000000000 | bytes 1024 | tf_op jit(solution)/shard_map/attention_back/pallas_call | solution.py:334
  184.3 3.4 %collective-permute-start.24 = (bf16[1,1024,128]{2,1,0:T(8,128)(2,1)S(1)}, bf16[1,1024,128]{2,1,0:T(8,128)(2,1)S(1)}, u32[]{:S(2)}, u32[]{:S(2)}) collective-permute-start(bf16[1,1024,128]{2,1,0:T(8,128)(2,1)S(1)} %get-tuple-element.128), channel_id=1, source_target_pairs={{0,4},{4,0},{8,12},{12,8},{16,20},{20,16},{24,28},{28,24},{1,5},{5... | collective-permute-start | bytes 786440 | tf_op jit(solution)/shard_map/ppermute | solution.py:560
  188.2 6.1 %collective-permute-done.24.got_ref = bf16[1,1024,128]{2,1,0:T(8,128)(2,1)S(1)} collective-permute-done((bf16[1,1024,128]{2,1,0:T(8,128)(2,1)S(1)}, bf16[1,1024,128]{2,1,0:T(8,128)(2,1)S(1)}, u32[]{:S(2)}, u32[]{:S(2)}) %collective-permute-start.24) | collective-permute-done | bytes 262176 | tf_op jit(solution)/shard_map/ppermute | solution.py:560
  195.1 7.5 %collective-permute-done.27 = bf16[2,256,768]{2,1,0:T(8,128)(2,1)S(1)} collective-permute-done((bf16[2,256,768]{2,1,0:T(8,128)(2,1)S(1)}, bf16[2,256,768]{2,1,0:T(8,128)(2,1)S(1)}, u32[]{:S(2)}, u32[]{:S(2)}) %collective-permute-start.27) | collective-permute-done | bytes 786464 | tf_op jit(solution)/shard_map/ppermute | solution.py:557
  203.4 2.9 %collective-permute-start.26 = (bf16[1,1024,128]{2,1,0:T(8,128)(2,1)S(1)}, bf16[1,1024,128]{2,1,0:T(8,128)(2,1)S(1)}, u32[]{:S(2)}, u32[]{:S(2)}) collective-permute-start(bf16[1,1024,128]{2,1,0:T(8,128)(2,1)S(1)} %get-tuple-element.141), channel_id=1, source_target_pairs={{0,16},{4,20},{8,24},{12,28},{16,0},{20,4},{24,8},{28,12},{1,17},{... | collective-permute-start | bytes 786440 | tf_op jit(solution)/shard_map/ppermute | solution.py:560
  206.4 16.4 %collective-permute-done.25.got_low.got_high = bf16[2,1024,128]{2,1,0:T(8,128)(2,1)S(1)} collective-permute-done((bf16[2,1024,128]{2,1,0:T(8,128)(2,1)S(1)}, bf16[2,1024,128]{2,1,0:T(8,128)(2,1)S(1)}, u32[]{:S(2)}, u32[]{:S(2)}) %collective-permute-start.25) | collective-permute-done | bytes 524320 | tf_op jit(solution)/shard_map/ppermute | solution.py:560
  224.8 2.8 %unpack.1 = (bf16[256,4096]{1,0:T(8,128)(2,1)}, bf16[256,1024]{1,0:T(8,128)(2,1)}, bf16[256,1024]{1,0:T(8,128)(2,1)}) custom-call(s32[10]{0:T(128)S(1)} %copy-done.17, bf16[256,768]{1,0:T(8,128)(2,1)S(1)} %get-tuple-element.160.refs_0_, bf16[256,768]{1,0:T(8,128)(2,1)S(1)} %get-tuple-element.167.refs_1_, bf16[256,768]{1,0:T(8,128)(2,1)S(1)} %get-tuple-element.168.refs_2_, ...), custom_call_target="tpu_custom_call" | custom-call | flops 200000000 | bytes 1024 | tf_op jit(solution)/shard_map/unpack/pallas_call | solution.py:142
  227.6 9.7 %collective-permute-done.29.got_ref = bf16[1,1024,128]{2,1,0:T(8,128)(2,1)S(1)} collective-permute-done((bf16[1,1024,128]{2,1,0:T(8,128)(2,1)S(1)}, bf16[1,1024,128]{2,1,0:T(8,128)(2,1)S(1)}, u32[]{:S(2)}, u32[]{:S(2)}) %collective-permute-start.29) | collective-permute-done | bytes 262176 | tf_op jit(solution)/shard_map/ppermute | solution.py:560
  (124 shorter events, 31.1 us)
Async XLA Ops:
  2.7 12.2 %collective-permute-start.2 = (bf16[256,768]{1,0:T(8,128)(2,1)}, bf16[256,768]{1,0:T(8,128)(2,1)S(1)}, u32[]{:S(2)}, u32[]{:S(2)}) collective-permute-start(bf16[256,768]{1,0:T(8,128)(2,1)} %get-tuple-element.88), channel_id=1, source_target_pairs={{0,3},{1,2},{2,1},{3,0},{4,7},{5,6},{6,5},{7,4},{8,11},{9,10},{10,... | collective-permute-start | bytes 1179656 | tf_op jit(solution)/shard_map/ppermute | solution.py:557
  5.1 18.3 %collective-permute-start.1 = (bf16[256,768]{1,0:T(8,128)(2,1)}, bf16[256,768]{1,0:T(8,128)(2,1)S(1)}, u32[]{:S(2)}, u32[]{:S(2)}) collective-permute-start(bf16[256,768]{1,0:T(8,128)(2,1)} %get-tuple-element.81), channel_id=1, source_target_pairs={{0,2},{1,3},{2,0},{3,1},{4,6},{5,7},{6,4},{7,5},{8,10},{9,11},{10,... | collective-permute-start | bytes 1179656 | tf_op jit(solution)/shard_map/ppermute | solution.py:557
  8.8 19.6 %copy-start.24 = (s32[1,8]{1,0:T(1,128)S(1)}, s32[1,8]{1,0:T(1,128)}, u32[]{:S(2)}) copy-start(s32[1,8]{1,0:T(1,128)} %param.11) | copy-start | bytes 100
  23.4 20.7 %collective-permute-start.3 = (bf16[256,4096]{1,0:T(8,128)(2,1)S(1)}, bf16[256,4096]{1,0:T(8,128)(2,1)}, u32[]{:S(2)}, u32[]{:S(2)}) collective-permute-start(bf16[256,4096]{1,0:T(8,128)(2,1)S(1)} %bitcast.27), channel_id=1, source_target_pairs={{0,1},{1,0},{2,3},{3,2},{4,5},{5,4},{6,7},{7,6},{8,9},{9,8},{10,11... | collective-permute-start | bytes 6291464 | tf_op jit(solution)/shard_map/ppermute | solution.py:557
  24.2 4.9 %collective-permute-start = (bf16[256,1536]{1,0:T(8,128)(2,1)}, bf16[256,1536]{1,0:T(8,128)(2,1)S(1)}, u32[]{:S(2)}, u32[]{:S(2)}) collective-permute-start(bf16[256,1536]{1,0:T(8,128)(2,1)} %get-tuple-element.87), channel_id=1, source_target_pairs={{0,1},{1,0},{2,3},{3,2},{4,5},{5,4},{6,7},{7,6},{8,9},{9,8},{10,11... | collective-permute-start | bytes 2359304 | tf_op jit(solution)/shard_map/ppermute | solution.py:557
  24.2 19.9 %collective-permute-start.4 = (bf16[256,768]{1,0:T(8,128)(2,1)}, bf16[256,768]{1,0:T(8,128)(2,1)}, u32[]{:S(2)}, u32[]{:S(2)}) collective-permute-start(bf16[256,768]{1,0:T(8,128)(2,1)} %get-tuple-element.92), channel_id=1, source_target_pairs={{0,2},{1,3},{2,0},{3,1},{4,6},{5,7},{6,4},{7,5},{8,10},{9,11},{10,... | collective-permute-start | bytes 1179656 | tf_op jit(solution)/shard_map/ppermute | solution.py:557
  26.6 18.2 %collective-permute-start.5 = (bf16[256,768]{1,0:T(8,128)(2,1)}, bf16[256,768]{1,0:T(8,128)(2,1)}, u32[]{:S(2)}, u32[]{:S(2)}) collective-permute-start(bf16[256,768]{1,0:T(8,128)(2,1)} %get-tuple-element.93), channel_id=1, source_target_pairs={{0,3},{1,2},{2,1},{3,0},{4,7},{5,6},{6,5},{7,4},{8,11},{9,10},{10,... | collective-permute-start | bytes 1179656 | tf_op jit(solution)/shard_map/ppermute | solution.py:557
  26.7 32.2 %collective-permute-start.6 = (bf16[256,1024]{1,0:T(8,128)(2,1)}, bf16[256,1024]{1,0:T(8,128)(2,1)S(1)}, u32[]{:S(2)}, u32[]{:S(2)}) collective-permute-start(bf16[256,1024]{1,0:T(8,128)(2,1)} %get-tuple-element.97), channel_id=1, source_target_pairs={{0,2},{1,3},{2,0},{3,1},{4,6},{5,7},{6,4},{7,5},{8,10},{9,11},{10,... | collective-permute-start | bytes 1572872 | tf_op jit(solution)/shard_map/ppermute | solution.py:557
  58.9 2.3 collective-permute-start.7
  59.2 14.3 %collective-permute-start.8 = (bf16[256,1024]{1,0:T(8,128)(2,1)}, bf16[256,1024]{1,0:T(8,128)(2,1)S(1)}, u32[]{:S(2)}, u32[]{:S(2)}) collective-permute-start(bf16[256,1024]{1,0:T(8,128)(2,1)} %get-tuple-element.102), channel_id=1, source_target_pairs={{0,2},{1,3},{2,0},{3,1},{4,6},{5,7},{6,4},{7,5},{8,10},{9,11},{10,... | collective-permute-start | bytes 1572872 | tf_op jit(solution)/shard_map/ppermute | solution.py:557
  73.6 2.1 collective-permute-start.9
  73.6 14.3 %collective-permute-start.10 = (bf16[256,1024]{1,0:T(8,128)(2,1)S(1)}, bf16[256,1024]{1,0:T(8,128)(2,1)S(1)}, u32[]{:S(2)}, u32[]{:S(2)}) collective-permute-start(bf16[256,1024]{1,0:T(8,128)(2,1)S(1)} %copy-done.26), channel_id=1, source_target_pairs={{0,2},{1,3},{2,0},{3,1},{4,6},{5,7},{6,4},{7,5},{8,10},{9,11},{10,... | collective-permute-start | bytes 1572872 | tf_op jit(solution)/shard_map/ppermute | solution.py:557
  75.4 27.6 %collective-permute-start.12 = (bf16[4,1024,128]{2,1,0:T(8,128)(2,1)S(1)}, bf16[4,1024,128]{2,1,0:T(8,128)(2,1)S(1)}, u32[]{:S(2)}, u32[]{:S(2)}) collective-permute-start(bf16[4,1024,128]{2,1,0:T(8,128)(2,1)S(1)} %get-tuple-element.99), channel_id=1, source_target_pairs={{0,8},{4,12},{8,0},{12,4},{16,24},{20,28},{24,16},{28,20},{1,9},{5... | collective-permute-start | bytes 3145736 | tf_op jit(solution)/shard_map/ppermute | solution.py:560
  75.7 29.1 %slice-start = ((s8[8388608]{0:T(1024)(128)(4,1)}), s8[4194304]{0:T(1024)(128)(4,1)S(1)}, s32[]{:S(2)}) async-start(s8[8388608]{0:T(1024)(128)(4,1)} %bitcast.38), calls=%async_computation | async-start | bytes 8388608
  87.9 8.2 %collective-permute-start.11 = (bf16[256,1024]{1,0:T(8,128)(2,1)S(1)}, bf16[256,1024]{1,0:T(8,128)(2,1)S(1)}, u32[]{:S(2)}, u32[]{:S(2)}) collective-permute-start(bf16[256,1024]{1,0:T(8,128)(2,1)S(1)} %collective-permute-done.10.refs_6_.refs_7_), channel_id=1, source_target_pairs={{0,1},{1,0},{2,3},{3,2},{4,5},{5,4},{6,7},{7,6},{8,9},{9,8},{10,11... | collective-permute-start | bytes 1572872 | tf_op jit(solution)/shard_map/ppermute | solution.py:557
  87.9 26.5 %collective-permute-start.13 = (bf16[256,1024]{1,0:T(8,128)(2,1)S(1)}, bf16[256,1024]{1,0:T(8,128)(2,1)S(1)}, u32[]{:S(2)}, u32[]{:S(2)}) collective-permute-start(bf16[256,1024]{1,0:T(8,128)(2,1)S(1)} %copy-done.25), channel_id=1, source_target_pairs={{0,2},{1,3},{2,0},{3,1},{4,6},{5,7},{6,4},{7,5},{8,10},{9,11},{10,... | collective-permute-start | bytes 1572872 | tf_op jit(solution)/shard_map/ppermute | solution.py:557
  89.7 35.7 %collective-permute-start.15 = (bf16[4,1024,128]{2,1,0:T(8,128)(2,1)S(1)}, bf16[4,1024,128]{2,1,0:T(8,128)(2,1)S(1)}, u32[]{:S(2)}, u32[]{:S(2)}) collective-permute-start(bf16[4,1024,128]{2,1,0:T(8,128)(2,1)S(1)} %get-tuple-element.104), channel_id=1, source_target_pairs={{0,4},{4,0},{8,12},{12,8},{16,20},{20,16},{24,28},{28,24},{1,5},{5... | collective-permute-start | bytes 3145736 | tf_op jit(solution)/shard_map/ppermute | solution.py:560
  114.4 4.1 %collective-permute-start.14 = (bf16[256,1024]{1,0:T(8,128)(2,1)S(1)}, bf16[256,1024]{1,0:T(8,128)(2,1)S(1)}, u32[]{:S(2)}, u32[]{:S(2)}) collective-permute-start(bf16[256,1024]{1,0:T(8,128)(2,1)S(1)} %collective-permute-done.13.refs_6_.refs_3_), channel_id=1, source_target_pairs={{0,1},{1,0},{2,3},{3,2},{4,5},{5,4},{6,7},{7,6},{8,9},{9,8},{10,11... | collective-permute-start | bytes 1572872 | tf_op jit(solution)/shard_map/ppermute | solution.py:557
  114.5 40.7 %collective-permute-start.18 = (bf16[4,1024,128]{2,1,0:T(8,128)(2,1)}, bf16[4,1024,128]{2,1,0:T(8,128)(2,1)}, u32[]{:S(2)}, u32[]{:S(2)}) collective-permute-start(bf16[4,1024,128]{2,1,0:T(8,128)(2,1)} %get-tuple-element.112), channel_id=1, source_target_pairs={{0,4},{4,0},{8,12},{12,8},{16,20},{20,16},{24,28},{28,24},{1,5},{5... | collective-permute-start | bytes 3145736 | tf_op jit(solution)/shard_map/ppermute | solution.py:560
  118.5 34.5 %collective-permute-start.16 = (bf16[2,1024,128]{2,1,0:T(8,128)(2,1)}, bf16[2,1024,128]{2,1,0:T(8,128)(2,1)S(1)}, u32[]{:S(2)}, u32[]{:S(2)}) collective-permute-start(bf16[2,1024,128]{2,1,0:T(8,128)(2,1)} %get-tuple-element.114), channel_id=1, source_target_pairs={{0,16},{4,20},{8,24},{12,28},{16,0},{20,4},{24,8},{28,12},{1,17},{... | collective-permute-start | bytes 1572872 | tf_op jit(solution)/shard_map/ppermute | solution.py:560
  126.3 26.8 %collective-permute-start.17 = (bf16[2,1024,128]{2,1,0:T(8,128)(2,1)}, bf16[2,1024,128]{2,1,0:T(8,128)(2,1)}, u32[]{:S(2)}, u32[]{:S(2)}) collective-permute-start(bf16[2,1024,128]{2,1,0:T(8,128)(2,1)} %get-tuple-element.123), channel_id=1, source_target_pairs={{0,8},{4,12},{8,0},{12,4},{16,24},{20,28},{24,16},{28,20},{1,9},{5... | collective-permute-start | bytes 1572872 | tf_op jit(solution)/shard_map/ppermute | solution.py:560
  152.4 28.6 %collective-permute-start.21 = (bf16[2,256,768]{2,1,0:T(8,128)(2,1)}, bf16[2,256,768]{2,1,0:T(8,128)(2,1)}, u32[]{:S(2)}, u32[]{:S(2)}) collective-permute-start(bf16[2,256,768]{2,1,0:T(8,128)(2,1)} %slice.57), channel_id=1, source_target_pairs={{0,2},{1,3},{2,0},{3,1},{4,6},{5,7},{6,4},{7,5},{8,10},{9,11},{10,... | collective-permute-start | bytes 2359304 | tf_op jit(solution)/shard_map/ppermute | solution.py:557
  157.3 23.6 %collective-permute-start.20 = (bf16[2,1024,128]{2,1,0:T(8,128)(2,1)}, bf16[2,1024,128]{2,1,0:T(8,128)(2,1)S(1)}, u32[]{:S(2)}, u32[]{:S(2)}) collective-permute-start(bf16[2,1024,128]{2,1,0:T(8,128)(2,1)} %get-tuple-element.134), channel_id=1, source_target_pairs={{0,8},{4,12},{8,0},{12,4},{16,24},{20,28},{24,16},{28,20},{1,9},{5... | collective-permute-start | bytes 1572872 | tf_op jit(solution)/shard_map/ppermute | solution.py:560
  157.8 30.1 %collective-permute-start.23 = (bf16[4,1024,128]{2,1,0:T(8,128)(2,1)}, bf16[4,1024,128]{2,1,0:T(8,128)(2,1)S(1)}, u32[]{:S(2)}, u32[]{:S(2)}) collective-permute-start(bf16[4,1024,128]{2,1,0:T(8,128)(2,1)} %get-tuple-element.119), channel_id=1, source_target_pairs={{0,4},{4,0},{8,12},{12,8},{16,20},{20,16},{24,28},{28,24},{1,5},{5... | collective-permute-start | bytes 3145736 | tf_op jit(solution)/shard_map/ppermute | solution.py:560
  162.0 18.0 %collective-permute-start.19 = (bf16[1,1024,128]{2,1,0:T(8,128)(2,1)}, bf16[1,1024,128]{2,1,0:T(8,128)(2,1)S(1)}, u32[]{:S(2)}, u32[]{:S(2)}) collective-permute-start(bf16[1,1024,128]{2,1,0:T(8,128)(2,1)} %get-tuple-element.130), channel_id=1, source_target_pairs={{0,16},{4,20},{8,24},{12,28},{16,0},{20,4},{24,8},{28,12},{1,17},{... | collective-permute-start | bytes 786440 | tf_op jit(solution)/shard_map/ppermute | solution.py:560
  182.4 5.4 %collective-permute-start.22 = (bf16[2,256,768]{2,1,0:T(8,128)(2,1)S(1)}, bf16[2,256,768]{2,1,0:T(8,128)(2,1)S(1)}, u32[]{:S(2)}, u32[]{:S(2)}) collective-permute-start(bf16[2,256,768]{2,1,0:T(8,128)(2,1)S(1)} %pad_maximum_fusion), channel_id=1, source_target_pairs={{0,1},{1,0},{2,3},{3,2},{4,5},{5,4},{6,7},{7,6},{8,9},{9,8},{10,11... | collective-permute-start | bytes 2359304 | tf_op jit(solution)/shard_map/ppermute | solution.py:557
  182.7 19.8 %collective-permute-start.27 = (bf16[2,256,768]{2,1,0:T(8,128)(2,1)S(1)}, bf16[2,256,768]{2,1,0:T(8,128)(2,1)S(1)}, u32[]{:S(2)}, u32[]{:S(2)}) collective-permute-start(bf16[2,256,768]{2,1,0:T(8,128)(2,1)S(1)} %slice.63), channel_id=1, source_target_pairs={{0,2},{1,3},{2,0},{3,1},{4,6},{5,7},{6,4},{7,5},{8,10},{9,11},{10,... | collective-permute-start | bytes 2359304 | tf_op jit(solution)/shard_map/ppermute | solution.py:557
  184.3 9.9 %collective-permute-start.24 = (bf16[1,1024,128]{2,1,0:T(8,128)(2,1)S(1)}, bf16[1,1024,128]{2,1,0:T(8,128)(2,1)S(1)}, u32[]{:S(2)}, u32[]{:S(2)}) collective-permute-start(bf16[1,1024,128]{2,1,0:T(8,128)(2,1)S(1)} %get-tuple-element.128), channel_id=1, source_target_pairs={{0,4},{4,0},{8,12},{12,8},{16,20},{20,16},{24,28},{28,24},{1,5},{5... | collective-permute-start | bytes 786440 | tf_op jit(solution)/shard_map/ppermute | solution.py:560
  202.7 22.1 %collective-permute-start.28 = (bf16[2,256,768]{2,1,0:T(8,128)(2,1)S(1)}, bf16[2,256,768]{2,1,0:T(8,128)(2,1)S(1)}, u32[]{:S(2)}, u32[]{:S(2)}) collective-permute-start(bf16[2,256,768]{2,1,0:T(8,128)(2,1)S(1)} %pad_maximum_fusion.1), channel_id=1, source_target_pairs={{0,1},{1,0},{2,3},{3,2},{4,5},{5,4},{6,7},{7,6},{8,9},{9,8},{10,11... | collective-permute-start | bytes 2359304 | tf_op jit(solution)/shard_map/ppermute | solution.py:557
  202.8 20.0 %collective-permute-start.25 = (bf16[2,1024,128]{2,1,0:T(8,128)(2,1)S(1)}, bf16[2,1024,128]{2,1,0:T(8,128)(2,1)S(1)}, u32[]{:S(2)}, u32[]{:S(2)}) collective-permute-start(bf16[2,1024,128]{2,1,0:T(8,128)(2,1)S(1)} %get-tuple-element.146), channel_id=1, source_target_pairs={{0,8},{4,12},{8,0},{12,4},{16,24},{20,28},{24,16},{28,20},{1,9},{5... | collective-permute-start | bytes 1572872 | tf_op jit(solution)/shard_map/ppermute | solution.py:560
  203.4 20.5 %collective-permute-start.26 = (bf16[1,1024,128]{2,1,0:T(8,128)(2,1)S(1)}, bf16[1,1024,128]{2,1,0:T(8,128)(2,1)S(1)}, u32[]{:S(2)}, u32[]{:S(2)}) collective-permute-start(bf16[1,1024,128]{2,1,0:T(8,128)(2,1)S(1)} %get-tuple-element.141), channel_id=1, source_target_pairs={{0,16},{4,20},{8,24},{12,28},{16,0},{20,4},{24,8},{28,12},{1,17},{... | collective-permute-start | bytes 786440 | tf_op jit(solution)/shard_map/ppermute | solution.py:560
  222.8 14.5 %collective-permute-start.29 = (bf16[1,1024,128]{2,1,0:T(8,128)(2,1)S(1)}, bf16[1,1024,128]{2,1,0:T(8,128)(2,1)S(1)}, u32[]{:S(2)}, u32[]{:S(2)}) collective-permute-start(bf16[1,1024,128]{2,1,0:T(8,128)(2,1)S(1)} %get-tuple-element.149), channel_id=1, source_target_pairs={{0,16},{4,20},{8,24},{12,28},{16,0},{20,4},{24,8},{28,12},{1,17},{... | collective-permute-start | bytes 786440 | tf_op jit(solution)/shard_map/ppermute | solution.py:560
  (27 other events, 191.8 us)

commit v5 on v4

--- a/solution.py
+++ b/solution.py
@@ -185,6 +185,10 @@
     return slice(h * HEAD_DIM, (h + 1) * HEAD_DIM)
 
 
+def over_heads(tile):
+    return jnp.concatenate([tile] * GROUP, axis=1)
+
+
 def forward_kernel(parts, block, docs, info_ref, *refs):
     pieces = refs[:parts]
     out_ref, lse_ref = refs[parts : parts + 2]
@@ -194,7 +198,8 @@
     factor = math.log2(math.e) / math.sqrt(HEAD_DIM)
     prepare(parts, block, docs, info_ref, bias_ref, open_ref)
     for d in range(parts):
-        q_s[me ^ d] = pieces[d][:, :wide]
+        for h in range(GROUP):
+            q_s[me ^ d, h * block : (h + 1) * block] = pieces[d][:, head_cols(h)]
         k_s[me ^ d] = pieces[d][:, wide : wide + HEAD_DIM]
         vt_s[me ^ d] = flip(pieces[d][:, wide + HEAD_DIM :]).astype(jnp.bfloat16)
 
@@ -205,22 +210,25 @@
 
         def pair(back, carry):
             kb = qb - back
-            bias = bias_ref.at[pair_index(qb, kb)]
-            for h in range(GROUP):
-                raw = mm(k_s[kb], q_s[qb, :, head_cols(h)], NT) * factor + bias[...]
-                old = top_s[h]
-                top = jnp.maximum(old, jnp.max(raw, axis=0, keepdims=True))
-                shrink = jnp.exp2(old - top)
-                raised = jnp.exp2(raw - top)
-                top_s[h] = top
-                sum_s[h] = sum_s[h] * shrink + jnp.sum(raised, axis=0, keepdims=True)
-                acc_s[h] = acc_s[h] * shrink + mm(vt_s[kb], raised.astype(jnp.bfloat16))
+            bias = over_heads(bias_ref[pair_index(qb, kb)])
+            raw = mm(k_s[kb], q_s[qb], NT) * factor + bias
+            old = top_s[...]
+            top = jnp.maximum(old, jnp.max(raw, axis=0, keepdims=True))
+            shrink = jnp.exp2(old - top)
+            raised = jnp.exp2(raw - top)
+            top_s[...] = top
+            sum_s[...] = sum_s[...] * shrink + jnp.sum(raised, axis=0, keepdims=True)
+            acc_s[...] = acc_s[...] * shrink + mm(vt_s[kb], raised.astype(jnp.bfloat16))
             return carry
 
         lax.fori_loop(0, qb - open_ref[qb] + 1, pair, 0)
+        out = (acc_s[...] / sum_s[...]).astype(jnp.bfloat16)
+        spot = me ^ qb
         for h in range(GROUP):
-            out_ref[me ^ qb, head_cols(h)] = (acc_s[h] / sum_s[h]).astype(jnp.bfloat16)
-            lse_ref[h, me ^ qb] = jnp.broadcast_to(top_s[h] + jnp.log2(sum_s[h]), (8, block))
+            out_ref[head_cols(h), pl.ds(pl.multiple_of(spot * block, block), block)] = out[
+                :, h * block : (h + 1) * block
+            ]
+        lse_ref[spot] = jnp.broadcast_to(top_s[...] + jnp.log2(sum_s[...]), lse_ref.shape[1:])
         return carry
 
     lax.fori_loop(0, parts, rows_of, 0)
@@ -246,23 +254,23 @@
             grid=(1,),
             in_specs=[piece_block(block, cols, at) for x, at in pieces],
             out_specs=[
-                whole_block((parts, wide, block)),
-                whole_block((GROUP, parts, 8, block)),
+                whole_block((wide, parts * block)),
+                whole_block((parts, 8, GROUP * block)),
             ],
             scratch_shapes=[
                 vm((pairs, block, block), jnp.float32),
                 pltpu.SMEM((parts,), jnp.int32),
-                vm((parts, block, wide), jnp.bfloat16),
+                vm((parts, GROUP * block, HEAD_DIM), jnp.bfloat16),
                 vm((parts, block, HEAD_DIM), jnp.bfloat16),
                 vm((parts, HEAD_DIM, block), jnp.bfloat16),
-                vm((GROUP, 1, block), jnp.float32),
-                vm((GROUP, 1, block), jnp.float32),
-                vm((GROUP, HEAD_DIM, block), jnp.float32),
+                vm((1, GROUP * block), jnp.float32),
+                vm((1, GROUP * block), jnp.float32),
+                vm((HEAD_DIM, GROUP * block), jnp.float32),
             ],
         ),
         out_shape=[
-            shape((parts, wide, block)),
-            shape((GROUP, parts, 8, block), jnp.float32),
+            shape((wide, parts * block)),
+            shape((parts, 8, GROUP * block), jnp.float32),
         ],
         compiler_params=params(60),
         cost_estimate=cost(2.5),
@@ -274,14 +282,16 @@
     pieces = refs[:parts]
     grad_ref, out_ref, lse_ref = refs[parts : parts + 3]
     res_ref = refs[parts + 3]
-    bias_ref, open_ref, q_s, k_s, kt_s, v_s, dk_s, dv_s, dq_s, delta_s = refs[parts + 4 :]
+    bias_ref, open_ref, q_s, k_s, kt_s, v_s, do_s, dk_s, dv_s, dq_s = refs[parts + 4 :]
     me = info_ref[0]
     wide = GROUP * HEAD_DIM
     scale = 1.0 / math.sqrt(HEAD_DIM)
     factor = math.log2(math.e) * scale
     prepare(parts, block, docs, info_ref, bias_ref, open_ref)
     for d in range(parts):
-        q_s[me ^ d] = pieces[d][:, :wide]
+        for h in range(GROUP):
+            q_s[me ^ d, h * block : (h + 1) * block] = pieces[d][:, head_cols(h)]
+            do_s[me ^ d, h * block : (h + 1) * block] = grad_ref[d, :, head_cols(h)]
         k_s[me ^ d] = pieces[d][:, wide : wide + HEAD_DIM]
         kt_s[me ^ d] = flip(pieces[d][:, wide : wide + HEAD_DIM]).astype(jnp.bfloat16)
         v_s[me ^ d] = pieces[d][:, wide + HEAD_DIM :]
@@ -291,33 +301,25 @@
     def rows_of(qb, carry):
         spot = me ^ qb
         dq_s[...] = jnp.zeros_like(dq_s)
-        for h in range(GROUP):
-            product = flip(grad_ref[spot, :, head_cols(h)]) * out_ref[spot, head_cols(h)].astype(
-                jnp.float32
-            )
-            delta_s[h] = jnp.sum(product, axis=0, keepdims=True)
+        here = pl.ds(pl.multiple_of(spot * block, block), block)
+        out = jnp.concatenate([out_ref[head_cols(h), here] for h in range(GROUP)], axis=1)
+        delta = jnp.sum(flip(do_s[qb]) * out.astype(jnp.float32), axis=0, keepdims=True)
+        lse = lse_ref[spot, :1]
 
         def pair(back, carry):
             kb = qb - back
-            bias = bias_ref.at[pair_index(qb, kb)]
-            key, value = k_s[kb], v_s[kb]
-            dk = dk_s[kb]
-            dv = dv_s[kb]
-            for h in range(GROUP):
-                query, grad = q_s[qb, :, head_cols(h)], grad_ref[spot, :, head_cols(h)]
-                raw = mm(key, query, NT) * factor + bias[...]
-                probs = jnp.exp2(raw - lse_ref[h, spot, :1])
-                dv += mm(probs.astype(jnp.bfloat16), grad)
-                slope = (probs * (mm(value, grad, NT) - delta_s[h])).astype(jnp.bfloat16)
-                dk += mm(slope, query)
-                dq_s[h] += mm(kt_s[kb], slope)
-            dk_s[kb] = dk
-            dv_s[kb] = dv
+            bias = over_heads(bias_ref[pair_index(qb, kb)])
+            probs = jnp.exp2(mm(k_s[kb], q_s[qb], NT) * factor + bias - lse)
+            dv_s[kb] += mm(probs.astype(jnp.bfloat16), do_s[qb])
+            slope = (probs * (mm(v_s[kb], do_s[qb], NT) - delta)).astype(jnp.bfloat16)
+            dk_s[kb] += mm(slope, q_s[qb])
+            dq_s[...] += mm(kt_s[kb], slope)
             return carry
 
         lax.fori_loop(0, qb - open_ref[qb] + 1, pair, 0)
+        back = (jnp.transpose(dq_s[...]) * scale).astype(jnp.bfloat16)
         for h in range(GROUP):
-            res_ref[spot, :, head_cols(h)] = (jnp.transpose(dq_s[h]) * scale).astype(jnp.bfloat16)
+            res_ref[spot, :, head_cols(h)] = back[h * block : (h + 1) * block]
         return carry
 
     lax.fori_loop(0, parts, rows_of, 0)
@@ -339,21 +341,21 @@
             in_specs=[piece_block(block, cols, at) for x, at in pieces]
             + [
                 pl.BlockSpec((parts, block, wide), lambda i, info: (0, 0, gp)),
-                whole_block((parts, wide, block)),
-                whole_block((GROUP, parts, 8, block)),
+                whole_block((wide, parts * block)),
+                whole_block((parts, 8, GROUP * block)),
             ],
             out_specs=whole_block((parts, block, cols)),
             scratch_shapes=[
                 vm((pairs, block, block), jnp.float32),
                 pltpu.SMEM((parts,), jnp.int32),
-                vm((parts, block, wide), jnp.bfloat16),
+                vm((parts, GROUP * block, HEAD_DIM), jnp.bfloat16),
                 vm((parts, block, HEAD_DIM), jnp.bfloat16),
                 vm((parts, HEAD_DIM, block), jnp.bfloat16),
                 vm((parts, block, HEAD_DIM), jnp.bfloat16),
+                vm((parts, GROUP * block, HEAD_DIM), jnp.bfloat16),
                 vm((parts, block, HEAD_DIM), jnp.float32),
                 vm((parts, block, HEAD_DIM), jnp.float32),
-                vm((GROUP, HEAD_DIM, block), jnp.float32),
-                vm((GROUP, 1, block), jnp.float32),
+                vm((HEAD_DIM, GROUP * block), jnp.float32),
             ],
         ),
         out_shape=shape((parts, block, cols)),
@@ -391,10 +393,9 @@
     odd = ((info_ref[1] >> order[0]) & 1) == 1
     rows = GROUP * HEAD_DIM
     grads = [jnp.concatenate([lows[d][...], highs[d][...]], axis=1) for d in range(2)]
+    grads = jnp.concatenate(grads + [x[...] for x in chunk], axis=0)
     for gp in range(groups):
-        total = mm(outs[gp][0], grads[0]) + mm(outs[gp][1], grads[1])
-        for d in range(2, parts):
-            total += mm(outs[gp][d], chunk[d - 2][...])
+        total = mm(outs[gp][...], grads)
         low, high = total[:, :width], total[:, width:]
         spot = slice(gp * rows, (gp + 1) * rows)
         keep_ref[0, spot] = jnp.where(odd, high, low)
@@ -403,7 +404,7 @@
 
 def weight_terms(info, outs, near, chunk, token, shares, c, chunks, width, order):
     groups, parts = len(outs), 2 + len(chunk)
-    _, rows, block = outs[0].shape
+    rows, block = outs[0].shape[0], near[0].shape[0]
     half = shares // 2
     bits = half.bit_length() - 1
     spot = pl.BlockSpec((1, groups * rows, width), lambda t, info: (reverse_bits(t, bits), 0, 0))
@@ -423,7 +424,7 @@
         grid_spec=pltpu.PrefetchScalarGridSpec(
             num_scalar_prefetch=1,
             grid=(half,),
-            in_specs=[pl.BlockSpec((parts, rows, block), lambda t, info: (0, 0, 0))] * groups
+            in_specs=[pl.BlockSpec((rows, parts * block), lambda t, info: (0, 0))] * groups
             + [original(side, x) for side in range(2) for x in near]
             + [pl.BlockSpec((block, 2 * width), lambda t, info: (0, mate(t, info)))] * len(chunk),
             out_specs=[spot, spot],
@@ -606,11 +607,15 @@
     def hop(c, send, stage):
         return over_dp(send, 1 << orders[c][stage])
 
-    def weigh(c):
-        nonlocal token
+    def receive(c):
         fars[c] = []
         for x in gate(far_half[c], token):
             fars[c] += [x, over_seq(x, 1)]
+
+    def weigh(c):
+        nonlocal token
+        if c not in fars:
+            receive(c)
         keep, send = weight_terms(
             info, outs, near, fars[c], token, shares, c, chunks, width, orders[c]
         )
@@ -654,6 +659,7 @@
     last = chunks - 1
     for c in range(last):
         weigh(c)
+    receive(last)
     advance(0)
     if last:
         project_step(list(range(last)), False)
@@ -667,20 +673,17 @@
         send_back(gp)
     advance(1)
     advance(2)
+    advance(3)
     firsts = hand_over(0, token)
+    advance(0)
     token = (token, firsts[1])
     advance(3)
-    advance(0)
+    for _ in bits:
+        for c in range(chunks):
+            advance(c)
     lasts = [hand_over(gp, token) for gp in range(1, groups)]
-    advance(3)
-    for _ in bits:
-        for c in range(last):
-            advance(c)
     back = firsts + [x for group in lasts for x in group]
     grad_q, grad_k, grad_v = unpack(gate([info], token)[0], back, parts, groups)
-    token = grad_q
-    for _ in bits:
-        advance(last)
     return (grad_q[None], grad_k[None], grad_v[None], weight_grad)
 
 

time: 235 us -> 216 us (0.919); the launches traced: 238 us -> 215 us
  Pallas kernels: 120 us -> 97 us
  starting transfers between devices: 39.2 us -> 32.4 us
  waiting for transfers between devices: 64.3 us -> 69.1 us
    pallas_call x2, Pallas kernels: 34.5 us -> 22.9 us  [attention_back(): pl.pallas_call(functools.partial(backward_kernel, parts, block, docs), gr...]
    pallas_call x2, Pallas kernels: 28.2 us -> 16.7 us  [attention(): pl.pallas_call(functools.partial(forward_kernel, parts, block, docs), gri...]
    ppermute x18, waiting for transfers between devices: 32.1 us -> 39.1 us  [over_seq(): return lax.ppermute(x, 'seq', [(i, i ^ d) for i in range(parts)])]
    ppermute x12, starting transfers between devices: 23.8 us -> 17.5 us  [over_dp(): return lax.ppermute(x, 'dp', [(i, i ^ d) for i in range(shares)])]
    unnamed x58 -> x56, local copies, waits for them, and re-layouts: 8.11 us -> 10 us
  transfers between devices with their start and end apart: 30 -> 30, of which waited for: 9 -> 14; matrix products, arithmetic and copies ran while one was open for 2% -> 2% of each run, Pallas kernels for 49% -> 43%
where the time goes in v5:
time: 216 us; the launch traced here: 215 us
  Pallas kernels  97 us (45%)
  waiting for transfers between devices  69.1 us (32%)
  starting transfers between devices  32.4 us (15%)
  local copies, waits for them, and re-layouts  14.6 us (7%)
    ppermute x18, waiting for transfers between devices, over_seq(): return lax.ppermute(x, 'seq', [(i, i ^ d) for i in range(parts)])  39.1 us
    ppermute x12, waiting for transfers between devices, over_dp(): return lax.ppermute(x, 'dp', [(i, i ^ d) for i in range(shares)])  30 us
    pallas_call x2, Pallas kernels, attention_back(): pl.pallas_call(functools.partial(backward_kernel, parts, block, docs), gr...  22.9 us
    pallas_call x4, Pallas kernels, weight_terms(): pl.pallas_call(functools.partial(weight_kernel, parts, groups, width, ord...  21 us
    ppermute x12, starting transfers between devices, over_dp(): return lax.ppermute(x, 'dp', [(i, i ^ d) for i in range(shares)])  17.5 us
    pallas_call x2, Pallas kernels, attention(): pl.pallas_call(functools.partial(forward_kernel, parts, block, docs), gri...  16.7 us
    ppermute x18, starting transfers between devices, over_seq(): return lax.ppermute(x, 'seq', [(i, i ^ d) for i in range(parts)])  14.9 us
    pallas_call x2, Pallas kernels, project(): pl.pallas_call(functools.partial(project_kernel, parts, shares, width, le...  14.6 us
  transfers between devices with their start and end apart: 30, of which 14 were waited for; matrix products, arithmetic and copies ran while one was open for 2% of the time, Pallas kernels for 43%

profile of v5, /device:TPU:0, one launch (start us, length us, event | category | flops | bytes accessed | tf_op | source)
XLA Modules:
  0.0 214.7 jit_solution(12899252782963565132)
XLA Ops:
  0.6 2.0 pack.2
  2.7 2.4 %collective-permute-start.2 = (bf16[256,768]{1,0:T(8,128)(2,1)}, bf16[256,768]{1,0:T(8,128)(2,1)S(1)}, u32[]{:S(2)}, u32[]{:S(2)}) collective-permute-start(bf16[256,768]{1,0:T(8,128)(2,1)} %get-tuple-element.88), channel_id=1, source_target_pairs={{0,3},{1,2},{2,1},{3,0},{4,7},{5,6},{6,5},{7,4},{8,11},{9,10},{10,... | collective-permute-start | bytes 1179656 | tf_op jit(solution)/shard_map/ppermute | solution.py:558
  5.7 3.0 %pack.3 = (bf16[256,1536]{1,0:T(8,128)(2,1)}, bf16[256,1536]{1,0:T(8,128)(2,1)}, bf16[256,768]{1,0:T(8,128)(2,1)}, bf16[256,768]{1,0:T(8,128)(2,1)}) custom-call(s32[1]{0:T(128)} %bitcast.me_ref, bf16[256,4096]{1,0:T(8,128)(2,1)} %bitcast.42, bf16[256,1024]{1,0:T(8,128)(2,1)} %bitcast.50, bf16[256,1024]{1,0:T(8,128)(2,1)} %bitcast.58, ...), custom_call_target="tpu_custom_call" | custom-call | flops 200000000 | bytes 1024 | tf_op jit(solution)/shard_map/pack/pallas_call | solution.py:79
  8.8 4.0 %pack_chunks.1 = (bf16[256,1024]{1,0:T(8,128)(2,1)}, bf16[256,1024]{1,0:T(8,128)(2,1)}, bf16[256,1024]{1,0:T(8,128)(2,1)}, bf16[256,1024]{1,0:T(8,128)(2,1)}) custom-call(bf16[256,4096]{1,0:T(8,128)(2,1)} %bitcast.26), custom_call_target="tpu_custom_call" | custom-call | flops 200000000 | bytes 1024 | tf_op jit(solution)/shard_map/pack_chunks/pallas_call | solution.py:110
  12.8 2.1 collective-permute-done.2.refs_3_
  14.9 8.5 %collective-permute-done.1.refs_2_ = bf16[256,768]{1,0:T(8,128)(2,1)S(1)} collective-permute-done((bf16[256,768]{1,0:T(8,128)(2,1)}, bf16[256,768]{1,0:T(8,128)(2,1)S(1)}, u32[]{:S(2)}, u32[]{:S(2)}) %collective-permute-start.1) | collective-permute-done | bytes 393248 | tf_op jit(solution)/shard_map/ppermute | solution.py:558
  24.2 2.4 %collective-permute-start.4 = (bf16[256,768]{1,0:T(8,128)(2,1)}, bf16[256,768]{1,0:T(8,128)(2,1)S(1)}, u32[]{:S(2)}, u32[]{:S(2)}) collective-permute-start(bf16[256,768]{1,0:T(8,128)(2,1)} %get-tuple-element.92), channel_id=1, source_target_pairs={{0,2},{1,3},{2,0},{3,1},{4,6},{5,7},{6,4},{7,5},{8,10},{9,11},{10,... | collective-permute-start | bytes 1179656 | tf_op jit(solution)/shard_map/ppermute | solution.py:558
  29.9 8.4 %attention.2 = (bf16[512,1024]{1,0:T(8,128)(2,1)}, f32[4,8,1024]{2,1,0:T(8,128)}) custom-call(s32[10]{0:T(128)} %pad_add_fusion.info_ref, bf16[256,1536]{1,0:T(8,128)(2,1)} %get-tuple-element.83.refs_0_, bf16[256,1536]{1,0:T(8,128)(2,1)} %copy-done.18, bf16[256,768]{1,0:T(8,128)(2,1)} %copy-done.22, bf16[256,768]{1,0:T(8,128)(2,1)} %copy-done.21), custom_call_target="tpu_custom_call" | custom-call | flops 2500000000 | bytes 1024 | tf_op jit(solution)/shard_map/attention/pallas_call | solution.py:250
  38.3 6.4 %collective-permute-done.5.refs_3_ = bf16[256,768]{1,0:T(8,128)(2,1)} collective-permute-done((bf16[256,768]{1,0:T(8,128)(2,1)}, bf16[256,768]{1,0:T(8,128)(2,1)}, u32[]{:S(2)}, u32[]{:S(2)}) %collective-permute-start.5) | collective-permute-done | bytes 393248 | tf_op jit(solution)/shard_map/ppermute | solution.py:558
  44.7 8.3 %attention.3 = (bf16[512,1024]{1,0:T(8,128)(2,1)}, f32[4,8,1024]{2,1,0:T(8,128)}) custom-call(s32[10]{0:T(128)} %pad_add_fusion.info_ref, bf16[256,1536]{1,0:T(8,128)(2,1)} %get-tuple-element.83.refs_0_, bf16[256,1536]{1,0:T(8,128)(2,1)} %copy-done.18, bf16[256,768]{1,0:T(8,128)(2,1)} %copy-done.20, bf16[256,768]{1,0:T(8,128)(2,1)} %collective-permute-done.5.refs_3_), custom_call_target="tpu_custom_call" | custom-call | flops 2500000000 | bytes 1024 | tf_op jit(solution)/shard_map/attention/pallas_call | solution.py:250
  53.1 3.0 %collective-permute-done.6.refs_6_.refs_3_ = bf16[256,1024]{1,0:T(8,128)(2,1)S(1)} collective-permute-done((bf16[256,1024]{1,0:T(8,128)(2,1)}, bf16[256,1024]{1,0:T(8,128)(2,1)S(1)}, u32[]{:S(2)}, u32[]{:S(2)}) %collective-permute-start.6) | collective-permute-done | bytes 524320 | tf_op jit(solution)/shard_map/ppermute | solution.py:558
  59.3 4.8 %weight_terms.4 = (f32[4,1024,128]{2,1,0:T(8,128)S(1)}, bf16[4,1024,128]{2,1,0:T(8,128)(2,1)S(1)}) custom-call(s32[10]{0:T(128)S(1)} %copy-done.14, bf16[512,1024]{1,0:T(8,128)(2,1)S(1)} %copy-done.3, bf16[512,1024]{1,0:T(8,128)(2,1)S(1)} %copy-done.1, bf16[256,4096]{1,0:T(8,128)(2,1)S(1)} %bitcast.28, ...), custom_call_target="tpu_custom_call" | custom-call | flops 300000000 | bytes 1024 | tf_op jit(solution)/shard_map/weight_terms/pallas_call | solution.py:422
  64.1 6.6 %collective-permute-done.8.refs_6_.refs_5_ = bf16[256,1024]{1,0:T(8,128)(2,1)S(1)} collective-permute-done((bf16[256,1024]{1,0:T(8,128)(2,1)}, bf16[256,1024]{1,0:T(8,128)(2,1)S(1)}, u32[]{:S(2)}, u32[]{:S(2)}) %collective-permute-start.8) | collective-permute-done | bytes 524320 | tf_op jit(solution)/shard_map/ppermute | solution.py:558
  70.7 1.8 collective-permute-start.10
  74.1 5.1 %weight_terms.5 = (f32[4,1024,128]{2,1,0:T(8,128)S(1)}, bf16[4,1024,128]{2,1,0:T(8,128)(2,1)S(1)}) custom-call(s32[10]{0:T(128)S(1)} %copy-done.14, bf16[512,1024]{1,0:T(8,128)(2,1)S(1)} %copy-done.3, bf16[512,1024]{1,0:T(8,128)(2,1)S(1)} %copy-done.1, bf16[256,4096]{1,0:T(8,128)(2,1)S(1)} %bitcast.30, ...), custom_call_target="tpu_custom_call" | custom-call | flops 300000000 | bytes 1024 | tf_op jit(solution)/shard_map/weight_terms/pallas_call | solution.py:422
  79.2 5.8 %collective-permute-done.10.refs_6_.refs_7_ = bf16[256,1024]{1,0:T(8,128)(2,1)S(1)} collective-permute-done((bf16[256,1024]{1,0:T(8,128)(2,1)S(1)}, bf16[256,1024]{1,0:T(8,128)(2,1)S(1)}, u32[]{:S(2)}, u32[]{:S(2)}) %collective-permute-start.10) | collective-permute-done | bytes 524320 | tf_op jit(solution)/shard_map/ppermute | solution.py:558
  88.4 5.5 %weight_terms.6 = (f32[4,1024,128]{2,1,0:T(8,128)S(1)}, bf16[4,1024,128]{2,1,0:T(8,128)(2,1)}) custom-call(s32[10]{0:T(128)S(1)} %copy-done.14, bf16[512,1024]{1,0:T(8,128)(2,1)S(1)} %copy-done.3, bf16[512,1024]{1,0:T(8,128)(2,1)S(1)} %copy-done.1, bf16[256,4096]{1,0:T(8,128)(2,1)S(1)} %bitcast.32, ...), custom_call_target="tpu_custom_call" | custom-call | flops 300000000 | bytes 1024 | tf_op jit(solution)/shard_map/weight_terms/pallas_call | solution.py:422
  95.2 4.2 %collective-permute-done.13.refs_6_.refs_3_ = bf16[256,1024]{1,0:T(8,128)(2,1)S(1)} collective-permute-done((bf16[256,1024]{1,0:T(8,128)(2,1)S(1)}, bf16[256,1024]{1,0:T(8,128)(2,1)S(1)}, u32[]{:S(2)}, u32[]{:S(2)}) %collective-permute-start.13) | collective-permute-done | bytes 524320 | tf_op jit(solution)/shard_map/ppermute | solution.py:558
  103.0 2.6 %collective-permute-start.16 = (bf16[2,1024,128]{2,1,0:T(8,128)(2,1)}, bf16[2,1024,128]{2,1,0:T(8,128)(2,1)}, u32[]{:S(2)}, u32[]{:S(2)}) collective-permute-start(bf16[2,1024,128]{2,1,0:T(8,128)(2,1)} %get-tuple-element.112), channel_id=1, source_target_pairs={{0,16},{4,20},{8,24},{12,28},{16,0},{20,4},{24,8},{28,12},{1,17},{... | collective-permute-start | bytes 1572872 | tf_op jit(solution)/shard_map/ppermute | solution.py:561
  105.6 9.4 %project.2.refs_5_ = f32[4,256,1024]{2,1,0:T(8,128)S(1)} custom-call(bf16[1024,4096]{1,0:T(8,128)(2,1)S(1)} %bitcast.39, bf16[256,4096]{1,0:T(8,128)(2,1)S(1)} %bitcast.34, bf16[256,4096]{1,0:T(8,128)(2,1)} %collective-permute-done.3.refs_3_.refs_5_.refs_2_, bf16[256,1024]{1,0:T(8,128)(2,1)S(1)} %collective-permute-done.6.refs_6_.refs_3_, ...), custom_call_target="tpu_custom_call" | custom-call | flops 500000000 | bytes 1024 | tf_op jit(solution)/shard_map/project/pallas_call | solution.py:521
  115.0 5.5 %weight_terms.7 = (f32[4,1024,128]{2,1,0:T(8,128)S(1)}, bf16[4,1024,128]{2,1,0:T(8,128)(2,1)}) custom-call(s32[10]{0:T(128)S(1)} %copy-done.14, bf16[512,1024]{1,0:T(8,128)(2,1)S(1)} %copy-done.4, bf16[512,1024]{1,0:T(8,128)(2,1)S(1)} %copy-done.2, bf16[256,4096]{1,0:T(8,128)(2,1)S(1)} %bitcast.35, ...), custom_call_target="tpu_custom_call" | custom-call | flops 300000000 | bytes 1024 | tf_op jit(solution)/shard_map/weight_terms/pallas_call | solution.py:422
  124.8 5.3 %project.3.refs_4_ = bf16[4,256,1024]{2,1,0:T(8,128)(2,1)S(1)} custom-call(bf16[1024,4096]{1,0:T(8,128)(2,1)S(1)} %bitcast.39, bf16[256,4096]{1,0:T(8,128)(2,1)S(1)} %bitcast.37, bf16[256,4096]{1,0:T(8,128)(2,1)} %collective-permute-done.3.refs_3_.refs_5_.refs_2_, bf16[256,1024]{1,0:T(8,128)(2,1)S(1)} %collective-permute-done.13.refs_6_.refs_3_, ...), custom_call_target="tpu_custom_call" | custom-call | flops 500000000 | bytes 1024 | tf_op jit(solution)/shard_map/project/pallas_call | solution.py:521
  131.5 11.4 %attention_back.2 = bf16[4,256,768]{2,1,0:T(8,128)(2,1)} custom-call(s32[10]{0:T(128)} %pad_add_fusion.info_ref, bf16[256,1536]{1,0:T(8,128)(2,1)} %get-tuple-element.83.refs_0_, bf16[256,1536]{1,0:T(8,128)(2,1)} %copy-done.18, bf16[256,768]{1,0:T(8,128)(2,1)} %copy-done.22, bf16[256,768]{1,0:T(8,128)(2,1)} %copy-done.21, bf16[4,256,1024]{2,1,0:T(8,128)(2,1)} %copy-done.5, ...), custom_call_target="tpu_custom_call" | custom-call | flops 1000000000 | bytes 1024 | tf_op jit(solution)/shard_map/attention_back/pallas_call | solution.py:336
  142.8 2.2 %slice.57 = bf16[2,256,768]{2,1,0:T(8,128)(2,1)} slice(bf16[4,256,768]{2,1,0:T(8,128)(2,1)} %attention_back.2), slice={[2:4], [0:256], [0:768]} | slice | bytes 1572864 | tf_op jit(solution)/shard_map/slice | solution.py:648
  154.3 11.5 %attention_back.3 = bf16[4,256,768]{2,1,0:T(8,128)(2,1)} custom-call(s32[10]{0:T(128)} %pad_add_fusion.info_ref, bf16[256,1536]{1,0:T(8,128)(2,1)} %get-tuple-element.83.refs_0_, bf16[256,1536]{1,0:T(8,128)(2,1)} %copy-done.18, bf16[256,768]{1,0:T(8,128)(2,1)} %copy-done.20, bf16[256,768]{1,0:T(8,128)(2,1)} %collective-permute-done.5.refs_3_, ...), custom_call_target="tpu_custom_call" | custom-call | flops 1000000000 | bytes 1024 | tf_op jit(solution)/shard_map/attention_back/pallas_call | solution.py:336
  165.8 2.5 %collective-permute-done.19.got_ref = bf16[1,1024,128]{2,1,0:T(8,128)(2,1)S(1)} collective-permute-done((bf16[1,1024,128]{2,1,0:T(8,128)(2,1)}, bf16[1,1024,128]{2,1,0:T(8,128)(2,1)S(1)}, u32[]{:S(2)}, u32[]{:S(2)}) %collective-permute-start.19) | collective-permute-done | bytes 262176 | tf_op jit(solution)/shard_map/ppermute | solution.py:561
  173.5 2.5 %collective-permute-start.25 = (bf16[2,1024,128]{2,1,0:T(8,128)(2,1)S(1)}, bf16[2,1024,128]{2,1,0:T(8,128)(2,1)S(1)}, u32[]{:S(2)}, u32[]{:S(2)}) collective-permute-start(bf16[2,1024,128]{2,1,0:T(8,128)(2,1)S(1)} %get-tuple-element.144), channel_id=1, source_target_pairs={{0,8},{4,12},{8,0},{12,4},{16,24},{20,28},{24,16},{28,20},{1,9},{5... | collective-permute-start | bytes 1572872 | tf_op jit(solution)/shard_map/ppermute | solution.py:561
  179.1 5.6 %collective-permute-done.22.got_ref = bf16[1,1024,128]{2,1,0:T(8,128)(2,1)S(1)} collective-permute-done((bf16[1,1024,128]{2,1,0:T(8,128)(2,1)S(1)}, bf16[1,1024,128]{2,1,0:T(8,128)(2,1)S(1)}, u32[]{:S(2)}, u32[]{:S(2)}) %collective-permute-start.22) | collective-permute-done | bytes 262176 | tf_op jit(solution)/shard_map/ppermute | solution.py:561
  185.6 8.5 %collective-permute-done.25.got_low.got_high = bf16[2,1024,128]{2,1,0:T(8,128)(2,1)S(1)} collective-permute-done((bf16[2,1024,128]{2,1,0:T(8,128)(2,1)S(1)}, bf16[2,1024,128]{2,1,0:T(8,128)(2,1)S(1)}, u32[]{:S(2)}, u32[]{:S(2)}) %collective-permute-start.25) | collective-permute-done | bytes 524320 | tf_op jit(solution)/shard_map/ppermute | solution.py:561
  195.6 12.9 %collective-permute-done.27.got_ref = bf16[1,1024,128]{2,1,0:T(8,128)(2,1)S(1)} collective-permute-done((bf16[1,1024,128]{2,1,0:T(8,128)(2,1)S(1)}, bf16[1,1024,128]{2,1,0:T(8,128)(2,1)S(1)}, u32[]{:S(2)}, u32[]{:S(2)}) %collective-permute-start.27) | collective-permute-done | bytes 262176 | tf_op jit(solution)/shard_map/ppermute | solution.py:561
  209.6 2.3 %collective-permute-done.29 = bf16[2,256,768]{2,1,0:T(8,128)(2,1)S(1)} collective-permute-done((bf16[2,256,768]{2,1,0:T(8,128)(2,1)S(1)}, bf16[2,256,768]{2,1,0:T(8,128)(2,1)S(1)}, u32[]{:S(2)}, u32[]{:S(2)}) %collective-permute-start.29) | collective-permute-done | bytes 786464 | tf_op jit(solution)/shard_map/ppermute | solution.py:558
  211.9 2.8 %unpack.1 = (bf16[256,4096]{1,0:T(8,128)(2,1)}, bf16[256,1024]{1,0:T(8,128)(2,1)}, bf16[256,1024]{1,0:T(8,128)(2,1)}) custom-call(s32[10]{0:T(128)S(1)} %copy-done.15, bf16[256,768]{1,0:T(8,128)(2,1)S(1)} %get-tuple-element.160.refs_0_, bf16[256,768]{1,0:T(8,128)(2,1)S(1)} %get-tuple-element.167.refs_1_, bf16[256,768]{1,0:T(8,128)(2,1)S(1)} %get-tuple-element.168.refs_2_, ...), custom_call_target="tpu_custom_call" | custom-call | flops 200000000 | bytes 1024 | tf_op jit(solution)/shard_map/unpack/pallas_call | solution.py:142
  (122 shorter events, 44.1 us)
Async XLA Ops:
  2.7 12.2 %collective-permute-start.2 = (bf16[256,768]{1,0:T(8,128)(2,1)}, bf16[256,768]{1,0:T(8,128)(2,1)S(1)}, u32[]{:S(2)}, u32[]{:S(2)}) collective-permute-start(bf16[256,768]{1,0:T(8,128)(2,1)} %get-tuple-element.88), channel_id=1, source_target_pairs={{0,3},{1,2},{2,1},{3,0},{4,7},{5,6},{6,5},{7,4},{8,11},{9,10},{10,... | collective-permute-start | bytes 1179656 | tf_op jit(solution)/shard_map/ppermute | solution.py:558
  5.1 18.3 %collective-permute-start.1 = (bf16[256,768]{1,0:T(8,128)(2,1)}, bf16[256,768]{1,0:T(8,128)(2,1)S(1)}, u32[]{:S(2)}, u32[]{:S(2)}) collective-permute-start(bf16[256,768]{1,0:T(8,128)(2,1)} %get-tuple-element.81), channel_id=1, source_target_pairs={{0,2},{1,3},{2,0},{3,1},{4,6},{5,7},{6,4},{7,5},{8,10},{9,11},{10,... | collective-permute-start | bytes 1179656 | tf_op jit(solution)/shard_map/ppermute | solution.py:558
  23.4 14.9 %collective-permute-start.3 = (bf16[256,4096]{1,0:T(8,128)(2,1)S(1)}, bf16[256,4096]{1,0:T(8,128)(2,1)}, u32[]{:S(2)}, u32[]{:S(2)}) collective-permute-start(bf16[256,4096]{1,0:T(8,128)(2,1)S(1)} %bitcast.27), channel_id=1, source_target_pairs={{0,1},{1,0},{2,3},{3,2},{4,5},{5,4},{6,7},{7,6},{8,9},{9,8},{10,11... | collective-permute-start | bytes 6291464 | tf_op jit(solution)/shard_map/ppermute | solution.py:558
  24.2 4.8 %collective-permute-start = (bf16[256,1536]{1,0:T(8,128)(2,1)}, bf16[256,1536]{1,0:T(8,128)(2,1)S(1)}, u32[]{:S(2)}, u32[]{:S(2)}) collective-permute-start(bf16[256,1536]{1,0:T(8,128)(2,1)} %get-tuple-element.87), channel_id=1, source_target_pairs={{0,1},{1,0},{2,3},{3,2},{4,5},{5,4},{6,7},{7,6},{8,9},{9,8},{10,11... | collective-permute-start | bytes 2359304 | tf_op jit(solution)/shard_map/ppermute | solution.py:558
  24.2 14.1 %collective-permute-start.4 = (bf16[256,768]{1,0:T(8,128)(2,1)}, bf16[256,768]{1,0:T(8,128)(2,1)S(1)}, u32[]{:S(2)}, u32[]{:S(2)}) collective-permute-start(bf16[256,768]{1,0:T(8,128)(2,1)} %get-tuple-element.92), channel_id=1, source_target_pairs={{0,2},{1,3},{2,0},{3,1},{4,6},{5,7},{6,4},{7,5},{8,10},{9,11},{10,... | collective-permute-start | bytes 1179656 | tf_op jit(solution)/shard_map/ppermute | solution.py:558
  26.6 18.2 %collective-permute-start.5 = (bf16[256,768]{1,0:T(8,128)(2,1)}, bf16[256,768]{1,0:T(8,128)(2,1)}, u32[]{:S(2)}, u32[]{:S(2)}) collective-permute-start(bf16[256,768]{1,0:T(8,128)(2,1)} %get-tuple-element.93), channel_id=1, source_target_pairs={{0,3},{1,2},{2,1},{3,0},{4,7},{5,6},{6,5},{7,4},{8,11},{9,10},{10,... | collective-permute-start | bytes 1179656 | tf_op jit(solution)/shard_map/ppermute | solution.py:558
  26.6 29.5 %collective-permute-start.6 = (bf16[256,1024]{1,0:T(8,128)(2,1)}, bf16[256,1024]{1,0:T(8,128)(2,1)S(1)}, u32[]{:S(2)}, u32[]{:S(2)}) collective-permute-start(bf16[256,1024]{1,0:T(8,128)(2,1)} %get-tuple-element.97), channel_id=1, source_target_pairs={{0,2},{1,3},{2,0},{3,1},{4,6},{5,7},{6,4},{7,5},{8,10},{9,11},{10,... | collective-permute-start | bytes 1572872 | tf_op jit(solution)/shard_map/ppermute | solution.py:558
  56.1 1.9 collective-permute-start.7
  56.1 14.6 %collective-permute-start.8 = (bf16[256,1024]{1,0:T(8,128)(2,1)}, bf16[256,1024]{1,0:T(8,128)(2,1)S(1)}, u32[]{:S(2)}, u32[]{:S(2)}) collective-permute-start(bf16[256,1024]{1,0:T(8,128)(2,1)} %get-tuple-element.103), channel_id=1, source_target_pairs={{0,2},{1,3},{2,0},{3,1},{4,6},{5,7},{6,4},{7,5},{8,10},{9,11},{10,... | collective-permute-start | bytes 1572872 | tf_op jit(solution)/shard_map/ppermute | solution.py:558
  70.7 3.4 %collective-permute-start.9 = (bf16[256,1024]{1,0:T(8,128)(2,1)S(1)}, bf16[256,1024]{1,0:T(8,128)(2,1)S(1)}, u32[]{:S(2)}, u32[]{:S(2)}) collective-permute-start(bf16[256,1024]{1,0:T(8,128)(2,1)S(1)} %collective-permute-done.8.refs_6_.refs_5_), channel_id=1, source_target_pairs={{0,1},{1,0},{2,3},{3,2},{4,5},{5,4},{6,7},{7,6},{8,9},{9,8},{10,11... | collective-permute-start | bytes 1572872 | tf_op jit(solution)/shard_map/ppermute | solution.py:558
  70.7 14.3 %collective-permute-start.10 = (bf16[256,1024]{1,0:T(8,128)(2,1)S(1)}, bf16[256,1024]{1,0:T(8,128)(2,1)S(1)}, u32[]{:S(2)}, u32[]{:S(2)}) collective-permute-start(bf16[256,1024]{1,0:T(8,128)(2,1)S(1)} %copy-done.25), channel_id=1, source_target_pairs={{0,2},{1,3},{2,0},{3,1},{4,6},{5,7},{6,4},{7,5},{8,10},{9,11},{10,... | collective-permute-start | bytes 1572872 | tf_op jit(solution)/shard_map/ppermute | solution.py:558
  72.5 28.6 %collective-permute-start.12 = (bf16[4,1024,128]{2,1,0:T(8,128)(2,1)S(1)}, bf16[4,1024,128]{2,1,0:T(8,128)(2,1)S(1)}, u32[]{:S(2)}, u32[]{:S(2)}) collective-permute-start(bf16[4,1024,128]{2,1,0:T(8,128)(2,1)S(1)} %get-tuple-element.100), channel_id=1, source_target_pairs={{0,8},{4,12},{8,0},{12,4},{16,24},{20,28},{24,16},{28,20},{1,9},{5... | collective-permute-start | bytes 3145736 | tf_op jit(solution)/shard_map/ppermute | solution.py:561
  74.1 31.5 %slice-start = ((s8[8388608]{0:T(1024)(128)(4,1)}), s8[4194304]{0:T(1024)(128)(4,1)S(1)}, s32[]{:S(2)}) async-start(s8[8388608]{0:T(1024)(128)(4,1)} %bitcast.38), calls=%async_computation | async-start | bytes 8388608
  85.1 20.5 %slice-start.1 = ((s8[8388608]{0:T(1024)(128)(4,1)}), s8[4194304]{0:T(1024)(128)(4,1)S(1)}, s32[]{:S(2)}) async-start(s8[8388608]{0:T(1024)(128)(4,1)} %bitcast.38), calls=%async_computation.1 | async-start | bytes 8388608
  85.1 3.3 %collective-permute-start.11 = (bf16[256,1024]{1,0:T(8,128)(2,1)S(1)}, bf16[256,1024]{1,0:T(8,128)(2,1)S(1)}, u32[]{:S(2)}, u32[]{:S(2)}) collective-permute-start(bf16[256,1024]{1,0:T(8,128)(2,1)S(1)} %collective-permute-done.10.refs_6_.refs_7_), channel_id=1, source_target_pairs={{0,1},{1,0},{2,3},{3,2},{4,5},{5,4},{6,7},{7,6},{8,9},{9,8},{10,11... | collective-permute-start | bytes 1572872 | tf_op jit(solution)/shard_map/ppermute | solution.py:558
  85.1 14.3 %collective-permute-start.13 = (bf16[256,1024]{1,0:T(8,128)(2,1)S(1)}, bf16[256,1024]{1,0:T(8,128)(2,1)S(1)}, u32[]{:S(2)}, u32[]{:S(2)}) collective-permute-start(bf16[256,1024]{1,0:T(8,128)(2,1)S(1)} %copy-done.24), channel_id=1, source_target_pairs={{0,2},{1,3},{2,0},{3,1},{4,6},{5,7},{6,4},{7,5},{8,10},{9,11},{10,... | collective-permute-start | bytes 1572872 | tf_op jit(solution)/shard_map/ppermute | solution.py:558
  86.9 34.9 %collective-permute-start.15 = (bf16[4,1024,128]{2,1,0:T(8,128)(2,1)S(1)}, bf16[4,1024,128]{2,1,0:T(8,128)(2,1)S(1)}, u32[]{:S(2)}, u32[]{:S(2)}) collective-permute-start(bf16[4,1024,128]{2,1,0:T(8,128)(2,1)S(1)} %get-tuple-element.105), channel_id=1, source_target_pairs={{0,4},{4,0},{8,12},{12,8},{16,20},{20,16},{24,28},{28,24},{1,5},{5... | collective-permute-start | bytes 3145736 | tf_op jit(solution)/shard_map/ppermute | solution.py:561
  99.4 15.5 %collective-permute-start.14 = (bf16[256,1024]{1,0:T(8,128)(2,1)S(1)}, bf16[256,1024]{1,0:T(8,128)(2,1)S(1)}, u32[]{:S(2)}, u32[]{:S(2)}) collective-permute-start(bf16[256,1024]{1,0:T(8,128)(2,1)S(1)} %collective-permute-done.13.refs_6_.refs_3_), channel_id=1, source_target_pairs={{0,1},{1,0},{2,3},{3,2},{4,5},{5,4},{6,7},{7,6},{8,9},{9,8},{10,11... | collective-permute-start | bytes 1572872 | tf_op jit(solution)/shard_map/ppermute | solution.py:558
  99.4 49.9 %collective-permute-start.18 = (bf16[4,1024,128]{2,1,0:T(8,128)(2,1)}, bf16[4,1024,128]{2,1,0:T(8,128)(2,1)}, u32[]{:S(2)}, u32[]{:S(2)}) collective-permute-start(bf16[4,1024,128]{2,1,0:T(8,128)(2,1)} %get-tuple-element.110), channel_id=1, source_target_pairs={{0,4},{4,0},{8,12},{12,8},{16,20},{20,16},{24,28},{28,24},{1,5},{5... | collective-permute-start | bytes 3145736 | tf_op jit(solution)/shard_map/ppermute | solution.py:561
  103.0 43.6 %collective-permute-start.16 = (bf16[2,1024,128]{2,1,0:T(8,128)(2,1)}, bf16[2,1024,128]{2,1,0:T(8,128)(2,1)}, u32[]{:S(2)}, u32[]{:S(2)}) collective-permute-start(bf16[2,1024,128]{2,1,0:T(8,128)(2,1)} %get-tuple-element.112), channel_id=1, source_target_pairs={{0,16},{4,20},{8,24},{12,28},{16,0},{20,4},{24,8},{28,12},{1,17},{... | collective-permute-start | bytes 1572872 | tf_op jit(solution)/shard_map/ppermute | solution.py:561
  122.7 25.0 %collective-permute-start.17 = (bf16[2,1024,128]{2,1,0:T(8,128)(2,1)}, bf16[2,1024,128]{2,1,0:T(8,128)(2,1)S(1)}, u32[]{:S(2)}, u32[]{:S(2)}) collective-permute-start(bf16[2,1024,128]{2,1,0:T(8,128)(2,1)} %get-tuple-element.124), channel_id=1, source_target_pairs={{0,8},{4,12},{8,0},{12,4},{16,24},{20,28},{24,16},{28,20},{1,9},{5... | collective-permute-start | bytes 1572872 | tf_op jit(solution)/shard_map/ppermute | solution.py:561
  124.3 45.2 %collective-permute-start.21 = (bf16[4,1024,128]{2,1,0:T(8,128)(2,1)}, bf16[4,1024,128]{2,1,0:T(8,128)(2,1)}, u32[]{:S(2)}, u32[]{:S(2)}) collective-permute-start(bf16[4,1024,128]{2,1,0:T(8,128)(2,1)} %get-tuple-element.120), channel_id=1, source_target_pairs={{0,4},{4,0},{8,12},{12,8},{16,20},{20,16},{24,28},{28,24},{1,5},{5... | collective-permute-start | bytes 3145736 | tf_op jit(solution)/shard_map/ppermute | solution.py:561
  145.1 27.0 %collective-permute-start.23 = (bf16[2,256,768]{2,1,0:T(8,128)(2,1)}, bf16[2,256,768]{2,1,0:T(8,128)(2,1)}, u32[]{:S(2)}, u32[]{:S(2)}) collective-permute-start(bf16[2,256,768]{2,1,0:T(8,128)(2,1)} %slice.57), channel_id=1, source_target_pairs={{0,2},{1,3},{2,0},{3,1},{4,6},{5,7},{6,4},{7,5},{8,10},{9,11},{10,... | collective-permute-start | bytes 2359304 | tf_op jit(solution)/shard_map/ppermute | solution.py:558
  150.8 18.6 %collective-permute-start.20 = (bf16[2,1024,128]{2,1,0:T(8,128)(2,1)S(1)}, bf16[2,1024,128]{2,1,0:T(8,128)(2,1)S(1)}, u32[]{:S(2)}, u32[]{:S(2)}) collective-permute-start(bf16[2,1024,128]{2,1,0:T(8,128)(2,1)S(1)} %get-tuple-element.135), channel_id=1, source_target_pairs={{0,8},{4,12},{8,0},{12,4},{16,24},{20,28},{24,16},{28,20},{1,9},{5... | collective-permute-start | bytes 1572872 | tf_op jit(solution)/shard_map/ppermute | solution.py:561
  152.1 16.2 %collective-permute-start.19 = (bf16[1,1024,128]{2,1,0:T(8,128)(2,1)}, bf16[1,1024,128]{2,1,0:T(8,128)(2,1)S(1)}, u32[]{:S(2)}, u32[]{:S(2)}) collective-permute-start(bf16[1,1024,128]{2,1,0:T(8,128)(2,1)} %get-tuple-element.131), channel_id=1, source_target_pairs={{0,16},{4,20},{8,24},{12,28},{16,0},{20,4},{24,8},{28,12},{1,17},{... | collective-permute-start | bytes 786440 | tf_op jit(solution)/shard_map/ppermute | solution.py:561
  173.4 12.1 %collective-permute-start.24 = (bf16[2,256,768]{2,1,0:T(8,128)(2,1)S(1)}, bf16[2,256,768]{2,1,0:T(8,128)(2,1)S(1)}, u32[]{:S(2)}, u32[]{:S(2)}) collective-permute-start(bf16[2,256,768]{2,1,0:T(8,128)(2,1)S(1)} %pad_maximum_fusion), channel_id=1, source_target_pairs={{0,1},{1,0},{2,3},{3,2},{4,5},{5,4},{6,7},{7,6},{8,9},{9,8},{10,11... | collective-permute-start | bytes 2359304 | tf_op jit(solution)/shard_map/ppermute | solution.py:558
  173.5 20.6 %collective-permute-start.25 = (bf16[2,1024,128]{2,1,0:T(8,128)(2,1)S(1)}, bf16[2,1024,128]{2,1,0:T(8,128)(2,1)S(1)}, u32[]{:S(2)}, u32[]{:S(2)}) collective-permute-start(bf16[2,1024,128]{2,1,0:T(8,128)(2,1)S(1)} %get-tuple-element.144), channel_id=1, source_target_pairs={{0,8},{4,12},{8,0},{12,4},{16,24},{20,28},{24,16},{28,20},{1,9},{5... | collective-permute-start | bytes 1572872 | tf_op jit(solution)/shard_map/ppermute | solution.py:561
  176.1 33.3 %collective-permute-start.28 = (bf16[2,256,768]{2,1,0:T(8,128)(2,1)S(1)}, bf16[2,256,768]{2,1,0:T(8,128)(2,1)S(1)}, u32[]{:S(2)}, u32[]{:S(2)}) collective-permute-start(bf16[2,256,768]{2,1,0:T(8,128)(2,1)S(1)} %slice.63), channel_id=1, source_target_pairs={{0,2},{1,3},{2,0},{3,1},{4,6},{5,7},{6,4},{7,5},{8,10},{9,11},{10,... | collective-permute-start | bytes 2359304 | tf_op jit(solution)/shard_map/ppermute | solution.py:558
  176.6 8.1 %collective-permute-start.22 = (bf16[1,1024,128]{2,1,0:T(8,128)(2,1)S(1)}, bf16[1,1024,128]{2,1,0:T(8,128)(2,1)S(1)}, u32[]{:S(2)}, u32[]{:S(2)}) collective-permute-start(bf16[1,1024,128]{2,1,0:T(8,128)(2,1)S(1)} %get-tuple-element.129), channel_id=1, source_target_pairs={{0,4},{4,0},{8,12},{12,8},{16,20},{20,16},{24,28},{28,24},{1,5},{5... | collective-permute-start | bytes 786440 | tf_op jit(solution)/shard_map/ppermute | solution.py:561
  178.1 16.7 %collective-permute-start.26 = (bf16[1,1024,128]{2,1,0:T(8,128)(2,1)S(1)}, bf16[1,1024,128]{2,1,0:T(8,128)(2,1)S(1)}, u32[]{:S(2)}, u32[]{:S(2)}) collective-permute-start(bf16[1,1024,128]{2,1,0:T(8,128)(2,1)S(1)} %get-tuple-element.140), channel_id=1, source_target_pairs={{0,16},{4,20},{8,24},{12,28},{16,0},{20,4},{24,8},{28,12},{1,17},{... | collective-permute-start | bytes 786440 | tf_op jit(solution)/shard_map/ppermute | solution.py:561
  194.2 14.3 %collective-permute-start.27 = (bf16[1,1024,128]{2,1,0:T(8,128)(2,1)S(1)}, bf16[1,1024,128]{2,1,0:T(8,128)(2,1)S(1)}, u32[]{:S(2)}, u32[]{:S(2)}) collective-permute-start(bf16[1,1024,128]{2,1,0:T(8,128)(2,1)S(1)} %get-tuple-element.150), channel_id=1, source_target_pairs={{0,16},{4,20},{8,24},{12,28},{16,0},{20,4},{24,8},{28,12},{1,17},{... | collective-permute-start | bytes 786440 | tf_op jit(solution)/shard_map/ppermute | solution.py:561
  209.5 2.4 %collective-permute-start.29 = (bf16[2,256,768]{2,1,0:T(8,128)(2,1)S(1)}, bf16[2,256,768]{2,1,0:T(8,128)(2,1)S(1)}, u32[]{:S(2)}, u32[]{:S(2)}) collective-permute-start(bf16[2,256,768]{2,1,0:T(8,128)(2,1)S(1)} %pad_maximum_fusion.1), channel_id=1, source_target_pairs={{0,1},{1,0},{2,3},{3,2},{4,5},{5,4},{6,7},{7,6},{8,9},{9,8},{10,11... | collective-permute-start | bytes 2359304 | tf_op jit(solution)/shard_map/ppermute | solution.py:558
  (26 other events, 183.5 us)

commit v6 on v5

--- a/solution.py
+++ b/solution.py
@@ -272,7 +272,7 @@
             shape((wide, parts * block)),
             shape((parts, 8, GROUP * block), jnp.float32),
         ],
-        compiler_params=params(60),
+        compiler_params=params(24),
         cost_estimate=cost(2.5),
         name="attention",
     )(gate([info], token)[0], *[x for x, at in pieces])
@@ -359,7 +359,7 @@
             ],
         ),
         out_shape=shape((parts, block, cols)),
-        compiler_params=params(60),
+        compiler_params=params(32),
         cost_estimate=cost(1.0),
         name="attention_back",
     )(gate([info], token)[0], *[x for x, at in pieces], grads, out, lse)
@@ -434,7 +434,7 @@
             shape((half, groups * rows, width)),
         ],
         compiler_params=params(16),
-        cost_estimate=cost(0.3),
+        cost_estimate=cost(0.2),
         name="weight_terms",
     )(gate([info], token)[0], *outs, *near, *near, *chunk)
 
@@ -530,7 +530,7 @@
         out_specs=block,
         out_shape=shape((parts, rows, feats), jnp.bfloat16 if last else jnp.float32),
         compiler_params=params(24),
-        cost_estimate=cost(0.5),
+        cost_estimate=cost(0.2),
         name="project",
     )(gate([out_weight], token)[0], *near, *flat, *([] if first else [acc]))
 
@@ -657,31 +657,29 @@
         return out
 
     last = chunks - 1
-    for c in range(last):
+    for c in range(chunks):
+        if c > 1:
+            advance(c - 2)
         weigh(c)
-    receive(last)
-    advance(0)
-    if last:
-        project_step(list(range(last)), False)
-    weigh(last)
-    advance(1)
-    project_step([last], True)
+        if c == last and c > 1:
+            advance(0)
+        project_step([c], c == last)
     send_back(0)
-    for c in (0, 1, 2):
-        advance(c)
+    advance(last - 2)
+    advance(last - 1)
     for gp in range(1, groups):
         send_back(gp)
-    advance(1)
-    advance(2)
-    advance(3)
+    advance(last - 1)
+    advance(last - 2)
+    advance(last)
     firsts = hand_over(0, token)
     advance(0)
     token = (token, firsts[1])
-    advance(3)
+    advance(last)
+    lasts = [hand_over(gp, token) for gp in range(1, groups)]
     for _ in bits:
         for c in range(chunks):
             advance(c)
-    lasts = [hand_over(gp, token) for gp in range(1, groups)]
     back = firsts + [x for group in lasts for x in group]
     grad_q, grad_k, grad_v = unpack(gate([info], token)[0], back, parts, groups)
     return (grad_q[None], grad_k[None], grad_v[None], weight_grad)

time: 216 us -> 220 us (1.019)
  waiting for transfers between devices: 69.1 us -> 81 us
  local copies, waits for them, and re-layouts: 14.6 us -> 6.44 us
  starting transfers between devices: 32.4 us -> 35 us
    ppermute x12, waiting for transfers between devices: 30 us -> 57.8 us  [over_dp(): return lax.ppermute(x, 'dp', [(i, i ^ d) for i in range(shares)])]
    ppermute x18, waiting for transfers between devices: 39.1 us -> 23.3 us  [over_seq(): return lax.ppermute(x, 'seq', [(i, i ^ d) for i in range(parts)])]
    pallas_call x2 -> x4, Pallas kernels: 14.6 us -> 21.3 us  [project(): pl.pallas_call(functools.partial(project_kernel, parts, shares, width, le...]
    pallas_call x8, Pallas kernels: 6.54 us -> 1.89 us  [merge(): pl.pallas_call(merge_kernel, grid=(half,), in_specs=[low, high, low, high...]
    unnamed x56 -> x34, local copies, waits for them, and re-layouts: 10 us -> 6.02 us
    pallas_call x2, Pallas kernels: 22.9 us -> 20.5 us  [attention_back(): pl.pallas_call(functools.partial(backward_kernel, parts, block, docs), gr...]
  transfers between devices with their start and end apart: 30 -> 30, of which waited for: 14 -> 17; matrix products, arithmetic and copies ran while one was open for 2% -> 0% of each run, Pallas kernels for 43% -> 41%
where the time goes in v6:
time: 220 us; the launch traced here: 219 us
  Pallas kernels  95.5 us (43%)
  waiting for transfers between devices  81 us (37%)
  starting transfers between devices  35 us (16%)
  local copies, waits for them, and re-layouts  6.44 us (3%)
    ppermute x12, waiting for transfers between devices, over_dp(): return lax.ppermute(x, 'dp', [(i, i ^ d) for i in range(shares)])  57.8 us
    ppermute x18, waiting for transfers between devices, over_seq(): return lax.ppermute(x, 'seq', [(i, i ^ d) for i in range(parts)])  23.3 us
    pallas_call x4, Pallas kernels, project(): pl.pallas_call(functools.partial(project_kernel, parts, shares, width, le...  21.3 us
    pallas_call x4, Pallas kernels, weight_terms(): pl.pallas_call(functools.partial(weight_kernel, parts, groups, width, ord...  20.8 us
    pallas_call x2, Pallas kernels, attention_back(): pl.pallas_call(functools.partial(backward_kernel, parts, block, docs), gr...  20.5 us
    ppermute x12, starting transfers between devices, over_dp(): return lax.ppermute(x, 'dp', [(i, i ^ d) for i in range(shares)])  18.7 us
    ppermute x18, starting transfers between devices, over_seq(): return lax.ppermute(x, 'seq', [(i, i ^ d) for i in range(parts)])  16.3 us
    pallas_call x2, Pallas kernels, attention(): pl.pallas_call(functools.partial(forward_kernel, parts, block, docs), gri...  15.8 us
  transfers between devices with their start and end apart: 30, of which 17 were waited for; matrix products, arithmetic and copies ran while one was open for 0% of the time, Pallas kernels for 41%

profile of v6, /device:TPU:0, one launch (start us, length us, event | category | flops | bytes accessed | tf_op | source)
XLA Modules:
  0.0 219.2 jit_solution(5531635483024879885)
XLA Ops:
  0.6 2.1 pack.2
  2.7 2.4 %collective-permute-start.2 = (bf16[256,768]{1,0:T(8,128)(2,1)}, bf16[256,768]{1,0:T(8,128)(2,1)S(1)}, u32[]{:S(2)}, u32[]{:S(2)}) collective-permute-start(bf16[256,768]{1,0:T(8,128)(2,1)} %get-tuple-element.90), channel_id=1, source_target_pairs={{0,3},{1,2},{2,1},{3,0},{4,7},{5,6},{6,5},{7,4},{8,11},{9,10},{10,... | collective-permute-start | bytes 1179656 | tf_op jit(solution)/shard_map/ppermute | solution.py:558
  5.8 3.0 %pack.3 = (bf16[256,1536]{1,0:T(8,128)(2,1)}, bf16[256,1536]{1,0:T(8,128)(2,1)}, bf16[256,768]{1,0:T(8,128)(2,1)}, bf16[256,768]{1,0:T(8,128)(2,1)}) custom-call(s32[1]{0:T(128)} %bitcast.me_ref, bf16[256,4096]{1,0:T(8,128)(2,1)} %bitcast.44, bf16[256,1024]{1,0:T(8,128)(2,1)} %bitcast.52, bf16[256,1024]{1,0:T(8,128)(2,1)} %bitcast.60, ...), custom_call_target="tpu_custom_call" | custom-call | flops 200000000 | bytes 1024 | tf_op jit(solution)/shard_map/pack/pallas_call | solution.py:79
  8.8 4.0 %pack_chunks.1 = (bf16[256,1024]{1,0:T(8,128)(2,1)}, bf16[256,1024]{1,0:T(8,128)(2,1)}, bf16[256,1024]{1,0:T(8,128)(2,1)}, bf16[256,1024]{1,0:T(8,128)(2,1)}) custom-call(bf16[256,4096]{1,0:T(8,128)(2,1)} %bitcast.26), custom_call_target="tpu_custom_call" | custom-call | flops 200000000 | bytes 1024 | tf_op jit(solution)/shard_map/pack_chunks/pallas_call | solution.py:110
  15.7 7.7 %collective-permute-done.1.refs_2_ = bf16[256,768]{1,0:T(8,128)(2,1)S(1)} collective-permute-done((bf16[256,768]{1,0:T(8,128)(2,1)}, bf16[256,768]{1,0:T(8,128)(2,1)S(1)}, u32[]{:S(2)}, u32[]{:S(2)}) %collective-permute-start.1) | collective-permute-done | bytes 393248 | tf_op jit(solution)/shard_map/ppermute | solution.py:558
  24.7 2.3 %collective-permute-start.4 = (bf16[256,768]{1,0:T(8,128)(2,1)}, bf16[256,768]{1,0:T(8,128)(2,1)S(1)}, u32[]{:S(2)}, u32[]{:S(2)}) collective-permute-start(bf16[256,768]{1,0:T(8,128)(2,1)} %get-tuple-element.94), channel_id=1, source_target_pairs={{0,2},{1,3},{2,0},{3,1},{4,6},{5,7},{6,4},{7,5},{8,10},{9,11},{10,... | collective-permute-start | bytes 1179656 | tf_op jit(solution)/shard_map/ppermute | solution.py:558
  32.5 7.2 %attention.2 = (bf16[512,1024]{1,0:T(8,128)(2,1)S(1)}, f32[4,8,1024]{2,1,0:T(8,128)S(1)}) custom-call(s32[10]{0:T(128)S(1)} %pad_add_fusion.info_ref, bf16[256,1536]{1,0:T(8,128)(2,1)S(1)} %copy-done.3, bf16[256,1536]{1,0:T(8,128)(2,1)S(1)} %collective-permute-done.refs_1_, bf16[256,768]{1,0:T(8,128)(2,1)S(1)} %copy-done.9, bf16[256,768]{1,0:T(8,128)(2,1)S(1)} %copy-done.6), custom_call_target="tpu_custom_call" | custom-call | flops 2500000000 | bytes 1024 | tf_op jit(solution)/shard_map/attention/pallas_call | solution.py:250
  39.8 5.5 %collective-permute-done.5.refs_3_ = bf16[256,768]{1,0:T(8,128)(2,1)} collective-permute-done((bf16[256,768]{1,0:T(8,128)(2,1)}, bf16[256,768]{1,0:T(8,128)(2,1)}, u32[]{:S(2)}, u32[]{:S(2)}) %collective-permute-start.5) | collective-permute-done | bytes 393248 | tf_op jit(solution)/shard_map/ppermute | solution.py:558
  45.3 8.6 %attention.3 = (bf16[512,1024]{1,0:T(8,128)(2,1)S(1)}, f32[4,8,1024]{2,1,0:T(8,128)S(1)}) custom-call(s32[10]{0:T(128)S(1)} %pad_add_fusion.info_ref, bf16[256,1536]{1,0:T(8,128)(2,1)S(1)} %copy-done.3, bf16[256,1536]{1,0:T(8,128)(2,1)S(1)} %collective-permute-done.refs_1_, bf16[256,768]{1,0:T(8,128)(2,1)S(1)} %collective-permute-done.4.refs_2_, ...), custom_call_target="tpu_custom_call" | custom-call | flops 2500000000 | bytes 1024 | tf_op jit(solution)/shard_map/attention/pallas_call | solution.py:250
  53.8 2.4 %collective-permute-done.6.refs_6_.refs_3_ = bf16[256,1024]{1,0:T(8,128)(2,1)S(1)} collective-permute-done((bf16[256,1024]{1,0:T(8,128)(2,1)}, bf16[256,1024]{1,0:T(8,128)(2,1)S(1)}, u32[]{:S(2)}, u32[]{:S(2)}) %collective-permute-start.6) | collective-permute-done | bytes 524320 | tf_op jit(solution)/shard_map/ppermute | solution.py:558
  58.2 4.8 %weight_terms.4 = (f32[4,1024,128]{2,1,0:T(8,128)S(1)}, bf16[4,1024,128]{2,1,0:T(8,128)(2,1)S(1)}) custom-call(s32[10]{0:T(128)S(1)} %pad_add_fusion.info_ref, bf16[512,1024]{1,0:T(8,128)(2,1)S(1)} %get-tuple-element.91.refs_0_.refs_5_, bf16[512,1024]{1,0:T(8,128)(2,1)S(1)} %get-tuple-element.96.refs_1_.refs_5_, bf16[256,4096]{1,0:T(8,128)(2,1)S(1)} %bitcast.28, ...), custom_call_target="tpu_custom_call" | custom-call | flops 200000000 | bytes 1024 | tf_op jit(solution)/shard_map/weight_terms/pallas_call | solution.py:422
  64.9 5.2 %project.4.refs_5_ = f32[4,256,1024]{2,1,0:T(8,128)S(1)} custom-call(bf16[1024,4096]{1,0:T(8,128)(2,1)S(1)} %bitcast.41, bf16[256,4096]{1,0:T(8,128)(2,1)S(1)} %bitcast.30, bf16[256,4096]{1,0:T(8,128)(2,1)} %collective-permute-done.3.refs_3_.refs_5_.refs_2_, bf16[256,1024]{1,0:T(8,128)(2,1)S(1)} %collective-permute-done.6.refs_6_.refs_3_, ...), custom_call_target="tpu_custom_call" | custom-call | flops 200000000 | bytes 1024 | tf_op jit(solution)/shard_map/project/pallas_call | solution.py:521
  72.5 4.8 %weight_terms.5 = (f32[4,1024,128]{2,1,0:T(8,128)S(1)}, bf16[4,1024,128]{2,1,0:T(8,128)(2,1)S(1)}) custom-call(s32[10]{0:T(128)S(1)} %pad_add_fusion.info_ref, bf16[512,1024]{1,0:T(8,128)(2,1)S(1)} %get-tuple-element.91.refs_0_.refs_5_, bf16[512,1024]{1,0:T(8,128)(2,1)S(1)} %get-tuple-element.96.refs_1_.refs_5_, bf16[256,4096]{1,0:T(8,128)(2,1)S(1)} %bitcast.31, ...), custom_call_target="tpu_custom_call" | custom-call | flops 200000000 | bytes 1024 | tf_op jit(solution)/shard_map/weight_terms/pallas_call | solution.py:422
  79.1 5.3 %project.5.refs_5_ = f32[4,256,1024]{2,1,0:T(8,128)S(1)} custom-call(bf16[1024,4096]{1,0:T(8,128)(2,1)S(1)} %bitcast.41, bf16[256,4096]{1,0:T(8,128)(2,1)S(1)} %bitcast.33, bf16[256,4096]{1,0:T(8,128)(2,1)} %collective-permute-done.3.refs_3_.refs_5_.refs_2_, bf16[256,1024]{1,0:T(8,128)(2,1)S(1)} %collective-permute-done.8.refs_6_.refs_3_, ...), custom_call_target="tpu_custom_call" | custom-call | flops 200000000 | bytes 1024 | tf_op jit(solution)/shard_map/project/pallas_call | solution.py:521
  84.4 3.9 %collective-permute-done.10.got_low.got_high = bf16[4,1024,128]{2,1,0:T(8,128)(2,1)S(1)} collective-permute-done((bf16[4,1024,128]{2,1,0:T(8,128)(2,1)S(1)}, bf16[4,1024,128]{2,1,0:T(8,128)(2,1)S(1)}, u32[]{:S(2)}, u32[]{:S(2)}) %collective-permute-start.10) | collective-permute-done | bytes 1048608 | tf_op jit(solution)/shard_map/ppermute | solution.py:561
  90.5 5.5 %weight_terms.6 = (f32[4,1024,128]{2,1,0:T(8,128)S(1)}, bf16[4,1024,128]{2,1,0:T(8,128)(2,1)}) custom-call(s32[10]{0:T(128)S(1)} %pad_add_fusion.info_ref, bf16[512,1024]{1,0:T(8,128)(2,1)S(1)} %get-tuple-element.91.refs_0_.refs_5_, bf16[512,1024]{1,0:T(8,128)(2,1)S(1)} %get-tuple-element.96.refs_1_.refs_5_, bf16[256,4096]{1,0:T(8,128)(2,1)S(1)} %bitcast.34, ...), custom_call_target="tpu_custom_call" | custom-call | flops 200000000 | bytes 1024 | tf_op jit(solution)/shard_map/weight_terms/pallas_call | solution.py:422
  97.4 5.3 %project.6.refs_5_ = f32[4,256,1024]{2,1,0:T(8,128)S(1)} custom-call(bf16[1024,4096]{1,0:T(8,128)(2,1)S(1)} %bitcast.41, bf16[256,4096]{1,0:T(8,128)(2,1)S(1)} %bitcast.36, bf16[256,4096]{1,0:T(8,128)(2,1)} %collective-permute-done.3.refs_3_.refs_5_.refs_2_, bf16[256,1024]{1,0:T(8,128)(2,1)S(1)} %collective-permute-done.11.refs_6_.refs_3_, ...), custom_call_target="tpu_custom_call" | custom-call | flops 200000000 | bytes 1024 | tf_op jit(solution)/shard_map/project/pallas_call | solution.py:521
  105.4 2.6 %collective-permute-start.16 = (bf16[2,1024,128]{2,1,0:T(8,128)(2,1)S(1)}, bf16[2,1024,128]{2,1,0:T(8,128)(2,1)S(1)}, u32[]{:S(2)}, u32[]{:S(2)}) collective-permute-start(bf16[2,1024,128]{2,1,0:T(8,128)(2,1)S(1)} %get-tuple-element.112), channel_id=1, source_target_pairs={{0,16},{4,20},{8,24},{12,28},{16,0},{20,4},{24,8},{28,12},{1,17},{... | collective-permute-start | bytes 1572872 | tf_op jit(solution)/shard_map/ppermute | solution.py:561
  109.6 5.5 %weight_terms.7 = (f32[4,1024,128]{2,1,0:T(8,128)S(1)}, bf16[4,1024,128]{2,1,0:T(8,128)(2,1)}) custom-call(s32[10]{0:T(128)S(1)} %pad_add_fusion.info_ref, bf16[512,1024]{1,0:T(8,128)(2,1)S(1)} %get-tuple-element.91.refs_0_.refs_5_, bf16[512,1024]{1,0:T(8,128)(2,1)S(1)} %get-tuple-element.96.refs_1_.refs_5_, bf16[256,4096]{1,0:T(8,128)(2,1)S(1)} %bitcast.37, ...), custom_call_target="tpu_custom_call" | custom-call | flops 200000000 | bytes 1024 | tf_op jit(solution)/shard_map/weight_terms/pallas_call | solution.py:422
  115.6 15.9 %collective-permute-done.16.got_low.got_high = bf16[2,1024,128]{2,1,0:T(8,128)(2,1)S(1)} collective-permute-done((bf16[2,1024,128]{2,1,0:T(8,128)(2,1)S(1)}, bf16[2,1024,128]{2,1,0:T(8,128)(2,1)S(1)}, u32[]{:S(2)}, u32[]{:S(2)}) %collective-permute-start.16) | collective-permute-done | bytes 524320 | tf_op jit(solution)/shard_map/ppermute | solution.py:561
  131.7 5.5 %project.7.refs_4_ = bf16[4,256,1024]{2,1,0:T(8,128)(2,1)S(1)} custom-call(bf16[1024,4096]{1,0:T(8,128)(2,1)S(1)} %bitcast.41, bf16[256,4096]{1,0:T(8,128)(2,1)S(1)} %bitcast.39, bf16[256,4096]{1,0:T(8,128)(2,1)} %collective-permute-done.3.refs_3_.refs_5_.refs_2_, bf16[256,1024]{1,0:T(8,128)(2,1)S(1)} %collective-permute-done.14.refs_6_.refs_3_, ...), custom_call_target="tpu_custom_call" | custom-call | flops 200000000 | bytes 1024 | tf_op jit(solution)/shard_map/project/pallas_call | solution.py:521
  137.2 9.7 %attention_back.2 = bf16[4,256,768]{2,1,0:T(8,128)(2,1)S(1)} custom-call(s32[10]{0:T(128)S(1)} %pad_add_fusion.info_ref, bf16[256,1536]{1,0:T(8,128)(2,1)S(1)} %copy-done.4, bf16[256,1536]{1,0:T(8,128)(2,1)S(1)} %collective-permute-done.refs_1_, bf16[256,768]{1,0:T(8,128)(2,1)S(1)} %copy-done.10, bf16[256,768]{1,0:T(8,128)(2,1)S(1)} %copy-done.7, ...), custom_call_target="tpu_custom_call" | custom-call | flops 1000000000 | bytes 1024 | tf_op jit(solution)/shard_map/attention_back/pallas_call | solution.py:336
  149.1 3.1 %collective-permute-start.20 = (bf16[1,1024,128]{2,1,0:T(8,128)(2,1)S(1)}, bf16[1,1024,128]{2,1,0:T(8,128)(2,1)S(1)}, u32[]{:S(2)}, u32[]{:S(2)}) collective-permute-start(bf16[1,1024,128]{2,1,0:T(8,128)(2,1)S(1)} %get-tuple-element.136), channel_id=1, source_target_pairs={{0,16},{4,20},{8,24},{12,28},{16,0},{20,4},{24,8},{28,12},{1,17},{... | collective-permute-start | bytes 786440 | tf_op jit(solution)/shard_map/ppermute | solution.py:561
  152.2 10.7 %attention_back.3 = bf16[4,256,768]{2,1,0:T(8,128)(2,1)S(1)} custom-call(s32[10]{0:T(128)S(1)} %pad_add_fusion.info_ref, bf16[256,1536]{1,0:T(8,128)(2,1)S(1)} %copy-done.4, bf16[256,1536]{1,0:T(8,128)(2,1)S(1)} %collective-permute-done.refs_1_, bf16[256,768]{1,0:T(8,128)(2,1)S(1)} %collective-permute-done.4.refs_2_, ...), custom_call_target="tpu_custom_call" | custom-call | flops 1000000000 | bytes 1024 | tf_op jit(solution)/shard_map/attention_back/pallas_call | solution.py:336
  163.0 4.4 %collective-permute-done.19.got_low.got_high = bf16[2,1024,128]{2,1,0:T(8,128)(2,1)S(1)} collective-permute-done((bf16[2,1024,128]{2,1,0:T(8,128)(2,1)S(1)}, bf16[2,1024,128]{2,1,0:T(8,128)(2,1)S(1)}, u32[]{:S(2)}, u32[]{:S(2)}) %collective-permute-start.19) | collective-permute-done | bytes 524320 | tf_op jit(solution)/shard_map/ppermute | solution.py:561
  170.5 2.1 collective-permute-start.25
  173.2 7.6 %collective-permute-done.22.got_ref = bf16[1,1024,128]{2,1,0:T(8,128)(2,1)S(1)} collective-permute-done((bf16[1,1024,128]{2,1,0:T(8,128)(2,1)S(1)}, bf16[1,1024,128]{2,1,0:T(8,128)(2,1)S(1)}, u32[]{:S(2)}, u32[]{:S(2)}) %collective-permute-start.22) | collective-permute-done | bytes 262176 | tf_op jit(solution)/shard_map/ppermute | solution.py:561
  181.7 3.3 %collective-permute-done.25.got_low.got_high = bf16[2,1024,128]{2,1,0:T(8,128)(2,1)S(1)} collective-permute-done((bf16[2,1024,128]{2,1,0:T(8,128)(2,1)S(1)}, bf16[2,1024,128]{2,1,0:T(8,128)(2,1)S(1)}, u32[]{:S(2)}, u32[]{:S(2)}) %collective-permute-start.25) | collective-permute-done | bytes 524320 | tf_op jit(solution)/shard_map/ppermute | solution.py:561
  185.0 3.9 %collective-permute-done.28 = bf16[2,256,768]{2,1,0:T(8,128)(2,1)S(1)} collective-permute-done((bf16[2,256,768]{2,1,0:T(8,128)(2,1)S(1)}, bf16[2,256,768]{2,1,0:T(8,128)(2,1)S(1)}, u32[]{:S(2)}, u32[]{:S(2)}) %collective-permute-start.28) | collective-permute-done | bytes 786464 | tf_op jit(solution)/shard_map/ppermute | solution.py:558
  192.1 18.3 %collective-permute-done.26.got_ref = bf16[1,1024,128]{2,1,0:T(8,128)(2,1)S(1)} collective-permute-done((bf16[1,1024,128]{2,1,0:T(8,128)(2,1)S(1)}, bf16[1,1024,128]{2,1,0:T(8,128)(2,1)S(1)}, u32[]{:S(2)}, u32[]{:S(2)}) %collective-permute-start.26) | collective-permute-done | bytes 262176 | tf_op jit(solution)/shard_map/ppermute | solution.py:561
  211.2 4.3 %collective-permute-done.27.got_ref = bf16[1,1024,128]{2,1,0:T(8,128)(2,1)S(1)} collective-permute-done((bf16[1,1024,128]{2,1,0:T(8,128)(2,1)S(1)}, bf16[1,1024,128]{2,1,0:T(8,128)(2,1)S(1)}, u32[]{:S(2)}, u32[]{:S(2)}) %collective-permute-start.27) | collective-permute-done | bytes 262176 | tf_op jit(solution)/shard_map/ppermute | solution.py:561
  216.5 2.8 %unpack.1 = (bf16[256,4096]{1,0:T(8,128)(2,1)}, bf16[256,1024]{1,0:T(8,128)(2,1)}, bf16[256,1024]{1,0:T(8,128)(2,1)}) custom-call(s32[10]{0:T(128)S(1)} %pad_add_fusion.info_ref, bf16[256,768]{1,0:T(8,128)(2,1)S(1)} %get-tuple-element.164.refs_0_, bf16[256,768]{1,0:T(8,128)(2,1)S(1)} %get-tuple-element.171.refs_1_, ...), custom_call_target="tpu_custom_call" | custom-call | flops 200000000 | bytes 1024 | tf_op jit(solution)/shard_map/unpack/pallas_call | solution.py:142
  (102 shorter events, 38.1 us)
Async XLA Ops:
  2.7 12.2 %collective-permute-start.2 = (bf16[256,768]{1,0:T(8,128)(2,1)}, bf16[256,768]{1,0:T(8,128)(2,1)S(1)}, u32[]{:S(2)}, u32[]{:S(2)}) collective-permute-start(bf16[256,768]{1,0:T(8,128)(2,1)} %get-tuple-element.90), channel_id=1, source_target_pairs={{0,3},{1,2},{2,1},{3,0},{4,7},{5,6},{6,5},{7,4},{8,11},{9,10},{10,... | collective-permute-start | bytes 1179656 | tf_op jit(solution)/shard_map/ppermute | solution.py:558
  5.1 18.3 %collective-permute-start.1 = (bf16[256,768]{1,0:T(8,128)(2,1)}, bf16[256,768]{1,0:T(8,128)(2,1)S(1)}, u32[]{:S(2)}, u32[]{:S(2)}) collective-permute-start(bf16[256,768]{1,0:T(8,128)(2,1)} %get-tuple-element.83), channel_id=1, source_target_pairs={{0,2},{1,3},{2,0},{3,1},{4,6},{5,7},{6,4},{7,5},{8,10},{9,11},{10,... | collective-permute-start | bytes 1179656 | tf_op jit(solution)/shard_map/ppermute | solution.py:558
  8.8 19.7 %copy-start.11 = (s32[1,8]{1,0:T(1,128)S(1)}, s32[1,8]{1,0:T(1,128)}, u32[]{:S(2)}) copy-start(s32[1,8]{1,0:T(1,128)} %param.11) | copy-start | bytes 100
  24.2 15.5 %collective-permute-start.3 = (bf16[256,4096]{1,0:T(8,128)(2,1)S(1)}, bf16[256,4096]{1,0:T(8,128)(2,1)}, u32[]{:S(2)}, u32[]{:S(2)}) collective-permute-start(bf16[256,4096]{1,0:T(8,128)(2,1)S(1)} %bitcast.27), channel_id=1, source_target_pairs={{0,1},{1,0},{2,3},{3,2},{4,5},{5,4},{6,7},{7,6},{8,9},{9,8},{10,11... | collective-permute-start | bytes 6291464 | tf_op jit(solution)/shard_map/ppermute | solution.py:558
  24.2 5.1 %collective-permute-start = (bf16[256,1536]{1,0:T(8,128)(2,1)}, bf16[256,1536]{1,0:T(8,128)(2,1)S(1)}, u32[]{:S(2)}, u32[]{:S(2)}) collective-permute-start(bf16[256,1536]{1,0:T(8,128)(2,1)} %get-tuple-element.89), channel_id=1, source_target_pairs={{0,1},{1,0},{2,3},{3,2},{4,5},{5,4},{6,7},{7,6},{8,9},{9,8},{10,11... | collective-permute-start | bytes 2359304 | tf_op jit(solution)/shard_map/ppermute | solution.py:558
  24.7 15.0 %collective-permute-start.4 = (bf16[256,768]{1,0:T(8,128)(2,1)}, bf16[256,768]{1,0:T(8,128)(2,1)S(1)}, u32[]{:S(2)}, u32[]{:S(2)}) collective-permute-start(bf16[256,768]{1,0:T(8,128)(2,1)} %get-tuple-element.94), channel_id=1, source_target_pairs={{0,2},{1,3},{2,0},{3,1},{4,6},{5,7},{6,4},{7,5},{8,10},{9,11},{10,... | collective-permute-start | bytes 1179656 | tf_op jit(solution)/shard_map/ppermute | solution.py:558
  27.0 18.2 %collective-permute-start.5 = (bf16[256,768]{1,0:T(8,128)(2,1)}, bf16[256,768]{1,0:T(8,128)(2,1)}, u32[]{:S(2)}, u32[]{:S(2)}) collective-permute-start(bf16[256,768]{1,0:T(8,128)(2,1)} %get-tuple-element.95), channel_id=1, source_target_pairs={{0,3},{1,2},{2,1},{3,0},{4,7},{5,6},{6,5},{7,4},{8,11},{9,10},{10,... | collective-permute-start | bytes 1179656 | tf_op jit(solution)/shard_map/ppermute | solution.py:558
  27.0 29.2 %collective-permute-start.6 = (bf16[256,1024]{1,0:T(8,128)(2,1)}, bf16[256,1024]{1,0:T(8,128)(2,1)S(1)}, u32[]{:S(2)}, u32[]{:S(2)}) collective-permute-start(bf16[256,1024]{1,0:T(8,128)(2,1)} %get-tuple-element.99), channel_id=1, source_target_pairs={{0,2},{1,3},{2,0},{3,1},{4,6},{5,7},{6,4},{7,5},{8,10},{9,11},{10,... | collective-permute-start | bytes 1572872 | tf_op jit(solution)/shard_map/ppermute | solution.py:558
  45.3 19.6 %slice-start = ((s8[8388608]{0:T(1024)(128)(4,1)}), s8[4194304]{0:T(1024)(128)(4,1)S(1)}, s32[]{:S(2)}) async-start(s8[8388608]{0:T(1024)(128)(4,1)} %bitcast.40), calls=%async_computation | async-start | bytes 8388608
  56.3 1.9 collective-permute-start.7
  56.3 14.3 %collective-permute-start.8 = (bf16[256,1024]{1,0:T(8,128)(2,1)S(1)}, bf16[256,1024]{1,0:T(8,128)(2,1)S(1)}, u32[]{:S(2)}, u32[]{:S(2)}) collective-permute-start(bf16[256,1024]{1,0:T(8,128)(2,1)S(1)} %copy-done.14), channel_id=1, source_target_pairs={{0,2},{1,3},{2,0},{3,1},{4,6},{5,7},{6,4},{7,5},{8,10},{9,11},{10,... | collective-permute-start | bytes 1572872 | tf_op jit(solution)/shard_map/ppermute | solution.py:558
  63.1 25.3 %collective-permute-start.10 = (bf16[4,1024,128]{2,1,0:T(8,128)(2,1)S(1)}, bf16[4,1024,128]{2,1,0:T(8,128)(2,1)S(1)}, u32[]{:S(2)}, u32[]{:S(2)}) collective-permute-start(bf16[4,1024,128]{2,1,0:T(8,128)(2,1)S(1)} %get-tuple-element.101), channel_id=1, source_target_pairs={{0,8},{4,12},{8,0},{12,4},{16,24},{20,28},{24,16},{28,20},{1,9},{5... | collective-permute-start | bytes 3145736 | tf_op jit(solution)/shard_map/ppermute | solution.py:561
  70.6 1.9 collective-permute-start.9
  70.6 17.9 %collective-permute-start.11 = (bf16[256,1024]{1,0:T(8,128)(2,1)S(1)}, bf16[256,1024]{1,0:T(8,128)(2,1)S(1)}, u32[]{:S(2)}, u32[]{:S(2)}) collective-permute-start(bf16[256,1024]{1,0:T(8,128)(2,1)S(1)} %copy-done.13), channel_id=1, source_target_pairs={{0,2},{1,3},{2,0},{3,1},{4,6},{5,7},{6,4},{7,5},{8,10},{9,11},{10,... | collective-permute-start | bytes 1572872 | tf_op jit(solution)/shard_map/ppermute | solution.py:558
  77.4 25.3 %collective-permute-start.13 = (bf16[4,1024,128]{2,1,0:T(8,128)(2,1)S(1)}, bf16[4,1024,128]{2,1,0:T(8,128)(2,1)S(1)}, u32[]{:S(2)}, u32[]{:S(2)}) collective-permute-start(bf16[4,1024,128]{2,1,0:T(8,128)(2,1)S(1)} %get-tuple-element.109), channel_id=1, source_target_pairs={{0,4},{4,0},{8,12},{12,8},{16,20},{20,16},{24,28},{28,24},{1,5},{5... | collective-permute-start | bytes 3145736 | tf_op jit(solution)/shard_map/ppermute | solution.py:561
  88.5 2.0 collective-permute-start.12
  88.6 14.9 %collective-permute-start.14 = (bf16[256,1024]{1,0:T(8,128)(2,1)S(1)}, bf16[256,1024]{1,0:T(8,128)(2,1)S(1)}, u32[]{:S(2)}, u32[]{:S(2)}) collective-permute-start(bf16[256,1024]{1,0:T(8,128)(2,1)S(1)} %copy-done.12), channel_id=1, source_target_pairs={{0,2},{1,3},{2,0},{3,1},{4,6},{5,7},{6,4},{7,5},{8,10},{9,11},{10,... | collective-permute-start | bytes 1572872 | tf_op jit(solution)/shard_map/ppermute | solution.py:558
  103.6 6.0 %collective-permute-start.15 = (bf16[256,1024]{1,0:T(8,128)(2,1)S(1)}, bf16[256,1024]{1,0:T(8,128)(2,1)S(1)}, u32[]{:S(2)}, u32[]{:S(2)}) collective-permute-start(bf16[256,1024]{1,0:T(8,128)(2,1)S(1)} %collective-permute-done.14.refs_6_.refs_3_), channel_id=1, source_target_pairs={{0,1},{1,0},{2,3},{3,2},{4,5},{5,4},{6,7},{7,6},{8,9},{9,8},{10,11... | collective-permute-start | bytes 1572872 | tf_op jit(solution)/shard_map/ppermute | solution.py:558
  103.7 45.0 %collective-permute-start.18 = (bf16[4,1024,128]{2,1,0:T(8,128)(2,1)}, bf16[4,1024,128]{2,1,0:T(8,128)(2,1)S(1)}, u32[]{:S(2)}, u32[]{:S(2)}) collective-permute-start(bf16[4,1024,128]{2,1,0:T(8,128)(2,1)} %get-tuple-element.117), channel_id=1, source_target_pairs={{0,4},{4,0},{8,12},{12,8},{16,20},{20,16},{24,28},{28,24},{1,5},{5... | collective-permute-start | bytes 3145736 | tf_op jit(solution)/shard_map/ppermute | solution.py:561
  105.4 26.2 %collective-permute-start.16 = (bf16[2,1024,128]{2,1,0:T(8,128)(2,1)S(1)}, bf16[2,1024,128]{2,1,0:T(8,128)(2,1)S(1)}, u32[]{:S(2)}, u32[]{:S(2)}) collective-permute-start(bf16[2,1024,128]{2,1,0:T(8,128)(2,1)S(1)} %get-tuple-element.112), channel_id=1, source_target_pairs={{0,16},{4,20},{8,24},{12,28},{16,0},{20,4},{24,8},{28,12},{1,17},{... | collective-permute-start | bytes 1572872 | tf_op jit(solution)/shard_map/ppermute | solution.py:561
  108.0 40.7 %collective-permute-start.17 = (bf16[2,1024,128]{2,1,0:T(8,128)(2,1)}, bf16[2,1024,128]{2,1,0:T(8,128)(2,1)S(1)}, u32[]{:S(2)}, u32[]{:S(2)}) collective-permute-start(bf16[2,1024,128]{2,1,0:T(8,128)(2,1)} %get-tuple-element.120), channel_id=1, source_target_pairs={{0,8},{4,12},{8,0},{12,4},{16,24},{20,28},{24,16},{28,20},{1,9},{5... | collective-permute-start | bytes 1572872 | tf_op jit(solution)/shard_map/ppermute | solution.py:561
  115.1 53.3 %collective-permute-start.21 = (bf16[4,1024,128]{2,1,0:T(8,128)(2,1)}, bf16[4,1024,128]{2,1,0:T(8,128)(2,1)S(1)}, u32[]{:S(2)}, u32[]{:S(2)}) collective-permute-start(bf16[4,1024,128]{2,1,0:T(8,128)(2,1)} %get-tuple-element.127), channel_id=1, source_target_pairs={{0,4},{4,0},{8,12},{12,8},{16,20},{20,16},{24,28},{28,24},{1,5},{5... | collective-permute-start | bytes 3145736 | tf_op jit(solution)/shard_map/ppermute | solution.py:561
  147.0 21.6 %collective-permute-start.23 = (bf16[2,256,768]{2,1,0:T(8,128)(2,1)S(1)}, bf16[2,256,768]{2,1,0:T(8,128)(2,1)S(1)}, u32[]{:S(2)}, u32[]{:S(2)}) collective-permute-start(bf16[2,256,768]{2,1,0:T(8,128)(2,1)S(1)} %slice.57), channel_id=1, source_target_pairs={{0,2},{1,3},{2,0},{3,1},{4,6},{5,7},{6,4},{7,5},{8,10},{9,11},{10,... | collective-permute-start | bytes 2359304 | tf_op jit(solution)/shard_map/ppermute | solution.py:558
  149.0 18.4 %collective-permute-start.19 = (bf16[2,1024,128]{2,1,0:T(8,128)(2,1)S(1)}, bf16[2,1024,128]{2,1,0:T(8,128)(2,1)S(1)}, u32[]{:S(2)}, u32[]{:S(2)}) collective-permute-start(bf16[2,1024,128]{2,1,0:T(8,128)(2,1)S(1)} %get-tuple-element.139), channel_id=1, source_target_pairs={{0,8},{4,12},{8,0},{12,4},{16,24},{20,28},{24,16},{28,20},{1,9},{5... | collective-permute-start | bytes 1572872 | tf_op jit(solution)/shard_map/ppermute | solution.py:561
  149.1 18.5 %collective-permute-start.20 = (bf16[1,1024,128]{2,1,0:T(8,128)(2,1)S(1)}, bf16[1,1024,128]{2,1,0:T(8,128)(2,1)S(1)}, u32[]{:S(2)}, u32[]{:S(2)}) collective-permute-start(bf16[1,1024,128]{2,1,0:T(8,128)(2,1)S(1)} %get-tuple-element.136), channel_id=1, source_target_pairs={{0,16},{4,20},{8,24},{12,28},{16,0},{20,4},{24,8},{28,12},{1,17},{... | collective-permute-start | bytes 786440 | tf_op jit(solution)/shard_map/ppermute | solution.py:561
  168.7 12.9 %collective-permute-start.24 = (bf16[2,256,768]{2,1,0:T(8,128)(2,1)S(1)}, bf16[2,256,768]{2,1,0:T(8,128)(2,1)S(1)}, u32[]{:S(2)}, u32[]{:S(2)}) collective-permute-start(bf16[2,256,768]{2,1,0:T(8,128)(2,1)S(1)} %pad_maximum_fusion), channel_id=1, source_target_pairs={{0,1},{1,0},{2,3},{3,2},{4,5},{5,4},{6,7},{7,6},{8,9},{9,8},{10,11... | collective-permute-start | bytes 2359304 | tf_op jit(solution)/shard_map/ppermute | solution.py:558
  168.9 20.0 %collective-permute-start.28 = (bf16[2,256,768]{2,1,0:T(8,128)(2,1)S(1)}, bf16[2,256,768]{2,1,0:T(8,128)(2,1)S(1)}, u32[]{:S(2)}, u32[]{:S(2)}) collective-permute-start(bf16[2,256,768]{2,1,0:T(8,128)(2,1)S(1)} %slice.63), channel_id=1, source_target_pairs={{0,2},{1,3},{2,0},{3,1},{4,6},{5,7},{6,4},{7,5},{8,10},{9,11},{10,... | collective-permute-start | bytes 2359304 | tf_op jit(solution)/shard_map/ppermute | solution.py:558
  170.5 14.4 %collective-permute-start.25 = (bf16[2,1024,128]{2,1,0:T(8,128)(2,1)S(1)}, bf16[2,1024,128]{2,1,0:T(8,128)(2,1)S(1)}, u32[]{:S(2)}, u32[]{:S(2)}) collective-permute-start(bf16[2,1024,128]{2,1,0:T(8,128)(2,1)S(1)} %get-tuple-element.148), channel_id=1, source_target_pairs={{0,8},{4,12},{8,0},{12,4},{16,24},{20,28},{24,16},{28,20},{1,9},{5... | collective-permute-start | bytes 1572872 | tf_op jit(solution)/shard_map/ppermute | solution.py:561
  172.6 8.1 %collective-permute-start.22 = (bf16[1,1024,128]{2,1,0:T(8,128)(2,1)S(1)}, bf16[1,1024,128]{2,1,0:T(8,128)(2,1)S(1)}, u32[]{:S(2)}, u32[]{:S(2)}) collective-permute-start(bf16[1,1024,128]{2,1,0:T(8,128)(2,1)S(1)} %get-tuple-element.129), channel_id=1, source_target_pairs={{0,4},{4,0},{8,12},{12,8},{16,20},{20,16},{24,28},{28,24},{1,5},{5... | collective-permute-start | bytes 786440 | tf_op jit(solution)/shard_map/ppermute | solution.py:561
  189.0 27.4 %collective-permute-start.29 = (bf16[2,256,768]{2,1,0:T(8,128)(2,1)S(1)}, bf16[2,256,768]{2,1,0:T(8,128)(2,1)S(1)}, u32[]{:S(2)}, u32[]{:S(2)}) collective-permute-start(bf16[2,256,768]{2,1,0:T(8,128)(2,1)S(1)} %pad_maximum_fusion.1), channel_id=1, source_target_pairs={{0,1},{1,0},{2,3},{3,2},{4,5},{5,4},{6,7},{7,6},{8,9},{9,8},{10,11... | collective-permute-start | bytes 2359304 | tf_op jit(solution)/shard_map/ppermute | solution.py:558
  189.1 21.3 %collective-permute-start.26 = (bf16[1,1024,128]{2,1,0:T(8,128)(2,1)S(1)}, bf16[1,1024,128]{2,1,0:T(8,128)(2,1)S(1)}, u32[]{:S(2)}, u32[]{:S(2)}) collective-permute-start(bf16[1,1024,128]{2,1,0:T(8,128)(2,1)S(1)} %get-tuple-element.143), channel_id=1, source_target_pairs={{0,16},{4,20},{8,24},{12,28},{16,0},{20,4},{24,8},{28,12},{1,17},{... | collective-permute-start | bytes 786440 | tf_op jit(solution)/shard_map/ppermute | solution.py:561
  190.7 24.9 %collective-permute-start.27 = (bf16[1,1024,128]{2,1,0:T(8,128)(2,1)S(1)}, bf16[1,1024,128]{2,1,0:T(8,128)(2,1)S(1)}, u32[]{:S(2)}, u32[]{:S(2)}) collective-permute-start(bf16[1,1024,128]{2,1,0:T(8,128)(2,1)S(1)} %get-tuple-element.154), channel_id=1, source_target_pairs={{0,16},{4,20},{8,24},{12,28},{16,0},{20,4},{24,8},{28,12},{1,17},{... | collective-permute-start | bytes 786440 | tf_op jit(solution)/shard_map/ppermute | solution.py:561
  (15 other events, 76.8 us)

commit v7 on v6

--- a/solution.py
+++ b/solution.py
@@ -272,7 +272,7 @@
             shape((wide, parts * block)),
             shape((parts, 8, GROUP * block), jnp.float32),
         ],
-        compiler_params=params(24),
+        compiler_params=params(60),
         cost_estimate=cost(2.5),
         name="attention",
     )(gate([info], token)[0], *[x for x, at in pieces])
@@ -661,12 +661,10 @@
         if c > 1:
             advance(c - 2)
         weigh(c)
-        if c == last and c > 1:
-            advance(0)
         project_step([c], c == last)
     send_back(0)
-    advance(last - 2)
-    advance(last - 1)
+    for c in range(last):
+        advance(c)
     for gp in range(1, groups):
         send_back(gp)
     advance(last - 1)
@@ -674,6 +672,7 @@
     advance(last)
     firsts = hand_over(0, token)
     advance(0)
+    advance(last - 1)
     token = (token, firsts[1])
     advance(last)
     lasts = [hand_over(gp, token) for gp in range(1, groups)]

time: 220 us -> 199 us (0.905)
  waiting for transfers between devices: 81 us -> 54.6 us
  local copies, waits for them, and re-layouts: 6.44 us -> 12.2 us
  starting transfers between devices: 35 us -> 32.4 us
    ppermute x12, waiting for transfers between devices: 57.8 us -> 34.7 us  [over_dp(): return lax.ppermute(x, 'dp', [(i, i ^ d) for i in range(shares)])]
    unnamed x34 -> x50, local copies, waits for them, and re-layouts: 6.02 us -> 11.8 us
    ppermute x18, waiting for transfers between devices: 23.3 us -> 19.9 us  [over_seq(): return lax.ppermute(x, 'seq', [(i, i ^ d) for i in range(parts)])]
    pallas_call x2, Pallas kernels: 15.8 us -> 18.1 us  [attention(): pl.pallas_call(functools.partial(forward_kernel, parts, block, docs), gri...]
  transfers between devices with their start and end apart: 30 -> 30, of which waited for: 17 -> 15; matrix products, arithmetic and copies ran while one was open for 0% -> 0% of each run, Pallas kernels for 41% -> 46%
where the time goes in v7:
time: 199 us; the launch traced here: 198 us
  Pallas kernels  96.8 us (49%)
  waiting for transfers between devices  54.6 us (27%)
  starting transfers between devices  32.4 us (16%)
  local copies, waits for them, and re-layouts  12.2 us (6%)
    ppermute x12, waiting for transfers between devices, over_dp(): return lax.ppermute(x, 'dp', [(i, i ^ d) for i in range(shares)])  34.7 us
    pallas_call x4, Pallas kernels, project(): pl.pallas_call(functools.partial(project_kernel, parts, shares, width, le...  21.3 us
    pallas_call x4, Pallas kernels, weight_terms(): pl.pallas_call(functools.partial(weight_kernel, parts, groups, width, ord...  20.8 us
    ppermute x18, waiting for transfers between devices, over_seq(): return lax.ppermute(x, 'seq', [(i, i ^ d) for i in range(parts)])  19.9 us
    pallas_call x2, Pallas kernels, attention_back(): pl.pallas_call(functools.partial(backward_kernel, parts, block, docs), gr...  18.9 us
    pallas_call x2, Pallas kernels, attention(): pl.pallas_call(functools.partial(forward_kernel, parts, block, docs), gri...  18.1 us
    ppermute x12, starting transfers between devices, over_dp(): return lax.ppermute(x, 'dp', [(i, i ^ d) for i in range(shares)])  16.8 us
    ppermute x18, starting transfers between devices, over_seq(): return lax.ppermute(x, 'seq', [(i, i ^ d) for i in range(parts)])  15.7 us
  transfers between devices with their start and end apart: 30, of which 15 were waited for; matrix products, arithmetic and copies ran while one was open for 0% of the time, Pallas kernels for 46%

profile of v7, /device:TPU:0, one launch (start us, length us, event | category | flops | bytes accessed | tf_op | source)
XLA Modules:
  0.0 197.8 jit_solution(4894040638438677385)
XLA Ops:
  0.6 2.1 %pack.2 = (bf16[256,768]{1,0:T(8,128)(2,1)}, bf16[256,768]{1,0:T(8,128)(2,1)}) custom-call(s32[1]{0:T(128)} %bitcast.me_ref, bf16[256,4096]{1,0:T(8,128)(2,1)} %bitcast.42, bf16[256,1024]{1,0:T(8,128)(2,1)} %bitcast.50, bf16[256,1024]{1,0:T(8,128)(2,1)} %bitcast.58, bf16[256,4096]{1,0:T(8,128)(2,1)} %bitcast.43, bf16[256,1024]{1,0:T(8,128)(2,1)} %bitcast.51, ...), custom_call_target="tpu_custom_call" | custom-call | flops 200000000 | bytes 1024 | tf_op jit(solution)/shard_map/pack/pallas_call | solution.py:79
  2.7 2.4 %collective-permute-start.2 = (bf16[256,768]{1,0:T(8,128)(2,1)}, bf16[256,768]{1,0:T(8,128)(2,1)S(1)}, u32[]{:S(2)}, u32[]{:S(2)}) collective-permute-start(bf16[256,768]{1,0:T(8,128)(2,1)} %get-tuple-element.90), channel_id=1, source_target_pairs={{0,3},{1,2},{2,1},{3,0},{4,7},{5,6},{6,5},{7,4},{8,11},{9,10},{10,... | collective-permute-start | bytes 1179656 | tf_op jit(solution)/shard_map/ppermute | solution.py:558
  5.8 3.0 %pack.3 = (bf16[256,1536]{1,0:T(8,128)(2,1)}, bf16[256,1536]{1,0:T(8,128)(2,1)}, bf16[256,768]{1,0:T(8,128)(2,1)}, bf16[256,768]{1,0:T(8,128)(2,1)}) custom-call(s32[1]{0:T(128)} %bitcast.me_ref, bf16[256,4096]{1,0:T(8,128)(2,1)} %bitcast.44, bf16[256,1024]{1,0:T(8,128)(2,1)} %bitcast.52, bf16[256,1024]{1,0:T(8,128)(2,1)} %bitcast.60, ...), custom_call_target="tpu_custom_call" | custom-call | flops 200000000 | bytes 1024 | tf_op jit(solution)/shard_map/pack/pallas_call | solution.py:79
  8.8 4.0 %pack_chunks.1 = (bf16[256,1024]{1,0:T(8,128)(2,1)}, bf16[256,1024]{1,0:T(8,128)(2,1)}, bf16[256,1024]{1,0:T(8,128)(2,1)}, bf16[256,1024]{1,0:T(8,128)(2,1)}) custom-call(bf16[256,4096]{1,0:T(8,128)(2,1)} %bitcast.26), custom_call_target="tpu_custom_call" | custom-call | flops 200000000 | bytes 1024 | tf_op jit(solution)/shard_map/pack_chunks/pallas_call | solution.py:110
  12.8 2.1 %collective-permute-done.2.refs_3_ = bf16[256,768]{1,0:T(8,128)(2,1)S(1)} collective-permute-done((bf16[256,768]{1,0:T(8,128)(2,1)}, bf16[256,768]{1,0:T(8,128)(2,1)S(1)}, u32[]{:S(2)}, u32[]{:S(2)}) %collective-permute-start.2) | collective-permute-done | bytes 393248 | tf_op jit(solution)/shard_map/ppermute | solution.py:558
  15.0 8.5 %collective-permute-done.1.refs_2_ = bf16[256,768]{1,0:T(8,128)(2,1)S(1)} collective-permute-done((bf16[256,768]{1,0:T(8,128)(2,1)}, bf16[256,768]{1,0:T(8,128)(2,1)S(1)}, u32[]{:S(2)}, u32[]{:S(2)}) %collective-permute-start.1) | collective-permute-done | bytes 393248 | tf_op jit(solution)/shard_map/ppermute | solution.py:558
  24.2 2.4 %collective-permute-start.4 = (bf16[256,768]{1,0:T(8,128)(2,1)}, bf16[256,768]{1,0:T(8,128)(2,1)S(1)}, u32[]{:S(2)}, u32[]{:S(2)}) collective-permute-start(bf16[256,768]{1,0:T(8,128)(2,1)} %get-tuple-element.94), channel_id=1, source_target_pairs={{0,2},{1,3},{2,0},{3,1},{4,6},{5,7},{6,4},{7,5},{8,10},{9,11},{10,... | collective-permute-start | bytes 1179656 | tf_op jit(solution)/shard_map/ppermute | solution.py:558
  29.9 9.0 %attention.2 = (bf16[512,1024]{1,0:T(8,128)(2,1)}, f32[4,8,1024]{2,1,0:T(8,128)}) custom-call(s32[10]{0:T(128)} %pad_add_fusion.info_ref, bf16[256,1536]{1,0:T(8,128)(2,1)} %get-tuple-element.85.refs_0_, bf16[256,1536]{1,0:T(8,128)(2,1)} %copy-done.9, bf16[256,768]{1,0:T(8,128)(2,1)} %copy-done.15, bf16[256,768]{1,0:T(8,128)(2,1)} %copy-done.13), custom_call_target="tpu_custom_call" | custom-call | flops 2500000000 | bytes 1024 | tf_op jit(solution)/shard_map/attention/pallas_call | solution.py:250
  39.0 5.8 %collective-permute-done.5.refs_3_ = bf16[256,768]{1,0:T(8,128)(2,1)} collective-permute-done((bf16[256,768]{1,0:T(8,128)(2,1)}, bf16[256,768]{1,0:T(8,128)(2,1)}, u32[]{:S(2)}, u32[]{:S(2)}) %collective-permute-start.5) | collective-permute-done | bytes 393248 | tf_op jit(solution)/shard_map/ppermute | solution.py:558
  44.8 9.0 %attention.3 = (bf16[512,1024]{1,0:T(8,128)(2,1)}, f32[4,8,1024]{2,1,0:T(8,128)}) custom-call(s32[10]{0:T(128)} %pad_add_fusion.info_ref, bf16[256,1536]{1,0:T(8,128)(2,1)} %get-tuple-element.85.refs_0_, bf16[256,1536]{1,0:T(8,128)(2,1)} %copy-done.9, bf16[256,768]{1,0:T(8,128)(2,1)} %copy-done.11, bf16[256,768]{1,0:T(8,128)(2,1)} %collective-permute-done.5.refs_3_), custom_call_target="tpu_custom_call" | custom-call | flops 2500000000 | bytes 1024 | tf_op jit(solution)/shard_map/attention/pallas_call | solution.py:250
  53.8 2.4 %collective-permute-done.6.refs_6_.refs_3_ = bf16[256,1024]{1,0:T(8,128)(2,1)S(1)} collective-permute-done((bf16[256,1024]{1,0:T(8,128)(2,1)}, bf16[256,1024]{1,0:T(8,128)(2,1)S(1)}, u32[]{:S(2)}, u32[]{:S(2)}) %collective-permute-start.6) | collective-permute-done | bytes 524320 | tf_op jit(solution)/shard_map/ppermute | solution.py:558
  59.3 4.8 %weight_terms.4 = (f32[4,1024,128]{2,1,0:T(8,128)S(1)}, bf16[4,1024,128]{2,1,0:T(8,128)(2,1)S(1)}) custom-call(s32[10]{0:T(128)S(1)} %copy-done.19, bf16[512,1024]{1,0:T(8,128)(2,1)S(1)} %copy-done.5, bf16[512,1024]{1,0:T(8,128)(2,1)S(1)} %copy-done.3, bf16[256,4096]{1,0:T(8,128)(2,1)S(1)} %bitcast.28, ...), custom_call_target="tpu_custom_call" | custom-call | flops 200000000 | bytes 1024 | tf_op jit(solution)/shard_map/weight_terms/pallas_call | solution.py:422
  64.1 1.9 collective-permute-start.10
  66.0 3.4 %copy-done.1 = bf16[1024,4096]{1,0:T(8,128)(2,1)S(1)} copy-done((bf16[1024,4096]{1,0:T(8,128)(2,1)S(1)}, bf16[1024,4096]{1,0:T(8,128)(2,1)}, u32[]{:S(2)}) %copy-start.1) | copy-done | bytes 8388632
  69.4 5.3 %project.4.refs_5_ = f32[4,256,1024]{2,1,0:T(8,128)S(1)} custom-call(bf16[1024,4096]{1,0:T(8,128)(2,1)S(1)} %copy-done.1, bf16[256,4096]{1,0:T(8,128)(2,1)S(1)} %bitcast.30, bf16[256,4096]{1,0:T(8,128)(2,1)} %collective-permute-done.3.refs_3_.refs_5_.refs_2_, bf16[256,1024]{1,0:T(8,128)(2,1)S(1)} %collective-permute-done.6.refs_6_.refs_3_, ...), custom_call_target="tpu_custom_call" | custom-call | flops 200000000 | bytes 1024 | tf_op jit(solution)/shard_map/project/pallas_call | solution.py:521
  76.7 4.8 %weight_terms.5 = (f32[4,1024,128]{2,1,0:T(8,128)S(1)}, bf16[4,1024,128]{2,1,0:T(8,128)(2,1)S(1)}) custom-call(s32[10]{0:T(128)S(1)} %copy-done.19, bf16[512,1024]{1,0:T(8,128)(2,1)S(1)} %copy-done.5, bf16[512,1024]{1,0:T(8,128)(2,1)S(1)} %copy-done.4, bf16[256,4096]{1,0:T(8,128)(2,1)S(1)} %bitcast.31, ...), custom_call_target="tpu_custom_call" | custom-call | flops 200000000 | bytes 1024 | tf_op jit(solution)/shard_map/weight_terms/pallas_call | solution.py:422
  83.1 3.4 %copy-done.2 = bf16[1024,4096]{1,0:T(8,128)(2,1)S(1)} copy-done((bf16[1024,4096]{1,0:T(8,128)(2,1)S(1)}, bf16[1024,4096]{1,0:T(8,128)(2,1)}, u32[]{:S(2)}) %copy-start.2) | copy-done | bytes 8388632
  86.5 5.3 %project.5.refs_5_ = f32[4,256,1024]{2,1,0:T(8,128)S(1)} custom-call(bf16[1024,4096]{1,0:T(8,128)(2,1)S(1)} %copy-done.2, bf16[256,4096]{1,0:T(8,128)(2,1)S(1)} %bitcast.33, bf16[256,4096]{1,0:T(8,128)(2,1)} %collective-permute-done.3.refs_3_.refs_5_.refs_2_, bf16[256,1024]{1,0:T(8,128)(2,1)S(1)} %collective-permute-done.8.refs_6_.refs_3_, ...), custom_call_target="tpu_custom_call" | custom-call | flops 200000000 | bytes 1024 | tf_op jit(solution)/shard_map/project/pallas_call | solution.py:521
  95.7 5.5 %weight_terms.6 = (f32[4,1024,128]{2,1,0:T(8,128)S(1)}, bf16[4,1024,128]{2,1,0:T(8,128)(2,1)}) custom-call(s32[10]{0:T(128)S(1)} %copy-done.19, bf16[512,1024]{1,0:T(8,128)(2,1)S(1)} %copy-done.5, bf16[512,1024]{1,0:T(8,128)(2,1)S(1)} %copy-done.4, bf16[256,4096]{1,0:T(8,128)(2,1)S(1)} %bitcast.34, ...), custom_call_target="tpu_custom_call" | custom-call | flops 200000000 | bytes 1024 | tf_op jit(solution)/shard_map/weight_terms/pallas_call | solution.py:422
  101.2 5.3 %project.6.refs_5_ = f32[4,256,1024]{2,1,0:T(8,128)S(1)} custom-call(bf16[1024,4096]{1,0:T(8,128)(2,1)S(1)} %bitcast.41, bf16[256,4096]{1,0:T(8,128)(2,1)S(1)} %bitcast.36, bf16[256,4096]{1,0:T(8,128)(2,1)} %collective-permute-done.3.refs_3_.refs_5_.refs_2_, bf16[256,1024]{1,0:T(8,128)(2,1)S(1)} %collective-permute-done.11.refs_6_.refs_3_, ...), custom_call_target="tpu_custom_call" | custom-call | flops 200000000 | bytes 1024 | tf_op jit(solution)/shard_map/project/pallas_call | solution.py:521
  109.2 2.6 %collective-permute-start.16 = (bf16[2,1024,128]{2,1,0:T(8,128)(2,1)}, bf16[2,1024,128]{2,1,0:T(8,128)(2,1)S(1)}, u32[]{:S(2)}, u32[]{:S(2)}) collective-permute-start(bf16[2,1024,128]{2,1,0:T(8,128)(2,1)} %get-tuple-element.112), channel_id=1, source_target_pairs={{0,16},{4,20},{8,24},{12,28},{16,0},{20,4},{24,8},{28,12},{1,17},{... | collective-permute-start | bytes 1572872 | tf_op jit(solution)/shard_map/ppermute | solution.py:561
  112.3 5.5 %weight_terms.7 = (f32[4,1024,128]{2,1,0:T(8,128)S(1)}, bf16[4,1024,128]{2,1,0:T(8,128)(2,1)}) custom-call(s32[10]{0:T(128)S(1)} %copy-done.19, bf16[512,1024]{1,0:T(8,128)(2,1)S(1)} %copy-done.5, bf16[512,1024]{1,0:T(8,128)(2,1)S(1)} %copy-done.4, bf16[256,4096]{1,0:T(8,128)(2,1)S(1)} %bitcast.37, ...), custom_call_target="tpu_custom_call" | custom-call | flops 200000000 | bytes 1024 | tf_op jit(solution)/shard_map/weight_terms/pallas_call | solution.py:422
  118.8 5.4 %project.7.refs_4_ = bf16[4,256,1024]{2,1,0:T(8,128)(2,1)S(1)} custom-call(bf16[1024,4096]{1,0:T(8,128)(2,1)S(1)} %bitcast.41, bf16[256,4096]{1,0:T(8,128)(2,1)S(1)} %bitcast.39, bf16[256,4096]{1,0:T(8,128)(2,1)} %collective-permute-done.3.refs_3_.refs_5_.refs_2_, bf16[256,1024]{1,0:T(8,128)(2,1)S(1)} %collective-permute-done.14.refs_6_.refs_3_, ...), custom_call_target="tpu_custom_call" | custom-call | flops 200000000 | bytes 1024 | tf_op jit(solution)/shard_map/project/pallas_call | solution.py:521
  125.4 8.9 %attention_back.2 = bf16[4,256,768]{2,1,0:T(8,128)(2,1)S(1)} custom-call(s32[10]{0:T(128)S(1)} %copy-done.19, bf16[256,1536]{1,0:T(8,128)(2,1)S(1)} %copy-done.8, bf16[256,1536]{1,0:T(8,128)(2,1)S(1)} %copy-done.10, bf16[256,768]{1,0:T(8,128)(2,1)S(1)} %copy-done.16, bf16[256,768]{1,0:T(8,128)(2,1)S(1)} %copy-done.14, ...), custom_call_target="tpu_custom_call" | custom-call | flops 1000000000 | bytes 1024 | tf_op jit(solution)/shard_map/attention_back/pallas_call | solution.py:336
  139.3 10.0 %attention_back.3 = bf16[4,256,768]{2,1,0:T(8,128)(2,1)S(1)} custom-call(s32[10]{0:T(128)S(1)} %copy-done.19, bf16[256,1536]{1,0:T(8,128)(2,1)S(1)} %copy-done.8, bf16[256,1536]{1,0:T(8,128)(2,1)S(1)} %copy-done.10, bf16[256,768]{1,0:T(8,128)(2,1)S(1)} %copy-done.12, bf16[256,768]{1,0:T(8,128)(2,1)} %collective-permute-done.5.refs_3_, ...), custom_call_target="tpu_custom_call" | custom-call | flops 1000000000 | bytes 1024 | tf_op jit(solution)/shard_map/attention_back/pallas_call | solution.py:336
  149.3 6.6 %collective-permute-done.19.got_low.got_high = bf16[2,1024,128]{2,1,0:T(8,128)(2,1)S(1)} collective-permute-done((bf16[2,1024,128]{2,1,0:T(8,128)(2,1)S(1)}, bf16[2,1024,128]{2,1,0:T(8,128)(2,1)S(1)}, u32[]{:S(2)}, u32[]{:S(2)}) %collective-permute-start.19) | collective-permute-done | bytes 524320 | tf_op jit(solution)/shard_map/ppermute | solution.py:561
  160.6 2.1 %collective-permute-start.23 = (bf16[1,1024,128]{2,1,0:T(8,128)(2,1)S(1)}, bf16[1,1024,128]{2,1,0:T(8,128)(2,1)S(1)}, u32[]{:S(2)}, u32[]{:S(2)}) collective-permute-start(bf16[1,1024,128]{2,1,0:T(8,128)(2,1)S(1)} %get-tuple-element.143), channel_id=1, source_target_pairs={{0,16},{4,20},{8,24},{12,28},{16,0},{20,4},{24,8},{28,12},{1,17},{... | collective-permute-start | bytes 786440 | tf_op jit(solution)/shard_map/ppermute | solution.py:561
  162.7 5.1 %collective-permute-done.22.got_ref = bf16[1,1024,128]{2,1,0:T(8,128)(2,1)S(1)} collective-permute-done((bf16[1,1024,128]{2,1,0:T(8,128)(2,1)S(1)}, bf16[1,1024,128]{2,1,0:T(8,128)(2,1)S(1)}, u32[]{:S(2)}, u32[]{:S(2)}) %collective-permute-start.22) | collective-permute-done | bytes 262176 | tf_op jit(solution)/shard_map/ppermute | solution.py:561
  168.6 8.2 %collective-permute-done.23.got_ref = bf16[1,1024,128]{2,1,0:T(8,128)(2,1)S(1)} collective-permute-done((bf16[1,1024,128]{2,1,0:T(8,128)(2,1)S(1)}, bf16[1,1024,128]{2,1,0:T(8,128)(2,1)S(1)}, u32[]{:S(2)}, u32[]{:S(2)}) %collective-permute-start.23) | collective-permute-done | bytes 262176 | tf_op jit(solution)/shard_map/ppermute | solution.py:561
  178.9 2.5 %collective-permute-start.27 = (bf16[1,1024,128]{2,1,0:T(8,128)(2,1)S(1)}, bf16[1,1024,128]{2,1,0:T(8,128)(2,1)S(1)}, u32[]{:S(2)}, u32[]{:S(2)}) collective-permute-start(bf16[1,1024,128]{2,1,0:T(8,128)(2,1)S(1)} %get-tuple-element.155), channel_id=1, source_target_pairs={{0,16},{4,20},{8,24},{12,28},{16,0},{20,4},{24,8},{28,12},{1,17},{... | collective-permute-start | bytes 786440 | tf_op jit(solution)/shard_map/ppermute | solution.py:561
  181.5 12.7 %collective-permute-done.27.got_ref = bf16[1,1024,128]{2,1,0:T(8,128)(2,1)S(1)} collective-permute-done((bf16[1,1024,128]{2,1,0:T(8,128)(2,1)S(1)}, bf16[1,1024,128]{2,1,0:T(8,128)(2,1)S(1)}, u32[]{:S(2)}, u32[]{:S(2)}) %collective-permute-start.27) | collective-permute-done | bytes 262176 | tf_op jit(solution)/shard_map/ppermute | solution.py:561
  195.0 2.8 %unpack.1 = (bf16[256,4096]{1,0:T(8,128)(2,1)}, bf16[256,1024]{1,0:T(8,128)(2,1)}, bf16[256,1024]{1,0:T(8,128)(2,1)}) custom-call(s32[10]{0:T(128)S(1)} %copy-done.19, bf16[256,768]{1,0:T(8,128)(2,1)S(1)} %get-tuple-element.163.refs_0_, bf16[256,768]{1,0:T(8,128)(2,1)S(1)} %get-tuple-element.170.refs_1_, bf16[256,768]{1,0:T(8,128)(2,1)S(1)} %get-tuple-element.171.refs_2_, ...), custom_call_target="tpu_custom_call" | custom-call | flops 200000000 | bytes 1024 | tf_op jit(solution)/shard_map/unpack/pallas_call | solution.py:142
  (118 shorter events, 33.8 us)
Async XLA Ops:
  2.7 12.2 %collective-permute-start.2 = (bf16[256,768]{1,0:T(8,128)(2,1)}, bf16[256,768]{1,0:T(8,128)(2,1)S(1)}, u32[]{:S(2)}, u32[]{:S(2)}) collective-permute-start(bf16[256,768]{1,0:T(8,128)(2,1)} %get-tuple-element.90), channel_id=1, source_target_pairs={{0,3},{1,2},{2,1},{3,0},{4,7},{5,6},{6,5},{7,4},{8,11},{9,10},{10,... | collective-permute-start | bytes 1179656 | tf_op jit(solution)/shard_map/ppermute | solution.py:558
  5.1 18.3 %collective-permute-start.1 = (bf16[256,768]{1,0:T(8,128)(2,1)}, bf16[256,768]{1,0:T(8,128)(2,1)S(1)}, u32[]{:S(2)}, u32[]{:S(2)}) collective-permute-start(bf16[256,768]{1,0:T(8,128)(2,1)} %get-tuple-element.83), channel_id=1, source_target_pairs={{0,2},{1,3},{2,0},{3,1},{4,6},{5,7},{6,4},{7,5},{8,10},{9,11},{10,... | collective-permute-start | bytes 1179656 | tf_op jit(solution)/shard_map/ppermute | solution.py:558
  8.8 19.6 %copy-start.20 = (s32[1,8]{1,0:T(1,128)S(1)}, s32[1,8]{1,0:T(1,128)}, u32[]{:S(2)}) copy-start(s32[1,8]{1,0:T(1,128)} %param.11) | copy-start | bytes 100
  23.5 15.5 %collective-permute-start.3 = (bf16[256,4096]{1,0:T(8,128)(2,1)S(1)}, bf16[256,4096]{1,0:T(8,128)(2,1)}, u32[]{:S(2)}, u32[]{:S(2)}) collective-permute-start(bf16[256,4096]{1,0:T(8,128)(2,1)S(1)} %bitcast.27), channel_id=1, source_target_pairs={{0,1},{1,0},{2,3},{3,2},{4,5},{5,4},{6,7},{7,6},{8,9},{9,8},{10,11... | collective-permute-start | bytes 6291464 | tf_op jit(solution)/shard_map/ppermute | solution.py:558
  24.2 4.8 %collective-permute-start = (bf16[256,1536]{1,0:T(8,128)(2,1)}, bf16[256,1536]{1,0:T(8,128)(2,1)S(1)}, u32[]{:S(2)}, u32[]{:S(2)}) collective-permute-start(bf16[256,1536]{1,0:T(8,128)(2,1)} %get-tuple-element.89), channel_id=1, source_target_pairs={{0,1},{1,0},{2,3},{3,2},{4,5},{5,4},{6,7},{7,6},{8,9},{9,8},{10,11... | collective-permute-start | bytes 2359304 | tf_op jit(solution)/shard_map/ppermute | solution.py:558
  24.2 14.7 %collective-permute-start.4 = (bf16[256,768]{1,0:T(8,128)(2,1)}, bf16[256,768]{1,0:T(8,128)(2,1)S(1)}, u32[]{:S(2)}, u32[]{:S(2)}) collective-permute-start(bf16[256,768]{1,0:T(8,128)(2,1)} %get-tuple-element.94), channel_id=1, source_target_pairs={{0,2},{1,3},{2,0},{3,1},{4,6},{5,7},{6,4},{7,5},{8,10},{9,11},{10,... | collective-permute-start | bytes 1179656 | tf_op jit(solution)/shard_map/ppermute | solution.py:558
  26.6 18.2 %collective-permute-start.5 = (bf16[256,768]{1,0:T(8,128)(2,1)}, bf16[256,768]{1,0:T(8,128)(2,1)}, u32[]{:S(2)}, u32[]{:S(2)}) collective-permute-start(bf16[256,768]{1,0:T(8,128)(2,1)} %get-tuple-element.95), channel_id=1, source_target_pairs={{0,3},{1,2},{2,1},{3,0},{4,7},{5,6},{6,5},{7,4},{8,11},{9,10},{10,... | collective-permute-start | bytes 1179656 | tf_op jit(solution)/shard_map/ppermute | solution.py:558
  26.7 29.5 %collective-permute-start.6 = (bf16[256,1024]{1,0:T(8,128)(2,1)}, bf16[256,1024]{1,0:T(8,128)(2,1)S(1)}, u32[]{:S(2)}, u32[]{:S(2)}) collective-permute-start(bf16[256,1024]{1,0:T(8,128)(2,1)} %get-tuple-element.99), channel_id=1, source_target_pairs={{0,2},{1,3},{2,0},{3,1},{4,6},{5,7},{6,4},{7,5},{8,10},{9,11},{10,... | collective-permute-start | bytes 1572872 | tf_op jit(solution)/shard_map/ppermute | solution.py:558
  38.9 19.2 %copy-start.5 = (bf16[512,1024]{1,0:T(8,128)(2,1)S(1)}, bf16[512,1024]{1,0:T(8,128)(2,1)}, u32[]{:S(2)}) copy-start(bf16[512,1024]{1,0:T(8,128)(2,1)} %get-tuple-element.91.refs_0_.refs_5_) | copy-start | bytes 3145732
  56.2 1.9 collective-permute-start.7
  56.2 18.6 %collective-permute-start.8 = (bf16[256,1024]{1,0:T(8,128)(2,1)}, bf16[256,1024]{1,0:T(8,128)(2,1)S(1)}, u32[]{:S(2)}, u32[]{:S(2)}) collective-permute-start(bf16[256,1024]{1,0:T(8,128)(2,1)} %get-tuple-element.105), channel_id=1, source_target_pairs={{0,2},{1,3},{2,0},{3,1},{4,6},{5,7},{6,4},{7,5},{8,10},{9,11},{10,... | collective-permute-start | bytes 1572872 | tf_op jit(solution)/shard_map/ppermute | solution.py:558
  64.1 27.7 %collective-permute-start.10 = (bf16[4,1024,128]{2,1,0:T(8,128)(2,1)S(1)}, bf16[4,1024,128]{2,1,0:T(8,128)(2,1)S(1)}, u32[]{:S(2)}, u32[]{:S(2)}) collective-permute-start(bf16[4,1024,128]{2,1,0:T(8,128)(2,1)S(1)} %get-tuple-element.101), channel_id=1, source_target_pairs={{0,8},{4,12},{8,0},{12,4},{16,24},{20,28},{24,16},{28,20},{1,9},{5... | collective-permute-start | bytes 3145736 | tf_op jit(solution)/shard_map/ppermute | solution.py:561
  74.7 2.0 collective-permute-start.9
  74.8 18.9 %collective-permute-start.11 = (bf16[256,1024]{1,0:T(8,128)(2,1)S(1)}, bf16[256,1024]{1,0:T(8,128)(2,1)S(1)}, u32[]{:S(2)}, u32[]{:S(2)}) collective-permute-start(bf16[256,1024]{1,0:T(8,128)(2,1)S(1)} %copy-done.22), channel_id=1, source_target_pairs={{0,2},{1,3},{2,0},{3,1},{4,6},{5,7},{6,4},{7,5},{8,10},{9,11},{10,... | collective-permute-start | bytes 1572872 | tf_op jit(solution)/shard_map/ppermute | solution.py:558
  81.6 25.3 %collective-permute-start.13 = (bf16[4,1024,128]{2,1,0:T(8,128)(2,1)S(1)}, bf16[4,1024,128]{2,1,0:T(8,128)(2,1)S(1)}, u32[]{:S(2)}, u32[]{:S(2)}) collective-permute-start(bf16[4,1024,128]{2,1,0:T(8,128)(2,1)S(1)} %get-tuple-element.109), channel_id=1, source_target_pairs={{0,4},{4,0},{8,12},{12,8},{16,20},{20,16},{24,28},{28,24},{1,5},{5... | collective-permute-start | bytes 3145736 | tf_op jit(solution)/shard_map/ppermute | solution.py:561
  93.8 1.9 collective-permute-start.12
  93.8 14.3 %collective-permute-start.14 = (bf16[256,1024]{1,0:T(8,128)(2,1)S(1)}, bf16[256,1024]{1,0:T(8,128)(2,1)S(1)}, u32[]{:S(2)}, u32[]{:S(2)}) collective-permute-start(bf16[256,1024]{1,0:T(8,128)(2,1)S(1)} %copy-done.21), channel_id=1, source_target_pairs={{0,2},{1,3},{2,0},{3,1},{4,6},{5,7},{6,4},{7,5},{8,10},{9,11},{10,... | collective-permute-start | bytes 1572872 | tf_op jit(solution)/shard_map/ppermute | solution.py:558
  108.1 4.2 %collective-permute-start.15 = (bf16[256,1024]{1,0:T(8,128)(2,1)S(1)}, bf16[256,1024]{1,0:T(8,128)(2,1)S(1)}, u32[]{:S(2)}, u32[]{:S(2)}) collective-permute-start(bf16[256,1024]{1,0:T(8,128)(2,1)S(1)} %collective-permute-done.14.refs_6_.refs_3_), channel_id=1, source_target_pairs={{0,1},{1,0},{2,3},{3,2},{4,5},{5,4},{6,7},{7,6},{8,9},{9,8},{10,11... | collective-permute-start | bytes 1572872 | tf_op jit(solution)/shard_map/ppermute | solution.py:558
  108.1 28.9 %collective-permute-start.18 = (bf16[4,1024,128]{2,1,0:T(8,128)(2,1)}, bf16[4,1024,128]{2,1,0:T(8,128)(2,1)S(1)}, u32[]{:S(2)}, u32[]{:S(2)}) collective-permute-start(bf16[4,1024,128]{2,1,0:T(8,128)(2,1)} %get-tuple-element.117), channel_id=1, source_target_pairs={{0,4},{4,0},{8,12},{12,8},{16,20},{20,16},{24,28},{28,24},{1,5},{5... | collective-permute-start | bytes 3145736 | tf_op jit(solution)/shard_map/ppermute | solution.py:561
  109.2 26.8 %collective-permute-start.16 = (bf16[2,1024,128]{2,1,0:T(8,128)(2,1)}, bf16[2,1024,128]{2,1,0:T(8,128)(2,1)S(1)}, u32[]{:S(2)}, u32[]{:S(2)}) collective-permute-start(bf16[2,1024,128]{2,1,0:T(8,128)(2,1)} %get-tuple-element.112), channel_id=1, source_target_pairs={{0,16},{4,20},{8,24},{12,28},{16,0},{20,4},{24,8},{28,12},{1,17},{... | collective-permute-start | bytes 1572872 | tf_op jit(solution)/shard_map/ppermute | solution.py:561
  111.8 25.1 %collective-permute-start.17 = (bf16[2,1024,128]{2,1,0:T(8,128)(2,1)}, bf16[2,1024,128]{2,1,0:T(8,128)(2,1)S(1)}, u32[]{:S(2)}, u32[]{:S(2)}) collective-permute-start(bf16[2,1024,128]{2,1,0:T(8,128)(2,1)} %get-tuple-element.120), channel_id=1, source_target_pairs={{0,8},{4,12},{8,0},{12,4},{16,24},{20,28},{24,16},{28,20},{1,9},{5... | collective-permute-start | bytes 1572872 | tf_op jit(solution)/shard_map/ppermute | solution.py:561
  117.8 39.0 %collective-permute-start.21 = (bf16[4,1024,128]{2,1,0:T(8,128)(2,1)}, bf16[4,1024,128]{2,1,0:T(8,128)(2,1)S(1)}, u32[]{:S(2)}, u32[]{:S(2)}) collective-permute-start(bf16[4,1024,128]{2,1,0:T(8,128)(2,1)} %get-tuple-element.127), channel_id=1, source_target_pairs={{0,4},{4,0},{8,12},{12,8},{16,20},{20,16},{24,28},{28,24},{1,5},{5... | collective-permute-start | bytes 3145736 | tf_op jit(solution)/shard_map/ppermute | solution.py:561
  134.4 22.6 %collective-permute-start.24 = (bf16[2,256,768]{2,1,0:T(8,128)(2,1)S(1)}, bf16[2,256,768]{2,1,0:T(8,128)(2,1)S(1)}, u32[]{:S(2)}, u32[]{:S(2)}) collective-permute-start(bf16[2,256,768]{2,1,0:T(8,128)(2,1)S(1)} %slice.57), channel_id=1, source_target_pairs={{0,2},{1,3},{2,0},{3,1},{4,6},{5,7},{6,4},{7,5},{8,10},{9,11},{10,... | collective-permute-start | bytes 2359304 | tf_op jit(solution)/shard_map/ppermute | solution.py:558
  137.3 18.6 %collective-permute-start.19 = (bf16[2,1024,128]{2,1,0:T(8,128)(2,1)S(1)}, bf16[2,1024,128]{2,1,0:T(8,128)(2,1)S(1)}, u32[]{:S(2)}, u32[]{:S(2)}) collective-permute-start(bf16[2,1024,128]{2,1,0:T(8,128)(2,1)S(1)} %get-tuple-element.139), channel_id=1, source_target_pairs={{0,8},{4,12},{8,0},{12,4},{16,24},{20,28},{24,16},{28,20},{1,9},{5... | collective-permute-start | bytes 1572872 | tf_op jit(solution)/shard_map/ppermute | solution.py:561
  137.8 18.2 %collective-permute-start.20 = (bf16[1,1024,128]{2,1,0:T(8,128)(2,1)S(1)}, bf16[1,1024,128]{2,1,0:T(8,128)(2,1)S(1)}, u32[]{:S(2)}, u32[]{:S(2)}) collective-permute-start(bf16[1,1024,128]{2,1,0:T(8,128)(2,1)S(1)} %get-tuple-element.136), channel_id=1, source_target_pairs={{0,16},{4,20},{8,24},{12,28},{16,0},{20,4},{24,8},{28,12},{1,17},{... | collective-permute-start | bytes 786440 | tf_op jit(solution)/shard_map/ppermute | solution.py:561
  157.2 20.4 %collective-permute-start.25 = (bf16[2,256,768]{2,1,0:T(8,128)(2,1)S(1)}, bf16[2,256,768]{2,1,0:T(8,128)(2,1)S(1)}, u32[]{:S(2)}, u32[]{:S(2)}) collective-permute-start(bf16[2,256,768]{2,1,0:T(8,128)(2,1)S(1)} %pad_maximum_fusion), channel_id=1, source_target_pairs={{0,1},{1,0},{2,3},{3,2},{4,5},{5,4},{6,7},{7,6},{8,9},{9,8},{10,11... | collective-permute-start | bytes 2359304 | tf_op jit(solution)/shard_map/ppermute | solution.py:558
  157.3 21.3 %collective-permute-start.28 = (bf16[2,256,768]{2,1,0:T(8,128)(2,1)S(1)}, bf16[2,256,768]{2,1,0:T(8,128)(2,1)S(1)}, u32[]{:S(2)}, u32[]{:S(2)}) collective-permute-start(bf16[2,256,768]{2,1,0:T(8,128)(2,1)S(1)} %slice.63), channel_id=1, source_target_pairs={{0,2},{1,3},{2,0},{3,1},{4,6},{5,7},{6,4},{7,5},{8,10},{9,11},{10,... | collective-permute-start | bytes 2359304 | tf_op jit(solution)/shard_map/ppermute | solution.py:558
  158.9 19.7 %collective-permute-start.26 = (bf16[2,1024,128]{2,1,0:T(8,128)(2,1)S(1)}, bf16[2,1024,128]{2,1,0:T(8,128)(2,1)S(1)}, u32[]{:S(2)}, u32[]{:S(2)}) collective-permute-start(bf16[2,1024,128]{2,1,0:T(8,128)(2,1)S(1)} %get-tuple-element.149), channel_id=1, source_target_pairs={{0,8},{4,12},{8,0},{12,4},{16,24},{20,28},{24,16},{28,20},{1,9},{5... | collective-permute-start | bytes 1572872 | tf_op jit(solution)/shard_map/ppermute | solution.py:561
  159.6 8.1 %collective-permute-start.22 = (bf16[1,1024,128]{2,1,0:T(8,128)(2,1)S(1)}, bf16[1,1024,128]{2,1,0:T(8,128)(2,1)S(1)}, u32[]{:S(2)}, u32[]{:S(2)}) collective-permute-start(bf16[1,1024,128]{2,1,0:T(8,128)(2,1)S(1)} %get-tuple-element.132), channel_id=1, source_target_pairs={{0,4},{4,0},{8,12},{12,8},{16,20},{20,16},{24,28},{28,24},{1,5},{5... | collective-permute-start | bytes 786440 | tf_op jit(solution)/shard_map/ppermute | solution.py:561
  160.6 16.2 %collective-permute-start.23 = (bf16[1,1024,128]{2,1,0:T(8,128)(2,1)S(1)}, bf16[1,1024,128]{2,1,0:T(8,128)(2,1)S(1)}, u32[]{:S(2)}, u32[]{:S(2)}) collective-permute-start(bf16[1,1024,128]{2,1,0:T(8,128)(2,1)S(1)} %get-tuple-element.143), channel_id=1, source_target_pairs={{0,16},{4,20},{8,24},{12,28},{16,0},{20,4},{24,8},{28,12},{1,17},{... | collective-permute-start | bytes 786440 | tf_op jit(solution)/shard_map/ppermute | solution.py:561
  178.8 16.1 %collective-permute-start.29 = (bf16[2,256,768]{2,1,0:T(8,128)(2,1)S(1)}, bf16[2,256,768]{2,1,0:T(8,128)(2,1)S(1)}, u32[]{:S(2)}, u32[]{:S(2)}) collective-permute-start(bf16[2,256,768]{2,1,0:T(8,128)(2,1)S(1)} %pad_maximum_fusion.1), channel_id=1, source_target_pairs={{0,1},{1,0},{2,3},{3,2},{4,5},{5,4},{6,7},{7,6},{8,9},{9,8},{10,11... | collective-permute-start | bytes 2359304 | tf_op jit(solution)/shard_map/ppermute | solution.py:558
  178.9 15.2 %collective-permute-start.27 = (bf16[1,1024,128]{2,1,0:T(8,128)(2,1)S(1)}, bf16[1,1024,128]{2,1,0:T(8,128)(2,1)S(1)}, u32[]{:S(2)}, u32[]{:S(2)}) collective-permute-start(bf16[1,1024,128]{2,1,0:T(8,128)(2,1)S(1)} %get-tuple-element.155), channel_id=1, source_target_pairs={{0,16},{4,20},{8,24},{12,28},{16,0},{20,4},{24,8},{28,12},{1,17},{... | collective-permute-start | bytes 786440 | tf_op jit(solution)/shard_map/ppermute | solution.py:561
  (23 other events, 124.2 us)

commit v8 on v7

--- a/solution.py
+++ b/solution.py
@@ -529,7 +529,7 @@
         + ([] if first else [block]),
         out_specs=block,
         out_shape=shape((parts, rows, feats), jnp.bfloat16 if last else jnp.float32),
-        compiler_params=params(24),
+        compiler_params=params(54),
         cost_estimate=cost(0.2),
         name="project",
     )(gate([out_weight], token)[0], *near, *flat, *([] if first else [acc]))
@@ -544,8 +544,7 @@
     chunks = max(1, min(4, model // shares // 128))
     width = model // shares // chunks
     bits = tuple(range(shares.bit_length() - 1))
-    turned = bits[1:] + bits[:1]
-    orders = [turned if c == 0 else bits for c in range(chunks)]
+    orders = [bits] * chunks
     scale = 1.0 / math.sqrt(rows * parts * shares)
     info = jnp.concatenate(
         [
@@ -660,21 +659,23 @@
     for c in range(chunks):
         if c > 1:
             advance(c - 2)
+        if c == 3:
+            advance(0)
         weigh(c)
         project_step([c], c == last)
+    advance(1)
     send_back(0)
-    for c in range(last):
-        advance(c)
+    advance(0)
+    advance(2)
     for gp in range(1, groups):
         send_back(gp)
-    advance(last - 1)
-    advance(last - 2)
-    advance(last)
+    advance(3)
+    advance(2)
+    advance(1)
     firsts = hand_over(0, token)
-    advance(0)
-    advance(last - 1)
     token = (token, firsts[1])
-    advance(last)
+    advance(3)
+    advance(2)
     lasts = [hand_over(gp, token) for gp in range(1, groups)]
     for _ in bits:
         for c in range(chunks):

time: 199 us -> 222 us (1.12)
  Pallas kernels: 96.8 us -> 122 us
  starting transfers between devices: 32.4 us -> 27.4 us
  waiting for transfers between devices: 54.6 us -> 57.5 us
    pallas_call x4, Pallas kernels: 21.3 us -> 36.8 us  [project(): pl.pallas_call(functools.partial(project_kernel, parts, shares, width, le...]
    pallas_call x8, Pallas kernels: 2.56 us -> 8 us  [merge(): pl.pallas_call(merge_kernel, grid=(half,), in_specs=[low, high, low, high...]
    ppermute x12, waiting for transfers between devices: 34.7 us -> 39.7 us  [over_dp(): return lax.ppermute(x, 'dp', [(i, i ^ d) for i in range(shares)])]
    ppermute x12, starting transfers between devices: 16.8 us -> 12.2 us  [over_dp(): return lax.ppermute(x, 'dp', [(i, i ^ d) for i in range(shares)])]
    unnamed x50 -> x76, local copies, waits for them, and re-layouts: 11.8 us -> 12.4 us
  transfers between devices with their start and end apart: 30 -> 30, of which waited for: 15 -> 9; matrix products, arithmetic and copies ran while one was open for 0% -> 0% of each run, Pallas kernels for 46% -> 53%
where the time goes in v8:
time: 222 us
  Pallas kernels  122 us (55%)
  waiting for transfers between devices  57.5 us (26%)
  starting transfers between devices  27.4 us (12%)
  local copies, waits for them, and re-layouts  12.8 us (6%)
    ppermute x12, waiting for transfers between devices, over_dp(): return lax.ppermute(x, 'dp', [(i, i ^ d) for i in range(shares)])  39.7 us
    pallas_call x4, Pallas kernels, project(): pl.pallas_call(functools.partial(project_kernel, parts, shares, width, le...  36.8 us
    pallas_call x4, Pallas kernels, weight_terms(): pl.pallas_call(functools.partial(weight_kernel, parts, groups, width, ord...  22.3 us
    pallas_call x2, Pallas kernels, attention_back(): pl.pallas_call(functools.partial(backward_kernel, parts, block, docs), gr...  20.4 us
    pallas_call x2, Pallas kernels, attention(): pl.pallas_call(functools.partial(forward_kernel, parts, block, docs), gri...  19.3 us
    ppermute x18, waiting for transfers between devices, over_seq(): return lax.ppermute(x, 'seq', [(i, i ^ d) for i in range(parts)])  17.8 us
    ppermute x18, starting transfers between devices, over_seq(): return lax.ppermute(x, 'seq', [(i, i ^ d) for i in range(parts)])  15.2 us
    unnamed x76, local copies, waits for them, and re-layouts  12.4 us
  transfers between devices with their start and end apart: 30, of which 9 were waited for; matrix products, arithmetic and copies ran while one was open for 0% of the time, Pallas kernels for 53%

profile of v8, /device:TPU:0, one launch (start us, length us, event | category | flops | bytes accessed | tf_op | source)
XLA Modules:
  0.0 221.6 jit_solution(4866999489493099281)
XLA Ops:
  0.6 2.1 pack.2
  2.7 2.4 %collective-permute-start.2 = (bf16[256,768]{1,0:T(8,128)(2,1)}, bf16[256,768]{1,0:T(8,128)(2,1)S(1)}, u32[]{:S(2)}, u32[]{:S(2)}) collective-permute-start(bf16[256,768]{1,0:T(8,128)(2,1)} %get-tuple-element.90), channel_id=1, source_target_pairs={{0,3},{1,2},{2,1},{3,0},{4,7},{5,6},{6,5},{7,4},{8,11},{9,10},{10,... | collective-permute-start | bytes 1179656 | tf_op jit(solution)/shard_map/ppermute | solution.py:557
  5.7 3.0 %pack.3 = (bf16[256,1536]{1,0:T(8,128)(2,1)}, bf16[256,1536]{1,0:T(8,128)(2,1)}, bf16[256,768]{1,0:T(8,128)(2,1)}, bf16[256,768]{1,0:T(8,128)(2,1)}) custom-call(s32[1]{0:T(128)} %bitcast.me_ref, bf16[256,4096]{1,0:T(8,128)(2,1)} %bitcast.42, bf16[256,1024]{1,0:T(8,128)(2,1)} %bitcast.50, bf16[256,1024]{1,0:T(8,128)(2,1)} %bitcast.58, ...), custom_call_target="tpu_custom_call" | custom-call | flops 200000000 | bytes 1024 | tf_op jit(solution)/shard_map/pack/pallas_call | solution.py:79
  8.8 4.0 %pack_chunks.1 = (bf16[256,1024]{1,0:T(8,128)(2,1)}, bf16[256,1024]{1,0:T(8,128)(2,1)}, bf16[256,1024]{1,0:T(8,128)(2,1)}, bf16[256,1024]{1,0:T(8,128)(2,1)}) custom-call(bf16[256,4096]{1,0:T(8,128)(2,1)} %bitcast.26), custom_call_target="tpu_custom_call" | custom-call | flops 200000000 | bytes 1024 | tf_op jit(solution)/shard_map/pack_chunks/pallas_call | solution.py:110
  12.8 2.1 collective-permute-done.2.refs_3_
  14.9 8.5 %collective-permute-done.1.refs_2_ = bf16[256,768]{1,0:T(8,128)(2,1)S(1)} collective-permute-done((bf16[256,768]{1,0:T(8,128)(2,1)}, bf16[256,768]{1,0:T(8,128)(2,1)S(1)}, u32[]{:S(2)}, u32[]{:S(2)}) %collective-permute-start.1) | collective-permute-done | bytes 393248 | tf_op jit(solution)/shard_map/ppermute | solution.py:557
  24.2 2.4 %collective-permute-start.4 = (bf16[256,768]{1,0:T(8,128)(2,1)}, bf16[256,768]{1,0:T(8,128)(2,1)S(1)}, u32[]{:S(2)}, u32[]{:S(2)}) collective-permute-start(bf16[256,768]{1,0:T(8,128)(2,1)} %get-tuple-element.94), channel_id=1, source_target_pairs={{0,2},{1,3},{2,0},{3,1},{4,6},{5,7},{6,4},{7,5},{8,10},{9,11},{10,... | collective-permute-start | bytes 1179656 | tf_op jit(solution)/shard_map/ppermute | solution.py:557
  26.6 1.7 collective-permute-start.6
  29.9 9.7 %attention.2 = (bf16[512,1024]{1,0:T(8,128)(2,1)}, f32[4,8,1024]{2,1,0:T(8,128)}) custom-call(s32[10]{0:T(128)} %pad_add_fusion.info_ref, bf16[256,1536]{1,0:T(8,128)(2,1)} %get-tuple-element.85.refs_0_, bf16[256,1536]{1,0:T(8,128)(2,1)} %copy-done.17, bf16[256,768]{1,0:T(8,128)(2,1)} %copy-done.32, bf16[256,768]{1,0:T(8,128)(2,1)} %copy-done.30), custom_call_target="tpu_custom_call" | custom-call | flops 2500000000 | bytes 1024 | tf_op jit(solution)/shard_map/attention/pallas_call | solution.py:250
  39.6 5.1 %collective-permute-done.5.refs_3_ = bf16[256,768]{1,0:T(8,128)(2,1)} collective-permute-done((bf16[256,768]{1,0:T(8,128)(2,1)}, bf16[256,768]{1,0:T(8,128)(2,1)}, u32[]{:S(2)}, u32[]{:S(2)}) %collective-permute-start.5) | collective-permute-done | bytes 393248 | tf_op jit(solution)/shard_map/ppermute | solution.py:557
  44.7 9.7 %attention.3 = (bf16[512,1024]{1,0:T(8,128)(2,1)}, f32[4,8,1024]{2,1,0:T(8,128)}) custom-call(s32[10]{0:T(128)} %pad_add_fusion.info_ref, bf16[256,1536]{1,0:T(8,128)(2,1)} %get-tuple-element.85.refs_0_, bf16[256,1536]{1,0:T(8,128)(2,1)} %copy-done.17, bf16[256,768]{1,0:T(8,128)(2,1)} %copy-done.28, bf16[256,768]{1,0:T(8,128)(2,1)} %collective-permute-done.5.refs_3_), custom_call_target="tpu_custom_call" | custom-call | flops 2500000000 | bytes 1024 | tf_op jit(solution)/shard_map/attention/pallas_call | solution.py:250
  56.1 1.8 collective-permute-start.8
  59.3 5.5 %weight_terms.4 = (f32[4,1024,128]{2,1,0:T(8,128)S(1)}, bf16[4,1024,128]{2,1,0:T(8,128)(2,1)}) custom-call(s32[10]{0:T(128)S(1)} %copy-done.36, bf16[512,1024]{1,0:T(8,128)(2,1)S(1)} %copy-done.6, bf16[512,1024]{1,0:T(8,128)(2,1)S(1)} %copy-done.4, bf16[256,4096]{1,0:T(8,128)(2,1)S(1)} %bitcast.32, ...), custom_call_target="tpu_custom_call" | custom-call | flops 200000000 | bytes 1024 | tf_op jit(solution)/shard_map/weight_terms/pallas_call | solution.py:422
  66.1 1.7 collective-permute-start.10
  67.8 8.7 %project.4.refs_5_ = f32[4,256,1024]{2,1,0:T(8,128)} custom-call(bf16[1024,4096]{1,0:T(8,128)(2,1)} %refs_0_.3, bf16[256,4096]{1,0:T(8,128)(2,1)} %bitcast.27, bf16[256,4096]{1,0:T(8,128)(2,1)} %collective-permute-done.3.refs_3_.refs_5_.refs_2_, bf16[256,1024]{1,0:T(8,128)(2,1)} %copy-done.20, bf16[256,1024]{1,0:T(8,128)(2,1)} %copy-done.25), custom_call_target="tpu_custom_call" | custom-call | flops 200000000 | bytes 1024 | tf_op jit(solution)/shard_map/project/pallas_call | solution.py:521
  76.6 1.9 collective-permute-start.11
  78.5 5.5 %weight_terms.5 = (f32[4,1024,128]{2,1,0:T(8,128)S(1)}, bf16[4,1024,128]{2,1,0:T(8,128)(2,1)}) custom-call(s32[10]{0:T(128)S(1)} %copy-done.36, bf16[512,1024]{1,0:T(8,128)(2,1)S(1)} %copy-done.6, bf16[512,1024]{1,0:T(8,128)(2,1)S(1)} %copy-done.5, bf16[256,4096]{1,0:T(8,128)(2,1)S(1)} %bitcast.34, ...), custom_call_target="tpu_custom_call" | custom-call | flops 200000000 | bytes 1024 | tf_op jit(solution)/shard_map/weight_terms/pallas_call | solution.py:422
  84.9 9.6 %project.5.refs_5_ = f32[4,256,1024]{2,1,0:T(8,128)} custom-call(bf16[1024,4096]{1,0:T(8,128)(2,1)} %refs_0_.3, bf16[256,4096]{1,0:T(8,128)(2,1)} %bitcast.28, bf16[256,4096]{1,0:T(8,128)(2,1)} %collective-permute-done.3.refs_3_.refs_5_.refs_2_, bf16[256,1024]{1,0:T(8,128)(2,1)} %copy-done.21, bf16[256,1024]{1,0:T(8,128)(2,1)} %copy-done.23, ...), custom_call_target="tpu_custom_call" | custom-call | flops 200000000 | bytes 1024 | tf_op jit(solution)/shard_map/project/pallas_call | solution.py:521
  94.5 2.1 merge.8
  97.7 1.8 collective-permute-start.14
  101.0 5.8 %weight_terms.6 = (f32[4,1024,128]{2,1,0:T(8,128)S(1)}, bf16[4,1024,128]{2,1,0:T(8,128)(2,1)}) custom-call(s32[10]{0:T(128)S(1)} %copy-done.36, bf16[512,1024]{1,0:T(8,128)(2,1)S(1)} %copy-done.6, bf16[512,1024]{1,0:T(8,128)(2,1)S(1)} %copy-done.5, bf16[256,4096]{1,0:T(8,128)(2,1)S(1)} %bitcast.36, ...), custom_call_target="tpu_custom_call" | custom-call | flops 200000000 | bytes 1024 | tf_op jit(solution)/shard_map/weight_terms/pallas_call | solution.py:422
  106.8 9.5 %project.6.refs_5_ = f32[4,256,1024]{2,1,0:T(8,128)} custom-call(bf16[1024,4096]{1,0:T(8,128)(2,1)} %refs_0_.3, bf16[256,4096]{1,0:T(8,128)(2,1)} %bitcast.29, bf16[256,4096]{1,0:T(8,128)(2,1)} %collective-permute-done.3.refs_3_.refs_5_.refs_2_, bf16[256,1024]{1,0:T(8,128)(2,1)} %collective-permute-done.11.refs_6_.refs_3_, bf16[256,1024]{1,0:T(8,128)(2,1)} %copy-done.24, ...), custom_call_target="tpu_custom_call" | custom-call | flops 200000000 | bytes 1024 | tf_op jit(solution)/shard_map/project/pallas_call | solution.py:521
  119.4 1.9 merge.10
  124.1 5.5 %weight_terms.7 = (f32[4,1024,128]{2,1,0:T(8,128)S(1)}, bf16[4,1024,128]{2,1,0:T(8,128)(2,1)}) custom-call(s32[10]{0:T(128)S(1)} %copy-done.36, bf16[512,1024]{1,0:T(8,128)(2,1)S(1)} %copy-done.6, bf16[512,1024]{1,0:T(8,128)(2,1)S(1)} %copy-done.5, bf16[256,4096]{1,0:T(8,128)(2,1)S(1)} %bitcast.38, ...), custom_call_target="tpu_custom_call" | custom-call | flops 200000000 | bytes 1024 | tf_op jit(solution)/shard_map/weight_terms/pallas_call | solution.py:422
  132.0 2.6 %collective-permute-start.18 = (bf16[1,1024,128]{2,1,0:T(8,128)(2,1)}, bf16[1,1024,128]{2,1,0:T(8,128)(2,1)S(1)}, u32[]{:S(2)}, u32[]{:S(2)}) collective-permute-start(bf16[1,1024,128]{2,1,0:T(8,128)(2,1)} %get-tuple-element.123), channel_id=1, source_target_pairs={{0,16},{4,20},{8,24},{12,28},{16,0},{20,4},{24,8},{28,12},{1,17},{... | collective-permute-start | bytes 786440 | tf_op jit(solution)/shard_map/ppermute | solution.py:560
  134.6 9.1 %project.7.refs_4_ = bf16[4,256,1024]{2,1,0:T(8,128)(2,1)} custom-call(bf16[1024,4096]{1,0:T(8,128)(2,1)} %refs_0_.3, bf16[256,4096]{1,0:T(8,128)(2,1)} %bitcast.30, bf16[256,4096]{1,0:T(8,128)(2,1)} %collective-permute-done.3.refs_3_.refs_5_.refs_2_, bf16[256,1024]{1,0:T(8,128)(2,1)} %copy-done.19, bf16[256,1024]{1,0:T(8,128)(2,1)} %copy-done.22, ...), custom_call_target="tpu_custom_call" | custom-call | flops 200000000 | bytes 1024 | tf_op jit(solution)/shard_map/project/pallas_call | solution.py:521
  147.7 9.7 %attention_back.2 = bf16[4,256,768]{2,1,0:T(8,128)(2,1)S(1)} custom-call(s32[10]{0:T(128)S(1)} %copy-done.36, bf16[256,1536]{1,0:T(8,128)(2,1)S(1)} %copy-done.16, bf16[256,1536]{1,0:T(8,128)(2,1)S(1)} %copy-done.18, bf16[256,768]{1,0:T(8,128)(2,1)S(1)} %copy-done.33, bf16[256,768]{1,0:T(8,128)(2,1)S(1)} %copy-done.31, bf16[4,256,1024]{2,1,0:T(8,128)(2,1)S(1)} %copy-done.7, ...), custom_call_target="tpu_custom_call" | custom-call | flops 1000000000 | bytes 1024 | tf_op jit(solution)/shard_map/attention_back/pallas_call | solution.py:336
  161.5 10.7 %attention_back.3 = bf16[4,256,768]{2,1,0:T(8,128)(2,1)S(1)} custom-call(s32[10]{0:T(128)S(1)} %copy-done.36, bf16[256,1536]{1,0:T(8,128)(2,1)S(1)} %copy-done.16, bf16[256,1536]{1,0:T(8,128)(2,1)S(1)} %copy-done.18, bf16[256,768]{1,0:T(8,128)(2,1)S(1)} %copy-done.29, bf16[256,768]{1,0:T(8,128)(2,1)} %collective-permute-done.5.refs_3_, ...), custom_call_target="tpu_custom_call" | custom-call | flops 1000000000 | bytes 1024 | tf_op jit(solution)/shard_map/attention_back/pallas_call | solution.py:336
  172.5 7.0 %collective-permute-done.21.got_low.got_high = bf16[2,1024,128]{2,1,0:T(8,128)(2,1)S(1)} collective-permute-done((bf16[2,1024,128]{2,1,0:T(8,128)(2,1)S(1)}, bf16[2,1024,128]{2,1,0:T(8,128)(2,1)S(1)}, u32[]{:S(2)}, u32[]{:S(2)}) %collective-permute-start.21) | collective-permute-done | bytes 524320 | tf_op jit(solution)/shard_map/ppermute | solution.py:560
  183.1 18.5 %collective-permute-done.25.got_low.got_high = bf16[2,1024,128]{2,1,0:T(8,128)(2,1)S(1)} collective-permute-done((bf16[2,1024,128]{2,1,0:T(8,128)(2,1)S(1)}, bf16[2,1024,128]{2,1,0:T(8,128)(2,1)S(1)}, u32[]{:S(2)}, u32[]{:S(2)}) %collective-permute-start.25) | collective-permute-done | bytes 524320 | tf_op jit(solution)/shard_map/ppermute | solution.py:560
  203.8 14.1 %collective-permute-done.27.got_ref = bf16[1,1024,128]{2,1,0:T(8,128)(2,1)S(1)} collective-permute-done((bf16[1,1024,128]{2,1,0:T(8,128)(2,1)S(1)}, bf16[1,1024,128]{2,1,0:T(8,128)(2,1)S(1)}, u32[]{:S(2)}, u32[]{:S(2)}) %collective-permute-start.27) | collective-permute-done | bytes 262176 | tf_op jit(solution)/shard_map/ppermute | solution.py:560
  218.9 2.8 %unpack.1 = (bf16[256,4096]{1,0:T(8,128)(2,1)}, bf16[256,1024]{1,0:T(8,128)(2,1)}, bf16[256,1024]{1,0:T(8,128)(2,1)}) custom-call(s32[10]{0:T(128)S(1)} %copy-done.36, bf16[256,768]{1,0:T(8,128)(2,1)S(1)} %get-tuple-element.164.refs_0_, bf16[256,768]{1,0:T(8,128)(2,1)S(1)} %get-tuple-element.171.refs_1_, bf16[256,768]{1,0:T(8,128)(2,1)S(1)} %get-tuple-element.172.refs_2_, ...), custom_call_target="tpu_custom_call" | custom-call | flops 200000000 | bytes 1024 | tf_op jit(solution)/shard_map/unpack/pallas_call | solution.py:142
  (143 shorter events, 34.1 us)
Async XLA Ops:
  2.7 12.2 %collective-permute-start.2 = (bf16[256,768]{1,0:T(8,128)(2,1)}, bf16[256,768]{1,0:T(8,128)(2,1)S(1)}, u32[]{:S(2)}, u32[]{:S(2)}) collective-permute-start(bf16[256,768]{1,0:T(8,128)(2,1)} %get-tuple-element.90), channel_id=1, source_target_pairs={{0,3},{1,2},{2,1},{3,0},{4,7},{5,6},{6,5},{7,4},{8,11},{9,10},{10,... | collective-permute-start | bytes 1179656 | tf_op jit(solution)/shard_map/ppermute | solution.py:557
  5.1 18.3 %collective-permute-start.1 = (bf16[256,768]{1,0:T(8,128)(2,1)}, bf16[256,768]{1,0:T(8,128)(2,1)S(1)}, u32[]{:S(2)}, u32[]{:S(2)}) collective-permute-start(bf16[256,768]{1,0:T(8,128)(2,1)} %get-tuple-element.83), channel_id=1, source_target_pairs={{0,2},{1,3},{2,0},{3,1},{4,6},{5,7},{6,4},{7,5},{8,10},{9,11},{10,... | collective-permute-start | bytes 1179656 | tf_op jit(solution)/shard_map/ppermute | solution.py:557
  8.8 19.6 %copy-start.37 = (s32[1,8]{1,0:T(1,128)S(1)}, s32[1,8]{1,0:T(1,128)}, u32[]{:S(2)}) copy-start(s32[1,8]{1,0:T(1,128)} %param.11) | copy-start | bytes 100
  23.4 16.2 %collective-permute-start.3 = (bf16[256,4096]{1,0:T(8,128)(2,1)S(1)}, bf16[256,4096]{1,0:T(8,128)(2,1)}, u32[]{:S(2)}, u32[]{:S(2)}) collective-permute-start(bf16[256,4096]{1,0:T(8,128)(2,1)S(1)} %bitcast.31), channel_id=1, source_target_pairs={{0,1},{1,0},{2,3},{3,2},{4,5},{5,4},{6,7},{7,6},{8,9},{9,8},{10,11... | collective-permute-start | bytes 6291464 | tf_op jit(solution)/shard_map/ppermute | solution.py:557
  24.1 4.9 %collective-permute-start = (bf16[256,1536]{1,0:T(8,128)(2,1)}, bf16[256,1536]{1,0:T(8,128)(2,1)S(1)}, u32[]{:S(2)}, u32[]{:S(2)}) collective-permute-start(bf16[256,1536]{1,0:T(8,128)(2,1)} %get-tuple-element.89), channel_id=1, source_target_pairs={{0,1},{1,0},{2,3},{3,2},{4,5},{5,4},{6,7},{7,6},{8,9},{9,8},{10,11... | collective-permute-start | bytes 2359304 | tf_op jit(solution)/shard_map/ppermute | solution.py:557
  24.2 15.4 %collective-permute-start.4 = (bf16[256,768]{1,0:T(8,128)(2,1)}, bf16[256,768]{1,0:T(8,128)(2,1)S(1)}, u32[]{:S(2)}, u32[]{:S(2)}) collective-permute-start(bf16[256,768]{1,0:T(8,128)(2,1)} %get-tuple-element.94), channel_id=1, source_target_pairs={{0,2},{1,3},{2,0},{3,1},{4,6},{5,7},{6,4},{7,5},{8,10},{9,11},{10,... | collective-permute-start | bytes 1179656 | tf_op jit(solution)/shard_map/ppermute | solution.py:557
  26.6 18.2 %collective-permute-start.5 = (bf16[256,768]{1,0:T(8,128)(2,1)}, bf16[256,768]{1,0:T(8,128)(2,1)}, u32[]{:S(2)}, u32[]{:S(2)}) collective-permute-start(bf16[256,768]{1,0:T(8,128)(2,1)} %get-tuple-element.95), channel_id=1, source_target_pairs={{0,3},{1,2},{2,1},{3,0},{4,7},{5,6},{6,5},{7,4},{8,11},{9,10},{10,... | collective-permute-start | bytes 1179656 | tf_op jit(solution)/shard_map/ppermute | solution.py:557
  26.6 29.5 %collective-permute-start.6 = (bf16[256,1024]{1,0:T(8,128)(2,1)}, bf16[256,1024]{1,0:T(8,128)(2,1)S(1)}, u32[]{:S(2)}, u32[]{:S(2)}) collective-permute-start(bf16[256,1024]{1,0:T(8,128)(2,1)} %get-tuple-element.99), channel_id=1, source_target_pairs={{0,2},{1,3},{2,0},{3,1},{4,6},{5,7},{6,4},{7,5},{8,10},{9,11},{10,... | collective-permute-start | bytes 1572872 | tf_op jit(solution)/shard_map/ppermute | solution.py:557
  39.6 18.4 %copy-start.6 = (bf16[512,1024]{1,0:T(8,128)(2,1)S(1)}, bf16[512,1024]{1,0:T(8,128)(2,1)}, u32[]{:S(2)}) copy-start(bf16[512,1024]{1,0:T(8,128)(2,1)} %get-tuple-element.91.refs_0_.refs_5_) | copy-start | bytes 3145732
  56.1 1.9 collective-permute-start.7
  56.1 20.4 %collective-permute-start.8 = (bf16[256,1024]{1,0:T(8,128)(2,1)}, bf16[256,1024]{1,0:T(8,128)(2,1)S(1)}, u32[]{:S(2)}, u32[]{:S(2)}) collective-permute-start(bf16[256,1024]{1,0:T(8,128)(2,1)} %get-tuple-element.106), channel_id=1, source_target_pairs={{0,2},{1,3},{2,0},{3,1},{4,6},{5,7},{6,4},{7,5},{8,10},{9,11},{10,... | collective-permute-start | bytes 1572872 | tf_op jit(solution)/shard_map/ppermute | solution.py:557
  66.1 28.4 %collective-permute-start.10 = (bf16[4,1024,128]{2,1,0:T(8,128)(2,1)}, bf16[4,1024,128]{2,1,0:T(8,128)(2,1)}, u32[]{:S(2)}, u32[]{:S(2)}) collective-permute-start(bf16[4,1024,128]{2,1,0:T(8,128)(2,1)} %get-tuple-element.102), channel_id=1, source_target_pairs={{0,4},{4,0},{8,12},{12,8},{16,20},{20,16},{24,28},{28,24},{1,5},{5... | collective-permute-start | bytes 3145736 | tf_op jit(solution)/shard_map/ppermute | solution.py:560
  76.5 2.0 collective-permute-start.9
  76.6 21.1 %collective-permute-start.11 = (bf16[256,1024]{1,0:T(8,128)(2,1)}, bf16[256,1024]{1,0:T(8,128)(2,1)}, u32[]{:S(2)}, u32[]{:S(2)}) collective-permute-start(bf16[256,1024]{1,0:T(8,128)(2,1)} %get-tuple-element.116), channel_id=1, source_target_pairs={{0,2},{1,3},{2,0},{3,1},{4,6},{5,7},{6,4},{7,5},{8,10},{9,11},{10,... | collective-permute-start | bytes 1572872 | tf_op jit(solution)/shard_map/ppermute | solution.py:557
  84.1 32.3 %collective-permute-start.13 = (bf16[4,1024,128]{2,1,0:T(8,128)(2,1)}, bf16[4,1024,128]{2,1,0:T(8,128)(2,1)S(1)}, u32[]{:S(2)}, u32[]{:S(2)}) collective-permute-start(bf16[4,1024,128]{2,1,0:T(8,128)(2,1)} %get-tuple-element.108), channel_id=1, source_target_pairs={{0,4},{4,0},{8,12},{12,8},{16,20},{20,16},{24,28},{28,24},{1,5},{5... | collective-permute-start | bytes 3145736 | tf_op jit(solution)/shard_map/ppermute | solution.py:560
  97.7 3.3 %collective-permute-start.12 = (bf16[256,1024]{1,0:T(8,128)(2,1)}, bf16[256,1024]{1,0:T(8,128)(2,1)S(1)}, u32[]{:S(2)}, u32[]{:S(2)}) collective-permute-start(bf16[256,1024]{1,0:T(8,128)(2,1)} %collective-permute-done.11.refs_6_.refs_3_), channel_id=1, source_target_pairs={{0,1},{1,0},{2,3},{3,2},{4,5},{5,4},{6,7},{7,6},{8,9},{9,8},{10,11... | collective-permute-start | bytes 1572872 | tf_op jit(solution)/shard_map/ppermute | solution.py:557
  97.7 21.7 %collective-permute-start.14 = (bf16[2,1024,128]{2,1,0:T(8,128)(2,1)}, bf16[2,1024,128]{2,1,0:T(8,128)(2,1)}, u32[]{:S(2)}, u32[]{:S(2)}) collective-permute-start(bf16[2,1024,128]{2,1,0:T(8,128)(2,1)} %get-tuple-element.113), channel_id=1, source_target_pairs={{0,8},{4,12},{8,0},{12,4},{16,24},{20,28},{24,16},{28,20},{1,9},{5... | collective-permute-start | bytes 1572872 | tf_op jit(solution)/shard_map/ppermute | solution.py:560
  99.5 22.7 %collective-permute-start.15 = (bf16[256,1024]{1,0:T(8,128)(2,1)}, bf16[256,1024]{1,0:T(8,128)(2,1)S(1)}, u32[]{:S(2)}, u32[]{:S(2)}) collective-permute-start(bf16[256,1024]{1,0:T(8,128)(2,1)} %get-tuple-element.125), channel_id=1, source_target_pairs={{0,2},{1,3},{2,0},{3,1},{4,6},{5,7},{6,4},{7,5},{8,10},{9,11},{10,... | collective-permute-start | bytes 1572872 | tf_op jit(solution)/shard_map/ppermute | solution.py:557
  122.2 1.9 collective-permute-start.16
  122.2 37.5 %collective-permute-start.19 = (bf16[4,1024,128]{2,1,0:T(8,128)(2,1)}, bf16[4,1024,128]{2,1,0:T(8,128)(2,1)}, u32[]{:S(2)}, u32[]{:S(2)}) collective-permute-start(bf16[4,1024,128]{2,1,0:T(8,128)(2,1)} %get-tuple-element.118), channel_id=1, source_target_pairs={{0,4},{4,0},{8,12},{12,8},{16,20},{20,16},{24,28},{28,24},{1,5},{5... | collective-permute-start | bytes 3145736 | tf_op jit(solution)/shard_map/ppermute | solution.py:560
  123.3 20.4 %collective-permute-start.17 = (bf16[2,1024,128]{2,1,0:T(8,128)(2,1)}, bf16[2,1024,128]{2,1,0:T(8,128)(2,1)}, u32[]{:S(2)}, u32[]{:S(2)}) collective-permute-start(bf16[2,1024,128]{2,1,0:T(8,128)(2,1)} %get-tuple-element.121), channel_id=1, source_target_pairs={{0,8},{4,12},{8,0},{12,4},{16,24},{20,28},{24,16},{28,20},{1,9},{5... | collective-permute-start | bytes 1572872 | tf_op jit(solution)/shard_map/ppermute | solution.py:560
  131.0 41.3 %collective-permute-start.20 = (bf16[4,1024,128]{2,1,0:T(8,128)(2,1)}, bf16[4,1024,128]{2,1,0:T(8,128)(2,1)S(1)}, u32[]{:S(2)}, u32[]{:S(2)}) collective-permute-start(bf16[4,1024,128]{2,1,0:T(8,128)(2,1)} %get-tuple-element.131), channel_id=1, source_target_pairs={{0,4},{4,0},{8,12},{12,8},{16,20},{20,16},{24,28},{28,24},{1,5},{5... | collective-permute-start | bytes 3145736 | tf_op jit(solution)/shard_map/ppermute | solution.py:560
  132.0 26.8 %collective-permute-start.18 = (bf16[1,1024,128]{2,1,0:T(8,128)(2,1)}, bf16[1,1024,128]{2,1,0:T(8,128)(2,1)S(1)}, u32[]{:S(2)}, u32[]{:S(2)}) collective-permute-start(bf16[1,1024,128]{2,1,0:T(8,128)(2,1)} %get-tuple-element.123), channel_id=1, source_target_pairs={{0,16},{4,20},{8,24},{12,28},{16,0},{20,4},{24,8},{28,12},{1,17},{... | collective-permute-start | bytes 786440 | tf_op jit(solution)/shard_map/ppermute | solution.py:560
  157.5 23.0 %collective-permute-start.23 = (bf16[2,256,768]{2,1,0:T(8,128)(2,1)S(1)}, bf16[2,256,768]{2,1,0:T(8,128)(2,1)S(1)}, u32[]{:S(2)}, u32[]{:S(2)}) collective-permute-start(bf16[2,256,768]{2,1,0:T(8,128)(2,1)S(1)} %slice.57), channel_id=1, source_target_pairs={{0,2},{1,3},{2,0},{3,1},{4,6},{5,7},{6,4},{7,5},{8,10},{9,11},{10,... | collective-permute-start | bytes 2359304 | tf_op jit(solution)/shard_map/ppermute | solution.py:557
  161.1 18.5 %collective-permute-start.21 = (bf16[2,1024,128]{2,1,0:T(8,128)(2,1)S(1)}, bf16[2,1024,128]{2,1,0:T(8,128)(2,1)S(1)}, u32[]{:S(2)}, u32[]{:S(2)}) collective-permute-start(bf16[2,1024,128]{2,1,0:T(8,128)(2,1)S(1)} %get-tuple-element.139), channel_id=1, source_target_pairs={{0,8},{4,12},{8,0},{12,4},{16,24},{20,28},{24,16},{28,20},{1,9},{5... | collective-permute-start | bytes 1572872 | tf_op jit(solution)/shard_map/ppermute | solution.py:560
  161.1 18.5 %collective-permute-start.22 = (bf16[1,1024,128]{2,1,0:T(8,128)(2,1)S(1)}, bf16[1,1024,128]{2,1,0:T(8,128)(2,1)S(1)}, u32[]{:S(2)}, u32[]{:S(2)}) collective-permute-start(bf16[1,1024,128]{2,1,0:T(8,128)(2,1)S(1)} %get-tuple-element.134), channel_id=1, source_target_pairs={{0,16},{4,20},{8,24},{12,28},{16,0},{20,4},{24,8},{28,12},{1,17},{... | collective-permute-start | bytes 786440 | tf_op jit(solution)/shard_map/ppermute | solution.py:560
  180.7 2.4 %collective-permute-start.24 = (bf16[2,256,768]{2,1,0:T(8,128)(2,1)S(1)}, bf16[2,256,768]{2,1,0:T(8,128)(2,1)S(1)}, u32[]{:S(2)}, u32[]{:S(2)}) collective-permute-start(bf16[2,256,768]{2,1,0:T(8,128)(2,1)S(1)} %pad_maximum_fusion), channel_id=1, source_target_pairs={{0,1},{1,0},{2,3},{3,2},{4,5},{5,4},{6,7},{7,6},{8,9},{9,8},{10,11... | collective-permute-start | bytes 2359304 | tf_op jit(solution)/shard_map/ppermute | solution.py:557
  180.8 21.7 %collective-permute-start.28 = (bf16[2,256,768]{2,1,0:T(8,128)(2,1)S(1)}, bf16[2,256,768]{2,1,0:T(8,128)(2,1)S(1)}, u32[]{:S(2)}, u32[]{:S(2)}) collective-permute-start(bf16[2,256,768]{2,1,0:T(8,128)(2,1)S(1)} %slice.63), channel_id=1, source_target_pairs={{0,2},{1,3},{2,0},{3,1},{4,6},{5,7},{6,4},{7,5},{8,10},{9,11},{10,... | collective-permute-start | bytes 2359304 | tf_op jit(solution)/shard_map/ppermute | solution.py:557
  181.9 19.7 %collective-permute-start.25 = (bf16[2,1024,128]{2,1,0:T(8,128)(2,1)S(1)}, bf16[2,1024,128]{2,1,0:T(8,128)(2,1)S(1)}, u32[]{:S(2)}, u32[]{:S(2)}) collective-permute-start(bf16[2,1024,128]{2,1,0:T(8,128)(2,1)S(1)} %get-tuple-element.146), channel_id=1, source_target_pairs={{0,8},{4,12},{8,0},{12,4},{16,24},{20,28},{24,16},{28,20},{1,9},{5... | collective-permute-start | bytes 1572872 | tf_op jit(solution)/shard_map/ppermute | solution.py:560
  181.9 19.7 %collective-permute-start.26 = (bf16[1,1024,128]{2,1,0:T(8,128)(2,1)S(1)}, bf16[1,1024,128]{2,1,0:T(8,128)(2,1)S(1)}, u32[]{:S(2)}, u32[]{:S(2)}) collective-permute-start(bf16[1,1024,128]{2,1,0:T(8,128)(2,1)S(1)} %get-tuple-element.148), channel_id=1, source_target_pairs={{0,16},{4,20},{8,24},{12,28},{16,0},{20,4},{24,8},{28,12},{1,17},{... | collective-permute-start | bytes 786440 | tf_op jit(solution)/shard_map/ppermute | solution.py:560
  202.7 16.1 %collective-permute-start.29 = (bf16[2,256,768]{2,1,0:T(8,128)(2,1)S(1)}, bf16[2,256,768]{2,1,0:T(8,128)(2,1)S(1)}, u32[]{:S(2)}, u32[]{:S(2)}) collective-permute-start(bf16[2,256,768]{2,1,0:T(8,128)(2,1)S(1)} %pad_maximum_fusion.1), channel_id=1, source_target_pairs={{0,1},{1,0},{2,3},{3,2},{4,5},{5,4},{6,7},{7,6},{8,9},{9,8},{10,11... | collective-permute-start | bytes 2359304 | tf_op jit(solution)/shard_map/ppermute | solution.py:557
  202.7 15.2 %collective-permute-start.27 = (bf16[1,1024,128]{2,1,0:T(8,128)(2,1)S(1)}, bf16[1,1024,128]{2,1,0:T(8,128)(2,1)S(1)}, u32[]{:S(2)}, u32[]{:S(2)}) collective-permute-start(bf16[1,1024,128]{2,1,0:T(8,128)(2,1)S(1)} %get-tuple-element.154), channel_id=1, source_target_pairs={{0,16},{4,20},{8,24},{12,28},{16,0},{20,4},{24,8},{28,12},{1,17},{... | collective-permute-start | bytes 786440 | tf_op jit(solution)/shard_map/ppermute | solution.py:560
  (36 other events, 196.2 us)

commit v9 on v8

--- a/solution.py
+++ b/solution.py
@@ -272,7 +272,7 @@
             shape((wide, parts * block)),
             shape((parts, 8, GROUP * block), jnp.float32),
         ],
-        compiler_params=params(60),
+        compiler_params=params(24),
         cost_estimate=cost(2.5),
         name="attention",
     )(gate([info], token)[0], *[x for x, at in pieces])
@@ -360,7 +360,7 @@
         ),
         out_shape=shape((parts, block, cols)),
         compiler_params=params(32),
-        cost_estimate=cost(1.0),
+        cost_estimate=cost(0.3),
         name="attention_back",
     )(gate([info], token)[0], *[x for x, at in pieces], grads, out, lse)
 
@@ -529,7 +529,7 @@
         + ([] if first else [block]),
         out_specs=block,
         out_shape=shape((parts, rows, feats), jnp.bfloat16 if last else jnp.float32),
-        compiler_params=params(54),
+        compiler_params=params(24),
         cost_estimate=cost(0.2),
         name="project",
     )(gate([out_weight], token)[0], *near, *flat, *([] if first else [acc]))
@@ -664,18 +664,17 @@
         weigh(c)
         project_step([c], c == last)
     advance(1)
+    advance(2)
+    advance(0)
     send_back(0)
-    advance(0)
-    advance(2)
     for gp in range(1, groups):
         send_back(gp)
+    advance(1)
     advance(3)
     advance(2)
-    advance(1)
     firsts = hand_over(0, token)
     token = (token, firsts[1])
     advance(3)
-    advance(2)
     lasts = [hand_over(gp, token) for gp in range(1, groups)]
     for _ in bits:
         for c in range(chunks):

time: 222 us -> 216 us (0.973)
  Pallas kernels: 122 us -> 90 us
  waiting for transfers between devices: 57.5 us -> 81.2 us
  starting transfers between devices: 27.4 us -> 38.7 us
  local copies, waits for them, and re-layouts: 12.8 us -> 3.87 us
    pallas_call x4, Pallas kernels: 36.8 us -> 20.7 us  [project(): pl.pallas_call(functools.partial(project_kernel, parts, shares, width, le...]
    ppermute x12, waiting for transfers between devices: 39.7 us -> 55 us  [over_dp(): return lax.ppermute(x, 'dp', [(i, i ^ d) for i in range(shares)])]
    ppermute x12, starting transfers between devices: 12.2 us -> 23.7 us  [over_dp(): return lax.ppermute(x, 'dp', [(i, i ^ d) for i in range(shares)])]
    unnamed x76 -> x24, local copies, waits for them, and re-layouts: 12.4 us -> 3.46 us
    ppermute x18, waiting for transfers between devices: 17.8 us -> 26.1 us  [over_seq(): return lax.ppermute(x, 'seq', [(i, i ^ d) for i in range(parts)])]
    pallas_call x8, Pallas kernels: 8 us -> 1.18 us  [merge(): pl.pallas_call(merge_kernel, grid=(half,), in_specs=[low, high, low, high...]
    pallas_call x2, Pallas kernels: 19.3 us -> 14.5 us  [attention(): pl.pallas_call(functools.partial(forward_kernel, parts, block, docs), gri...]
    pallas_call x4, Pallas kernels: 22.3 us -> 19.4 us  [weight_terms(): pl.pallas_call(functools.partial(weight_kernel, parts, groups, width, ord...]
  transfers between devices with their start and end apart: 30 -> 30, of which waited for: 9 -> 18; matrix products, arithmetic and copies ran while one was open for 0% -> 0% of each run, Pallas kernels for 53% -> 40%
where the time goes in v9:
time: 216 us; the launch traced here: 215 us
  Pallas kernels  90 us (42%)
  waiting for transfers between devices  81.2 us (38%)
  starting transfers between devices  38.7 us (18%)
  local copies, waits for them, and re-layouts  3.87 us (2%)
    ppermute x12, waiting for transfers between devices, over_dp(): return lax.ppermute(x, 'dp', [(i, i ^ d) for i in range(shares)])  55 us
    ppermute x18, waiting for transfers between devices, over_seq(): return lax.ppermute(x, 'seq', [(i, i ^ d) for i in range(parts)])  26.1 us
    ppermute x12, starting transfers between devices, over_dp(): return lax.ppermute(x, 'dp', [(i, i ^ d) for i in range(shares)])  23.7 us
    pallas_call x4, Pallas kernels, project(): pl.pallas_call(functools.partial(project_kernel, parts, shares, width, le...  20.7 us
    pallas_call x4, Pallas kernels, weight_terms(): pl.pallas_call(functools.partial(weight_kernel, parts, groups, width, ord...  19.4 us
    pallas_call x2, Pallas kernels, attention_back(): pl.pallas_call(functools.partial(backward_kernel, parts, block, docs), gr...  19 us
    ppermute x18, starting transfers between devices, over_seq(): return lax.ppermute(x, 'seq', [(i, i ^ d) for i in range(parts)])  14.9 us
    pallas_call x2, Pallas kernels, attention(): pl.pallas_call(functools.partial(forward_kernel, parts, block, docs), gri...  14.5 us
  transfers between devices with their start and end apart: 30, of which 18 were waited for; matrix products, arithmetic and copies ran while one was open for 0% of the time, Pallas kernels for 40%

profile of v9, /device:TPU:0, one launch (start us, length us, event | category | flops | bytes accessed | tf_op | source)
XLA Modules:
  0.0 215.0 jit_solution(17027831381422887598)
XLA Ops:
  2.7 2.4 %collective-permute-start.2 = (bf16[256,768]{1,0:T(8,128)(2,1)}, bf16[256,768]{1,0:T(8,128)(2,1)S(1)}, u32[]{:S(2)}, u32[]{:S(2)}) collective-permute-start(bf16[256,768]{1,0:T(8,128)(2,1)} %get-tuple-element.90), channel_id=1, source_target_pairs={{0,3},{1,2},{2,1},{3,0},{4,7},{5,6},{6,5},{7,4},{8,11},{9,10},{10,... | collective-permute-start | bytes 1179656 | tf_op jit(solution)/shard_map/ppermute | solution.py:557
  5.8 3.0 %pack.3 = (bf16[256,1536]{1,0:T(8,128)(2,1)}, bf16[256,1536]{1,0:T(8,128)(2,1)}, bf16[256,768]{1,0:T(8,128)(2,1)}, bf16[256,768]{1,0:T(8,128)(2,1)}) custom-call(s32[1]{0:T(128)} %bitcast.me_ref, bf16[256,4096]{1,0:T(8,128)(2,1)} %bitcast.44, bf16[256,1024]{1,0:T(8,128)(2,1)} %bitcast.52, bf16[256,1024]{1,0:T(8,128)(2,1)} %bitcast.60, ...), custom_call_target="tpu_custom_call" | custom-call | flops 200000000 | bytes 1024 | tf_op jit(solution)/shard_map/pack/pallas_call | solution.py:79
  8.8 4.0 %pack_chunks.1 = (bf16[256,1024]{1,0:T(8,128)(2,1)}, bf16[256,1024]{1,0:T(8,128)(2,1)}, bf16[256,1024]{1,0:T(8,128)(2,1)}, bf16[256,1024]{1,0:T(8,128)(2,1)}) custom-call(bf16[256,4096]{1,0:T(8,128)(2,1)} %bitcast.26), custom_call_target="tpu_custom_call" | custom-call | flops 200000000 | bytes 1024 | tf_op jit(solution)/shard_map/pack_chunks/pallas_call | solution.py:110
  12.9 2.1 collective-permute-done.2.refs_3_
  14.9 8.5 %collective-permute-done.1.refs_2_ = bf16[256,768]{1,0:T(8,128)(2,1)S(1)} collective-permute-done((bf16[256,768]{1,0:T(8,128)(2,1)}, bf16[256,768]{1,0:T(8,128)(2,1)S(1)}, u32[]{:S(2)}, u32[]{:S(2)}) %collective-permute-start.1) | collective-permute-done | bytes 393248 | tf_op jit(solution)/shard_map/ppermute | solution.py:557
  24.7 2.3 %collective-permute-start.4 = (bf16[256,768]{1,0:T(8,128)(2,1)}, bf16[256,768]{1,0:T(8,128)(2,1)}, u32[]{:S(2)}, u32[]{:S(2)}) collective-permute-start(bf16[256,768]{1,0:T(8,128)(2,1)} %get-tuple-element.94), channel_id=1, source_target_pairs={{0,2},{1,3},{2,0},{3,1},{4,6},{5,7},{6,4},{7,5},{8,10},{9,11},{10,... | collective-permute-start | bytes 1179656 | tf_op jit(solution)/shard_map/ppermute | solution.py:557
  31.5 6.6 %attention.2 = (bf16[512,1024]{1,0:T(8,128)(2,1)S(1)}, f32[4,8,1024]{2,1,0:T(8,128)S(1)}) custom-call(s32[10]{0:T(128)S(1)} %pad_add_fusion.info_ref, bf16[256,1536]{1,0:T(8,128)(2,1)S(1)} %copy-done.1, bf16[256,1536]{1,0:T(8,128)(2,1)S(1)} %collective-permute-done.refs_1_, bf16[256,768]{1,0:T(8,128)(2,1)S(1)} %copy-done.4, ...), custom_call_target="tpu_custom_call" | custom-call | flops 2500000000 | bytes 1024 | tf_op jit(solution)/shard_map/attention/pallas_call | solution.py:250
  38.1 7.2 %collective-permute-done.5.refs_3_ = bf16[256,768]{1,0:T(8,128)(2,1)} collective-permute-done((bf16[256,768]{1,0:T(8,128)(2,1)}, bf16[256,768]{1,0:T(8,128)(2,1)}, u32[]{:S(2)}, u32[]{:S(2)}) %collective-permute-start.5) | collective-permute-done | bytes 393248 | tf_op jit(solution)/shard_map/ppermute | solution.py:557
  45.2 8.0 %attention.3 = (bf16[512,1024]{1,0:T(8,128)(2,1)S(1)}, f32[4,8,1024]{2,1,0:T(8,128)S(1)}) custom-call(s32[10]{0:T(128)S(1)} %pad_add_fusion.info_ref, bf16[256,1536]{1,0:T(8,128)(2,1)S(1)} %copy-done.1, bf16[256,1536]{1,0:T(8,128)(2,1)S(1)} %collective-permute-done.refs_1_, bf16[256,768]{1,0:T(8,128)(2,1)} %collective-permute-done.4.refs_2_, ...), custom_call_target="tpu_custom_call" | custom-call | flops 2500000000 | bytes 1024 | tf_op jit(solution)/shard_map/attention/pallas_call | solution.py:250
  53.2 3.0 %collective-permute-done.6.refs_6_.refs_3_ = bf16[256,1024]{1,0:T(8,128)(2,1)S(1)} collective-permute-done((bf16[256,1024]{1,0:T(8,128)(2,1)}, bf16[256,1024]{1,0:T(8,128)(2,1)S(1)}, u32[]{:S(2)}, u32[]{:S(2)}) %collective-permute-start.6) | collective-permute-done | bytes 524320 | tf_op jit(solution)/shard_map/ppermute | solution.py:557
  58.2 4.8 %weight_terms.4 = (f32[4,1024,128]{2,1,0:T(8,128)S(1)}, bf16[4,1024,128]{2,1,0:T(8,128)(2,1)S(1)}) custom-call(s32[10]{0:T(128)S(1)} %pad_add_fusion.info_ref, bf16[512,1024]{1,0:T(8,128)(2,1)S(1)} %get-tuple-element.91.refs_0_.refs_5_, bf16[512,1024]{1,0:T(8,128)(2,1)S(1)} %get-tuple-element.96.refs_1_.refs_5_, bf16[256,4096]{1,0:T(8,128)(2,1)S(1)} %bitcast.28, ...), custom_call_target="tpu_custom_call" | custom-call | flops 200000000 | bytes 1024 | tf_op jit(solution)/shard_map/weight_terms/pallas_call | solution.py:422
  64.7 4.9 %project.4.refs_5_ = f32[4,256,1024]{2,1,0:T(8,128)S(1)} custom-call(bf16[1024,4096]{1,0:T(8,128)(2,1)S(1)} %bitcast.41, bf16[256,4096]{1,0:T(8,128)(2,1)S(1)} %bitcast.30, bf16[256,4096]{1,0:T(8,128)(2,1)} %collective-permute-done.3.refs_3_.refs_5_.refs_2_, bf16[256,1024]{1,0:T(8,128)(2,1)S(1)} %collective-permute-done.6.refs_6_.refs_3_, ...), custom_call_target="tpu_custom_call" | custom-call | flops 200000000 | bytes 1024 | tf_op jit(solution)/shard_map/project/pallas_call | solution.py:521
  72.5 4.8 %weight_terms.5 = (f32[4,1024,128]{2,1,0:T(8,128)S(1)}, bf16[4,1024,128]{2,1,0:T(8,128)(2,1)S(1)}) custom-call(s32[10]{0:T(128)S(1)} %pad_add_fusion.info_ref, bf16[512,1024]{1,0:T(8,128)(2,1)S(1)} %get-tuple-element.91.refs_0_.refs_5_, bf16[512,1024]{1,0:T(8,128)(2,1)S(1)} %get-tuple-element.96.refs_1_.refs_5_, bf16[256,4096]{1,0:T(8,128)(2,1)S(1)} %bitcast.31, ...), custom_call_target="tpu_custom_call" | custom-call | flops 200000000 | bytes 1024 | tf_op jit(solution)/shard_map/weight_terms/pallas_call | solution.py:422
  79.1 5.3 %project.5.refs_5_ = f32[4,256,1024]{2,1,0:T(8,128)S(1)} custom-call(bf16[1024,4096]{1,0:T(8,128)(2,1)S(1)} %bitcast.41, bf16[256,4096]{1,0:T(8,128)(2,1)S(1)} %bitcast.33, bf16[256,4096]{1,0:T(8,128)(2,1)} %collective-permute-done.3.refs_3_.refs_5_.refs_2_, bf16[256,1024]{1,0:T(8,128)(2,1)S(1)} %collective-permute-done.8.refs_6_.refs_3_, ...), custom_call_target="tpu_custom_call" | custom-call | flops 200000000 | bytes 1024 | tf_op jit(solution)/shard_map/project/pallas_call | solution.py:521
  84.4 4.7 %collective-permute-done.10.got_low.got_high = bf16[4,1024,128]{2,1,0:T(8,128)(2,1)S(1)} collective-permute-done((bf16[4,1024,128]{2,1,0:T(8,128)(2,1)S(1)}, bf16[4,1024,128]{2,1,0:T(8,128)(2,1)S(1)}, u32[]{:S(2)}, u32[]{:S(2)}) %collective-permute-start.10) | collective-permute-done | bytes 1048608 | tf_op jit(solution)/shard_map/ppermute | solution.py:560
  92.8 4.8 %weight_terms.6 = (f32[4,1024,128]{2,1,0:T(8,128)S(1)}, bf16[4,1024,128]{2,1,0:T(8,128)(2,1)S(1)}) custom-call(s32[10]{0:T(128)S(1)} %pad_add_fusion.info_ref, bf16[512,1024]{1,0:T(8,128)(2,1)S(1)} %get-tuple-element.91.refs_0_.refs_5_, bf16[512,1024]{1,0:T(8,128)(2,1)S(1)} %get-tuple-element.96.refs_1_.refs_5_, bf16[256,4096]{1,0:T(8,128)(2,1)S(1)} %bitcast.34, ...), custom_call_target="tpu_custom_call" | custom-call | flops 200000000 | bytes 1024 | tf_op jit(solution)/shard_map/weight_terms/pallas_call | solution.py:422
  99.2 5.3 %project.6.refs_5_ = f32[4,256,1024]{2,1,0:T(8,128)S(1)} custom-call(bf16[1024,4096]{1,0:T(8,128)(2,1)S(1)} %bitcast.41, bf16[256,4096]{1,0:T(8,128)(2,1)S(1)} %bitcast.36, bf16[256,4096]{1,0:T(8,128)(2,1)} %collective-permute-done.3.refs_3_.refs_5_.refs_2_, bf16[256,1024]{1,0:T(8,128)(2,1)S(1)} %collective-permute-done.11.refs_6_.refs_3_, ...), custom_call_target="tpu_custom_call" | custom-call | flops 200000000 | bytes 1024 | tf_op jit(solution)/shard_map/project/pallas_call | solution.py:521
  104.5 7.1 %collective-permute-done.13.got_low.got_high = bf16[4,1024,128]{2,1,0:T(8,128)(2,1)S(1)} collective-permute-done((bf16[4,1024,128]{2,1,0:T(8,128)(2,1)S(1)}, bf16[4,1024,128]{2,1,0:T(8,128)(2,1)S(1)}, u32[]{:S(2)}, u32[]{:S(2)}) %collective-permute-start.13) | collective-permute-done | bytes 1048608 | tf_op jit(solution)/shard_map/ppermute | solution.py:560
  113.8 2.6 %collective-permute-start.19 = (bf16[1,1024,128]{2,1,0:T(8,128)(2,1)S(1)}, bf16[1,1024,128]{2,1,0:T(8,128)(2,1)S(1)}, u32[]{:S(2)}, u32[]{:S(2)}) collective-permute-start(bf16[1,1024,128]{2,1,0:T(8,128)(2,1)S(1)} %get-tuple-element.123), channel_id=1, source_target_pairs={{0,16},{4,20},{8,24},{12,28},{16,0},{20,4},{24,8},{28,12},{1,17},{... | collective-permute-start | bytes 786440 | tf_op jit(solution)/shard_map/ppermute | solution.py:560
  116.4 4.8 %weight_terms.7 = (f32[4,1024,128]{2,1,0:T(8,128)S(1)}, bf16[4,1024,128]{2,1,0:T(8,128)(2,1)S(1)}) custom-call(s32[10]{0:T(128)S(1)} %pad_add_fusion.info_ref, bf16[512,1024]{1,0:T(8,128)(2,1)S(1)} %get-tuple-element.91.refs_0_.refs_5_, bf16[512,1024]{1,0:T(8,128)(2,1)S(1)} %get-tuple-element.96.refs_1_.refs_5_, bf16[256,4096]{1,0:T(8,128)(2,1)S(1)} %bitcast.37, ...), custom_call_target="tpu_custom_call" | custom-call | flops 200000000 | bytes 1024 | tf_op jit(solution)/shard_map/weight_terms/pallas_call | solution.py:422
  122.8 5.2 %project.7.refs_4_ = bf16[4,256,1024]{2,1,0:T(8,128)(2,1)S(1)} custom-call(bf16[1024,4096]{1,0:T(8,128)(2,1)S(1)} %bitcast.41, bf16[256,4096]{1,0:T(8,128)(2,1)S(1)} %bitcast.39, bf16[256,4096]{1,0:T(8,128)(2,1)} %collective-permute-done.3.refs_3_.refs_5_.refs_2_, bf16[256,1024]{1,0:T(8,128)(2,1)S(1)} %collective-permute-done.15.refs_6_.refs_3_, ...), custom_call_target="tpu_custom_call" | custom-call | flops 200000000 | bytes 1024 | tf_op jit(solution)/shard_map/project/pallas_call | solution.py:521
  128.0 3.9 %collective-permute-done.17.got_low.got_high = bf16[2,1024,128]{2,1,0:T(8,128)(2,1)S(1)} collective-permute-done((bf16[2,1024,128]{2,1,0:T(8,128)(2,1)S(1)}, bf16[2,1024,128]{2,1,0:T(8,128)(2,1)S(1)}, u32[]{:S(2)}, u32[]{:S(2)}) %collective-permute-start.17) | collective-permute-done | bytes 524320 | tf_op jit(solution)/shard_map/ppermute | solution.py:560
  135.7 8.9 %attention_back.2 = bf16[4,256,768]{2,1,0:T(8,128)(2,1)S(1)} custom-call(s32[10]{0:T(128)S(1)} %pad_add_fusion.info_ref, bf16[256,1536]{1,0:T(8,128)(2,1)S(1)} %copy-done.2, bf16[256,1536]{1,0:T(8,128)(2,1)S(1)} %collective-permute-done.refs_1_, bf16[256,768]{1,0:T(8,128)(2,1)S(1)} %copy-done.5, bf16[256,768]{1,0:T(8,128)(2,1)S(1)} %collective-permute-done.2.refs_3_, ...), custom_call_target="tpu_custom_call" | custom-call | flops 300000000 | bytes 1024 | tf_op jit(solution)/shard_map/attention_back/pallas_call | solution.py:336
  147.2 3.4 %collective-permute-start.20 = (bf16[1,1024,128]{2,1,0:T(8,128)(2,1)S(1)}, bf16[1,1024,128]{2,1,0:T(8,128)(2,1)S(1)}, u32[]{:S(2)}, u32[]{:S(2)}) collective-permute-start(bf16[1,1024,128]{2,1,0:T(8,128)(2,1)S(1)} %get-tuple-element.135), channel_id=1, source_target_pairs={{0,16},{4,20},{8,24},{12,28},{16,0},{20,4},{24,8},{28,12},{1,17},{... | collective-permute-start | bytes 786440 | tf_op jit(solution)/shard_map/ppermute | solution.py:560
  150.6 10.1 %attention_back.3 = bf16[4,256,768]{2,1,0:T(8,128)(2,1)S(1)} custom-call(s32[10]{0:T(128)S(1)} %pad_add_fusion.info_ref, bf16[256,1536]{1,0:T(8,128)(2,1)S(1)} %copy-done.2, bf16[256,1536]{1,0:T(8,128)(2,1)S(1)} %collective-permute-done.refs_1_, bf16[256,768]{1,0:T(8,128)(2,1)} %collective-permute-done.4.refs_2_, ...), custom_call_target="tpu_custom_call" | custom-call | flops 300000000 | bytes 1024 | tf_op jit(solution)/shard_map/attention_back/pallas_call | solution.py:336
  164.9 3.8 %collective-permute-start.25 = (bf16[2,1024,128]{2,1,0:T(8,128)(2,1)S(1)}, bf16[2,1024,128]{2,1,0:T(8,128)(2,1)S(1)}, u32[]{:S(2)}, u32[]{:S(2)}) collective-permute-start(bf16[2,1024,128]{2,1,0:T(8,128)(2,1)S(1)} %get-tuple-element.147), channel_id=1, source_target_pairs={{0,8},{4,12},{8,0},{12,4},{16,24},{20,28},{24,16},{28,20},{1,9},{5... | collective-permute-start | bytes 1572872 | tf_op jit(solution)/shard_map/ppermute | solution.py:560
  168.9 12.2 %collective-permute-done.25.got_low.got_high = bf16[2,1024,128]{2,1,0:T(8,128)(2,1)S(1)} collective-permute-done((bf16[2,1024,128]{2,1,0:T(8,128)(2,1)S(1)}, bf16[2,1024,128]{2,1,0:T(8,128)(2,1)S(1)}, u32[]{:S(2)}, u32[]{:S(2)}) %collective-permute-start.25) | collective-permute-done | bytes 524320 | tf_op jit(solution)/shard_map/ppermute | solution.py:560
  181.1 3.4 %collective-permute-done.28 = bf16[2,256,768]{2,1,0:T(8,128)(2,1)S(1)} collective-permute-done((bf16[2,256,768]{2,1,0:T(8,128)(2,1)S(1)}, bf16[2,256,768]{2,1,0:T(8,128)(2,1)S(1)}, u32[]{:S(2)}, u32[]{:S(2)}) %collective-permute-start.28) | collective-permute-done | bytes 786464 | tf_op jit(solution)/shard_map/ppermute | solution.py:557
  184.7 2.9 %collective-permute-start.26 = (bf16[1,1024,128]{2,1,0:T(8,128)(2,1)S(1)}, bf16[1,1024,128]{2,1,0:T(8,128)(2,1)S(1)}, u32[]{:S(2)}, u32[]{:S(2)}) collective-permute-start(bf16[1,1024,128]{2,1,0:T(8,128)(2,1)S(1)} %get-tuple-element.149), channel_id=1, source_target_pairs={{0,16},{4,20},{8,24},{12,28},{16,0},{20,4},{24,8},{28,12},{1,17},{... | collective-permute-start | bytes 786440 | tf_op jit(solution)/shard_map/ppermute | solution.py:560
  187.7 18.3 %collective-permute-done.26.got_ref = bf16[1,1024,128]{2,1,0:T(8,128)(2,1)S(1)} collective-permute-done((bf16[1,1024,128]{2,1,0:T(8,128)(2,1)S(1)}, bf16[1,1024,128]{2,1,0:T(8,128)(2,1)S(1)}, u32[]{:S(2)}, u32[]{:S(2)}) %collective-permute-start.26) | collective-permute-done | bytes 262176 | tf_op jit(solution)/shard_map/ppermute | solution.py:560
  206.8 4.5 %collective-permute-done.27.got_ref = bf16[1,1024,128]{2,1,0:T(8,128)(2,1)S(1)} collective-permute-done((bf16[1,1024,128]{2,1,0:T(8,128)(2,1)S(1)}, bf16[1,1024,128]{2,1,0:T(8,128)(2,1)S(1)}, u32[]{:S(2)}, u32[]{:S(2)}) %collective-permute-start.27) | collective-permute-done | bytes 262176 | tf_op jit(solution)/shard_map/ppermute | solution.py:560
  212.2 2.8 %unpack.1 = (bf16[256,4096]{1,0:T(8,128)(2,1)}, bf16[256,1024]{1,0:T(8,128)(2,1)}, bf16[256,1024]{1,0:T(8,128)(2,1)}) custom-call(s32[10]{0:T(128)S(1)} %pad_add_fusion.info_ref, bf16[256,768]{1,0:T(8,128)(2,1)S(1)} %get-tuple-element.164.refs_0_, bf16[256,768]{1,0:T(8,128)(2,1)S(1)} %get-tuple-element.171.refs_1_, ...), custom_call_target="tpu_custom_call" | custom-call | flops 200000000 | bytes 1024 | tf_op jit(solution)/shard_map/unpack/pallas_call | solution.py:142
  (92 shorter events, 38.3 us)
Async XLA Ops:
  2.7 12.2 %collective-permute-start.2 = (bf16[256,768]{1,0:T(8,128)(2,1)}, bf16[256,768]{1,0:T(8,128)(2,1)S(1)}, u32[]{:S(2)}, u32[]{:S(2)}) collective-permute-start(bf16[256,768]{1,0:T(8,128)(2,1)} %get-tuple-element.90), channel_id=1, source_target_pairs={{0,3},{1,2},{2,1},{3,0},{4,7},{5,6},{6,5},{7,4},{8,11},{9,10},{10,... | collective-permute-start | bytes 1179656 | tf_op jit(solution)/shard_map/ppermute | solution.py:557
  5.1 18.3 %collective-permute-start.1 = (bf16[256,768]{1,0:T(8,128)(2,1)}, bf16[256,768]{1,0:T(8,128)(2,1)S(1)}, u32[]{:S(2)}, u32[]{:S(2)}) collective-permute-start(bf16[256,768]{1,0:T(8,128)(2,1)} %get-tuple-element.83), channel_id=1, source_target_pairs={{0,2},{1,3},{2,0},{3,1},{4,6},{5,7},{6,4},{7,5},{8,10},{9,11},{10,... | collective-permute-start | bytes 1179656 | tf_op jit(solution)/shard_map/ppermute | solution.py:557
  8.8 19.6 %copy-start.6 = (s32[1,8]{1,0:T(1,128)S(1)}, s32[1,8]{1,0:T(1,128)}, u32[]{:S(2)}) copy-start(s32[1,8]{1,0:T(1,128)} %param.11) | copy-start | bytes 100
  24.2 13.8 %collective-permute-start.3 = (bf16[256,4096]{1,0:T(8,128)(2,1)S(1)}, bf16[256,4096]{1,0:T(8,128)(2,1)}, u32[]{:S(2)}, u32[]{:S(2)}) collective-permute-start(bf16[256,4096]{1,0:T(8,128)(2,1)S(1)} %bitcast.27), channel_id=1, source_target_pairs={{0,1},{1,0},{2,3},{3,2},{4,5},{5,4},{6,7},{7,6},{8,9},{9,8},{10,11... | collective-permute-start | bytes 6291464 | tf_op jit(solution)/shard_map/ppermute | solution.py:557
  24.2 5.1 %collective-permute-start = (bf16[256,1536]{1,0:T(8,128)(2,1)}, bf16[256,1536]{1,0:T(8,128)(2,1)S(1)}, u32[]{:S(2)}, u32[]{:S(2)}) collective-permute-start(bf16[256,1536]{1,0:T(8,128)(2,1)} %get-tuple-element.89), channel_id=1, source_target_pairs={{0,1},{1,0},{2,3},{3,2},{4,5},{5,4},{6,7},{7,6},{8,9},{9,8},{10,11... | collective-permute-start | bytes 2359304 | tf_op jit(solution)/shard_map/ppermute | solution.py:557
  24.7 13.4 %collective-permute-start.4 = (bf16[256,768]{1,0:T(8,128)(2,1)}, bf16[256,768]{1,0:T(8,128)(2,1)}, u32[]{:S(2)}, u32[]{:S(2)}) collective-permute-start(bf16[256,768]{1,0:T(8,128)(2,1)} %get-tuple-element.94), channel_id=1, source_target_pairs={{0,2},{1,3},{2,0},{3,1},{4,6},{5,7},{6,4},{7,5},{8,10},{9,11},{10,... | collective-permute-start | bytes 1179656 | tf_op jit(solution)/shard_map/ppermute | solution.py:557
  27.0 18.2 %collective-permute-start.5 = (bf16[256,768]{1,0:T(8,128)(2,1)}, bf16[256,768]{1,0:T(8,128)(2,1)}, u32[]{:S(2)}, u32[]{:S(2)}) collective-permute-start(bf16[256,768]{1,0:T(8,128)(2,1)} %get-tuple-element.95), channel_id=1, source_target_pairs={{0,3},{1,2},{2,1},{3,0},{4,7},{5,6},{6,5},{7,4},{8,11},{9,10},{10,... | collective-permute-start | bytes 1179656 | tf_op jit(solution)/shard_map/ppermute | solution.py:557
  27.0 29.2 %collective-permute-start.6 = (bf16[256,1024]{1,0:T(8,128)(2,1)}, bf16[256,1024]{1,0:T(8,128)(2,1)S(1)}, u32[]{:S(2)}, u32[]{:S(2)}) collective-permute-start(bf16[256,1024]{1,0:T(8,128)(2,1)} %get-tuple-element.99), channel_id=1, source_target_pairs={{0,2},{1,3},{2,0},{3,1},{4,6},{5,7},{6,4},{7,5},{8,10},{9,11},{10,... | collective-permute-start | bytes 1572872 | tf_op jit(solution)/shard_map/ppermute | solution.py:557
  45.2 19.5 %slice-start = ((s8[8388608]{0:T(1024)(128)(4,1)}), s8[4194304]{0:T(1024)(128)(4,1)S(1)}, s32[]{:S(2)}) async-start(s8[8388608]{0:T(1024)(128)(4,1)} %bitcast.40), calls=%async_computation | async-start | bytes 8388608
  56.2 1.9 collective-permute-start.7
  56.3 14.3 %collective-permute-start.8 = (bf16[256,1024]{1,0:T(8,128)(2,1)S(1)}, bf16[256,1024]{1,0:T(8,128)(2,1)S(1)}, u32[]{:S(2)}, u32[]{:S(2)}) collective-permute-start(bf16[256,1024]{1,0:T(8,128)(2,1)S(1)} %copy-done.9), channel_id=1, source_target_pairs={{0,2},{1,3},{2,0},{3,1},{4,6},{5,7},{6,4},{7,5},{8,10},{9,11},{10,... | collective-permute-start | bytes 1572872 | tf_op jit(solution)/shard_map/ppermute | solution.py:557
  63.0 26.1 %collective-permute-start.10 = (bf16[4,1024,128]{2,1,0:T(8,128)(2,1)S(1)}, bf16[4,1024,128]{2,1,0:T(8,128)(2,1)S(1)}, u32[]{:S(2)}, u32[]{:S(2)}) collective-permute-start(bf16[4,1024,128]{2,1,0:T(8,128)(2,1)S(1)} %get-tuple-element.102), channel_id=1, source_target_pairs={{0,4},{4,0},{8,12},{12,8},{16,20},{20,16},{24,28},{28,24},{1,5},{5... | collective-permute-start | bytes 3145736 | tf_op jit(solution)/shard_map/ppermute | solution.py:560
  70.6 1.9 collective-permute-start.9
  70.6 18.7 %collective-permute-start.11 = (bf16[256,1024]{1,0:T(8,128)(2,1)S(1)}, bf16[256,1024]{1,0:T(8,128)(2,1)S(1)}, u32[]{:S(2)}, u32[]{:S(2)}) collective-permute-start(bf16[256,1024]{1,0:T(8,128)(2,1)S(1)} %copy-done.8), channel_id=1, source_target_pairs={{0,2},{1,3},{2,0},{3,1},{4,6},{5,7},{6,4},{7,5},{8,10},{9,11},{10,... | collective-permute-start | bytes 1572872 | tf_op jit(solution)/shard_map/ppermute | solution.py:557
  77.4 34.2 %collective-permute-start.13 = (bf16[4,1024,128]{2,1,0:T(8,128)(2,1)S(1)}, bf16[4,1024,128]{2,1,0:T(8,128)(2,1)S(1)}, u32[]{:S(2)}, u32[]{:S(2)}) collective-permute-start(bf16[4,1024,128]{2,1,0:T(8,128)(2,1)S(1)} %get-tuple-element.108), channel_id=1, source_target_pairs={{0,4},{4,0},{8,12},{12,8},{16,20},{20,16},{24,28},{28,24},{1,5},{5... | collective-permute-start | bytes 3145736 | tf_op jit(solution)/shard_map/ppermute | solution.py:560
  89.3 3.5 %collective-permute-start.12 = (bf16[256,1024]{1,0:T(8,128)(2,1)S(1)}, bf16[256,1024]{1,0:T(8,128)(2,1)S(1)}, u32[]{:S(2)}, u32[]{:S(2)}) collective-permute-start(bf16[256,1024]{1,0:T(8,128)(2,1)S(1)} %collective-permute-done.11.refs_6_.refs_3_), channel_id=1, source_target_pairs={{0,1},{1,0},{2,3},{3,2},{4,5},{5,4},{6,7},{7,6},{8,9},{9,8},{10,11... | collective-permute-start | bytes 1572872 | tf_op jit(solution)/shard_map/ppermute | solution.py:557
  89.4 22.4 %collective-permute-start.14 = (bf16[2,1024,128]{2,1,0:T(8,128)(2,1)S(1)}, bf16[2,1024,128]{2,1,0:T(8,128)(2,1)S(1)}, u32[]{:S(2)}, u32[]{:S(2)}) collective-permute-start(bf16[2,1024,128]{2,1,0:T(8,128)(2,1)S(1)} %get-tuple-element.113), channel_id=1, source_target_pairs={{0,8},{4,12},{8,0},{12,4},{16,24},{20,28},{24,16},{28,20},{1,9},{5... | collective-permute-start | bytes 1572872 | tf_op jit(solution)/shard_map/ppermute | solution.py:560
  91.2 20.7 %collective-permute-start.15 = (bf16[256,1024]{1,0:T(8,128)(2,1)S(1)}, bf16[256,1024]{1,0:T(8,128)(2,1)S(1)}, u32[]{:S(2)}, u32[]{:S(2)}) collective-permute-start(bf16[256,1024]{1,0:T(8,128)(2,1)S(1)} %copy-done.7), channel_id=1, source_target_pairs={{0,2},{1,3},{2,0},{3,1},{4,6},{5,7},{6,4},{7,5},{8,10},{9,11},{10,... | collective-permute-start | bytes 1572872 | tf_op jit(solution)/shard_map/ppermute | solution.py:557
  97.6 36.4 %collective-permute-start.18 = (bf16[4,1024,128]{2,1,0:T(8,128)(2,1)S(1)}, bf16[4,1024,128]{2,1,0:T(8,128)(2,1)S(1)}, u32[]{:S(2)}, u32[]{:S(2)}) collective-permute-start(bf16[4,1024,128]{2,1,0:T(8,128)(2,1)S(1)} %get-tuple-element.118), channel_id=1, source_target_pairs={{0,4},{4,0},{8,12},{12,8},{16,20},{20,16},{24,28},{28,24},{1,5},{5... | collective-permute-start | bytes 3145736 | tf_op jit(solution)/shard_map/ppermute | solution.py:560
  111.9 4.5 %collective-permute-start.16 = (bf16[256,1024]{1,0:T(8,128)(2,1)S(1)}, bf16[256,1024]{1,0:T(8,128)(2,1)S(1)}, u32[]{:S(2)}, u32[]{:S(2)}) collective-permute-start(bf16[256,1024]{1,0:T(8,128)(2,1)S(1)} %collective-permute-done.15.refs_6_.refs_3_), channel_id=1, source_target_pairs={{0,1},{1,0},{2,3},{3,2},{4,5},{5,4},{6,7},{7,6},{8,9},{9,8},{10,11... | collective-permute-start | bytes 1572872 | tf_op jit(solution)/shard_map/ppermute | solution.py:557
  112.0 20.0 %collective-permute-start.17 = (bf16[2,1024,128]{2,1,0:T(8,128)(2,1)S(1)}, bf16[2,1024,128]{2,1,0:T(8,128)(2,1)S(1)}, u32[]{:S(2)}, u32[]{:S(2)}) collective-permute-start(bf16[2,1024,128]{2,1,0:T(8,128)(2,1)S(1)} %get-tuple-element.121), channel_id=1, source_target_pairs={{0,8},{4,12},{8,0},{12,4},{16,24},{20,28},{24,16},{28,20},{1,9},{5... | collective-permute-start | bytes 1572872 | tf_op jit(solution)/shard_map/ppermute | solution.py:560
  113.8 20.5 %collective-permute-start.19 = (bf16[1,1024,128]{2,1,0:T(8,128)(2,1)S(1)}, bf16[1,1024,128]{2,1,0:T(8,128)(2,1)S(1)}, u32[]{:S(2)}, u32[]{:S(2)}) collective-permute-start(bf16[1,1024,128]{2,1,0:T(8,128)(2,1)S(1)} %get-tuple-element.123), channel_id=1, source_target_pairs={{0,16},{4,20},{8,24},{12,28},{16,0},{20,4},{24,8},{28,12},{1,17},{... | collective-permute-start | bytes 786440 | tf_op jit(solution)/shard_map/ppermute | solution.py:560
  121.2 42.1 %collective-permute-start.21 = (bf16[4,1024,128]{2,1,0:T(8,128)(2,1)S(1)}, bf16[4,1024,128]{2,1,0:T(8,128)(2,1)S(1)}, u32[]{:S(2)}, u32[]{:S(2)}) collective-permute-start(bf16[4,1024,128]{2,1,0:T(8,128)(2,1)S(1)} %get-tuple-element.129), channel_id=1, source_target_pairs={{0,4},{4,0},{8,12},{12,8},{16,20},{20,16},{24,28},{28,24},{1,5},{5... | collective-permute-start | bytes 3145736 | tf_op jit(solution)/shard_map/ppermute | solution.py:560
  144.6 19.6 %collective-permute-start.23 = (bf16[2,256,768]{2,1,0:T(8,128)(2,1)S(1)}, bf16[2,256,768]{2,1,0:T(8,128)(2,1)S(1)}, u32[]{:S(2)}, u32[]{:S(2)}) collective-permute-start(bf16[2,256,768]{2,1,0:T(8,128)(2,1)S(1)} %slice.57), channel_id=1, source_target_pairs={{0,2},{1,3},{2,0},{3,1},{4,6},{5,7},{6,4},{7,5},{8,10},{9,11},{10,... | collective-permute-start | bytes 2359304 | tf_op jit(solution)/shard_map/ppermute | solution.py:557
  146.4 17.7 %collective-permute-start.22 = (bf16[2,1024,128]{2,1,0:T(8,128)(2,1)S(1)}, bf16[2,1024,128]{2,1,0:T(8,128)(2,1)S(1)}, u32[]{:S(2)}, u32[]{:S(2)}) collective-permute-start(bf16[2,1024,128]{2,1,0:T(8,128)(2,1)S(1)} %get-tuple-element.137), channel_id=1, source_target_pairs={{0,8},{4,12},{8,0},{12,4},{16,24},{20,28},{24,16},{28,20},{1,9},{5... | collective-permute-start | bytes 1572872 | tf_op jit(solution)/shard_map/ppermute | solution.py:560
  147.2 15.2 %collective-permute-start.20 = (bf16[1,1024,128]{2,1,0:T(8,128)(2,1)S(1)}, bf16[1,1024,128]{2,1,0:T(8,128)(2,1)S(1)}, u32[]{:S(2)}, u32[]{:S(2)}) collective-permute-start(bf16[1,1024,128]{2,1,0:T(8,128)(2,1)S(1)} %get-tuple-element.135), channel_id=1, source_target_pairs={{0,16},{4,20},{8,24},{12,28},{16,0},{20,4},{24,8},{28,12},{1,17},{... | collective-permute-start | bytes 786440 | tf_op jit(solution)/shard_map/ppermute | solution.py:560
  164.4 4.4 %collective-permute-start.24 = (bf16[2,256,768]{2,1,0:T(8,128)(2,1)S(1)}, bf16[2,256,768]{2,1,0:T(8,128)(2,1)S(1)}, u32[]{:S(2)}, u32[]{:S(2)}) collective-permute-start(bf16[2,256,768]{2,1,0:T(8,128)(2,1)S(1)} %pad_maximum_fusion), channel_id=1, source_target_pairs={{0,1},{1,0},{2,3},{3,2},{4,5},{5,4},{6,7},{7,6},{8,9},{9,8},{10,11... | collective-permute-start | bytes 2359304 | tf_op jit(solution)/shard_map/ppermute | solution.py:557
  164.5 20.0 %collective-permute-start.28 = (bf16[2,256,768]{2,1,0:T(8,128)(2,1)S(1)}, bf16[2,256,768]{2,1,0:T(8,128)(2,1)S(1)}, u32[]{:S(2)}, u32[]{:S(2)}) collective-permute-start(bf16[2,256,768]{2,1,0:T(8,128)(2,1)S(1)} %slice.63), channel_id=1, source_target_pairs={{0,2},{1,3},{2,0},{3,1},{4,6},{5,7},{6,4},{7,5},{8,10},{9,11},{10,... | collective-permute-start | bytes 2359304 | tf_op jit(solution)/shard_map/ppermute | solution.py:557
  164.9 16.1 %collective-permute-start.25 = (bf16[2,1024,128]{2,1,0:T(8,128)(2,1)S(1)}, bf16[2,1024,128]{2,1,0:T(8,128)(2,1)S(1)}, u32[]{:S(2)}, u32[]{:S(2)}) collective-permute-start(bf16[2,1024,128]{2,1,0:T(8,128)(2,1)S(1)} %get-tuple-element.147), channel_id=1, source_target_pairs={{0,8},{4,12},{8,0},{12,4},{16,24},{20,28},{24,16},{28,20},{1,9},{5... | collective-permute-start | bytes 1572872 | tf_op jit(solution)/shard_map/ppermute | solution.py:560
  184.6 27.5 %collective-permute-start.29 = (bf16[2,256,768]{2,1,0:T(8,128)(2,1)S(1)}, bf16[2,256,768]{2,1,0:T(8,128)(2,1)S(1)}, u32[]{:S(2)}, u32[]{:S(2)}) collective-permute-start(bf16[2,256,768]{2,1,0:T(8,128)(2,1)S(1)} %pad_maximum_fusion.1), channel_id=1, source_target_pairs={{0,1},{1,0},{2,3},{3,2},{4,5},{5,4},{6,7},{7,6},{8,9},{9,8},{10,11... | collective-permute-start | bytes 2359304 | tf_op jit(solution)/shard_map/ppermute | solution.py:557
  184.7 21.3 %collective-permute-start.26 = (bf16[1,1024,128]{2,1,0:T(8,128)(2,1)S(1)}, bf16[1,1024,128]{2,1,0:T(8,128)(2,1)S(1)}, u32[]{:S(2)}, u32[]{:S(2)}) collective-permute-start(bf16[1,1024,128]{2,1,0:T(8,128)(2,1)S(1)} %get-tuple-element.149), channel_id=1, source_target_pairs={{0,16},{4,20},{8,24},{12,28},{16,0},{20,4},{24,8},{28,12},{1,17},{... | collective-permute-start | bytes 786440 | tf_op jit(solution)/shard_map/ppermute | solution.py:560
  187.6 23.8 %collective-permute-start.27 = (bf16[1,1024,128]{2,1,0:T(8,128)(2,1)S(1)}, bf16[1,1024,128]{2,1,0:T(8,128)(2,1)S(1)}, u32[]{:S(2)}, u32[]{:S(2)}) collective-permute-start(bf16[1,1024,128]{2,1,0:T(8,128)(2,1)S(1)} %get-tuple-element.154), channel_id=1, source_target_pairs={{0,16},{4,20},{8,24},{12,28},{16,0},{20,4},{24,8},{28,12},{1,17},{... | collective-permute-start | bytes 786440 | tf_op jit(solution)/shard_map/ppermute | solution.py:560
  (10 other events, 62.1 us)

commit v10 on v7

--- a/solution.py
+++ b/solution.py
@@ -272,7 +272,7 @@
             shape((wide, parts * block)),
             shape((parts, 8, GROUP * block), jnp.float32),
         ],
-        compiler_params=params(60),
+        compiler_params=params(24),
         cost_estimate=cost(2.5),
         name="attention",
     )(gate([info], token)[0], *[x for x, at in pieces])
@@ -667,9 +667,9 @@
         advance(c)
     for gp in range(1, groups):
         send_back(gp)
-    advance(last - 1)
     advance(last - 2)
     advance(last)
+    advance(last - 1)
     firsts = hand_over(0, token)
     advance(0)
     advance(last - 1)

time: 199 us -> 196 us (0.985)
  local copies, waits for them, and re-layouts: 12.2 us -> 7.4 us
  starting transfers between devices: 32.4 us -> 34.5 us
    unnamed x50 -> x38, local copies, waits for them, and re-layouts: 11.8 us -> 6.99 us
    ppermute x12, starting transfers between devices: 16.8 us -> 19.6 us  [over_dp(): return lax.ppermute(x, 'dp', [(i, i ^ d) for i in range(shares)])]
    pallas_call x2, Pallas kernels: 18.1 us -> 15.8 us  [attention(): pl.pallas_call(functools.partial(forward_kernel, parts, block, docs), gri...]
  transfers between devices with their start and end apart: 30 -> 30, of which waited for: 15 -> 16; matrix products, arithmetic and copies ran while one was open for 0% -> 0% of each run, Pallas kernels for 46% -> 47%
where the time goes in v10:
time: 196 us; the launch traced here: 195 us
  Pallas kernels  95.9 us (49%)
  waiting for transfers between devices  55.9 us (29%)
  starting transfers between devices  34.5 us (18%)
  local copies, waits for them, and re-layouts  7.4 us (4%)
    ppermute x12, waiting for transfers between devices, over_dp(): return lax.ppermute(x, 'dp', [(i, i ^ d) for i in range(shares)])  36.4 us
    pallas_call x4, Pallas kernels, project(): pl.pallas_call(functools.partial(project_kernel, parts, shares, width, le...  21.2 us
    pallas_call x4, Pallas kernels, weight_terms(): pl.pallas_call(functools.partial(weight_kernel, parts, groups, width, ord...  20.8 us
    pallas_call x2, Pallas kernels, attention_back(): pl.pallas_call(functools.partial(backward_kernel, parts, block, docs), gr...  20.5 us
    ppermute x12, starting transfers between devices, over_dp(): return lax.ppermute(x, 'dp', [(i, i ^ d) for i in range(shares)])  19.6 us
    ppermute x18, waiting for transfers between devices, over_seq(): return lax.ppermute(x, 'seq', [(i, i ^ d) for i in range(parts)])  19.5 us
    pallas_call x2, Pallas kernels, attention(): pl.pallas_call(functools.partial(forward_kernel, parts, block, docs), gri...  15.8 us
    ppermute x18, starting transfers between devices, over_seq(): return lax.ppermute(x, 'seq', [(i, i ^ d) for i in range(parts)])  14.9 us
  transfers between devices with their start and end apart: 30, of which 16 were waited for; matrix products, arithmetic and copies ran while one was open for 0% of the time, Pallas kernels for 47%

profile of v10, /device:TPU:0, one launch (start us, length us, event | category | flops | bytes accessed | tf_op | source)
XLA Modules:
  0.0 195.0 jit_solution(13652056317049967422)
XLA Ops:
  0.6 2.1 %pack.2 = (bf16[256,768]{1,0:T(8,128)(2,1)}, bf16[256,768]{1,0:T(8,128)(2,1)}) custom-call(s32[1]{0:T(128)} %bitcast.me_ref, bf16[256,4096]{1,0:T(8,128)(2,1)} %bitcast.42, bf16[256,1024]{1,0:T(8,128)(2,1)} %bitcast.50, bf16[256,1024]{1,0:T(8,128)(2,1)} %bitcast.58, bf16[256,4096]{1,0:T(8,128)(2,1)} %bitcast.43, bf16[256,1024]{1,0:T(8,128)(2,1)} %bitcast.51, ...), custom_call_target="tpu_custom_call" | custom-call | flops 200000000 | bytes 1024 | tf_op jit(solution)/shard_map/pack/pallas_call | solution.py:79
  2.7 2.4 %collective-permute-start.2 = (bf16[256,768]{1,0:T(8,128)(2,1)}, bf16[256,768]{1,0:T(8,128)(2,1)S(1)}, u32[]{:S(2)}, u32[]{:S(2)}) collective-permute-start(bf16[256,768]{1,0:T(8,128)(2,1)} %get-tuple-element.90), channel_id=1, source_target_pairs={{0,3},{1,2},{2,1},{3,0},{4,7},{5,6},{6,5},{7,4},{8,11},{9,10},{10,... | collective-permute-start | bytes 1179656 | tf_op jit(solution)/shard_map/ppermute | solution.py:558
  5.8 3.0 %pack.3 = (bf16[256,1536]{1,0:T(8,128)(2,1)}, bf16[256,1536]{1,0:T(8,128)(2,1)}, bf16[256,768]{1,0:T(8,128)(2,1)}, bf16[256,768]{1,0:T(8,128)(2,1)}) custom-call(s32[1]{0:T(128)} %bitcast.me_ref, bf16[256,4096]{1,0:T(8,128)(2,1)} %bitcast.44, bf16[256,1024]{1,0:T(8,128)(2,1)} %bitcast.52, bf16[256,1024]{1,0:T(8,128)(2,1)} %bitcast.60, ...), custom_call_target="tpu_custom_call" | custom-call | flops 200000000 | bytes 1024 | tf_op jit(solution)/shard_map/pack/pallas_call | solution.py:79
  8.8 4.0 %pack_chunks.1 = (bf16[256,1024]{1,0:T(8,128)(2,1)}, bf16[256,1024]{1,0:T(8,128)(2,1)}, bf16[256,1024]{1,0:T(8,128)(2,1)}, bf16[256,1024]{1,0:T(8,128)(2,1)}) custom-call(bf16[256,4096]{1,0:T(8,128)(2,1)} %bitcast.26), custom_call_target="tpu_custom_call" | custom-call | flops 200000000 | bytes 1024 | tf_op jit(solution)/shard_map/pack_chunks/pallas_call | solution.py:110
  12.8 2.1 %collective-permute-done.2.refs_3_ = bf16[256,768]{1,0:T(8,128)(2,1)S(1)} collective-permute-done((bf16[256,768]{1,0:T(8,128)(2,1)}, bf16[256,768]{1,0:T(8,128)(2,1)S(1)}, u32[]{:S(2)}, u32[]{:S(2)}) %collective-permute-start.2) | collective-permute-done | bytes 393248 | tf_op jit(solution)/shard_map/ppermute | solution.py:558
  15.7 7.7 %collective-permute-done.1.refs_2_ = bf16[256,768]{1,0:T(8,128)(2,1)S(1)} collective-permute-done((bf16[256,768]{1,0:T(8,128)(2,1)}, bf16[256,768]{1,0:T(8,128)(2,1)S(1)}, u32[]{:S(2)}, u32[]{:S(2)}) %collective-permute-start.1) | collective-permute-done | bytes 393248 | tf_op jit(solution)/shard_map/ppermute | solution.py:558
  24.7 2.3 %collective-permute-start.4 = (bf16[256,768]{1,0:T(8,128)(2,1)}, bf16[256,768]{1,0:T(8,128)(2,1)S(1)}, u32[]{:S(2)}, u32[]{:S(2)}) collective-permute-start(bf16[256,768]{1,0:T(8,128)(2,1)} %get-tuple-element.94), channel_id=1, source_target_pairs={{0,2},{1,3},{2,0},{3,1},{4,6},{5,7},{6,4},{7,5},{8,10},{9,11},{10,... | collective-permute-start | bytes 1179656 | tf_op jit(solution)/shard_map/ppermute | solution.py:558
  32.5 7.2 %attention.2 = (bf16[512,1024]{1,0:T(8,128)(2,1)S(1)}, f32[4,8,1024]{2,1,0:T(8,128)S(1)}) custom-call(s32[10]{0:T(128)S(1)} %pad_add_fusion.info_ref, bf16[256,1536]{1,0:T(8,128)(2,1)S(1)} %copy-done.3, bf16[256,1536]{1,0:T(8,128)(2,1)S(1)} %collective-permute-done.refs_1_, bf16[256,768]{1,0:T(8,128)(2,1)S(1)} %copy-done.11, bf16[256,768]{1,0:T(8,128)(2,1)S(1)} %copy-done.8), custom_call_target="tpu_custom_call" | custom-call | flops 2500000000 | bytes 1024 | tf_op jit(solution)/shard_map/attention/pallas_call | solution.py:250
  39.8 5.5 %collective-permute-done.5.refs_3_ = bf16[256,768]{1,0:T(8,128)(2,1)} collective-permute-done((bf16[256,768]{1,0:T(8,128)(2,1)}, bf16[256,768]{1,0:T(8,128)(2,1)}, u32[]{:S(2)}, u32[]{:S(2)}) %collective-permute-start.5) | collective-permute-done | bytes 393248 | tf_op jit(solution)/shard_map/ppermute | solution.py:558
  45.2 8.6 %attention.3 = (bf16[512,1024]{1,0:T(8,128)(2,1)S(1)}, f32[4,8,1024]{2,1,0:T(8,128)S(1)}) custom-call(s32[10]{0:T(128)S(1)} %pad_add_fusion.info_ref, bf16[256,1536]{1,0:T(8,128)(2,1)S(1)} %copy-done.3, bf16[256,1536]{1,0:T(8,128)(2,1)S(1)} %collective-permute-done.refs_1_, bf16[256,768]{1,0:T(8,128)(2,1)S(1)} %collective-permute-done.4.refs_2_, ...), custom_call_target="tpu_custom_call" | custom-call | flops 2500000000 | bytes 1024 | tf_op jit(solution)/shard_map/attention/pallas_call | solution.py:250
  53.8 2.4 %collective-permute-done.6.refs_6_.refs_3_ = bf16[256,1024]{1,0:T(8,128)(2,1)S(1)} collective-permute-done((bf16[256,1024]{1,0:T(8,128)(2,1)}, bf16[256,1024]{1,0:T(8,128)(2,1)S(1)}, u32[]{:S(2)}, u32[]{:S(2)}) %collective-permute-start.6) | collective-permute-done | bytes 524320 | tf_op jit(solution)/shard_map/ppermute | solution.py:558
  58.2 4.8 %weight_terms.4 = (f32[4,1024,128]{2,1,0:T(8,128)S(1)}, bf16[4,1024,128]{2,1,0:T(8,128)(2,1)S(1)}) custom-call(s32[10]{0:T(128)S(1)} %pad_add_fusion.info_ref, bf16[512,1024]{1,0:T(8,128)(2,1)S(1)} %get-tuple-element.91.refs_0_.refs_5_, bf16[512,1024]{1,0:T(8,128)(2,1)S(1)} %get-tuple-element.96.refs_1_.refs_5_, bf16[256,4096]{1,0:T(8,128)(2,1)S(1)} %bitcast.28, ...), custom_call_target="tpu_custom_call" | custom-call | flops 200000000 | bytes 1024 | tf_op jit(solution)/shard_map/weight_terms/pallas_call | solution.py:422
  63.0 1.8 collective-permute-start.10
  64.8 5.2 %project.4.refs_5_ = f32[4,256,1024]{2,1,0:T(8,128)S(1)} custom-call(bf16[1024,4096]{1,0:T(8,128)(2,1)S(1)} %bitcast.41, bf16[256,4096]{1,0:T(8,128)(2,1)S(1)} %bitcast.30, bf16[256,4096]{1,0:T(8,128)(2,1)} %collective-permute-done.3.refs_3_.refs_5_.refs_2_, bf16[256,1024]{1,0:T(8,128)(2,1)S(1)} %collective-permute-done.6.refs_6_.refs_3_, ...), custom_call_target="tpu_custom_call" | custom-call | flops 200000000 | bytes 1024 | tf_op jit(solution)/shard_map/project/pallas_call | solution.py:521
  72.5 4.8 %weight_terms.5 = (f32[4,1024,128]{2,1,0:T(8,128)S(1)}, bf16[4,1024,128]{2,1,0:T(8,128)(2,1)S(1)}) custom-call(s32[10]{0:T(128)S(1)} %pad_add_fusion.info_ref, bf16[512,1024]{1,0:T(8,128)(2,1)S(1)} %get-tuple-element.91.refs_0_.refs_5_, bf16[512,1024]{1,0:T(8,128)(2,1)S(1)} %get-tuple-element.96.refs_1_.refs_5_, bf16[256,4096]{1,0:T(8,128)(2,1)S(1)} %bitcast.31, ...), custom_call_target="tpu_custom_call" | custom-call | flops 200000000 | bytes 1024 | tf_op jit(solution)/shard_map/weight_terms/pallas_call | solution.py:422
  79.1 5.3 %project.5.refs_5_ = f32[4,256,1024]{2,1,0:T(8,128)S(1)} custom-call(bf16[1024,4096]{1,0:T(8,128)(2,1)S(1)} %bitcast.41, bf16[256,4096]{1,0:T(8,128)(2,1)S(1)} %bitcast.33, bf16[256,4096]{1,0:T(8,128)(2,1)} %collective-permute-done.3.refs_3_.refs_5_.refs_2_, bf16[256,1024]{1,0:T(8,128)(2,1)S(1)} %collective-permute-done.8.refs_6_.refs_3_, ...), custom_call_target="tpu_custom_call" | custom-call | flops 200000000 | bytes 1024 | tf_op jit(solution)/shard_map/project/pallas_call | solution.py:521
  84.4 3.9 %collective-permute-done.10.got_low.got_high = bf16[4,1024,128]{2,1,0:T(8,128)(2,1)S(1)} collective-permute-done((bf16[4,1024,128]{2,1,0:T(8,128)(2,1)S(1)}, bf16[4,1024,128]{2,1,0:T(8,128)(2,1)S(1)}, u32[]{:S(2)}, u32[]{:S(2)}) %collective-permute-start.10) | collective-permute-done | bytes 1048608 | tf_op jit(solution)/shard_map/ppermute | solution.py:561
  91.1 5.5 %weight_terms.6 = (f32[4,1024,128]{2,1,0:T(8,128)S(1)}, bf16[4,1024,128]{2,1,0:T(8,128)(2,1)}) custom-call(s32[10]{0:T(128)S(1)} %pad_add_fusion.info_ref, bf16[512,1024]{1,0:T(8,128)(2,1)S(1)} %get-tuple-element.91.refs_0_.refs_5_, bf16[512,1024]{1,0:T(8,128)(2,1)S(1)} %get-tuple-element.96.refs_1_.refs_5_, bf16[256,4096]{1,0:T(8,128)(2,1)S(1)} %bitcast.34, ...), custom_call_target="tpu_custom_call" | custom-call | flops 200000000 | bytes 1024 | tf_op jit(solution)/shard_map/weight_terms/pallas_call | solution.py:422
  96.6 5.3 %project.6.refs_5_ = f32[4,256,1024]{2,1,0:T(8,128)S(1)} custom-call(bf16[1024,4096]{1,0:T(8,128)(2,1)S(1)} %bitcast.41, bf16[256,4096]{1,0:T(8,128)(2,1)S(1)} %bitcast.36, bf16[256,4096]{1,0:T(8,128)(2,1)} %collective-permute-done.3.refs_3_.refs_5_.refs_2_, bf16[256,1024]{1,0:T(8,128)(2,1)S(1)} %collective-permute-done.11.refs_6_.refs_3_, ...), custom_call_target="tpu_custom_call" | custom-call | flops 200000000 | bytes 1024 | tf_op jit(solution)/shard_map/project/pallas_call | solution.py:521
  105.2 2.6 %collective-permute-start.16 = (bf16[2,1024,128]{2,1,0:T(8,128)(2,1)}, bf16[2,1024,128]{2,1,0:T(8,128)(2,1)S(1)}, u32[]{:S(2)}, u32[]{:S(2)}) collective-permute-start(bf16[2,1024,128]{2,1,0:T(8,128)(2,1)} %get-tuple-element.112), channel_id=1, source_target_pairs={{0,16},{4,20},{8,24},{12,28},{16,0},{20,4},{24,8},{28,12},{1,17},{... | collective-permute-start | bytes 1572872 | tf_op jit(solution)/shard_map/ppermute | solution.py:561
  109.4 5.5 %weight_terms.7 = (f32[4,1024,128]{2,1,0:T(8,128)S(1)}, bf16[4,1024,128]{2,1,0:T(8,128)(2,1)}) custom-call(s32[10]{0:T(128)S(1)} %pad_add_fusion.info_ref, bf16[512,1024]{1,0:T(8,128)(2,1)S(1)} %get-tuple-element.91.refs_0_.refs_5_, bf16[512,1024]{1,0:T(8,128)(2,1)S(1)} %get-tuple-element.96.refs_1_.refs_5_, bf16[256,4096]{1,0:T(8,128)(2,1)S(1)} %bitcast.37, ...), custom_call_target="tpu_custom_call" | custom-call | flops 200000000 | bytes 1024 | tf_op jit(solution)/shard_map/weight_terms/pallas_call | solution.py:422
  116.7 5.4 %project.7.refs_4_ = bf16[4,256,1024]{2,1,0:T(8,128)(2,1)S(1)} custom-call(bf16[1024,4096]{1,0:T(8,128)(2,1)S(1)} %bitcast.41, bf16[256,4096]{1,0:T(8,128)(2,1)S(1)} %bitcast.39, bf16[256,4096]{1,0:T(8,128)(2,1)} %collective-permute-done.3.refs_3_.refs_5_.refs_2_, bf16[256,1024]{1,0:T(8,128)(2,1)S(1)} %collective-permute-done.14.refs_6_.refs_3_, ...), custom_call_target="tpu_custom_call" | custom-call | flops 200000000 | bytes 1024 | tf_op jit(solution)/shard_map/project/pallas_call | solution.py:521
  123.2 9.7 %attention_back.2 = bf16[4,256,768]{2,1,0:T(8,128)(2,1)S(1)} custom-call(s32[10]{0:T(128)S(1)} %pad_add_fusion.info_ref, bf16[256,1536]{1,0:T(8,128)(2,1)S(1)} %copy-done.4, bf16[256,1536]{1,0:T(8,128)(2,1)S(1)} %copy-done.6, bf16[256,768]{1,0:T(8,128)(2,1)S(1)} %copy-done.12, bf16[256,768]{1,0:T(8,128)(2,1)S(1)} %copy-done.9, ...), custom_call_target="tpu_custom_call" | custom-call | flops 1000000000 | bytes 1024 | tf_op jit(solution)/shard_map/attention_back/pallas_call | solution.py:336
  136.2 10.7 %attention_back.3 = bf16[4,256,768]{2,1,0:T(8,128)(2,1)S(1)} custom-call(s32[10]{0:T(128)S(1)} %pad_add_fusion.info_ref, bf16[256,1536]{1,0:T(8,128)(2,1)S(1)} %copy-done.4, bf16[256,1536]{1,0:T(8,128)(2,1)S(1)} %copy-done.6, bf16[256,768]{1,0:T(8,128)(2,1)S(1)} %collective-permute-done.4.refs_2_, bf16[256,768]{1,0:T(8,128)(2,1)} %collective-permute-done.5.refs_3_, ...), custom_call_target="tpu_custom_call" | custom-call | flops 1000000000 | bytes 1024 | tf_op jit(solution)/shard_map/attention_back/pallas_call | solution.py:336
  147.0 4.8 %collective-permute-done.19.got_ref = bf16[1,1024,128]{2,1,0:T(8,128)(2,1)S(1)} collective-permute-done((bf16[1,1024,128]{2,1,0:T(8,128)(2,1)S(1)}, bf16[1,1024,128]{2,1,0:T(8,128)(2,1)S(1)}, u32[]{:S(2)}, u32[]{:S(2)}) %collective-permute-start.19) | collective-permute-done | bytes 262176 | tf_op jit(solution)/shard_map/ppermute | solution.py:561
  154.7 2.2 %collective-permute-start.26 = (bf16[2,1024,128]{2,1,0:T(8,128)(2,1)S(1)}, bf16[2,1024,128]{2,1,0:T(8,128)(2,1)S(1)}, u32[]{:S(2)}, u32[]{:S(2)}) collective-permute-start(bf16[2,1024,128]{2,1,0:T(8,128)(2,1)S(1)} %get-tuple-element.145), channel_id=1, source_target_pairs={{0,8},{4,12},{8,0},{12,4},{16,24},{20,28},{24,16},{28,20},{1,9},{5... | collective-permute-start | bytes 1572872 | tf_op jit(solution)/shard_map/ppermute | solution.py:561
  157.5 2.3 %collective-permute-start.23 = (bf16[1,1024,128]{2,1,0:T(8,128)(2,1)S(1)}, bf16[1,1024,128]{2,1,0:T(8,128)(2,1)S(1)}, u32[]{:S(2)}, u32[]{:S(2)}) collective-permute-start(bf16[1,1024,128]{2,1,0:T(8,128)(2,1)S(1)} %get-tuple-element.149), channel_id=1, source_target_pairs={{0,16},{4,20},{8,24},{12,28},{16,0},{20,4},{24,8},{28,12},{1,17},{... | collective-permute-start | bytes 786440 | tf_op jit(solution)/shard_map/ppermute | solution.py:561
  159.9 5.2 %collective-permute-done.22.got_ref = bf16[1,1024,128]{2,1,0:T(8,128)(2,1)S(1)} collective-permute-done((bf16[1,1024,128]{2,1,0:T(8,128)(2,1)S(1)}, bf16[1,1024,128]{2,1,0:T(8,128)(2,1)S(1)}, u32[]{:S(2)}, u32[]{:S(2)}) %collective-permute-start.22) | collective-permute-done | bytes 262176 | tf_op jit(solution)/shard_map/ppermute | solution.py:561
  165.9 8.2 %collective-permute-done.23.got_ref = bf16[1,1024,128]{2,1,0:T(8,128)(2,1)S(1)} collective-permute-done((bf16[1,1024,128]{2,1,0:T(8,128)(2,1)S(1)}, bf16[1,1024,128]{2,1,0:T(8,128)(2,1)S(1)}, u32[]{:S(2)}, u32[]{:S(2)}) %collective-permute-start.23) | collective-permute-done | bytes 262176 | tf_op jit(solution)/shard_map/ppermute | solution.py:561
  175.4 3.4 %collective-permute-start.27 = (bf16[1,1024,128]{2,1,0:T(8,128)(2,1)S(1)}, bf16[1,1024,128]{2,1,0:T(8,128)(2,1)S(1)}, u32[]{:S(2)}, u32[]{:S(2)}) collective-permute-start(bf16[1,1024,128]{2,1,0:T(8,128)(2,1)S(1)} %get-tuple-element.155), channel_id=1, source_target_pairs={{0,16},{4,20},{8,24},{12,28},{16,0},{20,4},{24,8},{28,12},{1,17},{... | collective-permute-start | bytes 786440 | tf_op jit(solution)/shard_map/ppermute | solution.py:561
  178.8 12.5 %collective-permute-done.27.got_ref = bf16[1,1024,128]{2,1,0:T(8,128)(2,1)S(1)} collective-permute-done((bf16[1,1024,128]{2,1,0:T(8,128)(2,1)S(1)}, bf16[1,1024,128]{2,1,0:T(8,128)(2,1)S(1)}, u32[]{:S(2)}, u32[]{:S(2)}) %collective-permute-start.27) | collective-permute-done | bytes 262176 | tf_op jit(solution)/shard_map/ppermute | solution.py:561
  192.2 2.8 %unpack.1 = (bf16[256,4096]{1,0:T(8,128)(2,1)}, bf16[256,1024]{1,0:T(8,128)(2,1)}, bf16[256,1024]{1,0:T(8,128)(2,1)}) custom-call(s32[10]{0:T(128)S(1)} %pad_add_fusion.info_ref, bf16[256,768]{1,0:T(8,128)(2,1)S(1)} %get-tuple-element.163.refs_0_, bf16[256,768]{1,0:T(8,128)(2,1)S(1)} %get-tuple-element.170.refs_1_, ...), custom_call_target="tpu_custom_call" | custom-call | flops 200000000 | bytes 1024 | tf_op jit(solution)/shard_map/unpack/pallas_call | solution.py:142
  (106 shorter events, 34.2 us)
Async XLA Ops:
  2.7 12.2 %collective-permute-start.2 = (bf16[256,768]{1,0:T(8,128)(2,1)}, bf16[256,768]{1,0:T(8,128)(2,1)S(1)}, u32[]{:S(2)}, u32[]{:S(2)}) collective-permute-start(bf16[256,768]{1,0:T(8,128)(2,1)} %get-tuple-element.90), channel_id=1, source_target_pairs={{0,3},{1,2},{2,1},{3,0},{4,7},{5,6},{6,5},{7,4},{8,11},{9,10},{10,... | collective-permute-start | bytes 1179656 | tf_op jit(solution)/shard_map/ppermute | solution.py:558
  5.1 18.3 %collective-permute-start.1 = (bf16[256,768]{1,0:T(8,128)(2,1)}, bf16[256,768]{1,0:T(8,128)(2,1)S(1)}, u32[]{:S(2)}, u32[]{:S(2)}) collective-permute-start(bf16[256,768]{1,0:T(8,128)(2,1)} %get-tuple-element.83), channel_id=1, source_target_pairs={{0,2},{1,3},{2,0},{3,1},{4,6},{5,7},{6,4},{7,5},{8,10},{9,11},{10,... | collective-permute-start | bytes 1179656 | tf_op jit(solution)/shard_map/ppermute | solution.py:558
  8.8 19.7 %copy-start.13 = (s32[1,8]{1,0:T(1,128)S(1)}, s32[1,8]{1,0:T(1,128)}, u32[]{:S(2)}) copy-start(s32[1,8]{1,0:T(1,128)} %param.11) | copy-start | bytes 100
  24.2 15.5 %collective-permute-start.3 = (bf16[256,4096]{1,0:T(8,128)(2,1)S(1)}, bf16[256,4096]{1,0:T(8,128)(2,1)}, u32[]{:S(2)}, u32[]{:S(2)}) collective-permute-start(bf16[256,4096]{1,0:T(8,128)(2,1)S(1)} %bitcast.27), channel_id=1, source_target_pairs={{0,1},{1,0},{2,3},{3,2},{4,5},{5,4},{6,7},{7,6},{8,9},{9,8},{10,11... | collective-permute-start | bytes 6291464 | tf_op jit(solution)/shard_map/ppermute | solution.py:558
  24.2 5.1 %collective-permute-start = (bf16[256,1536]{1,0:T(8,128)(2,1)}, bf16[256,1536]{1,0:T(8,128)(2,1)S(1)}, u32[]{:S(2)}, u32[]{:S(2)}) collective-permute-start(bf16[256,1536]{1,0:T(8,128)(2,1)} %get-tuple-element.89), channel_id=1, source_target_pairs={{0,1},{1,0},{2,3},{3,2},{4,5},{5,4},{6,7},{7,6},{8,9},{9,8},{10,11... | collective-permute-start | bytes 2359304 | tf_op jit(solution)/shard_map/ppermute | solution.py:558
  24.7 15.0 %collective-permute-start.4 = (bf16[256,768]{1,0:T(8,128)(2,1)}, bf16[256,768]{1,0:T(8,128)(2,1)S(1)}, u32[]{:S(2)}, u32[]{:S(2)}) collective-permute-start(bf16[256,768]{1,0:T(8,128)(2,1)} %get-tuple-element.94), channel_id=1, source_target_pairs={{0,2},{1,3},{2,0},{3,1},{4,6},{5,7},{6,4},{7,5},{8,10},{9,11},{10,... | collective-permute-start | bytes 1179656 | tf_op jit(solution)/shard_map/ppermute | solution.py:558
  27.0 18.2 %collective-permute-start.5 = (bf16[256,768]{1,0:T(8,128)(2,1)}, bf16[256,768]{1,0:T(8,128)(2,1)}, u32[]{:S(2)}, u32[]{:S(2)}) collective-permute-start(bf16[256,768]{1,0:T(8,128)(2,1)} %get-tuple-element.95), channel_id=1, source_target_pairs={{0,3},{1,2},{2,1},{3,0},{4,7},{5,6},{6,5},{7,4},{8,11},{9,10},{10,... | collective-permute-start | bytes 1179656 | tf_op jit(solution)/shard_map/ppermute | solution.py:558
  27.0 29.2 %collective-permute-start.6 = (bf16[256,1024]{1,0:T(8,128)(2,1)}, bf16[256,1024]{1,0:T(8,128)(2,1)S(1)}, u32[]{:S(2)}, u32[]{:S(2)}) collective-permute-start(bf16[256,1024]{1,0:T(8,128)(2,1)} %get-tuple-element.99), channel_id=1, source_target_pairs={{0,2},{1,3},{2,0},{3,1},{4,6},{5,7},{6,4},{7,5},{8,10},{9,11},{10,... | collective-permute-start | bytes 1572872 | tf_op jit(solution)/shard_map/ppermute | solution.py:558
  45.2 19.6 %slice-start = ((s8[8388608]{0:T(1024)(128)(4,1)}), s8[4194304]{0:T(1024)(128)(4,1)S(1)}, s32[]{:S(2)}) async-start(s8[8388608]{0:T(1024)(128)(4,1)} %bitcast.40), calls=%async_computation | async-start | bytes 8388608
  56.3 1.9 collective-permute-start.7
  56.3 14.3 %collective-permute-start.8 = (bf16[256,1024]{1,0:T(8,128)(2,1)S(1)}, bf16[256,1024]{1,0:T(8,128)(2,1)S(1)}, u32[]{:S(2)}, u32[]{:S(2)}) collective-permute-start(bf16[256,1024]{1,0:T(8,128)(2,1)S(1)} %copy-done.16), channel_id=1, source_target_pairs={{0,2},{1,3},{2,0},{3,1},{4,6},{5,7},{6,4},{7,5},{8,10},{9,11},{10,... | collective-permute-start | bytes 1572872 | tf_op jit(solution)/shard_map/ppermute | solution.py:558
  63.0 25.3 %collective-permute-start.10 = (bf16[4,1024,128]{2,1,0:T(8,128)(2,1)S(1)}, bf16[4,1024,128]{2,1,0:T(8,128)(2,1)S(1)}, u32[]{:S(2)}, u32[]{:S(2)}) collective-permute-start(bf16[4,1024,128]{2,1,0:T(8,128)(2,1)S(1)} %get-tuple-element.101), channel_id=1, source_target_pairs={{0,8},{4,12},{8,0},{12,4},{16,24},{20,28},{24,16},{28,20},{1,9},{5... | collective-permute-start | bytes 3145736 | tf_op jit(solution)/shard_map/ppermute | solution.py:561
  70.6 1.9 collective-permute-start.9
  70.6 18.6 %collective-permute-start.11 = (bf16[256,1024]{1,0:T(8,128)(2,1)S(1)}, bf16[256,1024]{1,0:T(8,128)(2,1)S(1)}, u32[]{:S(2)}, u32[]{:S(2)}) collective-permute-start(bf16[256,1024]{1,0:T(8,128)(2,1)S(1)} %copy-done.15), channel_id=1, source_target_pairs={{0,2},{1,3},{2,0},{3,1},{4,6},{5,7},{6,4},{7,5},{8,10},{9,11},{10,... | collective-permute-start | bytes 1572872 | tf_op jit(solution)/shard_map/ppermute | solution.py:558
  77.4 25.3 %collective-permute-start.13 = (bf16[4,1024,128]{2,1,0:T(8,128)(2,1)S(1)}, bf16[4,1024,128]{2,1,0:T(8,128)(2,1)S(1)}, u32[]{:S(2)}, u32[]{:S(2)}) collective-permute-start(bf16[4,1024,128]{2,1,0:T(8,128)(2,1)S(1)} %get-tuple-element.109), channel_id=1, source_target_pairs={{0,4},{4,0},{8,12},{12,8},{16,20},{20,16},{24,28},{28,24},{1,5},{5... | collective-permute-start | bytes 3145736 | tf_op jit(solution)/shard_map/ppermute | solution.py:561
  89.2 1.9 collective-permute-start.12
  89.2 14.3 %collective-permute-start.14 = (bf16[256,1024]{1,0:T(8,128)(2,1)S(1)}, bf16[256,1024]{1,0:T(8,128)(2,1)S(1)}, u32[]{:S(2)}, u32[]{:S(2)}) collective-permute-start(bf16[256,1024]{1,0:T(8,128)(2,1)S(1)} %copy-done.14), channel_id=1, source_target_pairs={{0,2},{1,3},{2,0},{3,1},{4,6},{5,7},{6,4},{7,5},{8,10},{9,11},{10,... | collective-permute-start | bytes 1572872 | tf_op jit(solution)/shard_map/ppermute | solution.py:558
  103.5 5.8 %collective-permute-start.15 = (bf16[256,1024]{1,0:T(8,128)(2,1)S(1)}, bf16[256,1024]{1,0:T(8,128)(2,1)S(1)}, u32[]{:S(2)}, u32[]{:S(2)}) collective-permute-start(bf16[256,1024]{1,0:T(8,128)(2,1)S(1)} %collective-permute-done.14.refs_6_.refs_3_), channel_id=1, source_target_pairs={{0,1},{1,0},{2,3},{3,2},{4,5},{5,4},{6,7},{7,6},{8,9},{9,8},{10,11... | collective-permute-start | bytes 1572872 | tf_op jit(solution)/shard_map/ppermute | solution.py:558
  103.5 31.3 %collective-permute-start.18 = (bf16[4,1024,128]{2,1,0:T(8,128)(2,1)}, bf16[4,1024,128]{2,1,0:T(8,128)(2,1)S(1)}, u32[]{:S(2)}, u32[]{:S(2)}) collective-permute-start(bf16[4,1024,128]{2,1,0:T(8,128)(2,1)} %get-tuple-element.117), channel_id=1, source_target_pairs={{0,4},{4,0},{8,12},{12,8},{16,20},{20,16},{24,28},{28,24},{1,5},{5... | collective-permute-start | bytes 3145736 | tf_op jit(solution)/shard_map/ppermute | solution.py:561
  105.2 29.4 %collective-permute-start.16 = (bf16[2,1024,128]{2,1,0:T(8,128)(2,1)}, bf16[2,1024,128]{2,1,0:T(8,128)(2,1)S(1)}, u32[]{:S(2)}, u32[]{:S(2)}) collective-permute-start(bf16[2,1024,128]{2,1,0:T(8,128)(2,1)} %get-tuple-element.112), channel_id=1, source_target_pairs={{0,16},{4,20},{8,24},{12,28},{16,0},{20,4},{24,8},{28,12},{1,17},{... | collective-permute-start | bytes 1572872 | tf_op jit(solution)/shard_map/ppermute | solution.py:561
  107.8 26.9 %collective-permute-start.17 = (bf16[2,1024,128]{2,1,0:T(8,128)(2,1)}, bf16[2,1024,128]{2,1,0:T(8,128)(2,1)S(1)}, u32[]{:S(2)}, u32[]{:S(2)}) collective-permute-start(bf16[2,1024,128]{2,1,0:T(8,128)(2,1)} %get-tuple-element.120), channel_id=1, source_target_pairs={{0,8},{4,12},{8,0},{12,4},{16,24},{20,28},{24,16},{28,20},{1,9},{5... | collective-permute-start | bytes 1572872 | tf_op jit(solution)/shard_map/ppermute | solution.py:561
  116.2 36.4 %collective-permute-start.20 = (bf16[4,1024,128]{2,1,0:T(8,128)(2,1)}, bf16[4,1024,128]{2,1,0:T(8,128)(2,1)S(1)}, u32[]{:S(2)}, u32[]{:S(2)}) collective-permute-start(bf16[4,1024,128]{2,1,0:T(8,128)(2,1)} %get-tuple-element.127), channel_id=1, source_target_pairs={{0,4},{4,0},{8,12},{12,8},{16,20},{20,16},{24,28},{28,24},{1,5},{5... | collective-permute-start | bytes 3145736 | tf_op jit(solution)/shard_map/ppermute | solution.py:561
  133.0 21.0 %collective-permute-start.24 = (bf16[2,256,768]{2,1,0:T(8,128)(2,1)S(1)}, bf16[2,256,768]{2,1,0:T(8,128)(2,1)S(1)}, u32[]{:S(2)}, u32[]{:S(2)}) collective-permute-start(bf16[2,256,768]{2,1,0:T(8,128)(2,1)S(1)} %slice.57), channel_id=1, source_target_pairs={{0,2},{1,3},{2,0},{3,1},{4,6},{5,7},{6,4},{7,5},{8,10},{9,11},{10,... | collective-permute-start | bytes 2359304 | tf_op jit(solution)/shard_map/ppermute | solution.py:558
  135.0 18.8 %collective-permute-start.21 = (bf16[2,1024,128]{2,1,0:T(8,128)(2,1)S(1)}, bf16[2,1024,128]{2,1,0:T(8,128)(2,1)S(1)}, u32[]{:S(2)}, u32[]{:S(2)}) collective-permute-start(bf16[2,1024,128]{2,1,0:T(8,128)(2,1)S(1)} %get-tuple-element.138), channel_id=1, source_target_pairs={{0,8},{4,12},{8,0},{12,4},{16,24},{20,28},{24,16},{28,20},{1,9},{5... | collective-permute-start | bytes 1572872 | tf_op jit(solution)/shard_map/ppermute | solution.py:561
  135.6 16.2 %collective-permute-start.19 = (bf16[1,1024,128]{2,1,0:T(8,128)(2,1)S(1)}, bf16[1,1024,128]{2,1,0:T(8,128)(2,1)S(1)}, u32[]{:S(2)}, u32[]{:S(2)}) collective-permute-start(bf16[1,1024,128]{2,1,0:T(8,128)(2,1)S(1)} %get-tuple-element.136), channel_id=1, source_target_pairs={{0,16},{4,20},{8,24},{12,28},{16,0},{20,4},{24,8},{28,12},{1,17},{... | collective-permute-start | bytes 786440 | tf_op jit(solution)/shard_map/ppermute | solution.py:561
  154.1 20.9 %collective-permute-start.25 = (bf16[2,256,768]{2,1,0:T(8,128)(2,1)S(1)}, bf16[2,256,768]{2,1,0:T(8,128)(2,1)S(1)}, u32[]{:S(2)}, u32[]{:S(2)}) collective-permute-start(bf16[2,256,768]{2,1,0:T(8,128)(2,1)S(1)} %pad_maximum_fusion), channel_id=1, source_target_pairs={{0,1},{1,0},{2,3},{3,2},{4,5},{5,4},{6,7},{7,6},{8,9},{9,8},{10,11... | collective-permute-start | bytes 2359304 | tf_op jit(solution)/shard_map/ppermute | solution.py:558
  154.2 20.9 %collective-permute-start.28 = (bf16[2,256,768]{2,1,0:T(8,128)(2,1)S(1)}, bf16[2,256,768]{2,1,0:T(8,128)(2,1)S(1)}, u32[]{:S(2)}, u32[]{:S(2)}) collective-permute-start(bf16[2,256,768]{2,1,0:T(8,128)(2,1)S(1)} %slice.63), channel_id=1, source_target_pairs={{0,2},{1,3},{2,0},{3,1},{4,6},{5,7},{6,4},{7,5},{8,10},{9,11},{10,... | collective-permute-start | bytes 2359304 | tf_op jit(solution)/shard_map/ppermute | solution.py:558
  154.7 20.3 %collective-permute-start.26 = (bf16[2,1024,128]{2,1,0:T(8,128)(2,1)S(1)}, bf16[2,1024,128]{2,1,0:T(8,128)(2,1)S(1)}, u32[]{:S(2)}, u32[]{:S(2)}) collective-permute-start(bf16[2,1024,128]{2,1,0:T(8,128)(2,1)S(1)} %get-tuple-element.145), channel_id=1, source_target_pairs={{0,8},{4,12},{8,0},{12,4},{16,24},{20,28},{24,16},{28,20},{1,9},{5... | collective-permute-start | bytes 1572872 | tf_op jit(solution)/shard_map/ppermute | solution.py:561
  157.0 8.1 %collective-permute-start.22 = (bf16[1,1024,128]{2,1,0:T(8,128)(2,1)S(1)}, bf16[1,1024,128]{2,1,0:T(8,128)(2,1)S(1)}, u32[]{:S(2)}, u32[]{:S(2)}) collective-permute-start(bf16[1,1024,128]{2,1,0:T(8,128)(2,1)S(1)} %get-tuple-element.132), channel_id=1, source_target_pairs={{0,4},{4,0},{8,12},{12,8},{16,20},{20,16},{24,28},{28,24},{1,5},{5... | collective-permute-start | bytes 786440 | tf_op jit(solution)/shard_map/ppermute | solution.py:561
  157.5 16.6 %collective-permute-start.23 = (bf16[1,1024,128]{2,1,0:T(8,128)(2,1)S(1)}, bf16[1,1024,128]{2,1,0:T(8,128)(2,1)S(1)}, u32[]{:S(2)}, u32[]{:S(2)}) collective-permute-start(bf16[1,1024,128]{2,1,0:T(8,128)(2,1)S(1)} %get-tuple-element.149), channel_id=1, source_target_pairs={{0,16},{4,20},{8,24},{12,28},{16,0},{20,4},{24,8},{28,12},{1,17},{... | collective-permute-start | bytes 786440 | tf_op jit(solution)/shard_map/ppermute | solution.py:561
  175.3 16.9 %collective-permute-start.29 = (bf16[2,256,768]{2,1,0:T(8,128)(2,1)S(1)}, bf16[2,256,768]{2,1,0:T(8,128)(2,1)S(1)}, u32[]{:S(2)}, u32[]{:S(2)}) collective-permute-start(bf16[2,256,768]{2,1,0:T(8,128)(2,1)S(1)} %pad_maximum_fusion.1), channel_id=1, source_target_pairs={{0,1},{1,0},{2,3},{3,2},{4,5},{5,4},{6,7},{7,6},{8,9},{9,8},{10,11... | collective-permute-start | bytes 2359304 | tf_op jit(solution)/shard_map/ppermute | solution.py:558
  175.4 16.0 %collective-permute-start.27 = (bf16[1,1024,128]{2,1,0:T(8,128)(2,1)S(1)}, bf16[1,1024,128]{2,1,0:T(8,128)(2,1)S(1)}, u32[]{:S(2)}, u32[]{:S(2)}) collective-permute-start(bf16[1,1024,128]{2,1,0:T(8,128)(2,1)S(1)} %get-tuple-element.155), channel_id=1, source_target_pairs={{0,16},{4,20},{8,24},{12,28},{16,0},{20,4},{24,8},{28,12},{1,17},{... | collective-permute-start | bytes 786440 | tf_op jit(solution)/shard_map/ppermute | solution.py:561
  (17 other events, 96.2 us)

commit v11 on v10

--- a/solution.py
+++ b/solution.py
@@ -677,10 +677,13 @@
     advance(last)
     lasts = [hand_over(gp, token) for gp in range(1, groups)]
     for _ in bits:
-        for c in range(chunks):
+        for c in range(last):
             advance(c)
     back = firsts + [x for group in lasts for x in group]
     grad_q, grad_k, grad_v = unpack(gate([info], token)[0], back, parts, groups)
+    token = grad_q
+    for _ in bits:
+        advance(last)
     return (grad_q[None], grad_k[None], grad_v[None], weight_grad)
 
 

time: 196 us -> 193 us (0.985)
  Pallas kernels: 95.9 us -> 93 us
    ppermute x12, waiting for transfers between devices: 36.4 us -> 33.6 us  [over_dp(): return lax.ppermute(x, 'dp', [(i, i ^ d) for i in range(shares)])]
where the time goes in v11:
time: 193 us; the launch traced here: 192 us
  Pallas kernels  93 us (48%)
  waiting for transfers between devices  54.4 us (28%)
  starting transfers between devices  36.1 us (19%)
  local copies, waits for them, and re-layouts  7.4 us (4%)
    ppermute x12, waiting for transfers between devices, over_dp(): return lax.ppermute(x, 'dp', [(i, i ^ d) for i in range(shares)])  33.6 us
    pallas_call x4, Pallas kernels, project(): pl.pallas_call(functools.partial(project_kernel, parts, shares, width, le...  21.2 us
    ppermute x12, starting transfers between devices, over_dp(): return lax.ppermute(x, 'dp', [(i, i ^ d) for i in range(shares)])  20.9 us
    ppermute x18, waiting for transfers between devices, over_seq(): return lax.ppermute(x, 'seq', [(i, i ^ d) for i in range(parts)])  20.9 us
    pallas_call x4, Pallas kernels, weight_terms(): pl.pallas_call(functools.partial(weight_kernel, parts, groups, width, ord...  20.8 us
    pallas_call x2, Pallas kernels, attention_back(): pl.pallas_call(functools.partial(backward_kernel, parts, block, docs), gr...  18.9 us
    ppermute x18, starting transfers between devices, over_seq(): return lax.ppermute(x, 'seq', [(i, i ^ d) for i in range(parts)])  15.2 us
    pallas_call x2, Pallas kernels, attention(): pl.pallas_call(functools.partial(forward_kernel, parts, block, docs), gri...  14.4 us
  transfers between devices with their start and end apart: 30, of which 16 were waited for; matrix products, arithmetic and copies ran while one was open for 0% of the time, Pallas kernels for 47%

profile of v11, /device:TPU:0, one launch (start us, length us, event | category | flops | bytes accessed | tf_op | source)
XLA Modules:
  0.0 192.1 jit_solution(9316680925408168963)
XLA Ops:
  0.6 2.1 %pack.2 = (bf16[256,768]{1,0:T(8,128)(2,1)}, bf16[256,768]{1,0:T(8,128)(2,1)}) custom-call(s32[1]{0:T(128)} %bitcast.me_ref, bf16[256,4096]{1,0:T(8,128)(2,1)} %bitcast.42, bf16[256,1024]{1,0:T(8,128)(2,1)} %bitcast.50, bf16[256,1024]{1,0:T(8,128)(2,1)} %bitcast.58, bf16[256,4096]{1,0:T(8,128)(2,1)} %bitcast.43, bf16[256,1024]{1,0:T(8,128)(2,1)} %bitcast.51, ...), custom_call_target="tpu_custom_call" | custom-call | flops 200000000 | bytes 1024 | tf_op jit(solution)/shard_map/pack/pallas_call | solution.py:79
  2.7 2.4 %collective-permute-start.2 = (bf16[256,768]{1,0:T(8,128)(2,1)}, bf16[256,768]{1,0:T(8,128)(2,1)S(1)}, u32[]{:S(2)}, u32[]{:S(2)}) collective-permute-start(bf16[256,768]{1,0:T(8,128)(2,1)} %get-tuple-element.90), channel_id=1, source_target_pairs={{0,3},{1,2},{2,1},{3,0},{4,7},{5,6},{6,5},{7,4},{8,11},{9,10},{10,... | collective-permute-start | bytes 1179656 | tf_op jit(solution)/shard_map/ppermute | solution.py:558
  5.8 3.0 %pack.3 = (bf16[256,1536]{1,0:T(8,128)(2,1)}, bf16[256,1536]{1,0:T(8,128)(2,1)}, bf16[256,768]{1,0:T(8,128)(2,1)}, bf16[256,768]{1,0:T(8,128)(2,1)}) custom-call(s32[1]{0:T(128)} %bitcast.me_ref, bf16[256,4096]{1,0:T(8,128)(2,1)} %bitcast.44, bf16[256,1024]{1,0:T(8,128)(2,1)} %bitcast.52, bf16[256,1024]{1,0:T(8,128)(2,1)} %bitcast.60, ...), custom_call_target="tpu_custom_call" | custom-call | flops 200000000 | bytes 1024 | tf_op jit(solution)/shard_map/pack/pallas_call | solution.py:79
  8.8 4.0 %pack_chunks.1 = (bf16[256,1024]{1,0:T(8,128)(2,1)}, bf16[256,1024]{1,0:T(8,128)(2,1)}, bf16[256,1024]{1,0:T(8,128)(2,1)}, bf16[256,1024]{1,0:T(8,128)(2,1)}) custom-call(bf16[256,4096]{1,0:T(8,128)(2,1)} %bitcast.26), custom_call_target="tpu_custom_call" | custom-call | flops 200000000 | bytes 1024 | tf_op jit(solution)/shard_map/pack_chunks/pallas_call | solution.py:110
  12.8 2.1 %collective-permute-done.2.refs_3_ = bf16[256,768]{1,0:T(8,128)(2,1)S(1)} collective-permute-done((bf16[256,768]{1,0:T(8,128)(2,1)}, bf16[256,768]{1,0:T(8,128)(2,1)S(1)}, u32[]{:S(2)}, u32[]{:S(2)}) %collective-permute-start.2) | collective-permute-done | bytes 393248 | tf_op jit(solution)/shard_map/ppermute | solution.py:558
  15.7 7.7 %collective-permute-done.1.refs_2_ = bf16[256,768]{1,0:T(8,128)(2,1)S(1)} collective-permute-done((bf16[256,768]{1,0:T(8,128)(2,1)}, bf16[256,768]{1,0:T(8,128)(2,1)S(1)}, u32[]{:S(2)}, u32[]{:S(2)}) %collective-permute-start.1) | collective-permute-done | bytes 393248 | tf_op jit(solution)/shard_map/ppermute | solution.py:558
  24.7 2.3 %collective-permute-start.4 = (bf16[256,768]{1,0:T(8,128)(2,1)}, bf16[256,768]{1,0:T(8,128)(2,1)S(1)}, u32[]{:S(2)}, u32[]{:S(2)}) collective-permute-start(bf16[256,768]{1,0:T(8,128)(2,1)} %get-tuple-element.94), channel_id=1, source_target_pairs={{0,2},{1,3},{2,0},{3,1},{4,6},{5,7},{6,4},{7,5},{8,10},{9,11},{10,... | collective-permute-start | bytes 1179656 | tf_op jit(solution)/shard_map/ppermute | solution.py:558
  32.5 6.6 %attention.2 = (bf16[512,1024]{1,0:T(8,128)(2,1)S(1)}, f32[4,8,1024]{2,1,0:T(8,128)S(1)}) custom-call(s32[10]{0:T(128)S(1)} %pad_add_fusion.info_ref, bf16[256,1536]{1,0:T(8,128)(2,1)S(1)} %copy-done.3, bf16[256,1536]{1,0:T(8,128)(2,1)S(1)} %collective-permute-done.refs_1_, bf16[256,768]{1,0:T(8,128)(2,1)S(1)} %copy-done.11, bf16[256,768]{1,0:T(8,128)(2,1)S(1)} %copy-done.8), custom_call_target="tpu_custom_call" | custom-call | flops 2500000000 | bytes 1024 | tf_op jit(solution)/shard_map/attention/pallas_call | solution.py:250
  39.1 6.2 %collective-permute-done.5.refs_3_ = bf16[256,768]{1,0:T(8,128)(2,1)} collective-permute-done((bf16[256,768]{1,0:T(8,128)(2,1)}, bf16[256,768]{1,0:T(8,128)(2,1)}, u32[]{:S(2)}, u32[]{:S(2)}) %collective-permute-start.5) | collective-permute-done | bytes 393248 | tf_op jit(solution)/shard_map/ppermute | solution.py:558
  45.2 7.9 %attention.3 = (bf16[512,1024]{1,0:T(8,128)(2,1)S(1)}, f32[4,8,1024]{2,1,0:T(8,128)S(1)}) custom-call(s32[10]{0:T(128)S(1)} %pad_add_fusion.info_ref, bf16[256,1536]{1,0:T(8,128)(2,1)S(1)} %copy-done.3, bf16[256,1536]{1,0:T(8,128)(2,1)S(1)} %collective-permute-done.refs_1_, bf16[256,768]{1,0:T(8,128)(2,1)S(1)} %collective-permute-done.4.refs_2_, ...), custom_call_target="tpu_custom_call" | custom-call | flops 2500000000 | bytes 1024 | tf_op jit(solution)/shard_map/attention/pallas_call | solution.py:250
  53.1 3.1 %collective-permute-done.6.refs_6_.refs_3_ = bf16[256,1024]{1,0:T(8,128)(2,1)S(1)} collective-permute-done((bf16[256,1024]{1,0:T(8,128)(2,1)}, bf16[256,1024]{1,0:T(8,128)(2,1)S(1)}, u32[]{:S(2)}, u32[]{:S(2)}) %collective-permute-start.6) | collective-permute-done | bytes 524320 | tf_op jit(solution)/shard_map/ppermute | solution.py:558
  58.2 4.8 %weight_terms.4 = (f32[4,1024,128]{2,1,0:T(8,128)S(1)}, bf16[4,1024,128]{2,1,0:T(8,128)(2,1)S(1)}) custom-call(s32[10]{0:T(128)S(1)} %pad_add_fusion.info_ref, bf16[512,1024]{1,0:T(8,128)(2,1)S(1)} %get-tuple-element.91.refs_0_.refs_5_, bf16[512,1024]{1,0:T(8,128)(2,1)S(1)} %get-tuple-element.96.refs_1_.refs_5_, bf16[256,4096]{1,0:T(8,128)(2,1)S(1)} %bitcast.28, ...), custom_call_target="tpu_custom_call" | custom-call | flops 200000000 | bytes 1024 | tf_op jit(solution)/shard_map/weight_terms/pallas_call | solution.py:422
  63.0 1.8 collective-permute-start.10
  64.8 5.2 %project.4.refs_5_ = f32[4,256,1024]{2,1,0:T(8,128)S(1)} custom-call(bf16[1024,4096]{1,0:T(8,128)(2,1)S(1)} %bitcast.41, bf16[256,4096]{1,0:T(8,128)(2,1)S(1)} %bitcast.30, bf16[256,4096]{1,0:T(8,128)(2,1)} %collective-permute-done.3.refs_3_.refs_5_.refs_2_, bf16[256,1024]{1,0:T(8,128)(2,1)S(1)} %collective-permute-done.6.refs_6_.refs_3_, ...), custom_call_target="tpu_custom_call" | custom-call | flops 200000000 | bytes 1024 | tf_op jit(solution)/shard_map/project/pallas_call | solution.py:521
  72.5 4.8 %weight_terms.5 = (f32[4,1024,128]{2,1,0:T(8,128)S(1)}, bf16[4,1024,128]{2,1,0:T(8,128)(2,1)S(1)}) custom-call(s32[10]{0:T(128)S(1)} %pad_add_fusion.info_ref, bf16[512,1024]{1,0:T(8,128)(2,1)S(1)} %get-tuple-element.91.refs_0_.refs_5_, bf16[512,1024]{1,0:T(8,128)(2,1)S(1)} %get-tuple-element.96.refs_1_.refs_5_, bf16[256,4096]{1,0:T(8,128)(2,1)S(1)} %bitcast.31, ...), custom_call_target="tpu_custom_call" | custom-call | flops 200000000 | bytes 1024 | tf_op jit(solution)/shard_map/weight_terms/pallas_call | solution.py:422
  79.1 5.3 %project.5.refs_5_ = f32[4,256,1024]{2,1,0:T(8,128)S(1)} custom-call(bf16[1024,4096]{1,0:T(8,128)(2,1)S(1)} %bitcast.41, bf16[256,4096]{1,0:T(8,128)(2,1)S(1)} %bitcast.33, bf16[256,4096]{1,0:T(8,128)(2,1)} %collective-permute-done.3.refs_3_.refs_5_.refs_2_, bf16[256,1024]{1,0:T(8,128)(2,1)S(1)} %collective-permute-done.8.refs_6_.refs_3_, ...), custom_call_target="tpu_custom_call" | custom-call | flops 200000000 | bytes 1024 | tf_op jit(solution)/shard_map/project/pallas_call | solution.py:521
  84.4 3.9 %collective-permute-done.10.got_low.got_high = bf16[4,1024,128]{2,1,0:T(8,128)(2,1)S(1)} collective-permute-done((bf16[4,1024,128]{2,1,0:T(8,128)(2,1)S(1)}, bf16[4,1024,128]{2,1,0:T(8,128)(2,1)S(1)}, u32[]{:S(2)}, u32[]{:S(2)}) %collective-permute-start.10) | collective-permute-done | bytes 1048608 | tf_op jit(solution)/shard_map/ppermute | solution.py:561
  91.1 5.5 %weight_terms.6 = (f32[4,1024,128]{2,1,0:T(8,128)S(1)}, bf16[4,1024,128]{2,1,0:T(8,128)(2,1)}) custom-call(s32[10]{0:T(128)S(1)} %pad_add_fusion.info_ref, bf16[512,1024]{1,0:T(8,128)(2,1)S(1)} %get-tuple-element.91.refs_0_.refs_5_, bf16[512,1024]{1,0:T(8,128)(2,1)S(1)} %get-tuple-element.96.refs_1_.refs_5_, bf16[256,4096]{1,0:T(8,128)(2,1)S(1)} %bitcast.34, ...), custom_call_target="tpu_custom_call" | custom-call | flops 200000000 | bytes 1024 | tf_op jit(solution)/shard_map/weight_terms/pallas_call | solution.py:422
  96.6 5.3 %project.6.refs_5_ = f32[4,256,1024]{2,1,0:T(8,128)S(1)} custom-call(bf16[1024,4096]{1,0:T(8,128)(2,1)S(1)} %bitcast.41, bf16[256,4096]{1,0:T(8,128)(2,1)S(1)} %bitcast.36, bf16[256,4096]{1,0:T(8,128)(2,1)} %collective-permute-done.3.refs_3_.refs_5_.refs_2_, bf16[256,1024]{1,0:T(8,128)(2,1)S(1)} %collective-permute-done.11.refs_6_.refs_3_, ...), custom_call_target="tpu_custom_call" | custom-call | flops 200000000 | bytes 1024 | tf_op jit(solution)/shard_map/project/pallas_call | solution.py:521
  105.2 2.6 %collective-permute-start.16 = (bf16[2,1024,128]{2,1,0:T(8,128)(2,1)}, bf16[2,1024,128]{2,1,0:T(8,128)(2,1)S(1)}, u32[]{:S(2)}, u32[]{:S(2)}) collective-permute-start(bf16[2,1024,128]{2,1,0:T(8,128)(2,1)} %get-tuple-element.112), channel_id=1, source_target_pairs={{0,16},{4,20},{8,24},{12,28},{16,0},{20,4},{24,8},{28,12},{1,17},{... | collective-permute-start | bytes 1572872 | tf_op jit(solution)/shard_map/ppermute | solution.py:561
  109.4 5.5 %weight_terms.7 = (f32[4,1024,128]{2,1,0:T(8,128)S(1)}, bf16[4,1024,128]{2,1,0:T(8,128)(2,1)}) custom-call(s32[10]{0:T(128)S(1)} %pad_add_fusion.info_ref, bf16[512,1024]{1,0:T(8,128)(2,1)S(1)} %get-tuple-element.91.refs_0_.refs_5_, bf16[512,1024]{1,0:T(8,128)(2,1)S(1)} %get-tuple-element.96.refs_1_.refs_5_, bf16[256,4096]{1,0:T(8,128)(2,1)S(1)} %bitcast.37, ...), custom_call_target="tpu_custom_call" | custom-call | flops 200000000 | bytes 1024 | tf_op jit(solution)/shard_map/weight_terms/pallas_call | solution.py:422
  116.7 5.4 %project.7.refs_4_ = bf16[4,256,1024]{2,1,0:T(8,128)(2,1)S(1)} custom-call(bf16[1024,4096]{1,0:T(8,128)(2,1)S(1)} %bitcast.41, bf16[256,4096]{1,0:T(8,128)(2,1)S(1)} %bitcast.39, bf16[256,4096]{1,0:T(8,128)(2,1)} %collective-permute-done.3.refs_3_.refs_5_.refs_2_, bf16[256,1024]{1,0:T(8,128)(2,1)S(1)} %collective-permute-done.14.refs_6_.refs_3_, ...), custom_call_target="tpu_custom_call" | custom-call | flops 200000000 | bytes 1024 | tf_op jit(solution)/shard_map/project/pallas_call | solution.py:521
  123.2 8.9 %attention_back.2 = bf16[4,256,768]{2,1,0:T(8,128)(2,1)S(1)} custom-call(s32[10]{0:T(128)S(1)} %pad_add_fusion.info_ref, bf16[256,1536]{1,0:T(8,128)(2,1)S(1)} %copy-done.4, bf16[256,1536]{1,0:T(8,128)(2,1)S(1)} %copy-done.6, bf16[256,768]{1,0:T(8,128)(2,1)S(1)} %copy-done.12, bf16[256,768]{1,0:T(8,128)(2,1)S(1)} %copy-done.9, ...), custom_call_target="tpu_custom_call" | custom-call | flops 1000000000 | bytes 1024 | tf_op jit(solution)/shard_map/attention_back/pallas_call | solution.py:336
  136.2 9.9 %attention_back.3 = bf16[4,256,768]{2,1,0:T(8,128)(2,1)S(1)} custom-call(s32[10]{0:T(128)S(1)} %pad_add_fusion.info_ref, bf16[256,1536]{1,0:T(8,128)(2,1)S(1)} %copy-done.4, bf16[256,1536]{1,0:T(8,128)(2,1)S(1)} %copy-done.6, bf16[256,768]{1,0:T(8,128)(2,1)S(1)} %collective-permute-done.4.refs_2_, bf16[256,768]{1,0:T(8,128)(2,1)} %collective-permute-done.5.refs_3_, ...), custom_call_target="tpu_custom_call" | custom-call | flops 1000000000 | bytes 1024 | tf_op jit(solution)/shard_map/attention_back/pallas_call | solution.py:336
  146.2 4.8 %collective-permute-done.19.got_ref = bf16[1,1024,128]{2,1,0:T(8,128)(2,1)S(1)} collective-permute-done((bf16[1,1024,128]{2,1,0:T(8,128)(2,1)S(1)}, bf16[1,1024,128]{2,1,0:T(8,128)(2,1)S(1)}, u32[]{:S(2)}, u32[]{:S(2)}) %collective-permute-start.19) | collective-permute-done | bytes 262176 | tf_op jit(solution)/shard_map/ppermute | solution.py:561
  154.2 2.8 %collective-permute-start.26 = (bf16[2,1024,128]{2,1,0:T(8,128)(2,1)S(1)}, bf16[2,1024,128]{2,1,0:T(8,128)(2,1)S(1)}, u32[]{:S(2)}, u32[]{:S(2)}) collective-permute-start(bf16[2,1024,128]{2,1,0:T(8,128)(2,1)S(1)} %get-tuple-element.145), channel_id=1, source_target_pairs={{0,8},{4,12},{8,0},{12,4},{16,24},{20,28},{24,16},{28,20},{1,9},{5... | collective-permute-start | bytes 1572872 | tf_op jit(solution)/shard_map/ppermute | solution.py:561
  157.5 2.3 %collective-permute-start.23 = (bf16[1,1024,128]{2,1,0:T(8,128)(2,1)S(1)}, bf16[1,1024,128]{2,1,0:T(8,128)(2,1)S(1)}, u32[]{:S(2)}, u32[]{:S(2)}) collective-permute-start(bf16[1,1024,128]{2,1,0:T(8,128)(2,1)S(1)} %get-tuple-element.149), channel_id=1, source_target_pairs={{0,16},{4,20},{8,24},{12,28},{16,0},{20,4},{24,8},{28,12},{1,17},{... | collective-permute-start | bytes 786440 | tf_op jit(solution)/shard_map/ppermute | solution.py:561
  159.9 5.2 %collective-permute-done.22.got_ref = bf16[1,1024,128]{2,1,0:T(8,128)(2,1)S(1)} collective-permute-done((bf16[1,1024,128]{2,1,0:T(8,128)(2,1)S(1)}, bf16[1,1024,128]{2,1,0:T(8,128)(2,1)S(1)}, u32[]{:S(2)}, u32[]{:S(2)}) %collective-permute-start.22) | collective-permute-done | bytes 262176 | tf_op jit(solution)/shard_map/ppermute | solution.py:561
  165.9 8.2 %collective-permute-done.23.got_ref = bf16[1,1024,128]{2,1,0:T(8,128)(2,1)S(1)} collective-permute-done((bf16[1,1024,128]{2,1,0:T(8,128)(2,1)S(1)}, bf16[1,1024,128]{2,1,0:T(8,128)(2,1)S(1)}, u32[]{:S(2)}, u32[]{:S(2)}) %collective-permute-start.23) | collective-permute-done | bytes 262176 | tf_op jit(solution)/shard_map/ppermute | solution.py:561
  175.4 3.4 %collective-permute-start.29 = (bf16[1,1024,128]{2,1,0:T(8,128)(2,1)S(1)}, bf16[1,1024,128]{2,1,0:T(8,128)(2,1)S(1)}, u32[]{:S(2)}, u32[]{:S(2)}) collective-permute-start(bf16[1,1024,128]{2,1,0:T(8,128)(2,1)S(1)} %get-tuple-element.154), channel_id=1, source_target_pairs={{0,16},{4,20},{8,24},{12,28},{16,0},{20,4},{24,8},{28,12},{1,17},{... | collective-permute-start | bytes 786440 | tf_op jit(solution)/shard_map/ppermute | solution.py:561
  178.9 2.8 %unpack.1 = (bf16[256,4096]{1,0:T(8,128)(2,1)}, bf16[256,1024]{1,0:T(8,128)(2,1)}, bf16[256,1024]{1,0:T(8,128)(2,1)}) custom-call(s32[10]{0:T(128)S(1)} %pad_add_fusion.info_ref, bf16[256,768]{1,0:T(8,128)(2,1)S(1)} %get-tuple-element.164.refs_0_, bf16[256,768]{1,0:T(8,128)(2,1)S(1)} %get-tuple-element.171.refs_1_, ...), custom_call_target="tpu_custom_call" | custom-call | flops 200000000 | bytes 1024 | tf_op jit(solution)/shard_map/unpack/pallas_call | solution.py:142
  181.6 9.7 %collective-permute-done.29.got_ref = bf16[1,1024,128]{2,1,0:T(8,128)(2,1)S(1)} collective-permute-done((bf16[1,1024,128]{2,1,0:T(8,128)(2,1)S(1)}, bf16[1,1024,128]{2,1,0:T(8,128)(2,1)S(1)}, u32[]{:S(2)}, u32[]{:S(2)}) %collective-permute-start.29) | collective-permute-done | bytes 262176 | tf_op jit(solution)/shard_map/ppermute | solution.py:561
  (106 shorter events, 35.3 us)
Async XLA Ops:
  2.7 12.2 %collective-permute-start.2 = (bf16[256,768]{1,0:T(8,128)(2,1)}, bf16[256,768]{1,0:T(8,128)(2,1)S(1)}, u32[]{:S(2)}, u32[]{:S(2)}) collective-permute-start(bf16[256,768]{1,0:T(8,128)(2,1)} %get-tuple-element.90), channel_id=1, source_target_pairs={{0,3},{1,2},{2,1},{3,0},{4,7},{5,6},{6,5},{7,4},{8,11},{9,10},{10,... | collective-permute-start | bytes 1179656 | tf_op jit(solution)/shard_map/ppermute | solution.py:558
  5.1 18.3 %collective-permute-start.1 = (bf16[256,768]{1,0:T(8,128)(2,1)}, bf16[256,768]{1,0:T(8,128)(2,1)S(1)}, u32[]{:S(2)}, u32[]{:S(2)}) collective-permute-start(bf16[256,768]{1,0:T(8,128)(2,1)} %get-tuple-element.83), channel_id=1, source_target_pairs={{0,2},{1,3},{2,0},{3,1},{4,6},{5,7},{6,4},{7,5},{8,10},{9,11},{10,... | collective-permute-start | bytes 1179656 | tf_op jit(solution)/shard_map/ppermute | solution.py:558
  8.8 19.7 %copy-start.13 = (s32[1,8]{1,0:T(1,128)S(1)}, s32[1,8]{1,0:T(1,128)}, u32[]{:S(2)}) copy-start(s32[1,8]{1,0:T(1,128)} %param.11) | copy-start | bytes 100
  24.2 14.8 %collective-permute-start.3 = (bf16[256,4096]{1,0:T(8,128)(2,1)S(1)}, bf16[256,4096]{1,0:T(8,128)(2,1)}, u32[]{:S(2)}, u32[]{:S(2)}) collective-permute-start(bf16[256,4096]{1,0:T(8,128)(2,1)S(1)} %bitcast.27), channel_id=1, source_target_pairs={{0,1},{1,0},{2,3},{3,2},{4,5},{5,4},{6,7},{7,6},{8,9},{9,8},{10,11... | collective-permute-start | bytes 6291464 | tf_op jit(solution)/shard_map/ppermute | solution.py:558
  24.2 5.1 %collective-permute-start = (bf16[256,1536]{1,0:T(8,128)(2,1)}, bf16[256,1536]{1,0:T(8,128)(2,1)S(1)}, u32[]{:S(2)}, u32[]{:S(2)}) collective-permute-start(bf16[256,1536]{1,0:T(8,128)(2,1)} %get-tuple-element.89), channel_id=1, source_target_pairs={{0,1},{1,0},{2,3},{3,2},{4,5},{5,4},{6,7},{7,6},{8,9},{9,8},{10,11... | collective-permute-start | bytes 2359304 | tf_op jit(solution)/shard_map/ppermute | solution.py:558
  24.7 14.4 %collective-permute-start.4 = (bf16[256,768]{1,0:T(8,128)(2,1)}, bf16[256,768]{1,0:T(8,128)(2,1)S(1)}, u32[]{:S(2)}, u32[]{:S(2)}) collective-permute-start(bf16[256,768]{1,0:T(8,128)(2,1)} %get-tuple-element.94), channel_id=1, source_target_pairs={{0,2},{1,3},{2,0},{3,1},{4,6},{5,7},{6,4},{7,5},{8,10},{9,11},{10,... | collective-permute-start | bytes 1179656 | tf_op jit(solution)/shard_map/ppermute | solution.py:558
  27.0 18.2 %collective-permute-start.5 = (bf16[256,768]{1,0:T(8,128)(2,1)}, bf16[256,768]{1,0:T(8,128)(2,1)}, u32[]{:S(2)}, u32[]{:S(2)}) collective-permute-start(bf16[256,768]{1,0:T(8,128)(2,1)} %get-tuple-element.95), channel_id=1, source_target_pairs={{0,3},{1,2},{2,1},{3,0},{4,7},{5,6},{6,5},{7,4},{8,11},{9,10},{10,... | collective-permute-start | bytes 1179656 | tf_op jit(solution)/shard_map/ppermute | solution.py:558
  27.0 29.2 %collective-permute-start.6 = (bf16[256,1024]{1,0:T(8,128)(2,1)}, bf16[256,1024]{1,0:T(8,128)(2,1)S(1)}, u32[]{:S(2)}, u32[]{:S(2)}) collective-permute-start(bf16[256,1024]{1,0:T(8,128)(2,1)} %get-tuple-element.99), channel_id=1, source_target_pairs={{0,2},{1,3},{2,0},{3,1},{4,6},{5,7},{6,4},{7,5},{8,10},{9,11},{10,... | collective-permute-start | bytes 1572872 | tf_op jit(solution)/shard_map/ppermute | solution.py:558
  45.2 19.6 %slice-start = ((s8[8388608]{0:T(1024)(128)(4,1)}), s8[4194304]{0:T(1024)(128)(4,1)S(1)}, s32[]{:S(2)}) async-start(s8[8388608]{0:T(1024)(128)(4,1)} %bitcast.40), calls=%async_computation | async-start | bytes 8388608
  56.3 1.9 collective-permute-start.7
  56.3 14.3 %collective-permute-start.8 = (bf16[256,1024]{1,0:T(8,128)(2,1)S(1)}, bf16[256,1024]{1,0:T(8,128)(2,1)S(1)}, u32[]{:S(2)}, u32[]{:S(2)}) collective-permute-start(bf16[256,1024]{1,0:T(8,128)(2,1)S(1)} %copy-done.16), channel_id=1, source_target_pairs={{0,2},{1,3},{2,0},{3,1},{4,6},{5,7},{6,4},{7,5},{8,10},{9,11},{10,... | collective-permute-start | bytes 1572872 | tf_op jit(solution)/shard_map/ppermute | solution.py:558
  63.0 25.3 %collective-permute-start.10 = (bf16[4,1024,128]{2,1,0:T(8,128)(2,1)S(1)}, bf16[4,1024,128]{2,1,0:T(8,128)(2,1)S(1)}, u32[]{:S(2)}, u32[]{:S(2)}) collective-permute-start(bf16[4,1024,128]{2,1,0:T(8,128)(2,1)S(1)} %get-tuple-element.101), channel_id=1, source_target_pairs={{0,8},{4,12},{8,0},{12,4},{16,24},{20,28},{24,16},{28,20},{1,9},{5... | collective-permute-start | bytes 3145736 | tf_op jit(solution)/shard_map/ppermute | solution.py:561
  70.6 1.9 collective-permute-start.9
  70.6 18.6 %collective-permute-start.11 = (bf16[256,1024]{1,0:T(8,128)(2,1)S(1)}, bf16[256,1024]{1,0:T(8,128)(2,1)S(1)}, u32[]{:S(2)}, u32[]{:S(2)}) collective-permute-start(bf16[256,1024]{1,0:T(8,128)(2,1)S(1)} %copy-done.15), channel_id=1, source_target_pairs={{0,2},{1,3},{2,0},{3,1},{4,6},{5,7},{6,4},{7,5},{8,10},{9,11},{10,... | collective-permute-start | bytes 1572872 | tf_op jit(solution)/shard_map/ppermute | solution.py:558
  77.4 25.3 %collective-permute-start.13 = (bf16[4,1024,128]{2,1,0:T(8,128)(2,1)S(1)}, bf16[4,1024,128]{2,1,0:T(8,128)(2,1)S(1)}, u32[]{:S(2)}, u32[]{:S(2)}) collective-permute-start(bf16[4,1024,128]{2,1,0:T(8,128)(2,1)S(1)} %get-tuple-element.109), channel_id=1, source_target_pairs={{0,4},{4,0},{8,12},{12,8},{16,20},{20,16},{24,28},{28,24},{1,5},{5... | collective-permute-start | bytes 3145736 | tf_op jit(solution)/shard_map/ppermute | solution.py:561
  89.2 1.9 collective-permute-start.12
  89.2 14.3 %collective-permute-start.14 = (bf16[256,1024]{1,0:T(8,128)(2,1)S(1)}, bf16[256,1024]{1,0:T(8,128)(2,1)S(1)}, u32[]{:S(2)}, u32[]{:S(2)}) collective-permute-start(bf16[256,1024]{1,0:T(8,128)(2,1)S(1)} %copy-done.14), channel_id=1, source_target_pairs={{0,2},{1,3},{2,0},{3,1},{4,6},{5,7},{6,4},{7,5},{8,10},{9,11},{10,... | collective-permute-start | bytes 1572872 | tf_op jit(solution)/shard_map/ppermute | solution.py:558
  103.5 5.8 %collective-permute-start.15 = (bf16[256,1024]{1,0:T(8,128)(2,1)S(1)}, bf16[256,1024]{1,0:T(8,128)(2,1)S(1)}, u32[]{:S(2)}, u32[]{:S(2)}) collective-permute-start(bf16[256,1024]{1,0:T(8,128)(2,1)S(1)} %collective-permute-done.14.refs_6_.refs_3_), channel_id=1, source_target_pairs={{0,1},{1,0},{2,3},{3,2},{4,5},{5,4},{6,7},{7,6},{8,9},{9,8},{10,11... | collective-permute-start | bytes 1572872 | tf_op jit(solution)/shard_map/ppermute | solution.py:558
  103.5 30.5 %collective-permute-start.18 = (bf16[4,1024,128]{2,1,0:T(8,128)(2,1)}, bf16[4,1024,128]{2,1,0:T(8,128)(2,1)S(1)}, u32[]{:S(2)}, u32[]{:S(2)}) collective-permute-start(bf16[4,1024,128]{2,1,0:T(8,128)(2,1)} %get-tuple-element.117), channel_id=1, source_target_pairs={{0,4},{4,0},{8,12},{12,8},{16,20},{20,16},{24,28},{28,24},{1,5},{5... | collective-permute-start | bytes 3145736 | tf_op jit(solution)/shard_map/ppermute | solution.py:561
  105.2 28.6 %collective-permute-start.16 = (bf16[2,1024,128]{2,1,0:T(8,128)(2,1)}, bf16[2,1024,128]{2,1,0:T(8,128)(2,1)S(1)}, u32[]{:S(2)}, u32[]{:S(2)}) collective-permute-start(bf16[2,1024,128]{2,1,0:T(8,128)(2,1)} %get-tuple-element.112), channel_id=1, source_target_pairs={{0,16},{4,20},{8,24},{12,28},{16,0},{20,4},{24,8},{28,12},{1,17},{... | collective-permute-start | bytes 1572872 | tf_op jit(solution)/shard_map/ppermute | solution.py:561
  107.8 26.1 %collective-permute-start.17 = (bf16[2,1024,128]{2,1,0:T(8,128)(2,1)}, bf16[2,1024,128]{2,1,0:T(8,128)(2,1)S(1)}, u32[]{:S(2)}, u32[]{:S(2)}) collective-permute-start(bf16[2,1024,128]{2,1,0:T(8,128)(2,1)} %get-tuple-element.120), channel_id=1, source_target_pairs={{0,8},{4,12},{8,0},{12,4},{16,24},{20,28},{24,16},{28,20},{1,9},{5... | collective-permute-start | bytes 1572872 | tf_op jit(solution)/shard_map/ppermute | solution.py:561
  116.2 35.6 %collective-permute-start.20 = (bf16[4,1024,128]{2,1,0:T(8,128)(2,1)}, bf16[4,1024,128]{2,1,0:T(8,128)(2,1)S(1)}, u32[]{:S(2)}, u32[]{:S(2)}) collective-permute-start(bf16[4,1024,128]{2,1,0:T(8,128)(2,1)} %get-tuple-element.127), channel_id=1, source_target_pairs={{0,4},{4,0},{8,12},{12,8},{16,20},{20,16},{24,28},{28,24},{1,5},{5... | collective-permute-start | bytes 3145736 | tf_op jit(solution)/shard_map/ppermute | solution.py:561
  132.2 21.0 %collective-permute-start.24 = (bf16[2,256,768]{2,1,0:T(8,128)(2,1)S(1)}, bf16[2,256,768]{2,1,0:T(8,128)(2,1)S(1)}, u32[]{:S(2)}, u32[]{:S(2)}) collective-permute-start(bf16[2,256,768]{2,1,0:T(8,128)(2,1)S(1)} %slice.57), channel_id=1, source_target_pairs={{0,2},{1,3},{2,0},{3,1},{4,6},{5,7},{6,4},{7,5},{8,10},{9,11},{10,... | collective-permute-start | bytes 2359304 | tf_op jit(solution)/shard_map/ppermute | solution.py:558
  134.2 18.8 %collective-permute-start.21 = (bf16[2,1024,128]{2,1,0:T(8,128)(2,1)S(1)}, bf16[2,1024,128]{2,1,0:T(8,128)(2,1)S(1)}, u32[]{:S(2)}, u32[]{:S(2)}) collective-permute-start(bf16[2,1024,128]{2,1,0:T(8,128)(2,1)S(1)} %get-tuple-element.138), channel_id=1, source_target_pairs={{0,8},{4,12},{8,0},{12,4},{16,24},{20,28},{24,16},{28,20},{1,9},{5... | collective-permute-start | bytes 1572872 | tf_op jit(solution)/shard_map/ppermute | solution.py:561
  134.8 16.2 %collective-permute-start.19 = (bf16[1,1024,128]{2,1,0:T(8,128)(2,1)S(1)}, bf16[1,1024,128]{2,1,0:T(8,128)(2,1)S(1)}, u32[]{:S(2)}, u32[]{:S(2)}) collective-permute-start(bf16[1,1024,128]{2,1,0:T(8,128)(2,1)S(1)} %get-tuple-element.136), channel_id=1, source_target_pairs={{0,16},{4,20},{8,24},{12,28},{16,0},{20,4},{24,8},{28,12},{1,17},{... | collective-permute-start | bytes 786440 | tf_op jit(solution)/shard_map/ppermute | solution.py:561
  153.3 21.7 %collective-permute-start.25 = (bf16[2,256,768]{2,1,0:T(8,128)(2,1)S(1)}, bf16[2,256,768]{2,1,0:T(8,128)(2,1)S(1)}, u32[]{:S(2)}, u32[]{:S(2)}) collective-permute-start(bf16[2,256,768]{2,1,0:T(8,128)(2,1)S(1)} %pad_maximum_fusion), channel_id=1, source_target_pairs={{0,1},{1,0},{2,3},{3,2},{4,5},{5,4},{6,7},{7,6},{8,9},{9,8},{10,11... | collective-permute-start | bytes 2359304 | tf_op jit(solution)/shard_map/ppermute | solution.py:558
  153.4 21.7 %collective-permute-start.27 = (bf16[2,256,768]{2,1,0:T(8,128)(2,1)S(1)}, bf16[2,256,768]{2,1,0:T(8,128)(2,1)S(1)}, u32[]{:S(2)}, u32[]{:S(2)}) collective-permute-start(bf16[2,256,768]{2,1,0:T(8,128)(2,1)S(1)} %slice.63), channel_id=1, source_target_pairs={{0,2},{1,3},{2,0},{3,1},{4,6},{5,7},{6,4},{7,5},{8,10},{9,11},{10,... | collective-permute-start | bytes 2359304 | tf_op jit(solution)/shard_map/ppermute | solution.py:558
  154.2 20.8 %collective-permute-start.26 = (bf16[2,1024,128]{2,1,0:T(8,128)(2,1)S(1)}, bf16[2,1024,128]{2,1,0:T(8,128)(2,1)S(1)}, u32[]{:S(2)}, u32[]{:S(2)}) collective-permute-start(bf16[2,1024,128]{2,1,0:T(8,128)(2,1)S(1)} %get-tuple-element.145), channel_id=1, source_target_pairs={{0,8},{4,12},{8,0},{12,4},{16,24},{20,28},{24,16},{28,20},{1,9},{5... | collective-permute-start | bytes 1572872 | tf_op jit(solution)/shard_map/ppermute | solution.py:561
  157.0 8.1 %collective-permute-start.22 = (bf16[1,1024,128]{2,1,0:T(8,128)(2,1)S(1)}, bf16[1,1024,128]{2,1,0:T(8,128)(2,1)S(1)}, u32[]{:S(2)}, u32[]{:S(2)}) collective-permute-start(bf16[1,1024,128]{2,1,0:T(8,128)(2,1)S(1)} %get-tuple-element.132), channel_id=1, source_target_pairs={{0,4},{4,0},{8,12},{12,8},{16,20},{20,16},{24,28},{28,24},{1,5},{5... | collective-permute-start | bytes 786440 | tf_op jit(solution)/shard_map/ppermute | solution.py:561
  157.5 16.6 %collective-permute-start.23 = (bf16[1,1024,128]{2,1,0:T(8,128)(2,1)S(1)}, bf16[1,1024,128]{2,1,0:T(8,128)(2,1)S(1)}, u32[]{:S(2)}, u32[]{:S(2)}) collective-permute-start(bf16[1,1024,128]{2,1,0:T(8,128)(2,1)S(1)} %get-tuple-element.149), channel_id=1, source_target_pairs={{0,16},{4,20},{8,24},{12,28},{16,0},{20,4},{24,8},{28,12},{1,17},{... | collective-permute-start | bytes 786440 | tf_op jit(solution)/shard_map/ppermute | solution.py:561
  175.3 3.5 %collective-permute-start.28 = (bf16[2,256,768]{2,1,0:T(8,128)(2,1)S(1)}, bf16[2,256,768]{2,1,0:T(8,128)(2,1)S(1)}, u32[]{:S(2)}, u32[]{:S(2)}) collective-permute-start(bf16[2,256,768]{2,1,0:T(8,128)(2,1)S(1)} %pad_maximum_fusion.1), channel_id=1, source_target_pairs={{0,1},{1,0},{2,3},{3,2},{4,5},{5,4},{6,7},{7,6},{8,9},{9,8},{10,11... | collective-permute-start | bytes 2359304 | tf_op jit(solution)/shard_map/ppermute | solution.py:558
  175.4 16.0 %collective-permute-start.29 = (bf16[1,1024,128]{2,1,0:T(8,128)(2,1)S(1)}, bf16[1,1024,128]{2,1,0:T(8,128)(2,1)S(1)}, u32[]{:S(2)}, u32[]{:S(2)}) collective-permute-start(bf16[1,1024,128]{2,1,0:T(8,128)(2,1)S(1)} %get-tuple-element.154), channel_id=1, source_target_pairs={{0,16},{4,20},{8,24},{12,28},{16,0},{20,4},{24,8},{28,12},{1,17},{... | collective-permute-start | bytes 786440 | tf_op jit(solution)/shard_map/ppermute | solution.py:561
  (17 other events, 96.9 us)
